TPU v7x, 32 devices: a whole 2x2x4 slice. The times are simulated.
32 devices in a mesh: grp: 2 (over x), row: 16 (over z, y, core).
Axes of the slice: x: 2, y: 2, z: 4, core: 2. Of those that a mesh axis runs over, the one named last changes fastest.
Arguments:
- green_occ: bfloat16 [2048, 1024], P(('grp', 'row')), parts along dimension 0, may hold values from -0.5 to 0.5
- green_virt: bfloat16 [2048, 1024], P(('grp', 'row')), parts along dimension 0, may hold values from -0.5 to 0.5
- coulomb3c: bfloat16 [16, 48, 128, 128], P('row'), may hold values from -1 to 1
- tile_list: int32 [16, 4, 4], P('row'), may hold values 0 or 1
- window: int32 [16, 4], replicated, may hold values from 0 to 31, as said below
Outputs:
- polar: float32 [1536, 240], P(('grp', 'row')), parts along dimension 0
There are 2 independent parts, one for each index of `grp`. A program takes and returns all parts, laid end to end along the dimension named above; an argument that names none is the same for every part. Nothing has to cross between parts.
Inputs may be any that keep to these rules, and one draw needn't show every extreme that they name: The 4 atoms of one RI atom's window are distinct; for an RI atom on row index d they are owned by row indices d - 1, d, d + 1 taken cyclically, atom a being owned by row index a // 2.
All inputs are finite; a program needn't handle non-finite values. No bound on the sum of `tile_list` on one device may be relied on, other than what follows from the above.
Results may differ from a plain program's by a relative error of at most 0.004.
Values may be sent and summed in bfloat16 or wider, within the bound.
No kernel may reach another device: no remote copies, remote signals or barrier semaphores. Data moves between devices by JAX's collectives and lax.ppermute only.
A program may use at most 128 MiB of HBM per device.

v0:
```python
import functools

import jax
import jax.numpy as jnp
from jax import lax
from jax.experimental import pallas as pl
from jax.experimental.pallas import tpu as pltpu
from jax.sharding import PartitionSpec as P

BF = jnp.bfloat16
F32 = jnp.float32
MISSING = -(1 << 20)


def dot(a, b):
    return lax.dot_general(a, b, (((1,), (0,)), ((), ())), preferred_element_type=F32)


def dot_t(a, b):
    return lax.dot_general(a, b, (((1,), (1,)), ((), ())), preferred_element_type=F32)


def iota(shape, dim):
    return lax.broadcasted_iota(jnp.int32, shape, dim)


def pick4(index, values):
    return jnp.where(
        index == 0, values[0], jnp.where(index == 1, values[1], jnp.where(index == 2, values[2], values[3]))
    )


def one_hot(shape, dim, bases):
    index = iota(shape, dim)
    position = pick4(index >> 5, bases) + (index & 31)
    return jnp.where(iota(shape, 1 - dim) == position, 1.0, 0.0).astype(BF)


def window_at(win, row):
    return [win[row, i] for i in range(4)]


def find(atoms, wanted):
    slot, there = jnp.int32(0), jnp.float32(0)
    for i in range(4):
        hit = atoms[i] == wanted
        slot = jnp.where(hit, jnp.int32(i), slot)
        there = jnp.where(hit, jnp.float32(1), there)
    return slot, there


def tile_mask(tiles, rows):
    shape = (4 * rows, 128)
    row, lane = iota(shape, 0) // rows, iota(shape, 1) >> 5
    mask = jnp.zeros(shape, F32)
    for i in range(4):
        for j in range(4):
            mask = jnp.where((row == i) & (lane == j), tiles[0, i, j].astype(F32), mask)
    return mask


def near(row, by, count):
    return lax.rem(row + by + count, count)


def column_chunk(row, count):
    return near(row, -1, count) >> 1


def prepare(count, win, tiles, occ, virt, half, g_self, g_right, g_left, far_right, far_left, xs):
    d = lax.axis_index("row")
    mine = window_at(win, d)
    funcs = half.shape[0]

    def greens(out, base, dest):
        first = column_chunk(dest, count)
        for c in range(2):
            chunk = lax.rem(first + c, count // 2)
            columns = pl.ds(pl.multiple_of(chunk * 128, 128), 128)
            out[base + 64 * c : base + 64 * c + 64, :] = occ[:, columns]
            out[base + 128 + 64 * c : base + 192 + 64 * c, :] = virt[:, columns]

    greens(g_self, 0, d)
    greens(g_right, 0, near(d, 1, count))
    greens(g_left, 0, near(d, -1, count))
    greens(far_right, funcs * 32, near(d, 2, count))
    short = tile_mask(tiles, 4)
    g_right[256:272, :] = short.astype(BF)

    mask = tile_mask(tiles, 32).astype(BF)
    left, right = near(d, -1, count) * 2, near(d, 1, count) * 2
    shape = (128, 256)
    column = iota(shape, 1)
    wanted = jnp.where(column < 128, left, right) + ((column >> 5) & 1)
    here = pick4(iota(shape, 0) >> 5, mine)
    same = (here == wanted) & ((iota(shape, 0) & 31) == (column & 31))
    select = jnp.where(same, 1.0, 0.0).astype(BF)
    for r in range(0, funcs, 4):
        block = (half[r : r + 4] * mask[None]).reshape(512, 128)
        x = dot(block, select)
        xs[0, r * 128 : r * 128 + 512, :] = x[:, :128]
        xs[1, r * 128 : r * 128 + 512, :] = x[:, 128:]
    lane = iota((funcs, 128), 1)
    for side, base, out in ((0, left, far_left), (1, right, far_right)):
        slot0, there0 = find(mine, base)
        slot1, there1 = find(mine, base + 1)
        weight = jnp.where(lane < 64, there0, there1)
        for t in range(0, 32, 2):
            parts = []
            for u in (t, t + 1):
                x0 = xs[side, pl.ds(slot0 * 32 + u, funcs, stride=128), :]
                x1 = xs[side, pl.ds(slot1 * 32 + u, funcs, stride=128), :]
                parts.append(jnp.where(lane < 64, x0, x1) * weight)
            out[t * funcs : (t + 2) * funcs, :] = jnp.concatenate(parts, axis=0).astype(BF)


def choose(count, far_rows, win, g_self, g_before, g_after, g_far, out):
    d = lax.axis_index("row")
    atoms = 2 * count
    mine = window_at(win, d)
    theirs = window_at(win, near(d, -1, count))
    row0 = near(d, -2, count) * 2
    col0 = column_chunk(d, count) * 4

    def position(atom, start):
        return lax.rem(atom - start + atoms, atoms) * 32

    def whole(base):
        blocks = []
        for c in range(2):
            at = base + 64 * c
            blocks.append(
                jnp.concatenate(
                    [
                        g_far[far_rows + at : far_rows + at + 64, :],
                        g_before[at : at + 64, :],
                        g_self[at : at + 64, :],
                        g_after[at : at + 64, :],
                    ],
                    axis=0,
                )
            )
        return jnp.concatenate(blocks, axis=1)

    occ, virt = whole(0), whole(128)
    rows_mine = [position(a, row0) for a in mine]
    rows_theirs = [position(a, row0) for a in theirs]
    columns_mine = [position(a, col0) for a in mine]
    columns_both = []
    for i in range(4):
        _, there = find(theirs, mine[i])
        columns_both.append(jnp.where(there > 0, columns_mine[i], jnp.int32(MISSING)))
    for base, rows, columns in ((0, rows_mine, columns_mine), (256, rows_theirs, columns_both)):
        left = one_hot((128, 256), 0, columns)
        x = dot_t(left, occ).astype(BF)
        out[base : base + 128, :] = dot(x, one_hot((256, 128), 1, rows)).astype(BF)
        y = dot(one_hot((128, 256), 0, rows), virt).astype(BF)
        out[base + 128 : base + 256, :] = dot(y, one_hot((256, 128), 1, columns)).astype(BF)


def frame_map(atoms_from, wanted):
    bases = []
    for w in wanted:
        slot, there = find(atoms_from, w)
        bases.append(jnp.where(there > 0, slot * 32, jnp.int32(MISSING)))
    return one_hot((128, 128), 1, bases)


def dress_own(count, win, tiles, tensor, g0, g1, polar0, flat, dressed, far_l, far_r, hs, ms):
    d = lax.axis_index("row")
    funcs = tensor.shape[1]
    mine = window_at(win, d)
    theirs = window_at(win, near(d, -1, count))
    mask = tile_mask(tiles, 32).astype(BF)
    occ = jnp.concatenate([g0[0:128, :], g1[0:128, :]], axis=0)

    def halves(i, carry):
        at = pl.multiple_of(i * 256, 256)
        m0 = tensor[0, 2 * i] * mask
        m1 = tensor[0, 2 * i + 1] * mask
        ms[pl.ds(at, 128), :] = m0.astype(F32)
        ms[pl.ds(at + 128, 128), :] = m1.astype(F32)
        h = dot(occ, jnp.concatenate([m0, m1], axis=1)).astype(BF).astype(F32)
        hs[0, pl.ds(at, 128), :] = h[:128, :128]
        hs[0, pl.ds(at + 128, 128), :] = h[:128, 128:]
        hs[1, pl.ds(at, 128), :] = h[128:, :128]
        hs[1, pl.ds(at + 128, 128), :] = h[128:, 128:]
        return carry

    lax.fori_loop(0, funcs // 2, halves, 0, unroll=2)

    def rows_at(ref, g, start):
        return [ref[g, pl.ds(start + t, funcs, stride=128), :] for t in range(8)]

    virt_a = g0[128:256, :]

    def same_frame(i, total):
        start = pl.multiple_of(i * 8, 8)
        x = dot(jnp.concatenate(rows_at(hs, 0, start), axis=0).astype(BF), virt_a).astype(BF)
        left = jnp.concatenate([x[t * funcs : (t + 1) * funcs] for t in range(8)], axis=1)
        right = jnp.concatenate(
            [ms[pl.ds(start + t, funcs, stride=128), :].astype(BF) for t in range(8)], axis=1
        )
        flat[:, pl.ds(pl.multiple_of(i * 1024, 1024), 1024)] = right
        return total + dot_t(left, right)

    polar0[...] = lax.fori_loop(0, 16, same_frame, jnp.zeros((funcs, funcs), F32))

    to_theirs = frame_map(mine, theirs)
    virts = [g0[128:256, :], g1[128:256, :]]
    slots = [find(mine, a) for a in theirs]
    for g in range(2):
        virt_b = dot(virts[g], to_theirs).astype(BF)

        def their_frame(i, carry):
            j = i >> 2
            slot = pick4(j, [s for s, _ in slots])
            there = pick4(j, [w for _, w in slots])
            start = slot * 32 + (i & 3) * 8
            rows = jnp.concatenate(rows_at(hs, g, start), axis=0) * there
            x = dot(rows.astype(BF), virt_b).astype(BF)
            block = jnp.concatenate([x[t * funcs : (t + 1) * funcs] for t in range(8)], axis=1)
            dressed[g * funcs : (g + 1) * funcs, pl.ds(pl.multiple_of(i * 1024, 1024), 1024)] = block
            return carry

        lax.fori_loop(0, 16, their_frame, 0)

        for by, out in ((-1, far_l), (1, far_r)):
            base = near(d, by, count) * 2
            pair = [base, base + 1, base, base + 1]
            two = dot(virts[g], frame_map(mine, pair)).astype(BF)
            lane = iota((128, 128), 1)
            zero = jnp.zeros((128, 128), BF)
            both = jnp.concatenate(
                [jnp.where(lane < 64, two, zero), jnp.where(lane < 64, zero, two)], axis=0
            )
            slot0, there0 = find(mine, base)
            slot1, there1 = find(mine, base + 1)

            def far_frame(i, carry):
                x0 = jnp.concatenate(rows_at(hs, g, slot0 * 32 + i * 8), axis=0) * there0
                x1 = jnp.concatenate(rows_at(hs, g, slot1 * 32 + i * 8), axis=0) * there1
                x = dot(jnp.concatenate([x0, x1], axis=1).astype(BF), both).astype(BF)
                block = jnp.concatenate([x[t * funcs : (t + 1) * funcs] for t in range(8)], axis=1)
                out[g * funcs : (g + 1) * funcs, pl.ds(pl.multiple_of(i * 1024, 1024), 1024)] = block
                return carry

            lax.fori_loop(0, 4, far_frame, 0)


def join(tensor, g_before, g0, g1, flat, dressed, far_l, far_r, from_left, from_right, own, other, up0, up1, hs, ms):
    funcs = tensor.shape[0]
    full = 2 * funcs
    short = g_before[256:272, :].astype(F32)
    mask = jnp.concatenate(
        [jnp.broadcast_to(short[4 * i : 4 * i + 1, :], (32, 128)) for i in range(4)], axis=0
    ).astype(BF)
    occ = jnp.concatenate([g0[256:384, :], g1[256:384, :]], axis=0)
    virts = [g0[384:512, :], g1[384:512, :]]

    def halves(i, carry):
        at = pl.multiple_of(i * 256, 256)
        m0 = tensor[2 * i] * mask
        m1 = tensor[2 * i + 1] * mask
        ms[pl.ds(at, 128), :] = m0.astype(F32)
        ms[pl.ds(at + 128, 128), :] = m1.astype(F32)
        h = dot(occ, jnp.concatenate([m0, m1], axis=1)).astype(BF).astype(F32)
        hs[0, pl.ds(at, 128), :] = h[:128, :128]
        hs[0, pl.ds(at + 128, 128), :] = h[:128, 128:]
        hs[1, pl.ds(at, 128), :] = h[128:, :128]
        hs[1, pl.ds(at + 128, 128), :] = h[128:, 128:]
        return carry

    lax.fori_loop(0, funcs // 2, halves, 0, unroll=2)

    def bands(i, carry):
        down, up = carry
        start = pl.multiple_of(i * 8, 8)
        columns = pl.ds(pl.multiple_of(i * 1024, 1024), 1024)
        xs = []
        for g in range(2):
            rows = [hs[g, pl.ds(start + t, funcs, stride=128), :] for t in range(8)]
            xs.append(dot(jnp.concatenate(rows, axis=0).astype(BF), virts[g]))
        left = jnp.concatenate(
            [
                jnp.concatenate([x[t * funcs : (t + 1) * funcs] for x in xs], axis=0).astype(BF)
                for t in range(8)
            ],
            axis=1,
        )
        right = jnp.concatenate(
            [ms[pl.ds(start + t, funcs, stride=128), :] for t in range(8)], axis=1
        ).astype(BF)
        return down + dot_t(dressed[:, columns], right), up + dot_t(left, flat[:, columns])

    down, up = lax.fori_loop(
        0, 16, bands, (jnp.zeros((2 * full, funcs), F32), jnp.zeros((full, full), F32))
    )

    def far(dressed_far, e):
        total = jnp.zeros((2 * full, funcs), F32)
        for i in range(4):
            rows = e[i * 8 * funcs : (i + 1) * 8 * funcs, :].astype(F32)
            right = jnp.concatenate([rows[t * funcs : (t + 1) * funcs] for t in range(8)], axis=1)
            total = total + dot_t(dressed_far[:, i * 1024 : (i + 1) * 1024], right.astype(BF))
        return total

    parts = jnp.concatenate(
        [far(far_l, from_left), down, far(far_r, from_right), jnp.zeros((2 * full, 128 - 3 * funcs), F32)], axis=1
    )
    own[...] = parts[:full]
    other[...] = parts[full:]
    up = jnp.concatenate([up, jnp.zeros((full, 128 - full), F32)], axis=1)
    up0[...] = up[:funcs]
    up1[...] = up[funcs:]


def assemble(polar0, own, recv, up0, up1, out):
    first = lax.rem(lax.axis_index("grp"), 2) == 0
    full = polar0.shape[0]
    funcs = full // 2
    a, b = own[...], recv[...]
    low, high = jnp.where(first, a, b), jnp.where(first, b, a)
    c, e = up0[...], up1[...]
    after = jnp.concatenate([jnp.where(first, c, e), jnp.where(first, e, c)], axis=0)
    pieces = []
    for i in range(3):
        part = slice(i * funcs, (i + 1) * funcs)
        if i == 2:
            pieces += [polar0[...], after[:, :full]]
        pieces += [low[:, part], high[:, part]]
    out[...] = jnp.concatenate(pieces, axis=1)


def vmem(count):
    return [pl.BlockSpec(memory_space=pltpu.VMEM)] * count


def smem(count):
    return [pl.BlockSpec(memory_space=pltpu.SMEM)] * count


def call(kernel, name, specs, outs, args, scratch=(), flops=0, moved=0):
    return pl.pallas_call(
        kernel,
        name=name,
        in_specs=specs,
        out_specs=tuple(vmem(len(outs))),
        out_shape=tuple(outs),
        scratch_shapes=list(scratch),
        compiler_params=pltpu.CompilerParams(vmem_limit_bytes=40 << 20),
        cost_estimate=pl.CostEstimate(flops=flops, bytes_accessed=moved, transcendentals=0),
    )(*args)


def body(groups, count, green_occ, green_virt, coulomb3c, tile_list, window):
    full = coulomb3c.shape[1]
    funcs = full // 2
    shape = jax.ShapeDtypeStruct
    half = lax.rem(lax.axis_index("grp"), 2)
    tensor = lax.dynamic_slice_in_dim(coulomb3c[0], half * funcs, funcs, 0)

    def send(array, row_by, swap=False):
        pairs = []
        for g in range(groups):
            for d in range(count):
                to = (g ^ 1 if swap else g) * count + (d + row_by) % count
                pairs.append((g * count + d, to))
        return lax.ppermute(array, ("grp", "row"), pairs)

    wide = send(tensor, 1)
    far_rows = funcs * 32
    g_self, g_right, g_left, far_right, far_left = call(
        functools.partial(prepare, count),
        "prepare",
        smem(2) + vmem(3),
        [
            shape((256, 128), BF),
            shape((272, 128), BF),
            shape((256, 128), BF),
            shape((far_rows + 256, 128), BF),
            shape((far_rows, 128), BF),
        ],
        (window, tile_list, green_occ, green_virt, tensor),
        [pltpu.VMEM((2, funcs * 128, 128), F32)],
        flops=2 * funcs * 128 * 128 * 256,
        moved=2 << 20,
    )
    g_before = send(g_right, 1)
    g_after = send(g_left, -1)
    from_left = send(far_right, 2)
    from_right = send(far_left, -2)
    (mine,) = call(
        functools.partial(choose, count, far_rows),
        "choose",
        smem(1) + vmem(4),
        [shape((512, 128), BF)],
        (window, g_self, g_before, g_after, from_left),
        flops=1 << 25,
        moved=1 << 19,
    )
    partner = send(mine, 0, True)
    polar0, flat, dressed, far_l, far_r = call(
        functools.partial(dress_own, count),
        "dress_own",
        smem(2) + vmem(3),
        [
            shape((full, full), F32),
            shape((full, 128 * 128), BF),
            shape((2 * full, 128 * 128), BF),
            shape((2 * full, 32 * 128), BF),
            shape((2 * full, 32 * 128), BF),
        ],
        (window, tile_list, coulomb3c, mine, partner),
        [pltpu.VMEM((2, full * 128, 128), F32), pltpu.VMEM((full * 128, 128), F32)],
        flops=1 << 31,
        moved=10 << 20,
    )
    own, other, up0, up1 = call(
        join,
        "join",
        vmem(10),
        [
            shape((full, 128), F32),
            shape((full, 128), F32),
            shape((funcs, 128), F32),
            shape((funcs, 128), F32),
        ],
        (wide, g_before, mine, partner, flat, dressed, far_l, far_r, from_left, from_right),
        [pltpu.VMEM((2, funcs * 128, 128), F32), pltpu.VMEM((funcs * 128, 128), F32)],
        flops=1 << 30,
        moved=8 << 20,
    )
    recv = send(other, 0, True)
    after0 = send(up0, -1)
    after1 = send(up1, -1, True)
    (out,) = call(
        assemble,
        "assemble",
        vmem(5),
        [shape((full, 5 * full), F32)],
        (polar0, own, recv, after0, after1),
        moved=1 << 17,
    )
    return out


def solution(mesh):
    placed = (
        P(("grp", "row"), None),
        P(("grp", "row"), None),
        P("row", None, None, None),
        P("row", None, None),
        P(),
    )
    return jax.shard_map(
        functools.partial(body, mesh.shape["grp"], mesh.shape["row"]),
        mesh=mesh,
        in_specs=placed,
        out_specs=P(("grp", "row"), None),
        check_vma=False,
    )
```

profile of v0, /device:TPU:0, one launch (start us, length us, event | category | flops | bytes accessed | tf_op | source)
XLA Modules:
  0.0 67.8 jit_solution(13812408165711306109)
XLA Ops:
  0.0 0.0 copy-start.4
  0.0 0.0 copy-start.3
  0.0 0.0 copy-start.2
  0.0 0.0 copy-start.1
  0.0 0.0 copy-start
  0.0 1.3 %dynamic-slice_bitcast_fusion.half = bf16[24,128,128]{2,1,0:T(8,128)(2,1)S(1)} fusion(bf16[1,48,128,128]{3,2,1,0:T(8,128)(2,1)} %tensor.1, s32[]{:T(128)S(6)} %select_n.3), kind=kLoop, calls=%fused_computation | loop fusion | bytes 1572868 | tf_op jit(solution)/shard_map/dynamic_slice | solution.py:361
  1.3 0.5 collective-permute-start.4
  1.9 0.0 copy-done.4
  1.9 0.1 copy.8.win
  2.0 0.0 copy-done.3
  2.0 0.0 copy-done.2
  2.0 0.0 copy-done.1
  2.0 2.4 %prepare.1 = (bf16[256,128]{1,0:T(8,128)(2,1)S(1)}, bf16[272,128]{1,0:T(8,128)(2,1)S(1)}, bf16[256,128]{1,0:T(8,128)(2,1)S(1)}, bf16[1024,128]{1,0:T(8,128)(2,1)S(1)}, bf16[768,128]{1,0:T(8,128)(2,1)S(1)}) custom-call(s32[16,4]{1,0:T(8,128)S(1)} %copy.8.win, s32[1,4,4]{2,1,0:T(4,128)S(1)} %copy-done.3, bf16[64,1024]{1,0:T(8,128)(2,1)S(1)} %copy-done.1, ...), custom_call_target="tpu_custom_call" | custom-call | flops 201326592 | bytes 2097152 | tf_op jit(solution)/shard_map/prepare/pallas_call | solution.py:344
  4.4 2.6 %collective-permute-start.2 = (bf16[1024,128]{1,0:T(8,128)(2,1)S(1)}, bf16[1024,128]{1,0:T(8,128)(2,1)S(1)}, u32[]{:S(2)}, u32[]{:S(2)}) collective-permute-start(bf16[1024,128]{1,0:T(8,128)(2,1)S(1)} %get-tuple-element.22), channel_id=1, source_target_pairs={{0,2},{1,3},{2,4},{3,5},{4,6},{5,7},{6,8},{7,9},{8,10},{9,11},{10,... | collective-permute-start | bytes 786440 | tf_op jit(solution)/shard_map/ppermute | solution.py:369
  7.0 1.3 %collective-permute-start = (bf16[272,128]{1,0:T(8,128)(2,1)S(1)}, bf16[272,128]{1,0:T(8,128)(2,1)S(1)}, u32[]{:S(2)}, u32[]{:S(2)}) collective-permute-start(bf16[272,128]{1,0:T(8,128)(2,1)S(1)} %get-tuple-element.20), channel_id=1, source_target_pairs={{0,1},{1,2},{2,3},{3,4},{4,5},{5,6},{6,7},{7,8},{8,9},{9,10},{10,1... | collective-permute-start | bytes 208904 | tf_op jit(solution)/shard_map/ppermute | solution.py:369
  8.3 3.1 %collective-permute-start.1 = (bf16[256,128]{1,0:T(8,128)(2,1)S(1)}, bf16[256,128]{1,0:T(8,128)(2,1)S(1)}, u32[]{:S(2)}, u32[]{:S(2)}) collective-permute-start(bf16[256,128]{1,0:T(8,128)(2,1)S(1)} %get-tuple-element.21), channel_id=1, source_target_pairs={{0,15},{1,0},{2,1},{3,2},{4,3},{5,4},{6,5},{7,6},{8,7},{9,8},{10,9... | collective-permute-start | bytes 196616 | tf_op jit(solution)/shard_map/ppermute | solution.py:369
  11.4 1.9 %collective-permute-done.1.g_after = bf16[256,128]{1,0:T(8,128)(2,1)S(1)} collective-permute-done((bf16[256,128]{1,0:T(8,128)(2,1)S(1)}, bf16[256,128]{1,0:T(8,128)(2,1)S(1)}, u32[]{:S(2)}, u32[]{:S(2)}) %collective-permute-start.1) | collective-permute-done | bytes 65568 | tf_op jit(solution)/shard_map/ppermute | solution.py:369
  13.3 9.7 %collective-permute-done.g_before = bf16[272,128]{1,0:T(8,128)(2,1)S(1)} collective-permute-done((bf16[272,128]{1,0:T(8,128)(2,1)S(1)}, bf16[272,128]{1,0:T(8,128)(2,1)S(1)}, u32[]{:S(2)}, u32[]{:S(2)}) %collective-permute-start) | collective-permute-done | bytes 69664 | tf_op jit(solution)/shard_map/ppermute | solution.py:369
  23.0 0.0 collective-permute-done.2.g_far.from_left
  23.0 1.3 %choose.1.g0 = bf16[512,128]{1,0:T(8,128)(2,1)S(1)} custom-call(s32[16,4]{1,0:T(8,128)S(1)} %copy.8.win, bf16[256,128]{1,0:T(8,128)(2,1)S(1)} %get-tuple-element.19.g_self, bf16[272,128]{1,0:T(8,128)(2,1)S(1)} %collective-permute-done.g_before, bf16[256,128]{1,0:T(8,128)(2,1)S(1)} %collective-permute-done.1.g_after, ...), custom_call_target="tpu_custom_call" | custom-call | flops 33554432 | bytes 524288 | tf_op jit(solution)/shard_map/choose/pallas_call | solution.py:344
  24.4 2.0 %collective-permute-start.3 = (bf16[512,128]{1,0:T(8,128)(2,1)S(1)}, bf16[512,128]{1,0:T(8,128)(2,1)S(1)}, u32[]{:S(2)}, u32[]{:S(2)}) collective-permute-start(bf16[512,128]{1,0:T(8,128)(2,1)S(1)} %choose.1.g0), channel_id=1, source_target_pairs={{0,16},{1,17},{2,18},{3,19},{4,20},{5,21},{6,22},{7,23},{8,24},{9,... | collective-permute-start | bytes 393224 | tf_op jit(solution)/shard_map/ppermute | solution.py:369
  26.4 2.5 %collective-permute-start.5 = (bf16[768,128]{1,0:T(8,128)(2,1)S(1)}, bf16[768,128]{1,0:T(8,128)(2,1)S(1)}, u32[]{:S(2)}, u32[]{:S(2)}) collective-permute-start(bf16[768,128]{1,0:T(8,128)(2,1)S(1)} %get-tuple-element.28), channel_id=1, source_target_pairs={{0,14},{1,15},{2,0},{3,1},{4,2},{5,3},{6,4},{7,5},{8,6},{9,7},{10,... | collective-permute-start | bytes 589832 | tf_op jit(solution)/shard_map/ppermute | solution.py:369
  28.8 1.6 %collective-permute-done.3.g1 = bf16[512,128]{1,0:T(8,128)(2,1)S(1)} collective-permute-done((bf16[512,128]{1,0:T(8,128)(2,1)S(1)}, bf16[512,128]{1,0:T(8,128)(2,1)S(1)}, u32[]{:S(2)}, u32[]{:S(2)}) %collective-permute-start.3) | collective-permute-done | bytes 131104 | tf_op jit(solution)/shard_map/ppermute | solution.py:369
  30.4 0.0 copy-done
  30.4 23.3 %dress_own.1 = (f32[48,48]{1,0:T(8,128)S(1)}, bf16[48,16384]{1,0:T(8,128)(2,1)S(1)}, bf16[96,16384]{1,0:T(8,128)(2,1)S(1)}, bf16[96,4096]{1,0:T(8,128)(2,1)S(1)}, bf16[96,4096]{1,0:T(8,128)(2,1)S(1)}) custom-call(s32[16,4]{1,0:T(8,128)S(1)} %copy.8.win, s32[1,4,4]{2,1,0:T(4,128)S(1)} %copy-done.3, bf16[1,48,128,128]{3,2,1,0:T(8,128)(2,1)S(1)} %copy-done, ...), custom_call_target="tpu_custom_call" | custom-call | flops 2147483648 | bytes 10485760 | tf_op jit(solution)/shard_map/dress_own/pallas_call | solution.py:344
  53.7 0.0 collective-permute-done.5.from_right
  53.7 0.0 collective-permute-done.4.tensor
  53.8 8.3 %join.1 = (f32[48,128]{1,0:T(8,128)S(1)}, f32[48,128]{1,0:T(8,128)S(1)}, f32[24,128]{1,0:T(8,128)S(1)}, f32[24,128]{1,0:T(8,128)S(1)}) custom-call(bf16[24,128,128]{2,1,0:T(8,128)(2,1)S(1)} %collective-permute-done.4.tensor, bf16[272,128]{1,0:T(8,128)(2,1)S(1)} %collective-permute-done.g_before, bf16[512,128]{1,0:T(8,128)(2,1)S(1)} %choose.1.g0, ...), custom_call_target="tpu_custom_call" | custom-call | flops 1073741824 | bytes 8388608 | tf_op jit(solution)/shard_map/join/pallas_call | solution.py:344
  62.1 1.8 %collective-permute-start.6 = (f32[48,128]{1,0:T(8,128)S(1)}, f32[48,128]{1,0:T(8,128)S(1)}, u32[]{:S(2)}, u32[]{:S(2)}) collective-permute-start(f32[48,128]{1,0:T(8,128)S(1)} %get-tuple-element.30), channel_id=1, source_target_pairs={{0,16},{1,17},{2,18},{3,19},{4,20},{5,21},{6,22},{7,23},{8,24},{9,... | collective-permute-start | bytes 73736 | tf_op jit(solution)/shard_map/ppermute | solution.py:369
  63.9 0.0 collective-permute-start.7
  63.9 1.7 %collective-permute-start.8 = (f32[24,128]{1,0:T(8,128)S(1)}, f32[24,128]{1,0:T(8,128)S(1)}, u32[]{:S(2)}, u32[]{:S(2)}) collective-permute-start(f32[24,128]{1,0:T(8,128)S(1)} %get-tuple-element.32), channel_id=1, source_target_pairs={{0,31},{1,16},{2,17},{3,18},{4,19},{5,20},{6,21},{7,22},{8,23},{9,... | collective-permute-start | bytes 36872 | tf_op jit(solution)/shard_map/ppermute | solution.py:369
  65.6 0.0 collective-permute-done.7.up0
  65.6 1.4 %collective-permute-done.8.up1 = f32[24,128]{1,0:T(8,128)S(1)} collective-permute-done((f32[24,128]{1,0:T(8,128)S(1)}, f32[24,128]{1,0:T(8,128)S(1)}, u32[]{:S(2)}, u32[]{:S(2)}) %collective-permute-start.8) | collective-permute-done | bytes 12320 | tf_op jit(solution)/shard_map/ppermute | solution.py:369
  67.0 0.0 collective-permute-done.6.recv
  67.1 0.7 %assemble.1 = f32[48,240]{1,0:T(8,128)} custom-call(f32[48,48]{1,0:T(8,128)S(1)} %get-tuple-element.23.polar0, f32[48,128]{1,0:T(8,128)S(1)} %get-tuple-element.29.own, f32[48,128]{1,0:T(8,128)S(1)} %collective-permute-done.6.recv, f32[24,128]{1,0:T(8,128)S(1)} %collective-permute-done.7.up0, f32[24,128]{1,0:T(8,128)S(1)} %collective-permute-done.8.up1), custom_call_target="tpu_custom_call" | custom-call | bytes 131072 | tf_op jit(solution)/shard_map/assemble/pallas_call | solution.py:344
Async XLA Ops:
  0.0 1.9 %copy-start.4 = (s32[16,4]{0,1:T(4,128)S(1)}, s32[16,4]{0,1:T(4,128)}, u32[]{:S(2)}) copy-start(s32[16,4]{0,1:T(4,128)} %param.9) | copy-start | bytes 772
  0.0 2.0 %copy-start.3 = (s32[1,4,4]{2,1,0:T(4,128)S(1)}, s32[1,4,4]{2,1,0:T(4,128)}, u32[]{:S(2)}) copy-start(s32[1,4,4]{2,1,0:T(4,128)} %tiles.3) | copy-start | bytes 196
  0.0 2.0 %copy-start.2 = (bf16[64,1024]{1,0:T(8,128)(2,1)S(1)}, bf16[64,1024]{1,0:T(8,128)(2,1)}, u32[]{:S(2)}) copy-start(bf16[64,1024]{1,0:T(8,128)(2,1)} %virt.1) | copy-start | bytes 393220
  0.0 2.0 %copy-start.1 = (bf16[64,1024]{1,0:T(8,128)(2,1)S(1)}, bf16[64,1024]{1,0:T(8,128)(2,1)}, u32[]{:S(2)}) copy-start(bf16[64,1024]{1,0:T(8,128)(2,1)} %occ.1) | copy-start | bytes 393220
  0.0 30.4 %copy-start = (bf16[1,48,128,128]{3,2,1,0:T(8,128)(2,1)S(1)}, bf16[1,48,128,128]{3,2,1,0:T(8,128)(2,1)}, u32[]{:S(2)}) copy-start(bf16[1,48,128,128]{3,2,1,0:T(8,128)(2,1)} %tensor.1) | copy-start | bytes 4718596
  1.3 52.4 %collective-permute-start.4 = (bf16[24,128,128]{2,1,0:T(8,128)(2,1)S(1)}, bf16[24,128,128]{2,1,0:T(8,128)(2,1)S(1)}, u32[]{:S(2)}, u32[]{:S(2)}) collective-permute-start(bf16[24,128,128]{2,1,0:T(8,128)(2,1)S(1)} %dynamic-slice_bitcast_fusion.half), channel_id=1, source_target_pairs={{0,1},{1,2},{2,3},{3,4},{4,5},{5,6},{6,7},{7,8},{8,9},{9,10},{10,1... | collective-permute-start | bytes 2359304 | tf_op jit(solution)/shard_map/ppermute | solution.py:369
  4.4 18.6 %collective-permute-start.2 = (bf16[1024,128]{1,0:T(8,128)(2,1)S(1)}, bf16[1024,128]{1,0:T(8,128)(2,1)S(1)}, u32[]{:S(2)}, u32[]{:S(2)}) collective-permute-start(bf16[1024,128]{1,0:T(8,128)(2,1)S(1)} %get-tuple-element.22), channel_id=1, source_target_pairs={{0,2},{1,3},{2,4},{3,5},{4,6},{5,7},{6,8},{7,9},{8,10},{9,11},{10,... | collective-permute-start | bytes 786440 | tf_op jit(solution)/shard_map/ppermute | solution.py:369
  7.0 16.0 %collective-permute-start = (bf16[272,128]{1,0:T(8,128)(2,1)S(1)}, bf16[272,128]{1,0:T(8,128)(2,1)S(1)}, u32[]{:S(2)}, u32[]{:S(2)}) collective-permute-start(bf16[272,128]{1,0:T(8,128)(2,1)S(1)} %get-tuple-element.20), channel_id=1, source_target_pairs={{0,1},{1,2},{2,3},{3,4},{4,5},{5,6},{6,7},{7,8},{8,9},{9,10},{10,1... | collective-permute-start | bytes 208904 | tf_op jit(solution)/shard_map/ppermute | solution.py:369
  8.3 5.0 %collective-permute-start.1 = (bf16[256,128]{1,0:T(8,128)(2,1)S(1)}, bf16[256,128]{1,0:T(8,128)(2,1)S(1)}, u32[]{:S(2)}, u32[]{:S(2)}) collective-permute-start(bf16[256,128]{1,0:T(8,128)(2,1)S(1)} %get-tuple-element.21), channel_id=1, source_target_pairs={{0,15},{1,0},{2,1},{3,2},{4,3},{5,4},{6,5},{7,6},{8,7},{9,8},{10,9... | collective-permute-start | bytes 196616 | tf_op jit(solution)/shard_map/ppermute | solution.py:369
  24.4 6.1 %collective-permute-start.3 = (bf16[512,128]{1,0:T(8,128)(2,1)S(1)}, bf16[512,128]{1,0:T(8,128)(2,1)S(1)}, u32[]{:S(2)}, u32[]{:S(2)}) collective-permute-start(bf16[512,128]{1,0:T(8,128)(2,1)S(1)} %choose.1.g0), channel_id=1, source_target_pairs={{0,16},{1,17},{2,18},{3,19},{4,20},{5,21},{6,22},{7,23},{8,24},{9,... | collective-permute-start | bytes 393224 | tf_op jit(solution)/shard_map/ppermute | solution.py:369
  26.4 27.4 %collective-permute-start.5 = (bf16[768,128]{1,0:T(8,128)(2,1)S(1)}, bf16[768,128]{1,0:T(8,128)(2,1)S(1)}, u32[]{:S(2)}, u32[]{:S(2)}) collective-permute-start(bf16[768,128]{1,0:T(8,128)(2,1)S(1)} %get-tuple-element.28), channel_id=1, source_target_pairs={{0,14},{1,15},{2,0},{3,1},{4,2},{5,3},{6,4},{7,5},{8,6},{9,7},{10,... | collective-permute-start | bytes 589832 | tf_op jit(solution)/shard_map/ppermute | solution.py:369
  62.1 4.9 %collective-permute-start.6 = (f32[48,128]{1,0:T(8,128)S(1)}, f32[48,128]{1,0:T(8,128)S(1)}, u32[]{:S(2)}, u32[]{:S(2)}) collective-permute-start(f32[48,128]{1,0:T(8,128)S(1)} %get-tuple-element.30), channel_id=1, source_target_pairs={{0,16},{1,17},{2,18},{3,19},{4,20},{5,21},{6,22},{7,23},{8,24},{9,... | collective-permute-start | bytes 73736 | tf_op jit(solution)/shard_map/ppermute | solution.py:369
  63.9 1.7 %collective-permute-start.7 = (f32[24,128]{1,0:T(8,128)S(1)}, f32[24,128]{1,0:T(8,128)S(1)}, u32[]{:S(2)}, u32[]{:S(2)}) collective-permute-start(f32[24,128]{1,0:T(8,128)S(1)} %get-tuple-element.31), channel_id=1, source_target_pairs={{0,15},{1,0},{2,1},{3,2},{4,3},{5,4},{6,5},{7,6},{8,7},{9,8},{10,9... | collective-permute-start | bytes 36872 | tf_op jit(solution)/shard_map/ppermute | solution.py:369
  63.9 3.1 %collective-permute-start.8 = (f32[24,128]{1,0:T(8,128)S(1)}, f32[24,128]{1,0:T(8,128)S(1)}, u32[]{:S(2)}, u32[]{:S(2)}) collective-permute-start(f32[24,128]{1,0:T(8,128)S(1)} %get-tuple-element.32), channel_id=1, source_target_pairs={{0,31},{1,16},{2,17},{3,18},{4,19},{5,20},{6,21},{7,22},{8,23},{9,... | collective-permute-start | bytes 36872 | tf_op jit(solution)/shard_map/ppermute | solution.py:369
where the time goes:
time: 68.9 us; the launch traced here: 67.8 us
  Pallas kernels  36.1 us (52%)
  starting transfers between devices  15.5 us (22%)
  waiting for transfers between devices  14.7 us (21%)
  local copies, waits for them, and re-layouts  1.42 us (2%)
    pallas_call x5, Pallas kernels, call(): pl.pallas_call(kernel, name=name, in_specs=specs, out_specs=tuple(vmem(le...  36.1 us
    ppermute x9, starting transfers between devices, send(): return lax.ppermute(array, ('grp', 'row'), pairs)  15.5 us
    ppermute x9, waiting for transfers between devices, send(): return lax.ppermute(array, ('grp', 'row'), pairs)  14.7 us
  transfers between devices with their start and end apart: 9, of which 4 were waited for; matrix products, arithmetic and copies ran while one was open for 0% of the time, Pallas kernels for 40%

commit v1 on v0

--- a/solution.py
+++ b/solution.py
@@ -67,27 +67,37 @@
     return near(row, -1, count) >> 1
 
 
-def prepare(count, win, tiles, occ, virt, half, g_self, g_right, g_left, far_right, far_left, xs):
+def spread(count, win, occ, virt, g_self, g_right, g_left, g_far):
     d = lax.axis_index("row")
-    mine = window_at(win, d)
-    funcs = half.shape[0]
-
-    def greens(out, base, dest):
+
+    def greens(out, dest):
         first = column_chunk(dest, count)
         for c in range(2):
             chunk = lax.rem(first + c, count // 2)
             columns = pl.ds(pl.multiple_of(chunk * 128, 128), 128)
-            out[base + 64 * c : base + 64 * c + 64, :] = occ[:, columns]
-            out[base + 128 + 64 * c : base + 192 + 64 * c, :] = virt[:, columns]
-
-    greens(g_self, 0, d)
-    greens(g_right, 0, near(d, 1, count))
-    greens(g_left, 0, near(d, -1, count))
-    greens(far_right, funcs * 32, near(d, 2, count))
-    short = tile_mask(tiles, 4)
-    g_right[256:272, :] = short.astype(BF)
-
+            out[64 * c : 64 * c + 64, :] = occ[:, columns]
+            out[128 + 64 * c : 192 + 64 * c, :] = virt[:, columns]
+
+    greens(g_self, d)
+    greens(g_right, near(d, 1, count))
+    greens(g_left, near(d, -1, count))
+    greens(g_far, near(d, 2, count))
+
+
+def mask_half(tiles, coulomb, token, tensor, sem):
+    funcs = tensor.shape[0]
+    half = lax.rem(lax.axis_index("grp"), 2)
+    copy = pltpu.make_async_copy(coulomb.at[0, pl.ds(half * funcs, funcs)], tensor, sem)
+    copy.start()
     mask = tile_mask(tiles, 32).astype(BF)
+    copy.wait()
+    tensor[...] = tensor[...] * mask[None]
+
+
+def far_tiles(count, win, half, far_right, far_left, xs):
+    d = lax.axis_index("row")
+    mine = window_at(win, d)
+    funcs = half.shape[0]
     left, right = near(d, -1, count) * 2, near(d, 1, count) * 2
     shape = (128, 256)
     column = iota(shape, 1)
@@ -96,7 +106,7 @@
     same = (here == wanted) & ((iota(shape, 0) & 31) == (column & 31))
     select = jnp.where(same, 1.0, 0.0).astype(BF)
     for r in range(0, funcs, 4):
-        block = (half[r : r + 4] * mask[None]).reshape(512, 128)
+        block = half[r : r + 4].reshape(512, 128)
         x = dot(block, select)
         xs[0, r * 128 : r * 128 + 512, :] = x[:, :128]
         xs[1, r * 128 : r * 128 + 512, :] = x[:, 128:]
@@ -114,7 +124,7 @@
             out[t * funcs : (t + 2) * funcs, :] = jnp.concatenate(parts, axis=0).astype(BF)
 
 
-def choose(count, far_rows, win, g_self, g_before, g_after, g_far, out):
+def choose(count, win, g_self, g_before, g_after, g_far, out):
     d = lax.axis_index("row")
     atoms = 2 * count
     mine = window_at(win, d)
@@ -132,7 +142,7 @@
             blocks.append(
                 jnp.concatenate(
                     [
-                        g_far[far_rows + at : far_rows + at + 64, :],
+                        g_far[at : at + 64, :],
                         g_before[at : at + 64, :],
                         g_self[at : at + 64, :],
                         g_after[at : at + 64, :],
@@ -175,22 +185,22 @@
     occ = jnp.concatenate([g0[0:128, :], g1[0:128, :]], axis=0)
 
     def halves(i, carry):
-        at = pl.multiple_of(i * 256, 256)
+        at = pl.multiple_of(i * 272, 8)
         m0 = tensor[0, 2 * i] * mask
         m1 = tensor[0, 2 * i + 1] * mask
         ms[pl.ds(at, 128), :] = m0.astype(F32)
-        ms[pl.ds(at + 128, 128), :] = m1.astype(F32)
-        h = dot(occ, jnp.concatenate([m0, m1], axis=1)).astype(BF).astype(F32)
+        ms[pl.ds(at + 136, 128), :] = m1.astype(F32)
+        h = dot(occ, jnp.concatenate([m0, m1], axis=1))
         hs[0, pl.ds(at, 128), :] = h[:128, :128]
-        hs[0, pl.ds(at + 128, 128), :] = h[:128, 128:]
+        hs[0, pl.ds(at + 136, 128), :] = h[:128, 128:]
         hs[1, pl.ds(at, 128), :] = h[128:, :128]
-        hs[1, pl.ds(at + 128, 128), :] = h[128:, 128:]
+        hs[1, pl.ds(at + 136, 128), :] = h[128:, 128:]
         return carry
 
     lax.fori_loop(0, funcs // 2, halves, 0, unroll=2)
 
     def rows_at(ref, g, start):
-        return [ref[g, pl.ds(start + t, funcs, stride=128), :] for t in range(8)]
+        return [ref[g, pl.ds(start + t, funcs, stride=136), :] for t in range(8)]
 
     virt_a = g0[128:256, :]
 
@@ -199,7 +209,7 @@
         x = dot(jnp.concatenate(rows_at(hs, 0, start), axis=0).astype(BF), virt_a).astype(BF)
         left = jnp.concatenate([x[t * funcs : (t + 1) * funcs] for t in range(8)], axis=1)
         right = jnp.concatenate(
-            [ms[pl.ds(start + t, funcs, stride=128), :].astype(BF) for t in range(8)], axis=1
+            [ms[pl.ds(start + t, funcs, stride=136), :].astype(BF) for t in range(8)], axis=1
         )
         flat[:, pl.ds(pl.multiple_of(i * 1024, 1024), 1024)] = right
         return total + dot_t(left, right)
@@ -248,27 +258,23 @@
             lax.fori_loop(0, 4, far_frame, 0)
 
 
-def join(tensor, g_before, g0, g1, flat, dressed, far_l, far_r, from_left, from_right, own, other, up0, up1, hs, ms):
+def join(tensor, g0, g1, flat, dressed, far_l, far_r, from_left, from_right, own, other, up0, up1, hs, ms):
     funcs = tensor.shape[0]
     full = 2 * funcs
-    short = g_before[256:272, :].astype(F32)
-    mask = jnp.concatenate(
-        [jnp.broadcast_to(short[4 * i : 4 * i + 1, :], (32, 128)) for i in range(4)], axis=0
-    ).astype(BF)
     occ = jnp.concatenate([g0[256:384, :], g1[256:384, :]], axis=0)
     virts = [g0[384:512, :], g1[384:512, :]]
 
     def halves(i, carry):
-        at = pl.multiple_of(i * 256, 256)
-        m0 = tensor[2 * i] * mask
-        m1 = tensor[2 * i + 1] * mask
+        at = i * 258
+        m0 = tensor[2 * i]
+        m1 = tensor[2 * i + 1]
         ms[pl.ds(at, 128), :] = m0.astype(F32)
-        ms[pl.ds(at + 128, 128), :] = m1.astype(F32)
-        h = dot(occ, jnp.concatenate([m0, m1], axis=1)).astype(BF).astype(F32)
+        ms[pl.ds(at + 129, 128), :] = m1.astype(F32)
+        h = dot(occ, jnp.concatenate([m0, m1], axis=1))
         hs[0, pl.ds(at, 128), :] = h[:128, :128]
-        hs[0, pl.ds(at + 128, 128), :] = h[:128, 128:]
+        hs[0, pl.ds(at + 129, 128), :] = h[:128, 128:]
         hs[1, pl.ds(at, 128), :] = h[128:, :128]
-        hs[1, pl.ds(at + 128, 128), :] = h[128:, 128:]
+        hs[1, pl.ds(at + 129, 128), :] = h[128:, 128:]
         return carry
 
     lax.fori_loop(0, funcs // 2, halves, 0, unroll=2)
@@ -279,7 +285,7 @@
         columns = pl.ds(pl.multiple_of(i * 1024, 1024), 1024)
         xs = []
         for g in range(2):
-            rows = [hs[g, pl.ds(start + t, funcs, stride=128), :] for t in range(8)]
+            rows = [hs[g, pl.ds(start + t, funcs, stride=129), :] for t in range(8)]
             xs.append(dot(jnp.concatenate(rows, axis=0).astype(BF), virts[g]))
         left = jnp.concatenate(
             [
@@ -289,7 +295,7 @@
             axis=1,
         )
         right = jnp.concatenate(
-            [ms[pl.ds(start + t, funcs, stride=128), :] for t in range(8)], axis=1
+            [ms[pl.ds(start + t, funcs, stride=129), :] for t in range(8)], axis=1
         ).astype(BF)
         return down + dot_t(dressed[:, columns], right), up + dot_t(left, flat[:, columns])
 
@@ -357,8 +363,6 @@
     full = coulomb3c.shape[1]
     funcs = full // 2
     shape = jax.ShapeDtypeStruct
-    half = lax.rem(lax.axis_index("grp"), 2)
-    tensor = lax.dynamic_slice_in_dim(coulomb3c[0], half * funcs, funcs, 0)
 
     def send(array, row_by, swap=False):
         pairs = []
@@ -368,36 +372,46 @@
                 pairs.append((g * count + d, to))
         return lax.ppermute(array, ("grp", "row"), pairs)
 
-    wide = send(tensor, 1)
     far_rows = funcs * 32
-    g_self, g_right, g_left, far_right, far_left = call(
-        functools.partial(prepare, count),
-        "prepare",
-        smem(2) + vmem(3),
-        [
-            shape((256, 128), BF),
-            shape((272, 128), BF),
-            shape((256, 128), BF),
-            shape((far_rows + 256, 128), BF),
-            shape((far_rows, 128), BF),
-        ],
-        (window, tile_list, green_occ, green_virt, tensor),
-        [pltpu.VMEM((2, funcs * 128, 128), F32)],
-        flops=2 * funcs * 128 * 128 * 256,
-        moved=2 << 20,
+    g_self, g_right, g_left, g_far = call(
+        functools.partial(spread, count),
+        "spread",
+        smem(1) + vmem(2),
+        [shape((256, 128), BF)] * 4,
+        (window, green_occ, green_virt),
     )
     g_before = send(g_right, 1)
     g_after = send(g_left, -1)
+    g_beyond = send(g_far, 2)
+    (tensor,) = call(
+        mask_half,
+        "mask_half",
+        smem(1) + [pl.BlockSpec(memory_space=pl.ANY)] * 2,
+        [shape((funcs, 128, 128), BF)],
+        (tile_list, coulomb3c, g_self),
+        [pltpu.SemaphoreType.DMA],
+    )
+    wide = send(tensor, 1)
+    far_right, far_left = call(
+        functools.partial(far_tiles, count),
+        "far_tiles",
+        smem(1) + vmem(1),
+        [shape((far_rows, 128), BF), shape((far_rows, 128), BF)],
+        (window, tensor),
+        [pltpu.VMEM((2, funcs * 128, 128), F32)],
+        flops=1 << 36,
+    )
     from_left = send(far_right, 2)
     from_right = send(far_left, -2)
+    g_before, g_after, g_beyond, far_right, far_left = lax.optimization_barrier(
+        (g_before, g_after, g_beyond, far_right, far_left)
+    )
     (mine,) = call(
-        functools.partial(choose, count, far_rows),
+        functools.partial(choose, count),
         "choose",
         smem(1) + vmem(4),
         [shape((512, 128), BF)],
-        (window, g_self, g_before, g_after, from_left),
-        flops=1 << 25,
-        moved=1 << 19,
+        (window, g_self, g_before, g_after, g_beyond),
     )
     partner = send(mine, 0, True)
     polar0, flat, dressed, far_l, far_r = call(
@@ -412,24 +426,20 @@
             shape((2 * full, 32 * 128), BF),
         ],
         (window, tile_list, coulomb3c, mine, partner),
-        [pltpu.VMEM((2, full * 128, 128), F32), pltpu.VMEM((full * 128, 128), F32)],
-        flops=1 << 31,
-        moved=10 << 20,
+        [pltpu.VMEM((2, full * 136, 128), F32), pltpu.VMEM((full * 136, 128), F32)],
     )
     own, other, up0, up1 = call(
         join,
         "join",
-        vmem(10),
+        vmem(9),
         [
             shape((full, 128), F32),
             shape((full, 128), F32),
             shape((funcs, 128), F32),
             shape((funcs, 128), F32),
         ],
-        (wide, g_before, mine, partner, flat, dressed, far_l, far_r, from_left, from_right),
-        [pltpu.VMEM((2, funcs * 128, 128), F32), pltpu.VMEM((funcs * 128, 128), F32)],
-        flops=1 << 30,
-        moved=8 << 20,
+        (wide, mine, partner, flat, dressed, far_l, far_r, from_left, from_right),
+        [pltpu.VMEM((2, funcs * 129, 128), F32), pltpu.VMEM((funcs * 129, 128), F32)],
     )
     recv = send(other, 0, True)
     after0 = send(up0, -1)
@@ -440,7 +450,6 @@
         vmem(5),
         [shape((full, 5 * full), F32)],
         (polar0, own, recv, after0, after1),
-        moved=1 << 17,
     )
     return out
 

time: 68.9 us -> 58.1 us (0.84)
  the two profiles are of different devices: /device:TPU:0 before, /device:TPU:1 now
where the time goes in v1:
time: 58.1 us; the launch traced here: 57.9 us
  Pallas kernels  30.4 us (52%)
  starting transfers between devices  14.5 us (25%)
  waiting for transfers between devices  8.22 us (14%)
  local copies, waits for them, and re-layouts  4.66 us (8%)
    pallas_call x7, Pallas kernels, call(): pl.pallas_call(kernel, name=name, in_specs=specs, out_specs=tuple(vmem(le...  30.4 us
    ppermute x10, starting transfers between devices, send(): return lax.ppermute(array, ('grp', 'row'), pairs)  14.5 us
    ppermute x10, waiting for transfers between devices, send(): return lax.ppermute(array, ('grp', 'row'), pairs)  8.22 us
    unnamed x11, local copies, waits for them, and re-layouts  4.66 us
  transfers between devices with their start and end apart: 10, of which 3 were waited for; matrix products, arithmetic and copies ran while one was open for 0% of the time, Pallas kernels for 39%

profile of v1, /device:TPU:1, one launch (start us, length us, event | category | flops | bytes accessed | tf_op | source)
XLA Modules:
  0.0 57.9 jit_solution(11504835358467330219)
XLA Ops:
  0.0 0.8 %copy.9.win = s32[16,4]{1,0:T(8,128)S(1)} copy(s32[16,4]{0,1:T(4,128)} %param.9) | data formatting | bytes 512 | tf_op args[4]
  0.8 0.0 copy-start.2
  0.8 0.9 %copy-done.2 = bf16[64,1024]{1,0:T(8,128)(2,1)S(1)} copy-done((bf16[64,1024]{1,0:T(8,128)(2,1)S(1)}, bf16[64,1024]{1,0:T(8,128)(2,1)}, u32[]{:S(2)}) %copy-start.2) | copy-done | bytes 131096
  1.7 0.0 copy-start.3
  1.7 0.9 %copy-done.3 = bf16[64,1024]{1,0:T(8,128)(2,1)S(1)} copy-done((bf16[64,1024]{1,0:T(8,128)(2,1)S(1)}, bf16[64,1024]{1,0:T(8,128)(2,1)}, u32[]{:S(2)}) %copy-start.3) | copy-done | bytes 131096
  2.6 0.7 %spread.1 = (bf16[256,128]{1,0:T(8,128)(2,1)S(1)}, bf16[256,128]{1,0:T(8,128)(2,1)S(1)}, bf16[256,128]{1,0:T(8,128)(2,1)S(1)}, bf16[256,128]{1,0:T(8,128)(2,1)S(1)}) custom-call(s32[16,4]{1,0:T(8,128)S(1)} %copy.9.win, bf16[64,1024]{1,0:T(8,128)(2,1)S(1)} %copy-done.2, bf16[64,1024]{1,0:T(8,128)(2,1)S(1)} %copy-done.3), custom_call_target="tpu_custom_call" | custom-call | tf_op jit(solution)/shard_map/spread/pallas_call | solution.py:350
  3.3 2.7 %collective-permute-start = (bf16[256,128]{1,0:T(8,128)(2,1)S(1)}, bf16[256,128]{1,0:T(8,128)(2,1)S(1)}, u32[]{:S(2)}, u32[]{:S(2)}) collective-permute-start(bf16[256,128]{1,0:T(8,128)(2,1)S(1)} %get-tuple-element.24), channel_id=1, source_target_pairs={{0,1},{1,2},{2,3},{3,4},{4,5},{5,6},{6,7},{7,8},{8,9},{9,10},{10,1... | collective-permute-start | bytes 196616 | tf_op jit(solution)/shard_map/ppermute | solution.py:373
  6.0 0.0 collective-permute-start.1
  6.0 1.2 %collective-permute-start.2 = (bf16[256,128]{1,0:T(8,128)(2,1)S(1)}, bf16[256,128]{1,0:T(8,128)(2,1)S(1)}, u32[]{:S(2)}, u32[]{:S(2)}) collective-permute-start(bf16[256,128]{1,0:T(8,128)(2,1)S(1)} %get-tuple-element.26), channel_id=1, source_target_pairs={{0,2},{1,3},{2,4},{3,5},{4,6},{5,7},{6,8},{7,9},{8,10},{9,11},{10,... | collective-permute-start | bytes 196616 | tf_op jit(solution)/shard_map/ppermute | solution.py:373
  7.3 0.0 copy-start
  7.3 1.4 %copy-done = bf16[1,48,128,128]{3,2,1,0:T(8,128)(2,1)S(1)} copy-done((bf16[1,48,128,128]{3,2,1,0:T(8,128)(2,1)S(1)}, bf16[1,48,128,128]{3,2,1,0:T(8,128)(2,1)}, u32[]{:S(2)}) %copy-start) | copy-done | bytes 1572888
  8.7 0.0 copy-start.4
  8.7 0.7 %copy-done.4 = s32[1,4,4]{2,1,0:T(4,128)S(1)} copy-done((s32[1,4,4]{2,1,0:T(4,128)S(1)}, s32[1,4,4]{2,1,0:T(4,128)}, u32[]{:S(2)}) %copy-start.4) | copy-done | bytes 88
  9.3 0.8 %mask_half.1.half = bf16[24,128,128]{2,1,0:T(8,128)(2,1)S(1)} custom-call(s32[1,4,4]{2,1,0:T(4,128)S(1)} %copy-done.4, bf16[1,48,128,128]{3,2,1,0:T(8,128)(2,1)S(1)} %copy-done, bf16[256,128]{1,0:T(8,128)(2,1)S(1)} %get-tuple-element.23.token.g_self), custom_call_target="tpu_custom_call" | custom-call | tf_op jit(solution)/shard_map/mask_half/pallas_call | solution.py:350
  10.1 0.0 copy-start.1
  10.1 3.0 %collective-permute-start.4 = (bf16[24,128,128]{2,1,0:T(8,128)(2,1)S(1)}, bf16[24,128,128]{2,1,0:T(8,128)(2,1)S(1)}, u32[]{:S(2)}, u32[]{:S(2)}) collective-permute-start(bf16[24,128,128]{2,1,0:T(8,128)(2,1)S(1)} %mask_half.1.half), channel_id=1, source_target_pairs={{0,1},{1,2},{2,3},{3,4},{4,5},{5,6},{6,7},{7,8},{8,9},{9,10},{10,1... | collective-permute-start | bytes 2359304 | tf_op jit(solution)/shard_map/ppermute | solution.py:373
  13.1 2.3 %far_tiles.1 = (bf16[768,128]{1,0:T(8,128)(2,1)S(1)}, bf16[768,128]{1,0:T(8,128)(2,1)S(1)}) custom-call(s32[16,4]{1,0:T(8,128)S(1)} %copy.9.win, bf16[24,128,128]{2,1,0:T(8,128)(2,1)S(1)} %mask_half.1.half), custom_call_target="tpu_custom_call" | custom-call | flops 68719476736 | tf_op jit(solution)/shard_map/far_tiles/pallas_call | solution.py:350
  15.4 0.4 collective-permute-start.5
  15.8 0.0 collective-permute-done.g_before
  15.8 3.8 %collective-permute-start.6 = (bf16[768,128]{1,0:T(8,128)(2,1)S(1)}, bf16[768,128]{1,0:T(8,128)(2,1)S(1)}, u32[]{:S(2)}, u32[]{:S(2)}) collective-permute-start(bf16[768,128]{1,0:T(8,128)(2,1)S(1)} %get-tuple-element.28), channel_id=1, source_target_pairs={{0,14},{1,15},{2,0},{3,1},{4,2},{5,3},{6,4},{7,5},{8,6},{9,7},{10,... | collective-permute-start | bytes 589832 | tf_op jit(solution)/shard_map/ppermute | solution.py:373
  19.6 0.0 collective-permute-done.1.g_after
  19.6 0.0 collective-permute-done.2.g_far
  19.6 1.4 %choose.1.g0 = bf16[512,128]{1,0:T(8,128)(2,1)S(1)} custom-call(s32[16,4]{1,0:T(8,128)S(1)} %copy.9.win, bf16[256,128]{1,0:T(8,128)(2,1)S(1)} %get-tuple-element.23.token.g_self, bf16[256,128]{1,0:T(8,128)(2,1)S(1)} %collective-permute-done.g_before, bf16[256,128]{1,0:T(8,128)(2,1)S(1)} %collective-permute-done.1.g_after, ...), custom_call_target="tpu_custom_call" | custom-call | tf_op jit(solution)/shard_map/choose/pallas_call | solution.py:350
  20.9 1.3 %collective-permute-start.3 = (bf16[512,128]{1,0:T(8,128)(2,1)S(1)}, bf16[512,128]{1,0:T(8,128)(2,1)S(1)}, u32[]{:S(2)}, u32[]{:S(2)}) collective-permute-start(bf16[512,128]{1,0:T(8,128)(2,1)S(1)} %choose.1.g0), channel_id=1, source_target_pairs={{0,16},{1,17},{2,18},{3,19},{4,20},{5,21},{6,22},{7,23},{8,24},{9,... | collective-permute-start | bytes 393224 | tf_op jit(solution)/shard_map/ppermute | solution.py:373
  22.2 4.2 %collective-permute-done.3.g1 = bf16[512,128]{1,0:T(8,128)(2,1)S(1)} collective-permute-done((bf16[512,128]{1,0:T(8,128)(2,1)S(1)}, bf16[512,128]{1,0:T(8,128)(2,1)S(1)}, u32[]{:S(2)}, u32[]{:S(2)}) %collective-permute-start.3) | collective-permute-done | bytes 131104 | tf_op jit(solution)/shard_map/ppermute | solution.py:373
  26.4 0.0 copy-done.1
  26.4 18.0 %dress_own.1 = (f32[48,48]{1,0:T(8,128)S(1)}, bf16[48,16384]{1,0:T(8,128)(2,1)S(1)}, bf16[96,16384]{1,0:T(8,128)(2,1)S(1)}, bf16[96,4096]{1,0:T(8,128)(2,1)S(1)}, bf16[96,4096]{1,0:T(8,128)(2,1)S(1)}) custom-call(s32[16,4]{1,0:T(8,128)S(1)} %copy.9.win, s32[1,4,4]{2,1,0:T(4,128)S(1)} %copy-done.4, bf16[1,48,128,128]{3,2,1,0:T(8,128)(2,1)S(1)} %copy-done.1, ...), custom_call_target="tpu_custom_call" | custom-call | tf_op jit(solution)/shard_map/dress_own/pallas_call | solution.py:350
  44.4 0.0 collective-permute-done.5.from_left
  44.4 0.0 collective-permute-done.6.from_right
  44.4 0.0 collective-permute-done.4.tensor
  44.4 6.6 %join.1 = (f32[48,128]{1,0:T(8,128)S(1)}, f32[48,128]{1,0:T(8,128)S(1)}, f32[24,128]{1,0:T(8,128)S(1)}, f32[24,128]{1,0:T(8,128)S(1)}) custom-call(bf16[24,128,128]{2,1,0:T(8,128)(2,1)S(1)} %collective-permute-done.4.tensor, bf16[512,128]{1,0:T(8,128)(2,1)S(1)} %choose.1.g0, bf16[512,128]{1,0:T(8,128)(2,1)S(1)} %collective-permute-done.3.g1, ...), custom_call_target="tpu_custom_call" | custom-call | tf_op jit(solution)/shard_map/join/pallas_call | solution.py:350
  51.0 1.1 %collective-permute-start.7 = (f32[48,128]{1,0:T(8,128)S(1)}, f32[48,128]{1,0:T(8,128)S(1)}, u32[]{:S(2)}, u32[]{:S(2)}) collective-permute-start(f32[48,128]{1,0:T(8,128)S(1)} %get-tuple-element.38), channel_id=1, source_target_pairs={{0,16},{1,17},{2,18},{3,19},{4,20},{5,21},{6,22},{7,23},{8,24},{9,... | collective-permute-start | bytes 73736 | tf_op jit(solution)/shard_map/ppermute | solution.py:373
  52.2 0.9 %collective-permute-start.8 = (f32[24,128]{1,0:T(8,128)S(1)}, f32[24,128]{1,0:T(8,128)S(1)}, u32[]{:S(2)}, u32[]{:S(2)}) collective-permute-start(f32[24,128]{1,0:T(8,128)S(1)} %get-tuple-element.39), channel_id=1, source_target_pairs={{0,15},{1,0},{2,1},{3,2},{4,3},{5,4},{6,5},{7,6},{8,7},{9,8},{10,9... | collective-permute-start | bytes 36872 | tf_op jit(solution)/shard_map/ppermute | solution.py:373
  53.1 0.0 collective-permute-start.9
  53.1 2.2 %collective-permute-done.8.up0 = f32[24,128]{1,0:T(8,128)S(1)} collective-permute-done((f32[24,128]{1,0:T(8,128)S(1)}, f32[24,128]{1,0:T(8,128)S(1)}, u32[]{:S(2)}, u32[]{:S(2)}) %collective-permute-start.8) | collective-permute-done | bytes 12320 | tf_op jit(solution)/shard_map/ppermute | solution.py:373
  55.3 1.8 %collective-permute-done.9.up1 = f32[24,128]{1,0:T(8,128)S(1)} collective-permute-done((f32[24,128]{1,0:T(8,128)S(1)}, f32[24,128]{1,0:T(8,128)S(1)}, u32[]{:S(2)}, u32[]{:S(2)}) %collective-permute-start.9) | collective-permute-done | bytes 12320 | tf_op jit(solution)/shard_map/ppermute | solution.py:373
  57.1 0.0 collective-permute-done.7.recv
  57.1 0.7 %assemble.1 = f32[48,240]{1,0:T(8,128)} custom-call(f32[48,48]{1,0:T(8,128)S(1)} %get-tuple-element.32.polar0, f32[48,128]{1,0:T(8,128)S(1)} %get-tuple-element.37.own, f32[48,128]{1,0:T(8,128)S(1)} %collective-permute-done.7.recv, f32[24,128]{1,0:T(8,128)S(1)} %collective-permute-done.8.up0, f32[24,128]{1,0:T(8,128)S(1)} %collective-permute-done.9.up1), custom_call_target="tpu_custom_call" | custom-call | tf_op jit(solution)/shard_map/assemble/pallas_call | solution.py:350
Async XLA Ops:
  0.8 0.9 %copy-start.2 = (bf16[64,1024]{1,0:T(8,128)(2,1)S(1)}, bf16[64,1024]{1,0:T(8,128)(2,1)}, u32[]{:S(2)}) copy-start(bf16[64,1024]{1,0:T(8,128)(2,1)} %occ.1) | copy-start | bytes 393220
  1.7 0.9 %copy-start.3 = (bf16[64,1024]{1,0:T(8,128)(2,1)S(1)}, bf16[64,1024]{1,0:T(8,128)(2,1)}, u32[]{:S(2)}) copy-start(bf16[64,1024]{1,0:T(8,128)(2,1)} %virt.1) | copy-start | bytes 393220
  3.3 12.4 %collective-permute-start = (bf16[256,128]{1,0:T(8,128)(2,1)S(1)}, bf16[256,128]{1,0:T(8,128)(2,1)S(1)}, u32[]{:S(2)}, u32[]{:S(2)}) collective-permute-start(bf16[256,128]{1,0:T(8,128)(2,1)S(1)} %get-tuple-element.24), channel_id=1, source_target_pairs={{0,1},{1,2},{2,3},{3,4},{4,5},{5,6},{6,7},{7,8},{8,9},{9,10},{10,1... | collective-permute-start | bytes 196616 | tf_op jit(solution)/shard_map/ppermute | solution.py:373
  6.0 13.6 %collective-permute-start.1 = (bf16[256,128]{1,0:T(8,128)(2,1)S(1)}, bf16[256,128]{1,0:T(8,128)(2,1)S(1)}, u32[]{:S(2)}, u32[]{:S(2)}) collective-permute-start(bf16[256,128]{1,0:T(8,128)(2,1)S(1)} %get-tuple-element.25), channel_id=1, source_target_pairs={{0,15},{1,0},{2,1},{3,2},{4,3},{5,4},{6,5},{7,6},{8,7},{9,8},{10,9... | collective-permute-start | bytes 196616 | tf_op jit(solution)/shard_map/ppermute | solution.py:373
  6.0 13.6 %collective-permute-start.2 = (bf16[256,128]{1,0:T(8,128)(2,1)S(1)}, bf16[256,128]{1,0:T(8,128)(2,1)S(1)}, u32[]{:S(2)}, u32[]{:S(2)}) collective-permute-start(bf16[256,128]{1,0:T(8,128)(2,1)S(1)} %get-tuple-element.26), channel_id=1, source_target_pairs={{0,2},{1,3},{2,4},{3,5},{4,6},{5,7},{6,8},{7,9},{8,10},{9,11},{10,... | collective-permute-start | bytes 196616 | tf_op jit(solution)/shard_map/ppermute | solution.py:373
  7.3 1.4 %copy-start = (bf16[1,48,128,128]{3,2,1,0:T(8,128)(2,1)S(1)}, bf16[1,48,128,128]{3,2,1,0:T(8,128)(2,1)}, u32[]{:S(2)}) copy-start(bf16[1,48,128,128]{3,2,1,0:T(8,128)(2,1)} %tensor.1) | copy-start | bytes 4718596
  8.7 0.7 %copy-start.4 = (s32[1,4,4]{2,1,0:T(4,128)S(1)}, s32[1,4,4]{2,1,0:T(4,128)}, u32[]{:S(2)}) copy-start(s32[1,4,4]{2,1,0:T(4,128)} %tiles.3) | copy-start | bytes 196
  10.1 16.3 %copy-start.1 = (bf16[1,48,128,128]{3,2,1,0:T(8,128)(2,1)S(1)}, bf16[1,48,128,128]{3,2,1,0:T(8,128)(2,1)}, u32[]{:S(2)}) copy-start(bf16[1,48,128,128]{3,2,1,0:T(8,128)(2,1)} %tensor.1) | copy-start | bytes 4718596
  10.1 34.3 %collective-permute-start.4 = (bf16[24,128,128]{2,1,0:T(8,128)(2,1)S(1)}, bf16[24,128,128]{2,1,0:T(8,128)(2,1)S(1)}, u32[]{:S(2)}, u32[]{:S(2)}) collective-permute-start(bf16[24,128,128]{2,1,0:T(8,128)(2,1)S(1)} %mask_half.1.half), channel_id=1, source_target_pairs={{0,1},{1,2},{2,3},{3,4},{4,5},{5,6},{6,7},{7,8},{8,9},{9,10},{10,1... | collective-permute-start | bytes 2359304 | tf_op jit(solution)/shard_map/ppermute | solution.py:373
  15.4 29.0 %collective-permute-start.5 = (bf16[768,128]{1,0:T(8,128)(2,1)S(1)}, bf16[768,128]{1,0:T(8,128)(2,1)S(1)}, u32[]{:S(2)}, u32[]{:S(2)}) collective-permute-start(bf16[768,128]{1,0:T(8,128)(2,1)S(1)} %get-tuple-element.27), channel_id=1, source_target_pairs={{0,2},{1,3},{2,4},{3,5},{4,6},{5,7},{6,8},{7,9},{8,10},{9,11},{10,... | collective-permute-start | bytes 589832 | tf_op jit(solution)/shard_map/ppermute | solution.py:373
  15.8 28.6 %collective-permute-start.6 = (bf16[768,128]{1,0:T(8,128)(2,1)S(1)}, bf16[768,128]{1,0:T(8,128)(2,1)S(1)}, u32[]{:S(2)}, u32[]{:S(2)}) collective-permute-start(bf16[768,128]{1,0:T(8,128)(2,1)S(1)} %get-tuple-element.28), channel_id=1, source_target_pairs={{0,14},{1,15},{2,0},{3,1},{4,2},{5,3},{6,4},{7,5},{8,6},{9,7},{10,... | collective-permute-start | bytes 589832 | tf_op jit(solution)/shard_map/ppermute | solution.py:373
  20.9 5.5 %collective-permute-start.3 = (bf16[512,128]{1,0:T(8,128)(2,1)S(1)}, bf16[512,128]{1,0:T(8,128)(2,1)S(1)}, u32[]{:S(2)}, u32[]{:S(2)}) collective-permute-start(bf16[512,128]{1,0:T(8,128)(2,1)S(1)} %choose.1.g0), channel_id=1, source_target_pairs={{0,16},{1,17},{2,18},{3,19},{4,20},{5,21},{6,22},{7,23},{8,24},{9,... | collective-permute-start | bytes 393224 | tf_op jit(solution)/shard_map/ppermute | solution.py:373
  51.0 6.1 %collective-permute-start.7 = (f32[48,128]{1,0:T(8,128)S(1)}, f32[48,128]{1,0:T(8,128)S(1)}, u32[]{:S(2)}, u32[]{:S(2)}) collective-permute-start(f32[48,128]{1,0:T(8,128)S(1)} %get-tuple-element.38), channel_id=1, source_target_pairs={{0,16},{1,17},{2,18},{3,19},{4,20},{5,21},{6,22},{7,23},{8,24},{9,... | collective-permute-start | bytes 73736 | tf_op jit(solution)/shard_map/ppermute | solution.py:373
  52.2 3.1 %collective-permute-start.8 = (f32[24,128]{1,0:T(8,128)S(1)}, f32[24,128]{1,0:T(8,128)S(1)}, u32[]{:S(2)}, u32[]{:S(2)}) collective-permute-start(f32[24,128]{1,0:T(8,128)S(1)} %get-tuple-element.39), channel_id=1, source_target_pairs={{0,15},{1,0},{2,1},{3,2},{4,3},{5,4},{6,5},{7,6},{8,7},{9,8},{10,9... | collective-permute-start | bytes 36872 | tf_op jit(solution)/shard_map/ppermute | solution.py:373
  53.1 4.0 %collective-permute-start.9 = (f32[24,128]{1,0:T(8,128)S(1)}, f32[24,128]{1,0:T(8,128)S(1)}, u32[]{:S(2)}, u32[]{:S(2)}) collective-permute-start(f32[24,128]{1,0:T(8,128)S(1)} %get-tuple-element.40), channel_id=1, source_target_pairs={{0,31},{1,16},{2,17},{3,18},{4,19},{5,20},{6,21},{7,22},{8,23},{9,... | collective-permute-start | bytes 36872 | tf_op jit(solution)/shard_map/ppermute | solution.py:373

commit v2 on v1

--- a/solution.py
+++ b/solution.py
@@ -67,21 +67,23 @@
     return near(row, -1, count) >> 1
 
 
-def spread(count, win, occ, virt, g_self, g_right, g_left, g_far):
+def spread(count, occ, virt, g_self, g_right, g_left, g_far, sem):
     d = lax.axis_index("row")
-
-    def greens(out, dest):
-        first = column_chunk(dest, count)
+    copies = []
+    for out, by in ((g_right, 1), (g_left, -1), (g_far, 2), (g_self, 0)):
+        first = column_chunk(near(d, by, count), count)
         for c in range(2):
             chunk = lax.rem(first + c, count // 2)
             columns = pl.ds(pl.multiple_of(chunk * 128, 128), 128)
-            out[64 * c : 64 * c + 64, :] = occ[:, columns]
-            out[128 + 64 * c : 192 + 64 * c, :] = virt[:, columns]
-
-    greens(g_self, d)
-    greens(g_right, near(d, 1, count))
-    greens(g_left, near(d, -1, count))
-    greens(g_far, near(d, 2, count))
+            for base, green in ((0, occ), (128, virt)):
+                at = base + 64 * c
+                copies.append(
+                    pltpu.make_async_copy(green.at[:, columns], out.at[at : at + 64], sem.at[len(copies)])
+                )
+    for copy in copies:
+        copy.start()
+    for copy in copies:
+        copy.wait()
 
 
 def mask_half(tiles, coulomb, token, tensor, sem):
@@ -176,149 +178,137 @@
     return one_hot((128, 128), 1, bases)
 
 
-def dress_own(count, win, tiles, tensor, g0, g1, polar0, flat, dressed, far_l, far_r, hs, ms):
+PITCH = 136
+
+
+def halves(occ, blocks, outs, ms):
+    rows = occ.shape[0] // len(outs)
+    for i in range(0, len(blocks), 2):
+        m0, m1 = blocks[i](), blocks[i + 1]()
+        if ms is not None:
+            ms[i * PITCH : i * PITCH + 128, :] = m0.astype(F32)
+            ms[(i + 1) * PITCH : (i + 1) * PITCH + 128, :] = m1.astype(F32)
+        h = dot(occ, jnp.concatenate([m0, m1], axis=1))
+        for n, out in enumerate(outs):
+            part = h[n * rows : (n + 1) * rows]
+            out[i * PITCH : i * PITCH + 128, :] = part[:, :128]
+            out[(i + 1) * PITCH : (i + 1) * PITCH + 128, :] = part[:, 128:]
+
+
+def gather(ref, funcs, start):
+    return [ref[pl.ds(start + t, funcs, stride=PITCH), :] for t in range(8)]
+
+
+def dress(count, own, win, tiles, tensor, greens, *refs):
+    if own:
+        polar0, flat, dressed, far, hs, ms, same = refs
+    else:
+        (dressed, far, hs), ms = refs, None
     d = lax.axis_index("row")
     funcs = tensor.shape[1]
     mine = window_at(win, d)
     theirs = window_at(win, near(d, -1, count))
+    left, right = near(d, -1, count) * 2, near(d, 1, count) * 2
     mask = tile_mask(tiles, 32).astype(BF)
-    occ = jnp.concatenate([g0[0:128, :], g1[0:128, :]], axis=0)
-
-    def halves(i, carry):
-        at = pl.multiple_of(i * 272, 8)
-        m0 = tensor[0, 2 * i] * mask
-        m1 = tensor[0, 2 * i + 1] * mask
-        ms[pl.ds(at, 128), :] = m0.astype(F32)
-        ms[pl.ds(at + 136, 128), :] = m1.astype(F32)
-        h = dot(occ, jnp.concatenate([m0, m1], axis=1))
-        hs[0, pl.ds(at, 128), :] = h[:128, :128]
-        hs[0, pl.ds(at + 136, 128), :] = h[:128, 128:]
-        hs[1, pl.ds(at, 128), :] = h[128:, :128]
-        hs[1, pl.ds(at + 136, 128), :] = h[128:, 128:]
-        return carry
-
-    lax.fori_loop(0, funcs // 2, halves, 0, unroll=2)
-
-    def rows_at(ref, g, start):
-        return [ref[g, pl.ds(start + t, funcs, stride=136), :] for t in range(8)]
-
-    virt_a = g0[128:256, :]
-
-    def same_frame(i, total):
-        start = pl.multiple_of(i * 8, 8)
-        x = dot(jnp.concatenate(rows_at(hs, 0, start), axis=0).astype(BF), virt_a).astype(BF)
-        left = jnp.concatenate([x[t * funcs : (t + 1) * funcs] for t in range(8)], axis=1)
-        right = jnp.concatenate(
-            [ms[pl.ds(start + t, funcs, stride=136), :].astype(BF) for t in range(8)], axis=1
-        )
-        flat[:, pl.ds(pl.multiple_of(i * 1024, 1024), 1024)] = right
-        return total + dot_t(left, right)
-
-    polar0[...] = lax.fori_loop(0, 16, same_frame, jnp.zeros((funcs, funcs), F32))
-
-    to_theirs = frame_map(mine, theirs)
-    virts = [g0[128:256, :], g1[128:256, :]]
-    slots = [find(mine, a) for a in theirs]
-    for g in range(2):
-        virt_b = dot(virts[g], to_theirs).astype(BF)
-
-        def their_frame(i, carry):
-            j = i >> 2
-            slot = pick4(j, [s for s, _ in slots])
-            there = pick4(j, [w for _, w in slots])
-            start = slot * 32 + (i & 3) * 8
-            rows = jnp.concatenate(rows_at(hs, g, start), axis=0) * there
-            x = dot(rows.astype(BF), virt_b).astype(BF)
-            block = jnp.concatenate([x[t * funcs : (t + 1) * funcs] for t in range(8)], axis=1)
-            dressed[g * funcs : (g + 1) * funcs, pl.ds(pl.multiple_of(i * 1024, 1024), 1024)] = block
-            return carry
-
-        lax.fori_loop(0, 16, their_frame, 0)
-
-        for by, out in ((-1, far_l), (1, far_r)):
-            base = near(d, by, count) * 2
-            pair = [base, base + 1, base, base + 1]
-            two = dot(virts[g], frame_map(mine, pair)).astype(BF)
-            lane = iota((128, 128), 1)
-            zero = jnp.zeros((128, 128), BF)
-            both = jnp.concatenate(
-                [jnp.where(lane < 64, two, zero), jnp.where(lane < 64, zero, two)], axis=0
-            )
-            slot0, there0 = find(mine, base)
-            slot1, there1 = find(mine, base + 1)
-
-            def far_frame(i, carry):
-                x0 = jnp.concatenate(rows_at(hs, g, slot0 * 32 + i * 8), axis=0) * there0
-                x1 = jnp.concatenate(rows_at(hs, g, slot1 * 32 + i * 8), axis=0) * there1
-                x = dot(jnp.concatenate([x0, x1], axis=1).astype(BF), both).astype(BF)
-                block = jnp.concatenate([x[t * funcs : (t + 1) * funcs] for t in range(8)], axis=1)
-                out[g * funcs : (g + 1) * funcs, pl.ds(pl.multiple_of(i * 1024, 1024), 1024)] = block
-                return carry
-
-            lax.fori_loop(0, 4, far_frame, 0)
-
-
-def join(tensor, g0, g1, flat, dressed, far_l, far_r, from_left, from_right, own, other, up0, up1, hs, ms):
+    occ, virt = greens[0:128, :], greens[128:256, :]
+    halves(occ, [functools.partial(lambda r: tensor[0, r] * mask, r) for r in range(funcs)], [hs], ms)
+    frames = [
+        dot(virt, frame_map(mine, theirs)).astype(BF),
+        dot(virt, frame_map(mine, [left, left + 1, right, right + 1])).astype(BF),
+    ]
+    outs = [dressed, far]
+    if own:
+        frames, outs = [virt] + frames, [same] + outs
+    wide = jnp.concatenate(frames, axis=1)
+    for i in range(16):
+        x = dot(jnp.concatenate(gather(hs, funcs, i * 8), axis=0).astype(BF), wide)
+        for t in range(8):
+            at = (i * 8 + t) * 128
+            block = x[t * funcs : (t + 1) * funcs].astype(BF)
+            for n, out in enumerate(outs):
+                out[:, at : at + 128] = block[:, n * 128 : (n + 1) * 128]
+        if own:
+            for t, rows in enumerate(gather(ms, funcs, i * 8)):
+                at = (i * 8 + t) * 128
+                flat[:, at : at + 128] = rows.astype(BF)
+    if own:
+        polar0[...] = dot_t(same[...], flat[...])
+
+
+def join(
+    count,
+    win,
+    tensor,
+    g0,
+    g1,
+    flat,
+    dressed0,
+    dressed1,
+    far0,
+    far1,
+    from_left,
+    from_right,
+    own,
+    other,
+    up0,
+    up1,
+    hs0,
+    hs1,
+    ms,
+    backs,
+    moved,
+    tiles_far,
+):
+    d = lax.axis_index("row")
     funcs = tensor.shape[0]
     full = 2 * funcs
+    mine = window_at(win, d)
+    theirs = window_at(win, near(d, -1, count))
+    left, right = near(d, -1, count), near(d, 1, count)
     occ = jnp.concatenate([g0[256:384, :], g1[256:384, :]], axis=0)
+    halves(occ, [functools.partial(lambda r: tensor[r], r) for r in range(funcs)], [hs0, hs1], ms)
     virts = [g0[384:512, :], g1[384:512, :]]
-
-    def halves(i, carry):
-        at = i * 258
-        m0 = tensor[2 * i]
-        m1 = tensor[2 * i + 1]
-        ms[pl.ds(at, 128), :] = m0.astype(F32)
-        ms[pl.ds(at + 129, 128), :] = m1.astype(F32)
-        h = dot(occ, jnp.concatenate([m0, m1], axis=1))
-        hs[0, pl.ds(at, 128), :] = h[:128, :128]
-        hs[0, pl.ds(at + 129, 128), :] = h[:128, 128:]
-        hs[1, pl.ds(at, 128), :] = h[128:, :128]
-        hs[1, pl.ds(at + 129, 128), :] = h[128:, 128:]
-        return carry
-
-    lax.fori_loop(0, funcs // 2, halves, 0, unroll=2)
-
-    def bands(i, carry):
-        down, up = carry
-        start = pl.multiple_of(i * 8, 8)
-        columns = pl.ds(pl.multiple_of(i * 1024, 1024), 1024)
+    lane = iota((funcs, 128), 1)
+    for i in range(16):
+        slot, there = find(theirs, mine[i // 4])
         xs = []
-        for g in range(2):
-            rows = [hs[g, pl.ds(start + t, funcs, stride=129), :] for t in range(8)]
-            xs.append(dot(jnp.concatenate(rows, axis=0).astype(BF), virts[g]))
-        left = jnp.concatenate(
+        for hs, virt in zip((hs0, hs1), virts):
+            xs.append(dot(jnp.concatenate(gather(hs, funcs, i * 8), axis=0).astype(BF), virt))
+        rows = gather(ms, funcs, slot * 32 + (i % 4) * 8)
+        for t in range(8):
+            at = (i * 8 + t) * 128
+            part = slice(t * funcs, (t + 1) * funcs)
+            backs[:, at : at + 128] = jnp.concatenate([x[part] for x in xs], axis=0).astype(BF)
+            moved[:, at : at + 128] = (rows[t] * there).astype(BF)
+    for t in range(0, 32, 2):
+        pair = slice(t * funcs, (t + 2) * funcs)
+        for side, e, row in ((0, from_left, left), (1, from_right, right)):
+            both = e[pair, :].astype(F32)
+            for u in range(2):
+                x = both[u * funcs : (u + 1) * funcs]
+                turned = pltpu.roll(x, 64, 1)
+                for i in range(4):
+                    odd = lax.rem(mine[i], 2)
+                    here = (lane < 64) if side == 0 else (lane >= 64)
+                    value = jnp.where(odd == side, x, turned)
+                    at = (i * 32 + t + u) * 128
+                    kept = here & (jnp.broadcast_to(mine[i] >> 1, lane.shape) == row)
+                    tiles_far[side, :, at : at + 128] = jnp.where(kept, value, 0.0).astype(BF)
+    up = dot_t(backs[...], flat[...])
+    up = jnp.concatenate([up, jnp.zeros((full, 128 - full), F32)], axis=1)
+    up0[...] = up[:funcs]
+    up1[...] = up[funcs:]
+    for dressed, far, out in ((dressed0, far0, own), (dressed1, far1, other)):
+        far_dressed = far[...]
+        out[...] = jnp.concatenate(
             [
-                jnp.concatenate([x[t * funcs : (t + 1) * funcs] for x in xs], axis=0).astype(BF)
-                for t in range(8)
+                dot_t(far_dressed, tiles_far[0]),
+                dot_t(dressed[...], moved[...]),
+                dot_t(far_dressed, tiles_far[1]),
+                jnp.zeros((full, 128 - 3 * funcs), F32),
             ],
             axis=1,
         )
-        right = jnp.concatenate(
-            [ms[pl.ds(start + t, funcs, stride=129), :] for t in range(8)], axis=1
-        ).astype(BF)
-        return down + dot_t(dressed[:, columns], right), up + dot_t(left, flat[:, columns])
-
-    down, up = lax.fori_loop(
-        0, 16, bands, (jnp.zeros((2 * full, funcs), F32), jnp.zeros((full, full), F32))
-    )
-
-    def far(dressed_far, e):
-        total = jnp.zeros((2 * full, funcs), F32)
-        for i in range(4):
-            rows = e[i * 8 * funcs : (i + 1) * 8 * funcs, :].astype(F32)
-            right = jnp.concatenate([rows[t * funcs : (t + 1) * funcs] for t in range(8)], axis=1)
-            total = total + dot_t(dressed_far[:, i * 1024 : (i + 1) * 1024], right.astype(BF))
-        return total
-
-    parts = jnp.concatenate(
-        [far(far_l, from_left), down, far(far_r, from_right), jnp.zeros((2 * full, 128 - 3 * funcs), F32)], axis=1
-    )
-    own[...] = parts[:full]
-    other[...] = parts[full:]
-    up = jnp.concatenate([up, jnp.zeros((full, 128 - full), F32)], axis=1)
-    up0[...] = up[:funcs]
-    up1[...] = up[funcs:]
 
 
 def assemble(polar0, own, recv, up0, up1, out):
@@ -342,6 +332,10 @@
     return [pl.BlockSpec(memory_space=pltpu.VMEM)] * count
 
 
+def hbm(count):
+    return [pl.BlockSpec(memory_space=pltpu.HBM)] * count
+
+
 def smem(count):
     return [pl.BlockSpec(memory_space=pltpu.SMEM)] * count
 
@@ -376,9 +370,10 @@
     g_self, g_right, g_left, g_far = call(
         functools.partial(spread, count),
         "spread",
-        smem(1) + vmem(2),
+        hbm(2),
         [shape((256, 128), BF)] * 4,
-        (window, green_occ, green_virt),
+        (green_occ, green_virt),
+        [pltpu.SemaphoreType.DMA((16,))],
     )
     g_before = send(g_right, 1)
     g_after = send(g_left, -1)
@@ -386,7 +381,7 @@
     (tensor,) = call(
         mask_half,
         "mask_half",
-        smem(1) + [pl.BlockSpec(memory_space=pl.ANY)] * 2,
+        smem(1) + hbm(1) + [pl.BlockSpec(memory_space=pl.ANY)],
         [shape((funcs, 128, 128), BF)],
         (tile_list, coulomb3c, g_self),
         [pltpu.SemaphoreType.DMA],
@@ -414,32 +409,44 @@
         (window, g_self, g_before, g_after, g_beyond),
     )
     partner = send(mine, 0, True)
-    polar0, flat, dressed, far_l, far_r = call(
-        functools.partial(dress_own, count),
+    flat_shape = shape((full, 128 * 128), BF)
+    tall = pltpu.VMEM((full * PITCH, 128), F32)
+    polar0, flat, dressed0, far0 = call(
+        functools.partial(dress, count, True),
         "dress_own",
-        smem(2) + vmem(3),
-        [
-            shape((full, full), F32),
-            shape((full, 128 * 128), BF),
-            shape((2 * full, 128 * 128), BF),
-            shape((2 * full, 32 * 128), BF),
-            shape((2 * full, 32 * 128), BF),
-        ],
-        (window, tile_list, coulomb3c, mine, partner),
-        [pltpu.VMEM((2, full * 136, 128), F32), pltpu.VMEM((full * 136, 128), F32)],
-    )
+        smem(2) + vmem(2),
+        [shape((full, full), F32), flat_shape, flat_shape, flat_shape],
+        (window, tile_list, coulomb3c, mine),
+        [tall, tall, pltpu.VMEM((full, 128 * 128), BF)],
+    )
+    dressed1, far1 = call(
+        functools.partial(dress, count, False),
+        "dress_partner",
+        smem(2) + vmem(2),
+        [flat_shape, flat_shape],
+        (window, tile_list, coulomb3c, partner),
+        [tall],
+    )
+    short = pltpu.VMEM((funcs * PITCH, 128), F32)
     own, other, up0, up1 = call(
-        join,
+        functools.partial(join, count),
         "join",
-        vmem(9),
+        smem(1) + vmem(10),
         [
             shape((full, 128), F32),
             shape((full, 128), F32),
             shape((funcs, 128), F32),
             shape((funcs, 128), F32),
         ],
-        (wide, mine, partner, flat, dressed, far_l, far_r, from_left, from_right),
-        [pltpu.VMEM((2, funcs * 129, 128), F32), pltpu.VMEM((funcs * 129, 128), F32)],
+        (window, wide, mine, partner, flat, dressed0, dressed1, far0, far1, from_left, from_right),
+        [
+            short,
+            short,
+            short,
+            pltpu.VMEM((full, 128 * 128), BF),
+            pltpu.VMEM((funcs, 128 * 128), BF),
+            pltpu.VMEM((2, funcs, 128 * 128), BF),
+        ],
     )
     recv = send(other, 0, True)
     after0 = send(up0, -1)

time: 58.1 us -> 46 us (0.79)
  the two profiles are of different devices: /device:TPU:1 before, /device:TPU:0 now
where the time goes in v2:
time: 46 us; the launch traced here: 45.8 us
  Pallas kernels  17 us (37%)
  starting transfers between devices  15.5 us (34%)
  waiting for transfers between devices  9.23 us (20%)
  local copies, waits for them, and re-layouts  3.99 us (9%)
    pallas_call x8, Pallas kernels, call(): pl.pallas_call(kernel, name=name, in_specs=specs, out_specs=tuple(vmem(le...  17 us
    ppermute x10, starting transfers between devices, send(): return lax.ppermute(array, ('grp', 'row'), pairs)  15.5 us
    ppermute x10, waiting for transfers between devices, send(): return lax.ppermute(array, ('grp', 'row'), pairs)  9.23 us
    unnamed x15, local copies, waits for them, and re-layouts  3.99 us
  transfers between devices with their start and end apart: 10, of which 4 were waited for; matrix products, arithmetic and copies ran while one was open for 0% of the time, Pallas kernels for 22%

profile of v2, /device:TPU:0, one launch (start us, length us, event | category | flops | bytes accessed | tf_op | source)
XLA Modules:
  0.0 45.8 jit_solution(3054762787219872694)
XLA Ops:
  0.0 0.0 copy-start.2
  0.0 0.9 %copy-done.2 = bf16[64,1024]{1,0:T(8,128)(2,1)S(1)} copy-done((bf16[64,1024]{1,0:T(8,128)(2,1)S(1)}, bf16[64,1024]{1,0:T(8,128)(2,1)}, u32[]{:S(2)}) %copy-start.2) | copy-done | bytes 131096
  0.9 0.0 copy-start.3
  0.9 0.9 %copy-done.3 = bf16[64,1024]{1,0:T(8,128)(2,1)S(1)} copy-done((bf16[64,1024]{1,0:T(8,128)(2,1)S(1)}, bf16[64,1024]{1,0:T(8,128)(2,1)}, u32[]{:S(2)}) %copy-start.3) | copy-done | bytes 131096
  1.8 0.0 copy-start.6
  1.8 0.3 spread.1
  2.1 0.5 %collective-permute-start = (bf16[256,128]{1,0:T(8,128)(2,1)S(1)}, bf16[256,128]{1,0:T(8,128)(2,1)S(1)}, u32[]{:S(2)}, u32[]{:S(2)}) collective-permute-start(bf16[256,128]{1,0:T(8,128)(2,1)S(1)} %get-tuple-element.25), channel_id=1, source_target_pairs={{0,1},{1,2},{2,3},{3,4},{4,5},{5,6},{6,7},{7,8},{8,9},{9,10},{10,1... | collective-permute-start | bytes 196616 | tf_op jit(solution)/shard_map/ppermute | solution.py:367
  2.6 5.1 %collective-permute-start.1 = (bf16[256,128]{1,0:T(8,128)(2,1)S(1)}, bf16[256,128]{1,0:T(8,128)(2,1)S(1)}, u32[]{:S(2)}, u32[]{:S(2)}) collective-permute-start(bf16[256,128]{1,0:T(8,128)(2,1)S(1)} %get-tuple-element.26), channel_id=1, source_target_pairs={{0,15},{1,0},{2,1},{3,2},{4,3},{5,4},{6,5},{7,6},{8,7},{9,8},{10,9... | collective-permute-start | bytes 196616 | tf_op jit(solution)/shard_map/ppermute | solution.py:367
  7.6 0.0 collective-permute-start.2
  7.6 0.0 copy-start
  7.6 1.4 %copy-done = bf16[1,48,128,128]{3,2,1,0:T(8,128)(2,1)S(1)} copy-done((bf16[1,48,128,128]{3,2,1,0:T(8,128)(2,1)S(1)}, bf16[1,48,128,128]{3,2,1,0:T(8,128)(2,1)}, u32[]{:S(2)}) %copy-start) | copy-done | bytes 1572888
  9.1 0.0 copy-start.4
  9.1 0.7 %copy-done.4 = s32[1,4,4]{2,1,0:T(4,128)S(1)} copy-done((s32[1,4,4]{2,1,0:T(4,128)S(1)}, s32[1,4,4]{2,1,0:T(4,128)}, u32[]{:S(2)}) %copy-start.4) | copy-done | bytes 88
  9.7 0.8 %mask_half.1.half = bf16[24,128,128]{2,1,0:T(8,128)(2,1)S(1)} custom-call(s32[1,4,4]{2,1,0:T(4,128)S(1)} %copy-done.4, bf16[1,48,128,128]{3,2,1,0:T(8,128)(2,1)S(1)} %copy-done, bf16[256,128]{1,0:T(8,128)(2,1)S(1)} %get-tuple-element.24.token.g_self), custom_call_target="tpu_custom_call" | custom-call | tf_op jit(solution)/shard_map/mask_half/pallas_call | solution.py:344
  10.5 0.1 collective-permute-start.3
  10.6 0.0 copy-done.6
  10.6 0.1 copy.8.win
  10.7 0.0 copy-start.1
  10.7 0.0 copy-start.5
  10.7 2.3 %far_tiles.1 = (bf16[768,128]{1,0:T(8,128)(2,1)S(1)}, bf16[768,128]{1,0:T(8,128)(2,1)S(1)}) custom-call(s32[16,4]{1,0:T(8,128)S(1)} %copy.8.win, bf16[24,128,128]{2,1,0:T(8,128)(2,1)S(1)} %mask_half.1.half), custom_call_target="tpu_custom_call" | custom-call | flops 68719476736 | tf_op jit(solution)/shard_map/far_tiles/pallas_call | solution.py:344
  12.9 1.7 %collective-permute-start.5 = (bf16[768,128]{1,0:T(8,128)(2,1)S(1)}, bf16[768,128]{1,0:T(8,128)(2,1)S(1)}, u32[]{:S(2)}, u32[]{:S(2)}) collective-permute-start(bf16[768,128]{1,0:T(8,128)(2,1)S(1)} %get-tuple-element.28), channel_id=1, source_target_pairs={{0,2},{1,3},{2,4},{3,5},{4,6},{5,7},{6,8},{7,9},{8,10},{9,11},{10,... | collective-permute-start | bytes 589832 | tf_op jit(solution)/shard_map/ppermute | solution.py:367
  14.6 0.0 collective-permute-done.g_before
  14.6 3.2 %collective-permute-start.6 = (bf16[768,128]{1,0:T(8,128)(2,1)S(1)}, bf16[768,128]{1,0:T(8,128)(2,1)S(1)}, u32[]{:S(2)}, u32[]{:S(2)}) collective-permute-start(bf16[768,128]{1,0:T(8,128)(2,1)S(1)} %get-tuple-element.29), channel_id=1, source_target_pairs={{0,14},{1,15},{2,0},{3,1},{4,2},{5,3},{6,4},{7,5},{8,6},{9,7},{10,... | collective-permute-start | bytes 589832 | tf_op jit(solution)/shard_map/ppermute | solution.py:367
  17.8 0.0 collective-permute-done.1.g_after
  17.8 0.0 collective-permute-done.2.g_far
  17.8 1.4 %choose.1.greens.g0 = bf16[512,128]{1,0:T(8,128)(2,1)S(1)} custom-call(s32[16,4]{1,0:T(8,128)S(1)} %copy.8.win, bf16[256,128]{1,0:T(8,128)(2,1)S(1)} %get-tuple-element.24.token.g_self, bf16[256,128]{1,0:T(8,128)(2,1)S(1)} %collective-permute-done.g_before, bf16[256,128]{1,0:T(8,128)(2,1)S(1)} %collective-permute-done.1.g_after, ...), custom_call_target="tpu_custom_call" | custom-call | tf_op jit(solution)/shard_map/choose/pallas_call | solution.py:344
  19.2 1.9 %collective-permute-start.4 = (bf16[512,128]{1,0:T(8,128)(2,1)S(1)}, bf16[512,128]{1,0:T(8,128)(2,1)S(1)}, u32[]{:S(2)}, u32[]{:S(2)}) collective-permute-start(bf16[512,128]{1,0:T(8,128)(2,1)S(1)} %choose.1.greens.g0), channel_id=1, source_target_pairs={{0,16},{1,17},{2,18},{3,19},{4,20},{5,21},{6,22},{7,23},{8,24},{9,... | collective-permute-start | bytes 393224 | tf_op jit(solution)/shard_map/ppermute | solution.py:367
  21.1 0.0 copy-done.1
  21.1 0.0 copy-done.5
  21.1 3.6 %dress_own.1 = (f32[48,48]{1,0:T(8,128)S(1)}, bf16[48,16384]{1,0:T(8,128)(2,1)S(1)}, bf16[48,16384]{1,0:T(8,128)(2,1)S(1)}, bf16[48,16384]{1,0:T(8,128)(2,1)S(1)}) custom-call(s32[16,4]{1,0:T(8,128)S(1)} %copy.8.win, s32[1,4,4]{2,1,0:T(4,128)S(1)} %copy-done.5, bf16[1,48,128,128]{3,2,1,0:T(8,128)(2,1)S(1)} %copy-done.1, bf16[512,128]{1,0:T(8,128)(2,1)S(1)} %choose.1.greens.g0), custom_call_target="tpu_custom_call" | custom-call | tf_op jit(solution)/shard_map/dress_own/pallas_call | solution.py:344
  24.7 0.8 %collective-permute-done.4.greens.g1 = bf16[512,128]{1,0:T(8,128)(2,1)S(1)} collective-permute-done((bf16[512,128]{1,0:T(8,128)(2,1)S(1)}, bf16[512,128]{1,0:T(8,128)(2,1)S(1)}, u32[]{:S(2)}, u32[]{:S(2)}) %collective-permute-start.4) | collective-permute-done | bytes 131104 | tf_op jit(solution)/shard_map/ppermute | solution.py:367
  25.5 2.3 %dress_partner.1 = (bf16[48,16384]{1,0:T(8,128)(2,1)S(1)}, bf16[48,16384]{1,0:T(8,128)(2,1)S(1)}) custom-call(s32[16,4]{1,0:T(8,128)S(1)} %copy.8.win, s32[1,4,4]{2,1,0:T(4,128)S(1)} %copy-done.5, bf16[1,48,128,128]{3,2,1,0:T(8,128)(2,1)S(1)} %copy-done.1, bf16[512,128]{1,0:T(8,128)(2,1)S(1)} %collective-permute-done.4.greens.g1), custom_call_target="tpu_custom_call" | custom-call | tf_op jit(solution)/shard_map/dress_partner/pallas_call | solution.py:344
  27.8 0.0 collective-permute-done.5.from_left
  27.8 5.3 %collective-permute-done.6.from_right = bf16[768,128]{1,0:T(8,128)(2,1)S(1)} collective-permute-done((bf16[768,128]{1,0:T(8,128)(2,1)S(1)}, bf16[768,128]{1,0:T(8,128)(2,1)S(1)}, u32[]{:S(2)}, u32[]{:S(2)}) %collective-permute-start.6) | collective-permute-done | bytes 196640 | tf_op jit(solution)/shard_map/ppermute | solution.py:367
  33.1 0.0 collective-permute-done.3.tensor
  33.1 5.8 %join.1 = (f32[48,128]{1,0:T(8,128)S(1)}, f32[48,128]{1,0:T(8,128)S(1)}, f32[24,128]{1,0:T(8,128)S(1)}, f32[24,128]{1,0:T(8,128)S(1)}) custom-call(s32[16,4]{1,0:T(8,128)S(1)} %copy.8.win, bf16[24,128,128]{2,1,0:T(8,128)(2,1)S(1)} %collective-permute-done.3.tensor, bf16[512,128]{1,0:T(8,128)(2,1)S(1)} %choose.1.greens.g0, ...), custom_call_target="tpu_custom_call" | custom-call | tf_op jit(solution)/shard_map/join/pallas_call | solution.py:344
  38.9 1.9 %collective-permute-start.7 = (f32[48,128]{1,0:T(8,128)S(1)}, f32[48,128]{1,0:T(8,128)S(1)}, u32[]{:S(2)}, u32[]{:S(2)}) collective-permute-start(f32[48,128]{1,0:T(8,128)S(1)} %get-tuple-element.40), channel_id=1, source_target_pairs={{0,16},{1,17},{2,18},{3,19},{4,20},{5,21},{6,22},{7,23},{8,24},{9,... | collective-permute-start | bytes 73736 | tf_op jit(solution)/shard_map/ppermute | solution.py:367
  40.8 1.2 %collective-permute-start.8 = (f32[24,128]{1,0:T(8,128)S(1)}, f32[24,128]{1,0:T(8,128)S(1)}, u32[]{:S(2)}, u32[]{:S(2)}) collective-permute-start(f32[24,128]{1,0:T(8,128)S(1)} %get-tuple-element.41), channel_id=1, source_target_pairs={{0,15},{1,0},{2,1},{3,2},{4,3},{5,4},{6,5},{7,6},{8,7},{9,8},{10,9... | collective-permute-start | bytes 36872 | tf_op jit(solution)/shard_map/ppermute | solution.py:367
  42.0 0.0 collective-permute-start.9
  42.0 1.4 %collective-permute-done.8.up0 = f32[24,128]{1,0:T(8,128)S(1)} collective-permute-done((f32[24,128]{1,0:T(8,128)S(1)}, f32[24,128]{1,0:T(8,128)S(1)}, u32[]{:S(2)}, u32[]{:S(2)}) %collective-permute-start.8) | collective-permute-done | bytes 12320 | tf_op jit(solution)/shard_map/ppermute | solution.py:367
  43.4 1.7 %collective-permute-done.9.up1 = f32[24,128]{1,0:T(8,128)S(1)} collective-permute-done((f32[24,128]{1,0:T(8,128)S(1)}, f32[24,128]{1,0:T(8,128)S(1)}, u32[]{:S(2)}, u32[]{:S(2)}) %collective-permute-start.9) | collective-permute-done | bytes 12320 | tf_op jit(solution)/shard_map/ppermute | solution.py:367
  45.1 0.0 collective-permute-done.7.recv
  45.1 0.7 %assemble.1 = f32[48,240]{1,0:T(8,128)} custom-call(f32[48,48]{1,0:T(8,128)S(1)} %get-tuple-element.33.polar0, f32[48,128]{1,0:T(8,128)S(1)} %get-tuple-element.39.own, f32[48,128]{1,0:T(8,128)S(1)} %collective-permute-done.7.recv, f32[24,128]{1,0:T(8,128)S(1)} %collective-permute-done.8.up0, f32[24,128]{1,0:T(8,128)S(1)} %collective-permute-done.9.up1), custom_call_target="tpu_custom_call" | custom-call | tf_op jit(solution)/shard_map/assemble/pallas_call | solution.py:344
Async XLA Ops:
  0.0 0.9 %copy-start.2 = (bf16[64,1024]{1,0:T(8,128)(2,1)S(1)}, bf16[64,1024]{1,0:T(8,128)(2,1)}, u32[]{:S(2)}) copy-start(bf16[64,1024]{1,0:T(8,128)(2,1)} %occ.1) | copy-start | bytes 393220
  0.9 0.9 %copy-start.3 = (bf16[64,1024]{1,0:T(8,128)(2,1)S(1)}, bf16[64,1024]{1,0:T(8,128)(2,1)}, u32[]{:S(2)}) copy-start(bf16[64,1024]{1,0:T(8,128)(2,1)} %virt.1) | copy-start | bytes 393220
  1.8 8.8 %copy-start.6 = (s32[16,4]{0,1:T(4,128)S(1)}, s32[16,4]{0,1:T(4,128)}, u32[]{:S(2)}) copy-start(s32[16,4]{0,1:T(4,128)} %param.9) | copy-start | bytes 772
  2.1 12.5 %collective-permute-start = (bf16[256,128]{1,0:T(8,128)(2,1)S(1)}, bf16[256,128]{1,0:T(8,128)(2,1)S(1)}, u32[]{:S(2)}, u32[]{:S(2)}) collective-permute-start(bf16[256,128]{1,0:T(8,128)(2,1)S(1)} %get-tuple-element.25), channel_id=1, source_target_pairs={{0,1},{1,2},{2,3},{3,4},{4,5},{5,6},{6,7},{7,8},{8,9},{9,10},{10,1... | collective-permute-start | bytes 196616 | tf_op jit(solution)/shard_map/ppermute | solution.py:367
  2.6 15.2 %collective-permute-start.1 = (bf16[256,128]{1,0:T(8,128)(2,1)S(1)}, bf16[256,128]{1,0:T(8,128)(2,1)S(1)}, u32[]{:S(2)}, u32[]{:S(2)}) collective-permute-start(bf16[256,128]{1,0:T(8,128)(2,1)S(1)} %get-tuple-element.26), channel_id=1, source_target_pairs={{0,15},{1,0},{2,1},{3,2},{4,3},{5,4},{6,5},{7,6},{8,7},{9,8},{10,9... | collective-permute-start | bytes 196616 | tf_op jit(solution)/shard_map/ppermute | solution.py:367
  7.6 10.2 %collective-permute-start.2 = (bf16[256,128]{1,0:T(8,128)(2,1)S(1)}, bf16[256,128]{1,0:T(8,128)(2,1)S(1)}, u32[]{:S(2)}, u32[]{:S(2)}) collective-permute-start(bf16[256,128]{1,0:T(8,128)(2,1)S(1)} %get-tuple-element.27), channel_id=1, source_target_pairs={{0,2},{1,3},{2,4},{3,5},{4,6},{5,7},{6,8},{7,9},{8,10},{9,11},{10,... | collective-permute-start | bytes 196616 | tf_op jit(solution)/shard_map/ppermute | solution.py:367
  7.6 1.4 %copy-start = (bf16[1,48,128,128]{3,2,1,0:T(8,128)(2,1)S(1)}, bf16[1,48,128,128]{3,2,1,0:T(8,128)(2,1)}, u32[]{:S(2)}) copy-start(bf16[1,48,128,128]{3,2,1,0:T(8,128)(2,1)} %tensor.3) | copy-start | bytes 4718596
  9.1 0.7 %copy-start.4 = (s32[1,4,4]{2,1,0:T(4,128)S(1)}, s32[1,4,4]{2,1,0:T(4,128)}, u32[]{:S(2)}) copy-start(s32[1,4,4]{2,1,0:T(4,128)} %tiles.5) | copy-start | bytes 196
  10.5 22.6 %collective-permute-start.3 = (bf16[24,128,128]{2,1,0:T(8,128)(2,1)S(1)}, bf16[24,128,128]{2,1,0:T(8,128)(2,1)S(1)}, u32[]{:S(2)}, u32[]{:S(2)}) collective-permute-start(bf16[24,128,128]{2,1,0:T(8,128)(2,1)S(1)} %mask_half.1.half), channel_id=1, source_target_pairs={{0,1},{1,2},{2,3},{3,4},{4,5},{5,6},{6,7},{7,8},{8,9},{9,10},{10,1... | collective-permute-start | bytes 2359304 | tf_op jit(solution)/shard_map/ppermute | solution.py:367
  10.7 10.4 %copy-start.1 = (bf16[1,48,128,128]{3,2,1,0:T(8,128)(2,1)S(1)}, bf16[1,48,128,128]{3,2,1,0:T(8,128)(2,1)}, u32[]{:S(2)}) copy-start(bf16[1,48,128,128]{3,2,1,0:T(8,128)(2,1)} %tensor.3) | copy-start | bytes 4718596
  10.7 10.4 %copy-start.5 = (s32[1,4,4]{2,1,0:T(4,128)S(1)}, s32[1,4,4]{2,1,0:T(4,128)}, u32[]{:S(2)}) copy-start(s32[1,4,4]{2,1,0:T(4,128)} %tiles.5) | copy-start | bytes 196
  12.9 14.8 %collective-permute-start.5 = (bf16[768,128]{1,0:T(8,128)(2,1)S(1)}, bf16[768,128]{1,0:T(8,128)(2,1)S(1)}, u32[]{:S(2)}, u32[]{:S(2)}) collective-permute-start(bf16[768,128]{1,0:T(8,128)(2,1)S(1)} %get-tuple-element.28), channel_id=1, source_target_pairs={{0,2},{1,3},{2,4},{3,5},{4,6},{5,7},{6,8},{7,9},{8,10},{9,11},{10,... | collective-permute-start | bytes 589832 | tf_op jit(solution)/shard_map/ppermute | solution.py:367
  14.6 18.5 %collective-permute-start.6 = (bf16[768,128]{1,0:T(8,128)(2,1)S(1)}, bf16[768,128]{1,0:T(8,128)(2,1)S(1)}, u32[]{:S(2)}, u32[]{:S(2)}) collective-permute-start(bf16[768,128]{1,0:T(8,128)(2,1)S(1)} %get-tuple-element.29), channel_id=1, source_target_pairs={{0,14},{1,15},{2,0},{3,1},{4,2},{5,3},{6,4},{7,5},{8,6},{9,7},{10,... | collective-permute-start | bytes 589832 | tf_op jit(solution)/shard_map/ppermute | solution.py:367
  19.2 6.3 %collective-permute-start.4 = (bf16[512,128]{1,0:T(8,128)(2,1)S(1)}, bf16[512,128]{1,0:T(8,128)(2,1)S(1)}, u32[]{:S(2)}, u32[]{:S(2)}) collective-permute-start(bf16[512,128]{1,0:T(8,128)(2,1)S(1)} %choose.1.greens.g0), channel_id=1, source_target_pairs={{0,16},{1,17},{2,18},{3,19},{4,20},{5,21},{6,22},{7,23},{8,24},{9,... | collective-permute-start | bytes 393224 | tf_op jit(solution)/shard_map/ppermute | solution.py:367
  38.9 6.2 %collective-permute-start.7 = (f32[48,128]{1,0:T(8,128)S(1)}, f32[48,128]{1,0:T(8,128)S(1)}, u32[]{:S(2)}, u32[]{:S(2)}) collective-permute-start(f32[48,128]{1,0:T(8,128)S(1)} %get-tuple-element.40), channel_id=1, source_target_pairs={{0,16},{1,17},{2,18},{3,19},{4,20},{5,21},{6,22},{7,23},{8,24},{9,... | collective-permute-start | bytes 73736 | tf_op jit(solution)/shard_map/ppermute | solution.py:367
  40.8 2.6 %collective-permute-start.8 = (f32[24,128]{1,0:T(8,128)S(1)}, f32[24,128]{1,0:T(8,128)S(1)}, u32[]{:S(2)}, u32[]{:S(2)}) collective-permute-start(f32[24,128]{1,0:T(8,128)S(1)} %get-tuple-element.41), channel_id=1, source_target_pairs={{0,15},{1,0},{2,1},{3,2},{4,3},{5,4},{6,5},{7,6},{8,7},{9,8},{10,9... | collective-permute-start | bytes 36872 | tf_op jit(solution)/shard_map/ppermute | solution.py:367
  42.0 3.1 %collective-permute-start.9 = (f32[24,128]{1,0:T(8,128)S(1)}, f32[24,128]{1,0:T(8,128)S(1)}, u32[]{:S(2)}, u32[]{:S(2)}) collective-permute-start(f32[24,128]{1,0:T(8,128)S(1)} %get-tuple-element.42), channel_id=1, source_target_pairs={{0,31},{1,16},{2,17},{3,18},{4,19},{5,20},{6,21},{7,22},{8,23},{9,... | collective-permute-start | bytes 36872 | tf_op jit(solution)/shard_map/ppermute | solution.py:367

commit v3 on v2

--- a/solution.py
+++ b/solution.py
@@ -67,13 +67,17 @@
     return near(row, -1, count) >> 1
 
 
-def spread(count, occ, virt, g_self, g_right, g_left, g_far, sem):
-    d = lax.axis_index("row")
-    copies = []
+def first(count, occ, virt, tiles_hbm, coulomb, g_self, g_right, g_left, g_far, tensor, tiles, sem):
+    d = lax.axis_index("row")
+    funcs = tensor.shape[0]
+    half = lax.rem(lax.axis_index("grp"), 2)
+    list_copy = pltpu.make_async_copy(tiles_hbm, tiles, sem.at[0])
+    half_copy = pltpu.make_async_copy(coulomb.at[0, pl.ds(half * funcs, funcs)], tensor, sem.at[1])
+    copies = [list_copy, half_copy]
     for out, by in ((g_right, 1), (g_left, -1), (g_far, 2), (g_self, 0)):
-        first = column_chunk(near(d, by, count), count)
+        start = column_chunk(near(d, by, count), count)
         for c in range(2):
-            chunk = lax.rem(first + c, count // 2)
+            chunk = lax.rem(start + c, count // 2)
             columns = pl.ds(pl.multiple_of(chunk * 128, 128), 128)
             for base, green in ((0, occ), (128, virt)):
                 at = base + 64 * c
@@ -82,18 +86,12 @@
                 )
     for copy in copies:
         copy.start()
-    for copy in copies:
+    list_copy.wait()
+    mask = tile_mask(tiles, 32).astype(BF)
+    half_copy.wait()
+    tensor[...] = tensor[...] * mask[None]
+    for copy in copies[2:]:
         copy.wait()
-
-
-def mask_half(tiles, coulomb, token, tensor, sem):
-    funcs = tensor.shape[0]
-    half = lax.rem(lax.axis_index("grp"), 2)
-    copy = pltpu.make_async_copy(coulomb.at[0, pl.ds(half * funcs, funcs)], tensor, sem)
-    copy.start()
-    mask = tile_mask(tiles, 32).astype(BF)
-    copy.wait()
-    tensor[...] = tensor[...] * mask[None]
 
 
 def far_tiles(count, win, half, far_right, far_left, xs):
@@ -235,40 +233,15 @@
         polar0[...] = dot_t(same[...], flat[...])
 
 
-def join(
-    count,
-    win,
-    tensor,
-    g0,
-    g1,
-    flat,
-    dressed0,
-    dressed1,
-    far0,
-    far1,
-    from_left,
-    from_right,
-    own,
-    other,
-    up0,
-    up1,
-    hs0,
-    hs1,
-    ms,
-    backs,
-    moved,
-    tiles_far,
-):
+def join(count, win, tensor, g0, g1, flat, dressed0, dressed1, down0, down1, up0, up1, hs0, hs1, ms, backs, moved):
     d = lax.axis_index("row")
     funcs = tensor.shape[0]
     full = 2 * funcs
     mine = window_at(win, d)
     theirs = window_at(win, near(d, -1, count))
-    left, right = near(d, -1, count), near(d, 1, count)
     occ = jnp.concatenate([g0[256:384, :], g1[256:384, :]], axis=0)
     halves(occ, [functools.partial(lambda r: tensor[r], r) for r in range(funcs)], [hs0, hs1], ms)
     virts = [g0[384:512, :], g1[384:512, :]]
-    lane = iota((funcs, 128), 1)
     for i in range(16):
         slot, there = find(theirs, mine[i // 4])
         xs = []
@@ -280,6 +253,23 @@
             part = slice(t * funcs, (t + 1) * funcs)
             backs[:, at : at + 128] = jnp.concatenate([x[part] for x in xs], axis=0).astype(BF)
             moved[:, at : at + 128] = (rows[t] * there).astype(BF)
+    up = dot_t(backs[...], flat[...])
+    up = jnp.concatenate([up, jnp.zeros((full, 128 - full), F32)], axis=1)
+    up0[...] = up[:funcs]
+    up1[...] = up[funcs:]
+    for dressed, out in ((dressed0, down0), (dressed1, down1)):
+        out[...] = jnp.concatenate(
+            [dot_t(dressed[...], moved[...]), jnp.zeros((full, 128 - funcs), F32)], axis=1
+        )
+
+
+def join_far(count, win, far0, far1, from_left, from_right, down0, down1, own, other, tiles_far):
+    d = lax.axis_index("row")
+    full = far0.shape[0]
+    funcs = full // 2
+    mine = window_at(win, d)
+    left, right = near(d, -1, count), near(d, 1, count)
+    lane = iota((funcs, 128), 1)
     for t in range(0, 32, 2):
         pair = slice(t * funcs, (t + 2) * funcs)
         for side, e, row in ((0, from_left, left), (1, from_right, right)):
@@ -294,17 +284,13 @@
                     at = (i * 32 + t + u) * 128
                     kept = here & (jnp.broadcast_to(mine[i] >> 1, lane.shape) == row)
                     tiles_far[side, :, at : at + 128] = jnp.where(kept, value, 0.0).astype(BF)
-    up = dot_t(backs[...], flat[...])
-    up = jnp.concatenate([up, jnp.zeros((full, 128 - full), F32)], axis=1)
-    up0[...] = up[:funcs]
-    up1[...] = up[funcs:]
-    for dressed, far, out in ((dressed0, far0, own), (dressed1, far1, other)):
-        far_dressed = far[...]
+    for far, down, out in ((far0, down0, own), (far1, down1, other)):
+        dressed = far[...]
         out[...] = jnp.concatenate(
             [
-                dot_t(far_dressed, tiles_far[0]),
-                dot_t(dressed[...], moved[...]),
-                dot_t(far_dressed, tiles_far[1]),
+                dot_t(dressed, tiles_far[0]),
+                down[:, :funcs],
+                dot_t(dressed, tiles_far[1]),
                 jnp.zeros((full, 128 - 3 * funcs), F32),
             ],
             axis=1,
@@ -340,7 +326,7 @@
     return [pl.BlockSpec(memory_space=pltpu.SMEM)] * count
 
 
-def call(kernel, name, specs, outs, args, scratch=(), flops=0, moved=0):
+def call(kernel, name, specs, outs, args, scratch=(), flops=0, limit=40 << 20):
     return pl.pallas_call(
         kernel,
         name=name,
@@ -348,8 +334,8 @@
         out_specs=tuple(vmem(len(outs))),
         out_shape=tuple(outs),
         scratch_shapes=list(scratch),
-        compiler_params=pltpu.CompilerParams(vmem_limit_bytes=40 << 20),
-        cost_estimate=pl.CostEstimate(flops=flops, bytes_accessed=moved, transcendentals=0),
+        compiler_params=pltpu.CompilerParams(vmem_limit_bytes=limit),
+        cost_estimate=pl.CostEstimate(flops=flops, bytes_accessed=0, transcendentals=0),
     )(*args)
 
 
@@ -367,25 +353,18 @@
         return lax.ppermute(array, ("grp", "row"), pairs)
 
     far_rows = funcs * 32
-    g_self, g_right, g_left, g_far = call(
-        functools.partial(spread, count),
-        "spread",
-        hbm(2),
-        [shape((256, 128), BF)] * 4,
-        (green_occ, green_virt),
-        [pltpu.SemaphoreType.DMA((16,))],
+    g_self, g_right, g_left, g_far, tensor = call(
+        functools.partial(first, count),
+        "first",
+        hbm(4),
+        [shape((256, 128), BF)] * 4 + [shape((funcs, 128, 128), BF)],
+        (green_occ, green_virt, tile_list, coulomb3c),
+        [pltpu.SMEM((1, 4, 4), jnp.int32), pltpu.SemaphoreType.DMA((18,))],
+        limit=60 << 20,
     )
     g_before = send(g_right, 1)
     g_after = send(g_left, -1)
     g_beyond = send(g_far, 2)
-    (tensor,) = call(
-        mask_half,
-        "mask_half",
-        smem(1) + hbm(1) + [pl.BlockSpec(memory_space=pl.ANY)],
-        [shape((funcs, 128, 128), BF)],
-        (tile_list, coulomb3c, g_self),
-        [pltpu.SemaphoreType.DMA],
-    )
     wide = send(tensor, 1)
     far_right, far_left = call(
         functools.partial(far_tiles, count),
@@ -428,29 +407,26 @@
         [tall],
     )
     short = pltpu.VMEM((funcs * PITCH, 128), F32)
-    own, other, up0, up1 = call(
+    down0, down1, up0, up1 = call(
         functools.partial(join, count),
         "join",
-        smem(1) + vmem(10),
-        [
-            shape((full, 128), F32),
-            shape((full, 128), F32),
-            shape((funcs, 128), F32),
-            shape((funcs, 128), F32),
-        ],
-        (window, wide, mine, partner, flat, dressed0, dressed1, far0, far1, from_left, from_right),
-        [
-            short,
-            short,
-            short,
-            pltpu.VMEM((full, 128 * 128), BF),
-            pltpu.VMEM((funcs, 128 * 128), BF),
-            pltpu.VMEM((2, funcs, 128 * 128), BF),
-        ],
-    )
-    recv = send(other, 0, True)
+        smem(1) + vmem(6),
+        [shape((full, 128), F32)] * 2 + [shape((funcs, 128), F32)] * 2,
+        (window, wide, mine, partner, flat, dressed0, dressed1),
+        [short, short, short, pltpu.VMEM((full, 128 * 128), BF), pltpu.VMEM((funcs, 128 * 128), BF)],
+    )
     after0 = send(up0, -1)
     after1 = send(up1, -1, True)
+    own, other = call(
+        functools.partial(join_far, count),
+        "join_far",
+        smem(1) + vmem(6),
+        [shape((full, 128), F32)] * 2,
+        (window, far0, far1, from_left, from_right, down0, down1),
+        [pltpu.VMEM((2, funcs, 128 * 128), BF)],
+        flops=1 << 33,
+    )
+    recv = send(other, 0, True)
     (out,) = call(
         assemble,
         "assemble",

time: 46 us -> 41.7 us (0.907)
  waiting for transfers between devices: 9.23 us -> 3.41 us
  local copies, waits for them, and re-layouts: 3.99 us -> 1.23 us
  Pallas kernels: 17 us -> 19.4 us
  starting transfers between devices: 15.5 us -> 17.1 us
    ppermute x10, waiting for transfers between devices: 9.23 us -> 3.41 us  [send(): return lax.ppermute(array, ('grp', 'row'), pairs)]
    unnamed x15 -> x11, local copies, waits for them, and re-layouts: 3.99 us -> 1.23 us
    pallas_call x8, Pallas kernels: 17 us -> 19.4 us  [call(): pl.pallas_call(kernel, name=name, in_specs=specs, out_specs=tuple(vmem(le...]
    ppermute x10, starting transfers between devices: 15.5 us -> 17.1 us  [send(): return lax.ppermute(array, ('grp', 'row'), pairs)]
  transfers between devices with their start and end apart: 10 -> 10, of which waited for: 4 -> 3; matrix products, arithmetic and copies ran while one was open for 0% -> 0% of each run, Pallas kernels for 22% -> 32%
where the time goes in v3:
time: 41.7 us; the launch traced here: 41.3 us
  Pallas kernels  19.4 us (47%)
  starting transfers between devices  17.1 us (41%)
  waiting for transfers between devices  3.41 us (8%)
  local copies, waits for them, and re-layouts  1.23 us (3%)
    pallas_call x8, Pallas kernels, call(): pl.pallas_call(kernel, name=name, in_specs=specs, out_specs=tuple(vmem(le...  19.4 us
    ppermute x10, starting transfers between devices, send(): return lax.ppermute(array, ('grp', 'row'), pairs)  17.1 us
    ppermute x10, waiting for transfers between devices, send(): return lax.ppermute(array, ('grp', 'row'), pairs)  3.41 us
    unnamed x11, local copies, waits for them, and re-layouts  1.23 us
  transfers between devices with their start and end apart: 10, of which 3 were waited for; matrix products, arithmetic and copies ran while one was open for 0% of the time, Pallas kernels for 32%

profile of v3, /device:TPU:0, one launch (start us, length us, event | category | flops | bytes accessed | tf_op | source)
XLA Modules:
  0.0 41.3 jit_solution(12389553480019711009)
XLA Ops:
  0.0 0.0 copy-start.4
  0.0 2.4 %first.1 = (bf16[256,128]{1,0:T(8,128)(2,1)}, bf16[256,128]{1,0:T(8,128)(2,1)}, bf16[256,128]{1,0:T(8,128)(2,1)}, bf16[256,128]{1,0:T(8,128)(2,1)}, bf16[24,128,128]{2,1,0:T(8,128)(2,1)}) custom-call(bf16[64,1024]{1,0:T(8,128)(2,1)} %occ.1, bf16[64,1024]{1,0:T(8,128)(2,1)} %virt.1, s32[1,4,4]{2,1,0:T(4,128)} %tiles.3, bf16[1,48,128,128]{3,2,1,0:T(8,128)(2,1)} %tensor.3), custom_call_target="tpu_custom_call" | custom-call | tf_op jit(solution)/shard_map/first/pallas_call | solution.py:330
  2.4 0.5 %collective-permute-start = (bf16[256,128]{1,0:T(8,128)(2,1)}, bf16[256,128]{1,0:T(8,128)(2,1)S(1)}, u32[]{:S(2)}, u32[]{:S(2)}) collective-permute-start(bf16[256,128]{1,0:T(8,128)(2,1)} %get-tuple-element.28), channel_id=1, source_target_pairs={{0,1},{1,2},{2,3},{3,4},{4,5},{5,6},{6,7},{7,8},{8,9},{9,10},{10,1... | collective-permute-start | bytes 196616 | tf_op jit(solution)/shard_map/ppermute | solution.py:353
  2.9 5.1 %collective-permute-start.1 = (bf16[256,128]{1,0:T(8,128)(2,1)}, bf16[256,128]{1,0:T(8,128)(2,1)S(1)}, u32[]{:S(2)}, u32[]{:S(2)}) collective-permute-start(bf16[256,128]{1,0:T(8,128)(2,1)} %get-tuple-element.29), channel_id=1, source_target_pairs={{0,15},{1,0},{2,1},{3,2},{4,3},{5,4},{6,5},{7,6},{8,7},{9,8},{10,9... | collective-permute-start | bytes 196616 | tf_op jit(solution)/shard_map/ppermute | solution.py:353
  8.0 0.0 collective-permute-start.2
  8.0 0.0 collective-permute-start.6
  8.0 0.0 copy-done.4
  8.0 0.1 copy.8.win
  8.1 0.0 copy-start.3
  8.1 1.1 %copy-done.3 = bf16[24,128,128]{2,1,0:T(8,128)(2,1)S(1)} copy-done((bf16[24,128,128]{2,1,0:T(8,128)(2,1)S(1)}, bf16[24,128,128]{2,1,0:T(8,128)(2,1)}, u32[]{:S(2)}) %copy-start.3) | copy-done | bytes 786456
  9.2 0.0 copy-start.1
  9.2 0.0 copy-start
  9.2 0.0 copy-start.2
  9.2 2.3 %far_tiles.1 = (bf16[768,128]{1,0:T(8,128)(2,1)S(1)}, bf16[768,128]{1,0:T(8,128)(2,1)S(1)}) custom-call(s32[16,4]{1,0:T(8,128)S(1)} %copy.8.win, bf16[24,128,128]{2,1,0:T(8,128)(2,1)S(1)} %copy-done.3), custom_call_target="tpu_custom_call" | custom-call | flops 68719476736 | tf_op jit(solution)/shard_map/far_tiles/pallas_call | solution.py:330
  11.5 1.7 %collective-permute-start.4 = (bf16[768,128]{1,0:T(8,128)(2,1)S(1)}, bf16[768,128]{1,0:T(8,128)(2,1)S(1)}, u32[]{:S(2)}, u32[]{:S(2)}) collective-permute-start(bf16[768,128]{1,0:T(8,128)(2,1)S(1)} %get-tuple-element.32), channel_id=1, source_target_pairs={{0,2},{1,3},{2,4},{3,5},{4,6},{5,7},{6,8},{7,9},{8,10},{9,11},{10,... | collective-permute-start | bytes 589832 | tf_op jit(solution)/shard_map/ppermute | solution.py:353
  13.2 0.0 collective-permute-done.g_before
  13.2 3.2 %collective-permute-start.5 = (bf16[768,128]{1,0:T(8,128)(2,1)S(1)}, bf16[768,128]{1,0:T(8,128)(2,1)S(1)}, u32[]{:S(2)}, u32[]{:S(2)}) collective-permute-start(bf16[768,128]{1,0:T(8,128)(2,1)S(1)} %get-tuple-element.33), channel_id=1, source_target_pairs={{0,14},{1,15},{2,0},{3,1},{4,2},{5,3},{6,4},{7,5},{8,6},{9,7},{10,... | collective-permute-start | bytes 589832 | tf_op jit(solution)/shard_map/ppermute | solution.py:353
  16.3 0.0 collective-permute-done.1.g_after
  16.3 0.0 collective-permute-done.2.g_far
  16.3 0.0 copy-done.1
  16.3 1.3 %choose.1.greens.g0 = bf16[512,128]{1,0:T(8,128)(2,1)S(1)} custom-call(s32[16,4]{1,0:T(8,128)S(1)} %copy.8.win, bf16[256,128]{1,0:T(8,128)(2,1)S(1)} %copy-done.1, bf16[256,128]{1,0:T(8,128)(2,1)S(1)} %collective-permute-done.g_before, bf16[256,128]{1,0:T(8,128)(2,1)S(1)} %collective-permute-done.1.g_after, bf16[256,128]{1,0:T(8,128)(2,1)S(1)} %collective-permute-done.2.g_far), custom_call_target="tpu_custom_call" | custom-call | tf_op jit(solution)/shard_map/choose/pallas_call | solution.py:330
  17.7 1.9 %collective-permute-start.3 = (bf16[512,128]{1,0:T(8,128)(2,1)S(1)}, bf16[512,128]{1,0:T(8,128)(2,1)S(1)}, u32[]{:S(2)}, u32[]{:S(2)}) collective-permute-start(bf16[512,128]{1,0:T(8,128)(2,1)S(1)} %choose.1.greens.g0), channel_id=1, source_target_pairs={{0,16},{1,17},{2,18},{3,19},{4,20},{5,21},{6,22},{7,23},{8,24},{9,... | collective-permute-start | bytes 393224 | tf_op jit(solution)/shard_map/ppermute | solution.py:353
  19.6 0.0 copy-done
  19.6 0.0 copy-done.2
  19.6 3.6 %dress_own.1 = (f32[48,48]{1,0:T(8,128)S(1)}, bf16[48,16384]{1,0:T(8,128)(2,1)S(1)}, bf16[48,16384]{1,0:T(8,128)(2,1)S(1)}, bf16[48,16384]{1,0:T(8,128)(2,1)S(1)}) custom-call(s32[16,4]{1,0:T(8,128)S(1)} %copy.8.win, s32[1,4,4]{2,1,0:T(4,128)S(1)} %copy-done.2, bf16[1,48,128,128]{3,2,1,0:T(8,128)(2,1)S(1)} %copy-done, bf16[512,128]{1,0:T(8,128)(2,1)S(1)} %choose.1.greens.g0), custom_call_target="tpu_custom_call" | custom-call | tf_op jit(solution)/shard_map/dress_own/pallas_call | solution.py:330
  23.2 0.8 %collective-permute-done.3.greens.g1 = bf16[512,128]{1,0:T(8,128)(2,1)S(1)} collective-permute-done((bf16[512,128]{1,0:T(8,128)(2,1)S(1)}, bf16[512,128]{1,0:T(8,128)(2,1)S(1)}, u32[]{:S(2)}, u32[]{:S(2)}) %collective-permute-start.3) | collective-permute-done | bytes 131104 | tf_op jit(solution)/shard_map/ppermute | solution.py:353
  24.0 2.3 %dress_partner.1 = (bf16[48,16384]{1,0:T(8,128)(2,1)S(1)}, bf16[48,16384]{1,0:T(8,128)(2,1)S(1)}) custom-call(s32[16,4]{1,0:T(8,128)S(1)} %copy.8.win, s32[1,4,4]{2,1,0:T(4,128)S(1)} %copy-done.2, bf16[1,48,128,128]{3,2,1,0:T(8,128)(2,1)S(1)} %copy-done, bf16[512,128]{1,0:T(8,128)(2,1)S(1)} %collective-permute-done.3.greens.g1), custom_call_target="tpu_custom_call" | custom-call | tf_op jit(solution)/shard_map/dress_partner/pallas_call | solution.py:330
  26.3 0.0 collective-permute-done.6.tensor
  26.3 3.9 %join.1 = (f32[48,128]{1,0:T(8,128)S(1)}, f32[48,128]{1,0:T(8,128)S(1)}, f32[24,128]{1,0:T(8,128)S(1)}, f32[24,128]{1,0:T(8,128)S(1)}) custom-call(s32[16,4]{1,0:T(8,128)S(1)} %copy.8.win, bf16[24,128,128]{2,1,0:T(8,128)(2,1)S(1)} %collective-permute-done.6.tensor, bf16[512,128]{1,0:T(8,128)(2,1)S(1)} %choose.1.greens.g0, ...), custom_call_target="tpu_custom_call" | custom-call | tf_op jit(solution)/shard_map/join/pallas_call | solution.py:330
  30.2 0.0 collective-permute-done.4.from_left
  30.3 1.2 %collective-permute-done.5.from_right = bf16[768,128]{1,0:T(8,128)(2,1)S(1)} collective-permute-done((bf16[768,128]{1,0:T(8,128)(2,1)S(1)}, bf16[768,128]{1,0:T(8,128)(2,1)S(1)}, u32[]{:S(2)}, u32[]{:S(2)}) %collective-permute-start.5) | collective-permute-done | bytes 196640 | tf_op jit(solution)/shard_map/ppermute | solution.py:353
  31.4 2.9 %join_far.1 = (f32[48,128]{1,0:T(8,128)S(1)}, f32[48,128]{1,0:T(8,128)S(1)}) custom-call(s32[16,4]{1,0:T(8,128)S(1)} %copy.8.win, bf16[48,16384]{1,0:T(8,128)(2,1)S(1)} %get-tuple-element.38.far0, bf16[48,16384]{1,0:T(8,128)(2,1)S(1)} %get-tuple-element.39.far1, bf16[768,128]{1,0:T(8,128)(2,1)S(1)} %collective-permute-done.4.from_left, ...), custom_call_target="tpu_custom_call" | custom-call | flops 8589934592 | tf_op jit(solution)/shard_map/join_far/pallas_call | solution.py:330
  34.4 1.9 %collective-permute-start.7 = (f32[48,128]{1,0:T(8,128)S(1)}, f32[48,128]{1,0:T(8,128)S(1)}, u32[]{:S(2)}, u32[]{:S(2)}) collective-permute-start(f32[48,128]{1,0:T(8,128)S(1)} %get-tuple-element.46), channel_id=1, source_target_pairs={{0,16},{1,17},{2,18},{3,19},{4,20},{5,21},{6,22},{7,23},{8,24},{9,... | collective-permute-start | bytes 73736 | tf_op jit(solution)/shard_map/ppermute | solution.py:353
  36.3 0.5 %collective-permute-start.8 = (f32[24,128]{1,0:T(8,128)S(1)}, f32[24,128]{1,0:T(8,128)S(1)}, u32[]{:S(2)}, u32[]{:S(2)}) collective-permute-start(f32[24,128]{1,0:T(8,128)S(1)} %get-tuple-element.47), channel_id=1, source_target_pairs={{0,15},{1,0},{2,1},{3,2},{4,3},{5,4},{6,5},{7,6},{8,7},{9,8},{10,9... | collective-permute-start | bytes 36872 | tf_op jit(solution)/shard_map/ppermute | solution.py:353
  36.7 2.4 %collective-permute-start.9 = (f32[24,128]{1,0:T(8,128)S(1)}, f32[24,128]{1,0:T(8,128)S(1)}, u32[]{:S(2)}, u32[]{:S(2)}) collective-permute-start(f32[24,128]{1,0:T(8,128)S(1)} %get-tuple-element.48), channel_id=1, source_target_pairs={{0,31},{1,16},{2,17},{3,18},{4,19},{5,20},{6,21},{7,22},{8,23},{9,... | collective-permute-start | bytes 36872 | tf_op jit(solution)/shard_map/ppermute | solution.py:353
  39.1 0.0 collective-permute-done.8.up0
  39.1 1.4 %collective-permute-done.9.up1 = f32[24,128]{1,0:T(8,128)S(1)} collective-permute-done((f32[24,128]{1,0:T(8,128)S(1)}, f32[24,128]{1,0:T(8,128)S(1)}, u32[]{:S(2)}, u32[]{:S(2)}) %collective-permute-start.9) | collective-permute-done | bytes 12320 | tf_op jit(solution)/shard_map/ppermute | solution.py:353
  40.5 0.0 collective-permute-done.7.recv
  40.5 0.7 %assemble.1 = f32[48,240]{1,0:T(8,128)} custom-call(f32[48,48]{1,0:T(8,128)S(1)} %get-tuple-element.37.polar0, f32[48,128]{1,0:T(8,128)S(1)} %get-tuple-element.45.own, f32[48,128]{1,0:T(8,128)S(1)} %collective-permute-done.7.recv, f32[24,128]{1,0:T(8,128)S(1)} %collective-permute-done.8.up0, f32[24,128]{1,0:T(8,128)S(1)} %collective-permute-done.9.up1), custom_call_target="tpu_custom_call" | custom-call | tf_op jit(solution)/shard_map/assemble/pallas_call | solution.py:330
Async XLA Ops:
  0.0 8.0 %copy-start.4 = (s32[16,4]{0,1:T(4,128)S(1)}, s32[16,4]{0,1:T(4,128)}, u32[]{:S(2)}) copy-start(s32[16,4]{0,1:T(4,128)} %param.9) | copy-start | bytes 772
  2.4 10.7 %collective-permute-start = (bf16[256,128]{1,0:T(8,128)(2,1)}, bf16[256,128]{1,0:T(8,128)(2,1)S(1)}, u32[]{:S(2)}, u32[]{:S(2)}) collective-permute-start(bf16[256,128]{1,0:T(8,128)(2,1)} %get-tuple-element.28), channel_id=1, source_target_pairs={{0,1},{1,2},{2,3},{3,4},{4,5},{5,6},{6,7},{7,8},{8,9},{9,10},{10,1... | collective-permute-start | bytes 196616 | tf_op jit(solution)/shard_map/ppermute | solution.py:353
  2.9 13.4 %collective-permute-start.1 = (bf16[256,128]{1,0:T(8,128)(2,1)}, bf16[256,128]{1,0:T(8,128)(2,1)S(1)}, u32[]{:S(2)}, u32[]{:S(2)}) collective-permute-start(bf16[256,128]{1,0:T(8,128)(2,1)} %get-tuple-element.29), channel_id=1, source_target_pairs={{0,15},{1,0},{2,1},{3,2},{4,3},{5,4},{6,5},{7,6},{8,7},{9,8},{10,9... | collective-permute-start | bytes 196616 | tf_op jit(solution)/shard_map/ppermute | solution.py:353
  8.0 8.4 %collective-permute-start.2 = (bf16[256,128]{1,0:T(8,128)(2,1)}, bf16[256,128]{1,0:T(8,128)(2,1)S(1)}, u32[]{:S(2)}, u32[]{:S(2)}) collective-permute-start(bf16[256,128]{1,0:T(8,128)(2,1)} %get-tuple-element.30), channel_id=1, source_target_pairs={{0,2},{1,3},{2,4},{3,5},{4,6},{5,7},{6,8},{7,9},{8,10},{9,11},{10,... | collective-permute-start | bytes 196616 | tf_op jit(solution)/shard_map/ppermute | solution.py:353
  8.0 18.4 %collective-permute-start.6 = (bf16[24,128,128]{2,1,0:T(8,128)(2,1)}, bf16[24,128,128]{2,1,0:T(8,128)(2,1)S(1)}, u32[]{:S(2)}, u32[]{:S(2)}) collective-permute-start(bf16[24,128,128]{2,1,0:T(8,128)(2,1)} %get-tuple-element.31.half), channel_id=1, source_target_pairs={{0,1},{1,2},{2,3},{3,4},{4,5},{5,6},{6,7},{7,8},{8,9},{9,10},{10,1... | collective-permute-start | bytes 2359304 | tf_op jit(solution)/shard_map/ppermute | solution.py:353
  8.1 1.1 %copy-start.3 = (bf16[24,128,128]{2,1,0:T(8,128)(2,1)S(1)}, bf16[24,128,128]{2,1,0:T(8,128)(2,1)}, u32[]{:S(2)}) copy-start(bf16[24,128,128]{2,1,0:T(8,128)(2,1)} %get-tuple-element.31.half) | copy-start | bytes 2359300
  9.2 7.1 %copy-start.1 = (bf16[256,128]{1,0:T(8,128)(2,1)S(1)}, bf16[256,128]{1,0:T(8,128)(2,1)}, u32[]{:S(2)}) copy-start(bf16[256,128]{1,0:T(8,128)(2,1)} %get-tuple-element.27.g_self) | copy-start | bytes 196612
  9.2 10.4 %copy-start = (bf16[1,48,128,128]{3,2,1,0:T(8,128)(2,1)S(1)}, bf16[1,48,128,128]{3,2,1,0:T(8,128)(2,1)}, u32[]{:S(2)}) copy-start(bf16[1,48,128,128]{3,2,1,0:T(8,128)(2,1)} %tensor.3) | copy-start | bytes 4718596
  9.2 10.4 %copy-start.2 = (s32[1,4,4]{2,1,0:T(4,128)S(1)}, s32[1,4,4]{2,1,0:T(4,128)}, u32[]{:S(2)}) copy-start(s32[1,4,4]{2,1,0:T(4,128)} %tiles.3) | copy-start | bytes 196
  11.5 18.8 %collective-permute-start.4 = (bf16[768,128]{1,0:T(8,128)(2,1)S(1)}, bf16[768,128]{1,0:T(8,128)(2,1)S(1)}, u32[]{:S(2)}, u32[]{:S(2)}) collective-permute-start(bf16[768,128]{1,0:T(8,128)(2,1)S(1)} %get-tuple-element.32), channel_id=1, source_target_pairs={{0,2},{1,3},{2,4},{3,5},{4,6},{5,7},{6,8},{7,9},{8,10},{9,11},{10,... | collective-permute-start | bytes 589832 | tf_op jit(solution)/shard_map/ppermute | solution.py:353
  13.2 18.3 %collective-permute-start.5 = (bf16[768,128]{1,0:T(8,128)(2,1)S(1)}, bf16[768,128]{1,0:T(8,128)(2,1)S(1)}, u32[]{:S(2)}, u32[]{:S(2)}) collective-permute-start(bf16[768,128]{1,0:T(8,128)(2,1)S(1)} %get-tuple-element.33), channel_id=1, source_target_pairs={{0,14},{1,15},{2,0},{3,1},{4,2},{5,3},{6,4},{7,5},{8,6},{9,7},{10,... | collective-permute-start | bytes 589832 | tf_op jit(solution)/shard_map/ppermute | solution.py:353
  17.7 6.3 %collective-permute-start.3 = (bf16[512,128]{1,0:T(8,128)(2,1)S(1)}, bf16[512,128]{1,0:T(8,128)(2,1)S(1)}, u32[]{:S(2)}, u32[]{:S(2)}) collective-permute-start(bf16[512,128]{1,0:T(8,128)(2,1)S(1)} %choose.1.greens.g0), channel_id=1, source_target_pairs={{0,16},{1,17},{2,18},{3,19},{4,20},{5,21},{6,22},{7,23},{8,24},{9,... | collective-permute-start | bytes 393224 | tf_op jit(solution)/shard_map/ppermute | solution.py:353
  34.4 6.2 %collective-permute-start.7 = (f32[48,128]{1,0:T(8,128)S(1)}, f32[48,128]{1,0:T(8,128)S(1)}, u32[]{:S(2)}, u32[]{:S(2)}) collective-permute-start(f32[48,128]{1,0:T(8,128)S(1)} %get-tuple-element.46), channel_id=1, source_target_pairs={{0,16},{1,17},{2,18},{3,19},{4,20},{5,21},{6,22},{7,23},{8,24},{9,... | collective-permute-start | bytes 73736 | tf_op jit(solution)/shard_map/ppermute | solution.py:353
  36.3 2.8 %collective-permute-start.8 = (f32[24,128]{1,0:T(8,128)S(1)}, f32[24,128]{1,0:T(8,128)S(1)}, u32[]{:S(2)}, u32[]{:S(2)}) collective-permute-start(f32[24,128]{1,0:T(8,128)S(1)} %get-tuple-element.47), channel_id=1, source_target_pairs={{0,15},{1,0},{2,1},{3,2},{4,3},{5,4},{6,5},{7,6},{8,7},{9,8},{10,9... | collective-permute-start | bytes 36872 | tf_op jit(solution)/shard_map/ppermute | solution.py:353
  36.7 3.8 %collective-permute-start.9 = (f32[24,128]{1,0:T(8,128)S(1)}, f32[24,128]{1,0:T(8,128)S(1)}, u32[]{:S(2)}, u32[]{:S(2)}) collective-permute-start(f32[24,128]{1,0:T(8,128)S(1)} %get-tuple-element.48), channel_id=1, source_target_pairs={{0,31},{1,16},{2,17},{3,18},{4,19},{5,20},{6,21},{7,22},{8,23},{9,... | collective-permute-start | bytes 36872 | tf_op jit(solution)/shard_map/ppermute | solution.py:353

commit v4 on v3

--- a/solution.py
+++ b/solution.py
@@ -67,13 +67,13 @@
     return near(row, -1, count) >> 1
 
 
-def first(count, occ, virt, tiles_hbm, coulomb, g_self, g_right, g_left, g_far, tensor, tiles, sem):
+def first(count, occ, virt, tiles_hbm, coulomb, g_self, g_right, g_left, g_far, tensor, tiles, mask, sem):
     d = lax.axis_index("row")
     funcs = tensor.shape[0]
     half = lax.rem(lax.axis_index("grp"), 2)
     list_copy = pltpu.make_async_copy(tiles_hbm, tiles, sem.at[0])
-    half_copy = pltpu.make_async_copy(coulomb.at[0, pl.ds(half * funcs, funcs)], tensor, sem.at[1])
-    copies = [list_copy, half_copy]
+    list_copy.start()
+    copies = []
     for out, by in ((g_right, 1), (g_left, -1), (g_far, 2), (g_self, 0)):
         start = column_chunk(near(d, by, count), count)
         for c in range(2):
@@ -82,46 +82,44 @@
             for base, green in ((0, occ), (128, virt)):
                 at = base + 64 * c
                 copies.append(
-                    pltpu.make_async_copy(green.at[:, columns], out.at[at : at + 64], sem.at[len(copies)])
+                    pltpu.make_async_copy(green.at[:, columns], out.at[at : at + 64], sem.at[len(copies) + 1])
                 )
+    copies.append(pltpu.make_async_copy(coulomb.at[0, pl.ds(half * funcs, funcs)], tensor, sem.at[17]))
     for copy in copies:
         copy.start()
     list_copy.wait()
-    mask = tile_mask(tiles, 32).astype(BF)
-    half_copy.wait()
-    tensor[...] = tensor[...] * mask[None]
-    for copy in copies[2:]:
+    mask[...] = tile_mask(tiles, 4).astype(BF)
+    mask_copy = pltpu.make_async_copy(mask, g_right.at[256:272], sem.at[18])
+    mask_copy.start()
+    for copy in copies:
         copy.wait()
-
-
-def far_tiles(count, win, half, far_right, far_left, xs):
+    mask_copy.wait()
+
+
+def far_tiles(count, win, tiles, tensor, far_right, far_left, mask):
     d = lax.axis_index("row")
     mine = window_at(win, d)
-    funcs = half.shape[0]
-    left, right = near(d, -1, count) * 2, near(d, 1, count) * 2
-    shape = (128, 256)
-    column = iota(shape, 1)
-    wanted = jnp.where(column < 128, left, right) + ((column >> 5) & 1)
-    here = pick4(iota(shape, 0) >> 5, mine)
-    same = (here == wanted) & ((iota(shape, 0) & 31) == (column & 31))
-    select = jnp.where(same, 1.0, 0.0).astype(BF)
-    for r in range(0, funcs, 4):
-        block = half[r : r + 4].reshape(512, 128)
-        x = dot(block, select)
-        xs[0, r * 128 : r * 128 + 512, :] = x[:, :128]
-        xs[1, r * 128 : r * 128 + 512, :] = x[:, 128:]
-    lane = iota((funcs, 128), 1)
-    for side, base, out in ((0, left, far_left), (1, right, far_right)):
-        slot0, there0 = find(mine, base)
-        slot1, there1 = find(mine, base + 1)
-        weight = jnp.where(lane < 64, there0, there1)
-        for t in range(0, 32, 2):
-            parts = []
-            for u in (t, t + 1):
-                x0 = xs[side, pl.ds(slot0 * 32 + u, funcs, stride=128), :]
-                x1 = xs[side, pl.ds(slot1 * 32 + u, funcs, stride=128), :]
-                parts.append(jnp.where(lane < 64, x0, x1) * weight)
-            out[t * funcs : (t + 2) * funcs, :] = jnp.concatenate(parts, axis=0).astype(BF)
+    funcs = tensor.shape[1] // 2
+    start = lax.rem(lax.axis_index("grp"), 2) * funcs
+    mask[...] = tile_mask(tiles, 32).astype(BF)
+    for by, out in ((-1, far_left), (1, far_right)):
+        base = near(d, by, count) * 2
+        shape = (256, 128)
+        row, lane = iota(shape, 0), iota(shape, 1)
+        found = [find(mine, base), find(mine, base + 1)]
+        here = pick4((row & 127) >> 5, mine) == base + ((lane & 63) >> 5)
+        same = here & ((row & 31) == (lane & 31)) & ((row >> 7) == (lane >> 6))
+        weight = jnp.where(row < 128, found[0][1], found[1][1])
+        select = jnp.where(same, weight, 0.0).astype(BF)
+        places = [pl.ds(pl.multiple_of(slot * 32, 32), 32) for slot, _ in found]
+        masks = [mask[place, :] for place in places]
+        for r in range(0, funcs, 8):
+            sides = [
+                jnp.concatenate([tensor[0, start + r + u, place, :] * m for u in range(8)], axis=0)
+                for place, m in zip(places, masks)
+            ]
+            x = dot(jnp.concatenate(sides, axis=1), select)
+            out[r * 32 : r * 32 + 256, :] = x.astype(BF)
 
 
 def choose(count, win, g_self, g_before, g_after, g_far, out):
@@ -210,37 +208,61 @@
     mask = tile_mask(tiles, 32).astype(BF)
     occ, virt = greens[0:128, :], greens[128:256, :]
     halves(occ, [functools.partial(lambda r: tensor[0, r] * mask, r) for r in range(funcs)], [hs], ms)
-    frames = [
-        dot(virt, frame_map(mine, theirs)).astype(BF),
-        dot(virt, frame_map(mine, [left, left + 1, right, right + 1])).astype(BF),
-    ]
-    outs = [dressed, far]
+    wide, outs = dot(virt, frame_map(mine, theirs)).astype(BF), [dressed]
     if own:
-        frames, outs = [virt] + frames, [same] + outs
-    wide = jnp.concatenate(frames, axis=1)
-    for i in range(16):
-        x = dot(jnp.concatenate(gather(hs, funcs, i * 8), axis=0).astype(BF), wide)
+        wide, outs = jnp.concatenate([virt, wide], axis=1), [same, dressed]
+    lane = iota((128, 256), 1)
+    atom = jnp.where(lane < 128, left, right)
+    column_here = pick4(iota((128, 256), 0) >> 5, mine) == atom + ((lane & 63) >> 5)
+    column_here = column_here & ((iota((128, 256), 0) & 31) == (lane & 31))
+    both = dot(virt, jnp.where(column_here, 1.0, 0.0).astype(BF))
+    row_atom = atom + ((lane & 127) >> 6)
+    packs = jnp.concatenate([jnp.where(row_atom == a, both, 0.0).astype(BF) for a in mine], axis=0)
+    for c in range(4):
+        parts = []
+        for i in range(4):
+            parts.append(jnp.concatenate(gather(hs, funcs, i * 32 + c * 8), axis=0).astype(BF))
+            x = dot(parts[-1], wide)
+            for t in range(8):
+                at = (i * 32 + c * 8 + t) * 128
+                block = x[t * funcs : (t + 1) * funcs].astype(BF)
+                for n, out in enumerate(outs):
+                    out[:, at : at + 128] = block[:, n * 128 : (n + 1) * 128]
+            if own:
+                for t, rows in enumerate(gather(ms, funcs, i * 32 + c * 8)):
+                    at = (i * 32 + c * 8 + t) * 128
+                    flat[:, at : at + 128] = rows.astype(BF)
+        x = dot(jnp.concatenate(parts, axis=1), packs)
         for t in range(8):
-            at = (i * 8 + t) * 128
+            at = (c * 8 + t) * 128
             block = x[t * funcs : (t + 1) * funcs].astype(BF)
-            for n, out in enumerate(outs):
-                out[:, at : at + 128] = block[:, n * 128 : (n + 1) * 128]
-        if own:
-            for t, rows in enumerate(gather(ms, funcs, i * 8)):
-                at = (i * 8 + t) * 128
-                flat[:, at : at + 128] = rows.astype(BF)
+            far[:, at : at + 128] = block[:, :128]
+            far[:, 4096 + at : 4224 + at] = block[:, 128:]
     if own:
         polar0[...] = dot_t(same[...], flat[...])
 
 
-def join(count, win, tensor, g0, g1, flat, dressed0, dressed1, down0, down1, up0, up1, hs0, hs1, ms, backs, moved):
+def stacked(a, b, start, other):
+    total = None
+    for at in range(0, other.shape[1], 1024):
+        left = jnp.concatenate([x[:, start + at : start + at + 1024] for x in (a, b)], axis=0)
+        part = dot_t(left, other[:, at : at + 1024])
+        total = part if total is None else total + part
+    return total
+
+
+def join(count, win, tensor, g_before, g0, g1, flat, dressed0, dressed1, down, up, hs0, hs1, ms, backs, moved):
     d = lax.axis_index("row")
     funcs = tensor.shape[0]
     full = 2 * funcs
     mine = window_at(win, d)
     theirs = window_at(win, near(d, -1, count))
+    short = g_before[256:272, :].astype(F32)
+    mask = jnp.concatenate(
+        [jnp.broadcast_to(short[4 * i : 4 * i + 1, :], (32, 128)) for i in range(4)], axis=0
+    ).astype(BF)
     occ = jnp.concatenate([g0[256:384, :], g1[256:384, :]], axis=0)
-    halves(occ, [functools.partial(lambda r: tensor[r], r) for r in range(funcs)], [hs0, hs1], ms)
+    halves(occ, [functools.partial(lambda r: tensor[r] * mask, r) for r in range(funcs)], [hs0, hs1], ms)
     virts = [g0[384:512, :], g1[384:512, :]]
     for i in range(16):
         slot, there = find(theirs, mine[i // 4])
@@ -253,63 +275,51 @@
             part = slice(t * funcs, (t + 1) * funcs)
             backs[:, at : at + 128] = jnp.concatenate([x[part] for x in xs], axis=0).astype(BF)
             moved[:, at : at + 128] = (rows[t] * there).astype(BF)
-    up = dot_t(backs[...], flat[...])
-    up = jnp.concatenate([up, jnp.zeros((full, 128 - full), F32)], axis=1)
-    up0[...] = up[:funcs]
-    up1[...] = up[funcs:]
-    for dressed, out in ((dressed0, down0), (dressed1, down1)):
-        out[...] = jnp.concatenate(
-            [dot_t(dressed[...], moved[...]), jnp.zeros((full, 128 - funcs), F32)], axis=1
-        )
-
-
-def join_far(count, win, far0, far1, from_left, from_right, down0, down1, own, other, tiles_far):
-    d = lax.axis_index("row")
+    total = dot_t(backs[...], flat[...])
+    up[...] = jnp.concatenate([total, jnp.zeros((full, 128 - full), F32)], axis=1)
+    total = stacked(dressed0, dressed1, 0, moved)
+    down[...] = jnp.concatenate([total, jnp.zeros((2 * full, 128 - funcs), F32)], axis=1)
+
+
+FAR_PITCH = 40
+
+
+def join_far(far0, far1, from_left, from_right, down, after, own, other, es, turned):
     full = far0.shape[0]
     funcs = full // 2
-    mine = window_at(win, d)
-    left, right = near(d, -1, count), near(d, 1, count)
-    lane = iota((funcs, 128), 1)
-    for t in range(0, 32, 2):
-        pair = slice(t * funcs, (t + 2) * funcs)
-        for side, e, row in ((0, from_left, left), (1, from_right, right)):
-            both = e[pair, :].astype(F32)
-            for u in range(2):
-                x = both[u * funcs : (u + 1) * funcs]
-                turned = pltpu.roll(x, 64, 1)
-                for i in range(4):
-                    odd = lax.rem(mine[i], 2)
-                    here = (lane < 64) if side == 0 else (lane >= 64)
-                    value = jnp.where(odd == side, x, turned)
-                    at = (i * 32 + t + u) * 128
-                    kept = here & (jnp.broadcast_to(mine[i] >> 1, lane.shape) == row)
-                    tiles_far[side, :, at : at + 128] = jnp.where(kept, value, 0.0).astype(BF)
-    for far, down, out in ((far0, down0, own), (far1, down1, other)):
-        dressed = far[...]
+    for e in (from_left, from_right):
+        side = 0 if e is from_left else 1
+        for r in range(funcs):
+            at = r * FAR_PITCH
+            es[side, at : at + 32, :] = e[r * 32 : (r + 1) * 32, :].astype(F32)
+        for t in range(32):
+            rows = es[side, pl.ds(t, funcs, stride=FAR_PITCH), :]
+            turned[side, :, t * 128 : (t + 1) * 128] = rows.astype(BF)
+    far_left = stacked(far0, far1, 0, turned.at[0])
+    far_right = stacked(far0, far1, 4096, turned.at[1])
+    padding = jnp.zeros((full, 128 - 3 * funcs - full), F32)
+    for n, out in enumerate((own, other)):
+        part = slice(n * full, (n + 1) * full)
+        back = after[n * funcs : (n + 1) * funcs, :full]
+        back = jnp.concatenate([back, jnp.zeros((funcs, full), F32)], axis=0)
         out[...] = jnp.concatenate(
-            [
-                dot_t(dressed, tiles_far[0]),
-                down[:, :funcs],
-                dot_t(dressed, tiles_far[1]),
-                jnp.zeros((full, 128 - 3 * funcs), F32),
-            ],
-            axis=1,
+            [far_left[part], down[part, :funcs], far_right[part], back, padding], axis=1
         )
 
 
-def assemble(polar0, own, recv, up0, up1, out):
-    first = lax.rem(lax.axis_index("grp"), 2) == 0
+def assemble(polar0, own, recv, out):
+    is_first = lax.rem(lax.axis_index("grp"), 2) == 0
     full = polar0.shape[0]
     funcs = full // 2
     a, b = own[...], recv[...]
-    low, high = jnp.where(first, a, b), jnp.where(first, b, a)
-    c, e = up0[...], up1[...]
-    after = jnp.concatenate([jnp.where(first, c, e), jnp.where(first, e, c)], axis=0)
+    low, high = jnp.where(is_first, a, b), jnp.where(is_first, b, a)
+    back = slice(3 * funcs, 3 * funcs + full)
+    after = jnp.concatenate([low[:funcs, back], high[:funcs, back]], axis=0)
     pieces = []
     for i in range(3):
         part = slice(i * funcs, (i + 1) * funcs)
         if i == 2:
-            pieces += [polar0[...], after[:, :full]]
+            pieces += [polar0[...], after]
         pieces += [low[:, part], high[:, part]]
     out[...] = jnp.concatenate(pieces, axis=1)
 
@@ -326,12 +336,12 @@
     return [pl.BlockSpec(memory_space=pltpu.SMEM)] * count
 
 
-def call(kernel, name, specs, outs, args, scratch=(), flops=0, limit=40 << 20):
+def call(kernel, name, specs, outs, args, scratch=(), flops=0, limit=40 << 20, space=None):
     return pl.pallas_call(
         kernel,
         name=name,
         in_specs=specs,
-        out_specs=tuple(vmem(len(outs))),
+        out_specs=tuple((space or vmem)(len(outs))),
         out_shape=tuple(outs),
         scratch_shapes=list(scratch),
         compiler_params=pltpu.CompilerParams(vmem_limit_bytes=limit),
@@ -357,10 +367,17 @@
         functools.partial(first, count),
         "first",
         hbm(4),
-        [shape((256, 128), BF)] * 4 + [shape((funcs, 128, 128), BF)],
+        [
+            shape((256, 128), BF),
+            shape((272, 128), BF),
+            shape((256, 128), BF),
+            shape((256, 128), BF),
+            shape((funcs, 128, 128), BF),
+        ],
         (green_occ, green_virt, tile_list, coulomb3c),
-        [pltpu.SMEM((1, 4, 4), jnp.int32), pltpu.SemaphoreType.DMA((18,))],
+        [pltpu.SMEM((1, 4, 4), jnp.int32), pltpu.VMEM((16, 128), BF), pltpu.SemaphoreType.DMA((19,))],
         limit=60 << 20,
+        space=hbm,
     )
     g_before = send(g_right, 1)
     g_after = send(g_left, -1)
@@ -369,10 +386,10 @@
     far_right, far_left = call(
         functools.partial(far_tiles, count),
         "far_tiles",
-        smem(1) + vmem(1),
+        smem(2) + vmem(1),
         [shape((far_rows, 128), BF), shape((far_rows, 128), BF)],
-        (window, tensor),
-        [pltpu.VMEM((2, funcs * 128, 128), F32)],
+        (window, tile_list, coulomb3c),
+        [pltpu.VMEM((128, 128), BF)],
         flops=1 << 36,
     )
     from_left = send(far_right, 2)
@@ -388,13 +405,15 @@
         (window, g_self, g_before, g_after, g_beyond),
     )
     partner = send(mine, 0, True)
-    flat_shape = shape((full, 128 * 128), BF)
+    flat_shape, far_shape = shape((full, 128 * 128), BF), shape((full, 64 * 128), BF)
     tall = pltpu.VMEM((full * PITCH, 128), F32)
+    short = pltpu.VMEM((funcs * PITCH, 128), F32)
+    message = shape((full, 128), F32)
     polar0, flat, dressed0, far0 = call(
         functools.partial(dress, count, True),
         "dress_own",
         smem(2) + vmem(2),
-        [shape((full, full), F32), flat_shape, flat_shape, flat_shape],
+        [shape((full, full), F32), flat_shape, flat_shape, far_shape],
         (window, tile_list, coulomb3c, mine),
         [tall, tall, pltpu.VMEM((full, 128 * 128), BF)],
     )
@@ -402,37 +421,34 @@
         functools.partial(dress, count, False),
         "dress_partner",
         smem(2) + vmem(2),
-        [flat_shape, flat_shape],
+        [flat_shape, far_shape],
         (window, tile_list, coulomb3c, partner),
         [tall],
     )
-    short = pltpu.VMEM((funcs * PITCH, 128), F32)
-    down0, down1, up0, up1 = call(
+    down, up = call(
         functools.partial(join, count),
         "join",
-        smem(1) + vmem(6),
-        [shape((full, 128), F32)] * 2 + [shape((funcs, 128), F32)] * 2,
-        (window, wide, mine, partner, flat, dressed0, dressed1),
+        smem(1) + vmem(7),
+        [shape((2 * full, 128), F32), message],
+        (window, wide, g_before, mine, partner, flat, dressed0, dressed1),
         [short, short, short, pltpu.VMEM((full, 128 * 128), BF), pltpu.VMEM((funcs, 128 * 128), BF)],
     )
-    after0 = send(up0, -1)
-    after1 = send(up1, -1, True)
+    after = send(up, -1)
     own, other = call(
-        functools.partial(join_far, count),
+        join_far,
         "join_far",
-        smem(1) + vmem(6),
-        [shape((full, 128), F32)] * 2,
-        (window, far0, far1, from_left, from_right, down0, down1),
-        [pltpu.VMEM((2, funcs, 128 * 128), BF)],
-        flops=1 << 33,
+        vmem(6),
+        [message, message],
+        (far0, far1, from_left, from_right, down, after),
+        [pltpu.VMEM((2, funcs * FAR_PITCH, 128), F32), pltpu.VMEM((2, funcs, 32 * 128), BF)],
     )
     recv = send(other, 0, True)
     (out,) = call(
         assemble,
         "assemble",
-        vmem(5),
+        vmem(3),
         [shape((full, 5 * full), F32)],
-        (polar0, own, recv, after0, after1),
+        (polar0, own, recv),
     )
     return out
 

time: 41.7 us -> 67.6 us (1.62)
  Pallas kernels: 19.4 us -> 46.7 us
  waiting for transfers between devices: 3.41 us -> 7.04 us
  starting transfers between devices: 17.1 us -> 13.5 us
  local copies, waits for them, and re-layouts: 1.23 us -> 0.1 us
    pallas_call x8, Pallas kernels: 19.4 us -> 46.7 us  [call(): pl.pallas_call(kernel, name=name, in_specs=specs, out_specs=tuple((space...]
    ppermute x10 -> x9, starting transfers between devices: 17.1 us -> 13.5 us  [send(): return lax.ppermute(array, ('grp', 'row'), pairs)]
    ppermute x10 -> x9, waiting for transfers between devices: 3.41 us -> 7.04 us  [send(): return lax.ppermute(array, ('grp', 'row'), pairs)]
    unnamed x11 -> x9, local copies, waits for them, and re-layouts: 1.23 us -> 0.1 us
  transfers between devices with their start and end apart: 10 -> 9, of which waited for: 3 -> 6; matrix products, arithmetic and copies ran while one was open for 0% -> 0% of each run, Pallas kernels for 32% -> 18%
where the time goes in v4:
time: 67.6 us; the launch traced here: 67.4 us
  Pallas kernels  46.7 us (69%)
  starting transfers between devices  13.5 us (20%)
  waiting for transfers between devices  7.04 us (10%)
    pallas_call x8, Pallas kernels, call(): pl.pallas_call(kernel, name=name, in_specs=specs, out_specs=tuple((space...  46.7 us
    ppermute x9, starting transfers between devices, send(): return lax.ppermute(array, ('grp', 'row'), pairs)  13.5 us
    ppermute x9, waiting for transfers between devices, send(): return lax.ppermute(array, ('grp', 'row'), pairs)  7.04 us
  transfers between devices with their start and end apart: 9, of which 6 were waited for; matrix products, arithmetic and copies ran while one was open for 0% of the time, Pallas kernels for 18%

profile of v4, /device:TPU:0, one launch (start us, length us, event | category | flops | bytes accessed | tf_op | source)
XLA Modules:
  0.0 67.4 jit_solution(13976002802620430723)
XLA Ops:
  0.0 0.0 copy-start.2
  0.0 0.0 copy-start
  0.0 0.0 copy-start.3
  0.0 33.0 %first.1 = (bf16[256,128]{1,0:T(8,128)(2,1)}, bf16[272,128]{1,0:T(8,128)(2,1)}, bf16[256,128]{1,0:T(8,128)(2,1)}, bf16[256,128]{1,0:T(8,128)(2,1)}, bf16[24,128,128]{2,1,0:T(8,128)(2,1)}) custom-call(bf16[64,1024]{1,0:T(8,128)(2,1)} %occ.1, bf16[64,1024]{1,0:T(8,128)(2,1)} %virt.1, s32[1,4,4]{2,1,0:T(4,128)} %tiles.5, bf16[1,48,128,128]{3,2,1,0:T(8,128)(2,1)} %tensor.5), custom_call_target="tpu_custom_call" | custom-call | tf_op jit(solution)/shard_map/first/pallas_call | solution.py:340
  33.0 5.5 %collective-permute-start.1 = (bf16[256,128]{1,0:T(8,128)(2,1)}, bf16[256,128]{1,0:T(8,128)(2,1)S(1)}, u32[]{:S(2)}, u32[]{:S(2)}) collective-permute-start(bf16[256,128]{1,0:T(8,128)(2,1)} %get-tuple-element.27), channel_id=1, source_target_pairs={{0,15},{1,0},{2,1},{3,2},{4,3},{5,4},{6,5},{7,6},{8,7},{9,8},{10,9... | collective-permute-start | bytes 196616 | tf_op jit(solution)/shard_map/ppermute | solution.py:363
  38.6 0.0 collective-permute-start.2
  38.6 0.0 collective-permute-start
  38.6 0.0 collective-permute-start.6
  38.6 0.0 copy-done.3
  38.6 0.1 copy.8.win
  38.7 0.0 copy-done.2
  38.7 0.0 copy-done
  38.7 0.0 copy-start.1
  38.7 1.1 %far_tiles.1 = (bf16[768,128]{1,0:T(8,128)(2,1)S(1)}, bf16[768,128]{1,0:T(8,128)(2,1)S(1)}) custom-call(s32[16,4]{1,0:T(8,128)S(1)} %copy.8.win, s32[1,4,4]{2,1,0:T(4,128)S(1)} %copy-done.2, bf16[1,48,128,128]{3,2,1,0:T(8,128)(2,1)S(1)} %copy-done), custom_call_target="tpu_custom_call" | custom-call | flops 68719476736 | tf_op jit(solution)/shard_map/far_tiles/pallas_call | solution.py:340
  39.8 0.8 %collective-permute-start.4 = (bf16[768,128]{1,0:T(8,128)(2,1)S(1)}, bf16[768,128]{1,0:T(8,128)(2,1)S(1)}, u32[]{:S(2)}, u32[]{:S(2)}) collective-permute-start(bf16[768,128]{1,0:T(8,128)(2,1)S(1)} %get-tuple-element.29), channel_id=1, source_target_pairs={{0,2},{1,3},{2,4},{3,5},{4,6},{5,7},{6,8},{7,9},{8,10},{9,11},{10,... | collective-permute-start | bytes 589832 | tf_op jit(solution)/shard_map/ppermute | solution.py:363
  40.6 0.2 collective-permute-done.1.g_after
  40.8 4.0 %collective-permute-start.5 = (bf16[768,128]{1,0:T(8,128)(2,1)S(1)}, bf16[768,128]{1,0:T(8,128)(2,1)S(1)}, u32[]{:S(2)}, u32[]{:S(2)}) collective-permute-start(bf16[768,128]{1,0:T(8,128)(2,1)S(1)} %get-tuple-element.30), channel_id=1, source_target_pairs={{0,14},{1,15},{2,0},{3,1},{4,2},{5,3},{6,4},{7,5},{8,6},{9,7},{10,... | collective-permute-start | bytes 589832 | tf_op jit(solution)/shard_map/ppermute | solution.py:363
  44.8 1.7 %collective-permute-done.2.g_far = bf16[256,128]{1,0:T(8,128)(2,1)S(1)} collective-permute-done((bf16[256,128]{1,0:T(8,128)(2,1)}, bf16[256,128]{1,0:T(8,128)(2,1)S(1)}, u32[]{:S(2)}, u32[]{:S(2)}) %collective-permute-start.2) | collective-permute-done | bytes 65568 | tf_op jit(solution)/shard_map/ppermute | solution.py:363
  46.5 0.0 collective-permute-done.g_before
  46.5 0.0 copy-done.1
  46.5 1.4 %choose.1.greens.g0 = bf16[512,128]{1,0:T(8,128)(2,1)S(1)} custom-call(s32[16,4]{1,0:T(8,128)S(1)} %copy.8.win, bf16[256,128]{1,0:T(8,128)(2,1)S(1)} %copy-done.1, bf16[272,128]{1,0:T(8,128)(2,1)S(1)} %collective-permute-done.g_before, bf16[256,128]{1,0:T(8,128)(2,1)S(1)} %collective-permute-done.1.g_after, bf16[256,128]{1,0:T(8,128)(2,1)S(1)} %collective-permute-done.2.g_far), custom_call_target="tpu_custom_call" | custom-call | tf_op jit(solution)/shard_map/choose/pallas_call | solution.py:340
  47.8 1.6 %collective-permute-start.3 = (bf16[512,128]{1,0:T(8,128)(2,1)S(1)}, bf16[512,128]{1,0:T(8,128)(2,1)S(1)}, u32[]{:S(2)}, u32[]{:S(2)}) collective-permute-start(bf16[512,128]{1,0:T(8,128)(2,1)S(1)} %choose.1.greens.g0), channel_id=1, source_target_pairs={{0,16},{1,17},{2,18},{3,19},{4,20},{5,21},{6,22},{7,23},{8,24},{9,... | collective-permute-start | bytes 393224 | tf_op jit(solution)/shard_map/ppermute | solution.py:363
  49.4 3.5 %dress_own.1 = (f32[48,48]{1,0:T(8,128)S(1)}, bf16[48,16384]{1,0:T(8,128)(2,1)S(1)}, bf16[48,16384]{1,0:T(8,128)(2,1)S(1)}, bf16[48,8192]{1,0:T(8,128)(2,1)S(1)}) custom-call(s32[16,4]{1,0:T(8,128)S(1)} %copy.8.win, s32[1,4,4]{2,1,0:T(4,128)S(1)} %copy-done.2, bf16[1,48,128,128]{3,2,1,0:T(8,128)(2,1)S(1)} %copy-done, bf16[512,128]{1,0:T(8,128)(2,1)S(1)} %choose.1.greens.g0), custom_call_target="tpu_custom_call" | custom-call | tf_op jit(solution)/shard_map/dress_own/pallas_call | solution.py:340
  52.9 0.0 collective-permute-done.3.greens.g1
  52.9 2.3 %dress_partner.1 = (bf16[48,16384]{1,0:T(8,128)(2,1)S(1)}, bf16[48,8192]{1,0:T(8,128)(2,1)S(1)}) custom-call(s32[16,4]{1,0:T(8,128)S(1)} %copy.8.win, s32[1,4,4]{2,1,0:T(4,128)S(1)} %copy-done.2, bf16[1,48,128,128]{3,2,1,0:T(8,128)(2,1)S(1)} %copy-done, bf16[512,128]{1,0:T(8,128)(2,1)S(1)} %collective-permute-done.3.greens.g1), custom_call_target="tpu_custom_call" | custom-call | tf_op jit(solution)/shard_map/dress_partner/pallas_call | solution.py:340
  55.3 1.3 %collective-permute-done.6.tensor = bf16[24,128,128]{2,1,0:T(8,128)(2,1)S(1)} collective-permute-done((bf16[24,128,128]{2,1,0:T(8,128)(2,1)}, bf16[24,128,128]{2,1,0:T(8,128)(2,1)S(1)}, u32[]{:S(2)}, u32[]{:S(2)}) %collective-permute-start.6) | collective-permute-done | bytes 786464 | tf_op jit(solution)/shard_map/ppermute | solution.py:363
  56.6 3.9 %join.1 = (f32[96,128]{1,0:T(8,128)S(1)}, f32[48,128]{1,0:T(8,128)S(1)}) custom-call(s32[16,4]{1,0:T(8,128)S(1)} %copy.8.win, bf16[24,128,128]{2,1,0:T(8,128)(2,1)S(1)} %collective-permute-done.6.tensor, bf16[272,128]{1,0:T(8,128)(2,1)S(1)} %collective-permute-done.g_before, bf16[512,128]{1,0:T(8,128)(2,1)S(1)} %choose.1.greens.g0, ...), custom_call_target="tpu_custom_call" | custom-call | tf_op jit(solution)/shard_map/join/pallas_call | solution.py:340
  60.5 0.1 collective-permute-start.7
  60.6 0.0 collective-permute-done.4.from_left
  60.6 1.2 %collective-permute-done.5.from_right = bf16[768,128]{1,0:T(8,128)(2,1)S(1)} collective-permute-done((bf16[768,128]{1,0:T(8,128)(2,1)S(1)}, bf16[768,128]{1,0:T(8,128)(2,1)S(1)}, u32[]{:S(2)}, u32[]{:S(2)}) %collective-permute-start.5) | collective-permute-done | bytes 196640 | tf_op jit(solution)/shard_map/ppermute | solution.py:363
  61.8 0.3 collective-permute-done.7.after
  62.1 0.7 %join_far.1 = (f32[48,128]{1,0:T(8,128)S(1)}, f32[48,128]{1,0:T(8,128)S(1)}) custom-call(bf16[48,8192]{1,0:T(8,128)(2,1)S(1)} %get-tuple-element.35.far0, bf16[48,8192]{1,0:T(8,128)(2,1)S(1)} %get-tuple-element.36.far1, bf16[768,128]{1,0:T(8,128)(2,1)S(1)} %collective-permute-done.4.from_left, bf16[768,128]{1,0:T(8,128)(2,1)S(1)} %collective-permute-done.5.from_right, ...), custom_call_target="tpu_custom_call" | custom-call | tf_op jit(solution)/shard_map/join_far/pallas_call | solution.py:340
  62.8 1.6 %collective-permute-start.8 = (f32[48,128]{1,0:T(8,128)S(1)}, f32[48,128]{1,0:T(8,128)S(1)}, u32[]{:S(2)}, u32[]{:S(2)}) collective-permute-start(f32[48,128]{1,0:T(8,128)S(1)} %get-tuple-element.44), channel_id=1, source_target_pairs={{0,16},{1,17},{2,18},{3,19},{4,20},{5,21},{6,22},{7,23},{8,24},{9,... | collective-permute-start | bytes 73736 | tf_op jit(solution)/shard_map/ppermute | solution.py:363
  64.3 2.3 %collective-permute-done.8.recv = f32[48,128]{1,0:T(8,128)S(1)} collective-permute-done((f32[48,128]{1,0:T(8,128)S(1)}, f32[48,128]{1,0:T(8,128)S(1)}, u32[]{:S(2)}, u32[]{:S(2)}) %collective-permute-start.8) | collective-permute-done | bytes 24608 | tf_op jit(solution)/shard_map/ppermute | solution.py:363
  66.7 0.7 %assemble.1 = f32[48,240]{1,0:T(8,128)} custom-call(f32[48,48]{1,0:T(8,128)S(1)} %get-tuple-element.34.polar0, f32[48,128]{1,0:T(8,128)S(1)} %get-tuple-element.43.own, f32[48,128]{1,0:T(8,128)S(1)} %collective-permute-done.8.recv), custom_call_target="tpu_custom_call" | custom-call | tf_op jit(solution)/shard_map/assemble/pallas_call | solution.py:340
Async XLA Ops:
  0.0 38.7 %copy-start.2 = (s32[1,4,4]{2,1,0:T(4,128)S(1)}, s32[1,4,4]{2,1,0:T(4,128)}, u32[]{:S(2)}) copy-start(s32[1,4,4]{2,1,0:T(4,128)} %tiles.5) | copy-start | bytes 196
  0.0 38.7 %copy-start = (bf16[1,48,128,128]{3,2,1,0:T(8,128)(2,1)S(1)}, bf16[1,48,128,128]{3,2,1,0:T(8,128)(2,1)}, u32[]{:S(2)}) copy-start(bf16[1,48,128,128]{3,2,1,0:T(8,128)(2,1)} %tensor.5) | copy-start | bytes 4718596
  0.0 38.6 %copy-start.3 = (s32[16,4]{0,1:T(4,128)S(1)}, s32[16,4]{0,1:T(4,128)}, u32[]{:S(2)}) copy-start(s32[16,4]{0,1:T(4,128)} %param.9) | copy-start | bytes 772
  33.0 7.7 %collective-permute-start.1 = (bf16[256,128]{1,0:T(8,128)(2,1)}, bf16[256,128]{1,0:T(8,128)(2,1)S(1)}, u32[]{:S(2)}, u32[]{:S(2)}) collective-permute-start(bf16[256,128]{1,0:T(8,128)(2,1)} %get-tuple-element.27), channel_id=1, source_target_pairs={{0,15},{1,0},{2,1},{3,2},{4,3},{5,4},{6,5},{7,6},{8,7},{9,8},{10,9... | collective-permute-start | bytes 196616 | tf_op jit(solution)/shard_map/ppermute | solution.py:363
  38.6 7.9 %collective-permute-start.2 = (bf16[256,128]{1,0:T(8,128)(2,1)}, bf16[256,128]{1,0:T(8,128)(2,1)S(1)}, u32[]{:S(2)}, u32[]{:S(2)}) collective-permute-start(bf16[256,128]{1,0:T(8,128)(2,1)} %get-tuple-element.28), channel_id=1, source_target_pairs={{0,2},{1,3},{2,4},{3,5},{4,6},{5,7},{6,8},{7,9},{8,10},{9,11},{10,... | collective-permute-start | bytes 196616 | tf_op jit(solution)/shard_map/ppermute | solution.py:363
  38.6 7.9 %collective-permute-start = (bf16[272,128]{1,0:T(8,128)(2,1)}, bf16[272,128]{1,0:T(8,128)(2,1)S(1)}, u32[]{:S(2)}, u32[]{:S(2)}) collective-permute-start(bf16[272,128]{1,0:T(8,128)(2,1)} %get-tuple-element.26), channel_id=1, source_target_pairs={{0,1},{1,2},{2,3},{3,4},{4,5},{5,6},{6,7},{7,8},{8,9},{9,10},{10,1... | collective-permute-start | bytes 208904 | tf_op jit(solution)/shard_map/ppermute | solution.py:363
  38.6 18.0 %collective-permute-start.6 = (bf16[24,128,128]{2,1,0:T(8,128)(2,1)}, bf16[24,128,128]{2,1,0:T(8,128)(2,1)S(1)}, u32[]{:S(2)}, u32[]{:S(2)}) collective-permute-start(bf16[24,128,128]{2,1,0:T(8,128)(2,1)} %get-tuple-element.37), channel_id=1, source_target_pairs={{0,1},{1,2},{2,3},{3,4},{4,5},{5,6},{6,7},{7,8},{8,9},{9,10},{10,1... | collective-permute-start | bytes 2359304 | tf_op jit(solution)/shard_map/ppermute | solution.py:363
  38.7 7.8 %copy-start.1 = (bf16[256,128]{1,0:T(8,128)(2,1)S(1)}, bf16[256,128]{1,0:T(8,128)(2,1)}, u32[]{:S(2)}) copy-start(bf16[256,128]{1,0:T(8,128)(2,1)} %get-tuple-element.25.g_self) | copy-start | bytes 196612
  39.8 20.8 %collective-permute-start.4 = (bf16[768,128]{1,0:T(8,128)(2,1)S(1)}, bf16[768,128]{1,0:T(8,128)(2,1)S(1)}, u32[]{:S(2)}, u32[]{:S(2)}) collective-permute-start(bf16[768,128]{1,0:T(8,128)(2,1)S(1)} %get-tuple-element.29), channel_id=1, source_target_pairs={{0,2},{1,3},{2,4},{3,5},{4,6},{5,7},{6,8},{7,9},{8,10},{9,11},{10,... | collective-permute-start | bytes 589832 | tf_op jit(solution)/shard_map/ppermute | solution.py:363
  40.8 21.0 %collective-permute-start.5 = (bf16[768,128]{1,0:T(8,128)(2,1)S(1)}, bf16[768,128]{1,0:T(8,128)(2,1)S(1)}, u32[]{:S(2)}, u32[]{:S(2)}) collective-permute-start(bf16[768,128]{1,0:T(8,128)(2,1)S(1)} %get-tuple-element.30), channel_id=1, source_target_pairs={{0,14},{1,15},{2,0},{3,1},{4,2},{5,3},{6,4},{7,5},{8,6},{9,7},{10,... | collective-permute-start | bytes 589832 | tf_op jit(solution)/shard_map/ppermute | solution.py:363
  47.8 5.1 %collective-permute-start.3 = (bf16[512,128]{1,0:T(8,128)(2,1)S(1)}, bf16[512,128]{1,0:T(8,128)(2,1)S(1)}, u32[]{:S(2)}, u32[]{:S(2)}) collective-permute-start(bf16[512,128]{1,0:T(8,128)(2,1)S(1)} %choose.1.greens.g0), channel_id=1, source_target_pairs={{0,16},{1,17},{2,18},{3,19},{4,20},{5,21},{6,22},{7,23},{8,24},{9,... | collective-permute-start | bytes 393224 | tf_op jit(solution)/shard_map/ppermute | solution.py:363
  60.5 1.6 %collective-permute-start.7 = (f32[48,128]{1,0:T(8,128)S(1)}, f32[48,128]{1,0:T(8,128)S(1)}, u32[]{:S(2)}, u32[]{:S(2)}) collective-permute-start(f32[48,128]{1,0:T(8,128)S(1)} %get-tuple-element.42), channel_id=1, source_target_pairs={{0,15},{1,0},{2,1},{3,2},{4,3},{5,4},{6,5},{7,6},{8,7},{9,8},{10,9... | collective-permute-start | bytes 73736 | tf_op jit(solution)/shard_map/ppermute | solution.py:363
  62.8 3.9 %collective-permute-start.8 = (f32[48,128]{1,0:T(8,128)S(1)}, f32[48,128]{1,0:T(8,128)S(1)}, u32[]{:S(2)}, u32[]{:S(2)}) collective-permute-start(f32[48,128]{1,0:T(8,128)S(1)} %get-tuple-element.44), channel_id=1, source_target_pairs={{0,16},{1,17},{2,18},{3,19},{4,20},{5,21},{6,22},{7,23},{8,24},{9,... | collective-permute-start | bytes 73736 | tf_op jit(solution)/shard_map/ppermute | solution.py:363

commit v5 on v4

--- a/solution.py
+++ b/solution.py
@@ -67,33 +67,42 @@
     return near(row, -1, count) >> 1
 
 
-def first(count, occ, virt, tiles_hbm, coulomb, g_self, g_right, g_left, g_far, tensor, tiles, mask, sem):
+def first(count, occ, virt, tiles_hbm, coulomb, *refs):
+    outs, (tiles, gs, part, sem, done) = refs[:5], refs[5:]
     d = lax.axis_index("row")
-    funcs = tensor.shape[0]
+    funcs = part.shape[0]
     half = lax.rem(lax.axis_index("grp"), 2)
-    list_copy = pltpu.make_async_copy(tiles_hbm, tiles, sem.at[0])
+    list_copy = pltpu.make_async_copy(tiles_hbm, tiles, sem.at[16])
     list_copy.start()
-    copies = []
-    for out, by in ((g_right, 1), (g_left, -1), (g_far, 2), (g_self, 0)):
+    groups = []
+    for n, by in enumerate((0, 1, -1, 2)):
         start = column_chunk(near(d, by, count), count)
+        copies = []
         for c in range(2):
             chunk = lax.rem(start + c, count // 2)
             columns = pl.ds(pl.multiple_of(chunk * 128, 128), 128)
             for base, green in ((0, occ), (128, virt)):
                 at = base + 64 * c
-                copies.append(
-                    pltpu.make_async_copy(green.at[:, columns], out.at[at : at + 64], sem.at[len(copies) + 1])
-                )
-    copies.append(pltpu.make_async_copy(coulomb.at[0, pl.ds(half * funcs, funcs)], tensor, sem.at[17]))
-    for copy in copies:
-        copy.start()
+                place = gs.at[n, at : at + 64]
+                copies.append(pltpu.make_async_copy(green.at[:, columns], place, sem.at[4 * n + len(copies)]))
+        rows = outs[n].shape[0]
+        groups.append((copies, pltpu.make_async_copy(gs.at[n, 0:rows], outs[n], done.at[n])))
+    for n in range(3):
+        piece = pl.ds(half * funcs + n * 8, 8)
+        copy = pltpu.make_async_copy(coulomb.at[0, piece], part.at[n * 8 : n * 8 + 8], sem.at[17 + n])
+        out = pltpu.make_async_copy(part.at[n * 8 : n * 8 + 8], outs[4].at[n * 8 : n * 8 + 8], done.at[4 + n])
+        groups.append(([copy], out))
+    for copies, _ in groups:
+        for copy in copies:
+            copy.start()
     list_copy.wait()
-    mask[...] = tile_mask(tiles, 4).astype(BF)
-    mask_copy = pltpu.make_async_copy(mask, g_right.at[256:272], sem.at[18])
-    mask_copy.start()
-    for copy in copies:
-        copy.wait()
-    mask_copy.wait()
+    gs[1, 256:272, :] = tile_mask(tiles, 4).astype(BF)
+    for copies, out in groups:
+        for copy in copies:
+            copy.wait()
+        out.start()
+    for _, out in groups:
+        out.wait()
 
 
 def far_tiles(count, win, tiles, tensor, far_right, far_left, mask):
@@ -375,7 +384,13 @@
             shape((funcs, 128, 128), BF),
         ],
         (green_occ, green_virt, tile_list, coulomb3c),
-        [pltpu.SMEM((1, 4, 4), jnp.int32), pltpu.VMEM((16, 128), BF), pltpu.SemaphoreType.DMA((19,))],
+        [
+            pltpu.SMEM((1, 4, 4), jnp.int32),
+            pltpu.VMEM((4, 272, 128), BF),
+            pltpu.VMEM((funcs, 128, 128), BF),
+            pltpu.SemaphoreType.DMA((20,)),
+            pltpu.SemaphoreType.DMA((7,)),
+        ],
         limit=60 << 20,
         space=hbm,
     )

time: 67.6 us -> 36.9 us (0.55)
  Pallas kernels: 46.7 us -> 16 us
    pallas_call x8, Pallas kernels: 46.7 us -> 16 us  [call(): pl.pallas_call(kernel, name=name, in_specs=specs, out_specs=tuple((space...]
  transfers between devices with their start and end apart: 9 -> 9, of which waited for: 6 -> 6; matrix products, arithmetic and copies ran while one was open for 0% -> 0% of each run, Pallas kernels for 18% -> 33%
where the time goes in v5:
time: 36.9 us; the launch traced here: 36.7 us
  Pallas kernels  16 us (43%)
  starting transfers between devices  13.5 us (37%)
  waiting for transfers between devices  7.03 us (19%)
    pallas_call x8, Pallas kernels, call(): pl.pallas_call(kernel, name=name, in_specs=specs, out_specs=tuple((space...  16 us
    ppermute x9, starting transfers between devices, send(): return lax.ppermute(array, ('grp', 'row'), pairs)  13.5 us
    ppermute x9, waiting for transfers between devices, send(): return lax.ppermute(array, ('grp', 'row'), pairs)  7.03 us
  transfers between devices with their start and end apart: 9, of which 6 were waited for; matrix products, arithmetic and copies ran while one was open for 0% of the time, Pallas kernels for 33%

profile of v5, /device:TPU:0, one launch (start us, length us, event | category | flops | bytes accessed | tf_op | source)
XLA Modules:
  0.0 36.7 jit_solution(10381214338468870142)
XLA Ops:
  0.0 0.0 copy-start.2
  0.0 0.0 copy-start
  0.0 0.0 copy-start.3
  0.0 2.4 %first.1 = (bf16[256,128]{1,0:T(8,128)(2,1)}, bf16[272,128]{1,0:T(8,128)(2,1)}, bf16[256,128]{1,0:T(8,128)(2,1)}, bf16[256,128]{1,0:T(8,128)(2,1)}, bf16[24,128,128]{2,1,0:T(8,128)(2,1)}) custom-call(bf16[64,1024]{1,0:T(8,128)(2,1)} %occ.1, bf16[64,1024]{1,0:T(8,128)(2,1)} %virt.1, s32[1,4,4]{2,1,0:T(4,128)} %tiles.5, bf16[1,48,128,128]{3,2,1,0:T(8,128)(2,1)} %tensor.5), custom_call_target="tpu_custom_call" | custom-call | tf_op jit(solution)/shard_map/first/pallas_call | solution.py:349
  2.4 5.5 %collective-permute-start.1 = (bf16[256,128]{1,0:T(8,128)(2,1)}, bf16[256,128]{1,0:T(8,128)(2,1)S(1)}, u32[]{:S(2)}, u32[]{:S(2)}) collective-permute-start(bf16[256,128]{1,0:T(8,128)(2,1)} %get-tuple-element.27), channel_id=1, source_target_pairs={{0,15},{1,0},{2,1},{3,2},{4,3},{5,4},{6,5},{7,6},{8,7},{9,8},{10,9... | collective-permute-start | bytes 196616 | tf_op jit(solution)/shard_map/ppermute | solution.py:372
  7.9 0.0 collective-permute-start.2
  7.9 0.0 collective-permute-start
  7.9 0.0 collective-permute-start.6
  7.9 0.0 copy-done.3
  7.9 0.1 copy.8.win
  8.0 0.0 copy-done.2
  8.0 0.0 copy-done
  8.0 0.0 copy-start.1
  8.0 1.1 %far_tiles.1 = (bf16[768,128]{1,0:T(8,128)(2,1)S(1)}, bf16[768,128]{1,0:T(8,128)(2,1)S(1)}) custom-call(s32[16,4]{1,0:T(8,128)S(1)} %copy.8.win, s32[1,4,4]{2,1,0:T(4,128)S(1)} %copy-done.2, bf16[1,48,128,128]{3,2,1,0:T(8,128)(2,1)S(1)} %copy-done), custom_call_target="tpu_custom_call" | custom-call | flops 68719476736 | tf_op jit(solution)/shard_map/far_tiles/pallas_call | solution.py:349
  9.1 0.8 %collective-permute-start.4 = (bf16[768,128]{1,0:T(8,128)(2,1)S(1)}, bf16[768,128]{1,0:T(8,128)(2,1)S(1)}, u32[]{:S(2)}, u32[]{:S(2)}) collective-permute-start(bf16[768,128]{1,0:T(8,128)(2,1)S(1)} %get-tuple-element.29), channel_id=1, source_target_pairs={{0,2},{1,3},{2,4},{3,5},{4,6},{5,7},{6,8},{7,9},{8,10},{9,11},{10,... | collective-permute-start | bytes 589832 | tf_op jit(solution)/shard_map/ppermute | solution.py:372
  9.9 0.2 collective-permute-done.1.g_after
  10.1 4.0 %collective-permute-start.5 = (bf16[768,128]{1,0:T(8,128)(2,1)S(1)}, bf16[768,128]{1,0:T(8,128)(2,1)S(1)}, u32[]{:S(2)}, u32[]{:S(2)}) collective-permute-start(bf16[768,128]{1,0:T(8,128)(2,1)S(1)} %get-tuple-element.30), channel_id=1, source_target_pairs={{0,14},{1,15},{2,0},{3,1},{4,2},{5,3},{6,4},{7,5},{8,6},{9,7},{10,... | collective-permute-start | bytes 589832 | tf_op jit(solution)/shard_map/ppermute | solution.py:372
  14.1 1.7 %collective-permute-done.2.g_far = bf16[256,128]{1,0:T(8,128)(2,1)S(1)} collective-permute-done((bf16[256,128]{1,0:T(8,128)(2,1)}, bf16[256,128]{1,0:T(8,128)(2,1)S(1)}, u32[]{:S(2)}, u32[]{:S(2)}) %collective-permute-start.2) | collective-permute-done | bytes 65568 | tf_op jit(solution)/shard_map/ppermute | solution.py:372
  15.8 0.0 collective-permute-done.g_before
  15.8 0.0 copy-done.1
  15.8 1.4 %choose.1.greens.g0 = bf16[512,128]{1,0:T(8,128)(2,1)S(1)} custom-call(s32[16,4]{1,0:T(8,128)S(1)} %copy.8.win, bf16[256,128]{1,0:T(8,128)(2,1)S(1)} %copy-done.1, bf16[272,128]{1,0:T(8,128)(2,1)S(1)} %collective-permute-done.g_before, bf16[256,128]{1,0:T(8,128)(2,1)S(1)} %collective-permute-done.1.g_after, bf16[256,128]{1,0:T(8,128)(2,1)S(1)} %collective-permute-done.2.g_far), custom_call_target="tpu_custom_call" | custom-call | tf_op jit(solution)/shard_map/choose/pallas_call | solution.py:349
  17.2 1.6 %collective-permute-start.3 = (bf16[512,128]{1,0:T(8,128)(2,1)S(1)}, bf16[512,128]{1,0:T(8,128)(2,1)S(1)}, u32[]{:S(2)}, u32[]{:S(2)}) collective-permute-start(bf16[512,128]{1,0:T(8,128)(2,1)S(1)} %choose.1.greens.g0), channel_id=1, source_target_pairs={{0,16},{1,17},{2,18},{3,19},{4,20},{5,21},{6,22},{7,23},{8,24},{9,... | collective-permute-start | bytes 393224 | tf_op jit(solution)/shard_map/ppermute | solution.py:372
  18.7 3.5 %dress_own.1 = (f32[48,48]{1,0:T(8,128)S(1)}, bf16[48,16384]{1,0:T(8,128)(2,1)S(1)}, bf16[48,16384]{1,0:T(8,128)(2,1)S(1)}, bf16[48,8192]{1,0:T(8,128)(2,1)S(1)}) custom-call(s32[16,4]{1,0:T(8,128)S(1)} %copy.8.win, s32[1,4,4]{2,1,0:T(4,128)S(1)} %copy-done.2, bf16[1,48,128,128]{3,2,1,0:T(8,128)(2,1)S(1)} %copy-done, bf16[512,128]{1,0:T(8,128)(2,1)S(1)} %choose.1.greens.g0), custom_call_target="tpu_custom_call" | custom-call | tf_op jit(solution)/shard_map/dress_own/pallas_call | solution.py:349
  22.2 0.0 collective-permute-done.3.greens.g1
  22.3 2.3 %dress_partner.1 = (bf16[48,16384]{1,0:T(8,128)(2,1)S(1)}, bf16[48,8192]{1,0:T(8,128)(2,1)S(1)}) custom-call(s32[16,4]{1,0:T(8,128)S(1)} %copy.8.win, s32[1,4,4]{2,1,0:T(4,128)S(1)} %copy-done.2, bf16[1,48,128,128]{3,2,1,0:T(8,128)(2,1)S(1)} %copy-done, bf16[512,128]{1,0:T(8,128)(2,1)S(1)} %collective-permute-done.3.greens.g1), custom_call_target="tpu_custom_call" | custom-call | tf_op jit(solution)/shard_map/dress_partner/pallas_call | solution.py:349
  24.6 1.3 %collective-permute-done.6.tensor = bf16[24,128,128]{2,1,0:T(8,128)(2,1)S(1)} collective-permute-done((bf16[24,128,128]{2,1,0:T(8,128)(2,1)}, bf16[24,128,128]{2,1,0:T(8,128)(2,1)S(1)}, u32[]{:S(2)}, u32[]{:S(2)}) %collective-permute-start.6) | collective-permute-done | bytes 786464 | tf_op jit(solution)/shard_map/ppermute | solution.py:372
  25.9 3.9 %join.1 = (f32[96,128]{1,0:T(8,128)S(1)}, f32[48,128]{1,0:T(8,128)S(1)}) custom-call(s32[16,4]{1,0:T(8,128)S(1)} %copy.8.win, bf16[24,128,128]{2,1,0:T(8,128)(2,1)S(1)} %collective-permute-done.6.tensor, bf16[272,128]{1,0:T(8,128)(2,1)S(1)} %collective-permute-done.g_before, bf16[512,128]{1,0:T(8,128)(2,1)S(1)} %choose.1.greens.g0, ...), custom_call_target="tpu_custom_call" | custom-call | tf_op jit(solution)/shard_map/join/pallas_call | solution.py:349
  29.8 0.1 collective-permute-start.7
  29.9 0.0 collective-permute-done.4.from_left
  29.9 1.2 %collective-permute-done.5.from_right = bf16[768,128]{1,0:T(8,128)(2,1)S(1)} collective-permute-done((bf16[768,128]{1,0:T(8,128)(2,1)S(1)}, bf16[768,128]{1,0:T(8,128)(2,1)S(1)}, u32[]{:S(2)}, u32[]{:S(2)}) %collective-permute-start.5) | collective-permute-done | bytes 196640 | tf_op jit(solution)/shard_map/ppermute | solution.py:372
  31.1 0.3 collective-permute-done.7.after
  31.4 0.7 %join_far.1 = (f32[48,128]{1,0:T(8,128)S(1)}, f32[48,128]{1,0:T(8,128)S(1)}) custom-call(bf16[48,8192]{1,0:T(8,128)(2,1)S(1)} %get-tuple-element.35.far0, bf16[48,8192]{1,0:T(8,128)(2,1)S(1)} %get-tuple-element.36.far1, bf16[768,128]{1,0:T(8,128)(2,1)S(1)} %collective-permute-done.4.from_left, bf16[768,128]{1,0:T(8,128)(2,1)S(1)} %collective-permute-done.5.from_right, ...), custom_call_target="tpu_custom_call" | custom-call | tf_op jit(solution)/shard_map/join_far/pallas_call | solution.py:349
  32.1 1.6 %collective-permute-start.8 = (f32[48,128]{1,0:T(8,128)S(1)}, f32[48,128]{1,0:T(8,128)S(1)}, u32[]{:S(2)}, u32[]{:S(2)}) collective-permute-start(f32[48,128]{1,0:T(8,128)S(1)} %get-tuple-element.44), channel_id=1, source_target_pairs={{0,16},{1,17},{2,18},{3,19},{4,20},{5,21},{6,22},{7,23},{8,24},{9,... | collective-permute-start | bytes 73736 | tf_op jit(solution)/shard_map/ppermute | solution.py:372
  33.7 2.3 %collective-permute-done.8.recv = f32[48,128]{1,0:T(8,128)S(1)} collective-permute-done((f32[48,128]{1,0:T(8,128)S(1)}, f32[48,128]{1,0:T(8,128)S(1)}, u32[]{:S(2)}, u32[]{:S(2)}) %collective-permute-start.8) | collective-permute-done | bytes 24608 | tf_op jit(solution)/shard_map/ppermute | solution.py:372
  36.0 0.7 %assemble.1 = f32[48,240]{1,0:T(8,128)} custom-call(f32[48,48]{1,0:T(8,128)S(1)} %get-tuple-element.34.polar0, f32[48,128]{1,0:T(8,128)S(1)} %get-tuple-element.43.own, f32[48,128]{1,0:T(8,128)S(1)} %collective-permute-done.8.recv), custom_call_target="tpu_custom_call" | custom-call | tf_op jit(solution)/shard_map/assemble/pallas_call | solution.py:349
Async XLA Ops:
  0.0 8.0 %copy-start.2 = (s32[1,4,4]{2,1,0:T(4,128)S(1)}, s32[1,4,4]{2,1,0:T(4,128)}, u32[]{:S(2)}) copy-start(s32[1,4,4]{2,1,0:T(4,128)} %tiles.5) | copy-start | bytes 196
  0.0 8.0 %copy-start = (bf16[1,48,128,128]{3,2,1,0:T(8,128)(2,1)S(1)}, bf16[1,48,128,128]{3,2,1,0:T(8,128)(2,1)}, u32[]{:S(2)}) copy-start(bf16[1,48,128,128]{3,2,1,0:T(8,128)(2,1)} %tensor.5) | copy-start | bytes 4718596
  0.0 7.9 %copy-start.3 = (s32[16,4]{0,1:T(4,128)S(1)}, s32[16,4]{0,1:T(4,128)}, u32[]{:S(2)}) copy-start(s32[16,4]{0,1:T(4,128)} %param.9) | copy-start | bytes 772
  2.4 7.7 %collective-permute-start.1 = (bf16[256,128]{1,0:T(8,128)(2,1)}, bf16[256,128]{1,0:T(8,128)(2,1)S(1)}, u32[]{:S(2)}, u32[]{:S(2)}) collective-permute-start(bf16[256,128]{1,0:T(8,128)(2,1)} %get-tuple-element.27), channel_id=1, source_target_pairs={{0,15},{1,0},{2,1},{3,2},{4,3},{5,4},{6,5},{7,6},{8,7},{9,8},{10,9... | collective-permute-start | bytes 196616 | tf_op jit(solution)/shard_map/ppermute | solution.py:372
  7.9 7.9 %collective-permute-start.2 = (bf16[256,128]{1,0:T(8,128)(2,1)}, bf16[256,128]{1,0:T(8,128)(2,1)S(1)}, u32[]{:S(2)}, u32[]{:S(2)}) collective-permute-start(bf16[256,128]{1,0:T(8,128)(2,1)} %get-tuple-element.28), channel_id=1, source_target_pairs={{0,2},{1,3},{2,4},{3,5},{4,6},{5,7},{6,8},{7,9},{8,10},{9,11},{10,... | collective-permute-start | bytes 196616 | tf_op jit(solution)/shard_map/ppermute | solution.py:372
  7.9 7.9 %collective-permute-start = (bf16[272,128]{1,0:T(8,128)(2,1)}, bf16[272,128]{1,0:T(8,128)(2,1)S(1)}, u32[]{:S(2)}, u32[]{:S(2)}) collective-permute-start(bf16[272,128]{1,0:T(8,128)(2,1)} %get-tuple-element.26), channel_id=1, source_target_pairs={{0,1},{1,2},{2,3},{3,4},{4,5},{5,6},{6,7},{7,8},{8,9},{9,10},{10,1... | collective-permute-start | bytes 208904 | tf_op jit(solution)/shard_map/ppermute | solution.py:372
  7.9 18.0 %collective-permute-start.6 = (bf16[24,128,128]{2,1,0:T(8,128)(2,1)}, bf16[24,128,128]{2,1,0:T(8,128)(2,1)S(1)}, u32[]{:S(2)}, u32[]{:S(2)}) collective-permute-start(bf16[24,128,128]{2,1,0:T(8,128)(2,1)} %get-tuple-element.37), channel_id=1, source_target_pairs={{0,1},{1,2},{2,3},{3,4},{4,5},{5,6},{6,7},{7,8},{8,9},{9,10},{10,1... | collective-permute-start | bytes 2359304 | tf_op jit(solution)/shard_map/ppermute | solution.py:372
  8.0 7.8 %copy-start.1 = (bf16[256,128]{1,0:T(8,128)(2,1)S(1)}, bf16[256,128]{1,0:T(8,128)(2,1)}, u32[]{:S(2)}) copy-start(bf16[256,128]{1,0:T(8,128)(2,1)} %get-tuple-element.25.g_self) | copy-start | bytes 196612
  9.1 20.8 %collective-permute-start.4 = (bf16[768,128]{1,0:T(8,128)(2,1)S(1)}, bf16[768,128]{1,0:T(8,128)(2,1)S(1)}, u32[]{:S(2)}, u32[]{:S(2)}) collective-permute-start(bf16[768,128]{1,0:T(8,128)(2,1)S(1)} %get-tuple-element.29), channel_id=1, source_target_pairs={{0,2},{1,3},{2,4},{3,5},{4,6},{5,7},{6,8},{7,9},{8,10},{9,11},{10,... | collective-permute-start | bytes 589832 | tf_op jit(solution)/shard_map/ppermute | solution.py:372
  10.1 21.0 %collective-permute-start.5 = (bf16[768,128]{1,0:T(8,128)(2,1)S(1)}, bf16[768,128]{1,0:T(8,128)(2,1)S(1)}, u32[]{:S(2)}, u32[]{:S(2)}) collective-permute-start(bf16[768,128]{1,0:T(8,128)(2,1)S(1)} %get-tuple-element.30), channel_id=1, source_target_pairs={{0,14},{1,15},{2,0},{3,1},{4,2},{5,3},{6,4},{7,5},{8,6},{9,7},{10,... | collective-permute-start | bytes 589832 | tf_op jit(solution)/shard_map/ppermute | solution.py:372
  17.2 5.1 %collective-permute-start.3 = (bf16[512,128]{1,0:T(8,128)(2,1)S(1)}, bf16[512,128]{1,0:T(8,128)(2,1)S(1)}, u32[]{:S(2)}, u32[]{:S(2)}) collective-permute-start(bf16[512,128]{1,0:T(8,128)(2,1)S(1)} %choose.1.greens.g0), channel_id=1, source_target_pairs={{0,16},{1,17},{2,18},{3,19},{4,20},{5,21},{6,22},{7,23},{8,24},{9,... | collective-permute-start | bytes 393224 | tf_op jit(solution)/shard_map/ppermute | solution.py:372
  29.8 1.6 %collective-permute-start.7 = (f32[48,128]{1,0:T(8,128)S(1)}, f32[48,128]{1,0:T(8,128)S(1)}, u32[]{:S(2)}, u32[]{:S(2)}) collective-permute-start(f32[48,128]{1,0:T(8,128)S(1)} %get-tuple-element.42), channel_id=1, source_target_pairs={{0,15},{1,0},{2,1},{3,2},{4,3},{5,4},{6,5},{7,6},{8,7},{9,8},{10,9... | collective-permute-start | bytes 73736 | tf_op jit(solution)/shard_map/ppermute | solution.py:372
  32.1 3.9 %collective-permute-start.8 = (f32[48,128]{1,0:T(8,128)S(1)}, f32[48,128]{1,0:T(8,128)S(1)}, u32[]{:S(2)}, u32[]{:S(2)}) collective-permute-start(f32[48,128]{1,0:T(8,128)S(1)} %get-tuple-element.44), channel_id=1, source_target_pairs={{0,16},{1,17},{2,18},{3,19},{4,20},{5,21},{6,22},{7,23},{8,24},{9,... | collective-permute-start | bytes 73736 | tf_op jit(solution)/shard_map/ppermute | solution.py:372

commit v6 on v5

--- a/solution.py
+++ b/solution.py
@@ -105,7 +105,7 @@
         out.wait()
 
 
-def far_tiles(count, win, tiles, tensor, far_right, far_left, mask):
+def far_tiles(count, win, tiles, tensor, far_right, far_left, flat, mask, ms):
     d = lax.axis_index("row")
     mine = window_at(win, d)
     funcs = tensor.shape[1] // 2
@@ -129,6 +129,12 @@
             ]
             x = dot(jnp.concatenate(sides, axis=1), select)
             out[r * 32 : r * 32 + 256, :] = x.astype(BF)
+    whole = mask[...]
+    for r in range(2 * funcs):
+        ms[r * PITCH : r * PITCH + 128, :] = (tensor[0, r] * whole).astype(F32)
+    for m in range(128):
+        rows = ms[pl.ds(m, 2 * funcs, stride=PITCH), :]
+        flat[:, m * 128 : (m + 1) * 128] = rows.astype(BF)
 
 
 def choose(count, win, g_self, g_before, g_after, g_far, out):
@@ -186,13 +192,10 @@
 PITCH = 136
 
 
-def halves(occ, blocks, outs, ms):
+def halves(occ, blocks, outs):
     rows = occ.shape[0] // len(outs)
     for i in range(0, len(blocks), 2):
         m0, m1 = blocks[i](), blocks[i + 1]()
-        if ms is not None:
-            ms[i * PITCH : i * PITCH + 128, :] = m0.astype(F32)
-            ms[(i + 1) * PITCH : (i + 1) * PITCH + 128, :] = m1.astype(F32)
         h = dot(occ, jnp.concatenate([m0, m1], axis=1))
         for n, out in enumerate(outs):
             part = h[n * rows : (n + 1) * rows]
@@ -206,9 +209,9 @@
 
 def dress(count, own, win, tiles, tensor, greens, *refs):
     if own:
-        polar0, flat, dressed, far, hs, ms, same = refs
+        flat, polar0, dressed, far, hs, same = refs
     else:
-        (dressed, far, hs), ms = refs, None
+        dressed, far, hs = refs
     d = lax.axis_index("row")
     funcs = tensor.shape[1]
     mine = window_at(win, d)
@@ -216,7 +219,7 @@
     left, right = near(d, -1, count) * 2, near(d, 1, count) * 2
     mask = tile_mask(tiles, 32).astype(BF)
     occ, virt = greens[0:128, :], greens[128:256, :]
-    halves(occ, [functools.partial(lambda r: tensor[0, r] * mask, r) for r in range(funcs)], [hs], ms)
+    halves(occ, [functools.partial(lambda r: tensor[0, r] * mask, r) for r in range(funcs)], [hs])
     wide, outs = dot(virt, frame_map(mine, theirs)).astype(BF), [dressed]
     if own:
         wide, outs = jnp.concatenate([virt, wide], axis=1), [same, dressed]
@@ -237,10 +240,6 @@
                 block = x[t * funcs : (t + 1) * funcs].astype(BF)
                 for n, out in enumerate(outs):
                     out[:, at : at + 128] = block[:, n * 128 : (n + 1) * 128]
-            if own:
-                for t, rows in enumerate(gather(ms, funcs, i * 32 + c * 8)):
-                    at = (i * 32 + c * 8 + t) * 128
-                    flat[:, at : at + 128] = rows.astype(BF)
         x = dot(jnp.concatenate(parts, axis=1), packs)
         for t in range(8):
             at = (c * 8 + t) * 128
@@ -260,32 +259,47 @@
     return total
 
 
-def join(count, win, tensor, g_before, g0, g1, flat, dressed0, dressed1, down, up, hs0, hs1, ms, backs, moved):
+def neighbour_mask(g_before):
+    short = g_before[256:272, :].astype(F32)
+    return jnp.concatenate(
+        [jnp.broadcast_to(short[4 * i : 4 * i + 1, :], (32, 128)) for i in range(4)], axis=0
+    ).astype(BF)
+
+
+def join_back(tensor, g_before, g0, g1, flat, up, hs0, hs1, backs):
+    funcs = tensor.shape[0]
+    full = 2 * funcs
+    mask = neighbour_mask(g_before)
+    occ = jnp.concatenate([g0[256:384, :], g1[256:384, :]], axis=0)
+    halves(occ, [functools.partial(lambda r: tensor[r] * mask, r) for r in range(funcs)], [hs0, hs1])
+    virts = [g0[384:512, :], g1[384:512, :]]
+    for i in range(16):
+        xs = []
+        for hs, virt in zip((hs0, hs1), virts):
+            xs.append(dot(jnp.concatenate(gather(hs, funcs, i * 8), axis=0).astype(BF), virt))
+        for t in range(8):
+            at = (i * 8 + t) * 128
+            part = slice(t * funcs, (t + 1) * funcs)
+            backs[:, at : at + 128] = jnp.concatenate([x[part] for x in xs], axis=0).astype(BF)
+    total = dot_t(backs[...], flat[...])
+    up[...] = jnp.concatenate([total, jnp.zeros((full, 128 - full), F32)], axis=1)
+
+
+def join(count, win, tensor, g_before, dressed0, dressed1, down, ms, moved):
     d = lax.axis_index("row")
     funcs = tensor.shape[0]
     full = 2 * funcs
     mine = window_at(win, d)
     theirs = window_at(win, near(d, -1, count))
-    short = g_before[256:272, :].astype(F32)
-    mask = jnp.concatenate(
-        [jnp.broadcast_to(short[4 * i : 4 * i + 1, :], (32, 128)) for i in range(4)], axis=0
-    ).astype(BF)
-    occ = jnp.concatenate([g0[256:384, :], g1[256:384, :]], axis=0)
-    halves(occ, [functools.partial(lambda r: tensor[r] * mask, r) for r in range(funcs)], [hs0, hs1], ms)
-    virts = [g0[384:512, :], g1[384:512, :]]
+    mask = neighbour_mask(g_before)
+    for r in range(funcs):
+        ms[r * PITCH : r * PITCH + 128, :] = (tensor[r] * mask).astype(F32)
     for i in range(16):
         slot, there = find(theirs, mine[i // 4])
-        xs = []
-        for hs, virt in zip((hs0, hs1), virts):
-            xs.append(dot(jnp.concatenate(gather(hs, funcs, i * 8), axis=0).astype(BF), virt))
         rows = gather(ms, funcs, slot * 32 + (i % 4) * 8)
         for t in range(8):
             at = (i * 8 + t) * 128
-            part = slice(t * funcs, (t + 1) * funcs)
-            backs[:, at : at + 128] = jnp.concatenate([x[part] for x in xs], axis=0).astype(BF)
             moved[:, at : at + 128] = (rows[t] * there).astype(BF)
-    total = dot_t(backs[...], flat[...])
-    up[...] = jnp.concatenate([total, jnp.zeros((full, 128 - full), F32)], axis=1)
     total = stacked(dressed0, dressed1, 0, moved)
     down[...] = jnp.concatenate([total, jnp.zeros((2 * full, 128 - funcs), F32)], axis=1)
 
@@ -398,17 +412,19 @@
     g_after = send(g_left, -1)
     g_beyond = send(g_far, 2)
     wide = send(tensor, 1)
-    far_right, far_left = call(
+    flat_shape, far_shape = shape((full, 128 * 128), BF), shape((full, 64 * 128), BF)
+    tall = pltpu.VMEM((full * PITCH, 128), F32)
+    short = pltpu.VMEM((funcs * PITCH, 128), F32)
+    message = shape((full, 128), F32)
+    far_right, far_left, flat = call(
         functools.partial(far_tiles, count),
         "far_tiles",
         smem(2) + vmem(1),
-        [shape((far_rows, 128), BF), shape((far_rows, 128), BF)],
+        [shape((far_rows, 128), BF), shape((far_rows, 128), BF), flat_shape],
         (window, tile_list, coulomb3c),
-        [pltpu.VMEM((128, 128), BF)],
+        [pltpu.VMEM((128, 128), BF), tall],
         flops=1 << 36,
     )
-    from_left = send(far_right, 2)
-    from_right = send(far_left, -2)
     g_before, g_after, g_beyond, far_right, far_left = lax.optimization_barrier(
         (g_before, g_after, g_beyond, far_right, far_left)
     )
@@ -420,18 +436,17 @@
         (window, g_self, g_before, g_after, g_beyond),
     )
     partner = send(mine, 0, True)
-    flat_shape, far_shape = shape((full, 128 * 128), BF), shape((full, 64 * 128), BF)
-    tall = pltpu.VMEM((full * PITCH, 128), F32)
-    short = pltpu.VMEM((funcs * PITCH, 128), F32)
-    message = shape((full, 128), F32)
-    polar0, flat, dressed0, far0 = call(
+    polar0, dressed0, far0 = call(
         functools.partial(dress, count, True),
         "dress_own",
-        smem(2) + vmem(2),
-        [shape((full, full), F32), flat_shape, flat_shape, far_shape],
-        (window, tile_list, coulomb3c, mine),
-        [tall, tall, pltpu.VMEM((full, 128 * 128), BF)],
-    )
+        smem(2) + vmem(3),
+        [shape((full, full), F32), flat_shape, far_shape],
+        (window, tile_list, coulomb3c, mine, flat),
+        [tall, pltpu.VMEM((full, 128 * 128), BF)],
+    )
+    far_right, far_left, polar0 = lax.optimization_barrier((far_right, far_left, polar0))
+    from_left = send(far_right, 2)
+    from_right = send(far_left, -2)
     dressed1, far1 = call(
         functools.partial(dress, count, False),
         "dress_partner",
@@ -440,15 +455,24 @@
         (window, tile_list, coulomb3c, partner),
         [tall],
     )
-    down, up = call(
+    (up,) = call(
+        join_back,
+        "join_back",
+        vmem(5),
+        [message],
+        (wide, g_before, mine, partner, flat),
+        [short, short, pltpu.VMEM((full, 128 * 128), BF)],
+    )
+    after = send(up, -1)
+    (down,) = call(
         functools.partial(join, count),
         "join",
-        smem(1) + vmem(7),
-        [shape((2 * full, 128), F32), message],
-        (window, wide, g_before, mine, partner, flat, dressed0, dressed1),
-        [short, short, short, pltpu.VMEM((full, 128 * 128), BF), pltpu.VMEM((funcs, 128 * 128), BF)],
-    )
-    after = send(up, -1)
+        smem(1) + vmem(4),
+        [shape((2 * full, 128), F32)],
+        (window, wide, g_before, dressed0, dressed1),
+        [short, pltpu.VMEM((funcs, 128 * 128), BF)],
+        flops=1 << 34,
+    )
     own, other = call(
         join_far,
         "join_far",

time: 36.9 us -> 38.6 us (1.046)
  waiting for transfers between devices: 7.03 us -> 8.99 us
  starting transfers between devices: 13.5 us -> 12.4 us
  Pallas kernels: 16 us -> 16.8 us
    ppermute x9, waiting for transfers between devices: 7.03 us -> 8.99 us  [send(): return lax.ppermute(array, ('grp', 'row'), pairs)]
    ppermute x9, starting transfers between devices: 13.5 us -> 12.4 us  [send(): return lax.ppermute(array, ('grp', 'row'), pairs)]
    pallas_call x8 -> x9, Pallas kernels: 16 us -> 16.8 us  [call(): pl.pallas_call(kernel, name=name, in_specs=specs, out_specs=tuple((space...]
  transfers between devices with their start and end apart: 9 -> 9, of which waited for: 6 -> 3; matrix products, arithmetic and copies ran while one was open for 0% -> 0% of each run, Pallas kernels for 33% -> 34%
where the time goes in v6:
time: 38.6 us; the launch traced here: 38.5 us
  Pallas kernels  16.8 us (44%)
  starting transfers between devices  12.4 us (32%)
  waiting for transfers between devices  8.99 us (23%)
    pallas_call x9, Pallas kernels, call(): pl.pallas_call(kernel, name=name, in_specs=specs, out_specs=tuple((space...  16.8 us
    ppermute x9, starting transfers between devices, send(): return lax.ppermute(array, ('grp', 'row'), pairs)  12.4 us
    ppermute x9, waiting for transfers between devices, send(): return lax.ppermute(array, ('grp', 'row'), pairs)  8.99 us
  transfers between devices with their start and end apart: 9, of which 3 were waited for; matrix products, arithmetic and copies ran while one was open for 0% of the time, Pallas kernels for 34%

profile of v6, /device:TPU:0, one launch (start us, length us, event | category | flops | bytes accessed | tf_op | source)
XLA Modules:
  0.0 38.5 jit_solution(3477139723394373976)
XLA Ops:
  0.0 0.0 copy-start.2
  0.0 0.0 copy-start
  0.0 0.0 copy-start.3
  0.0 2.4 %first.1 = (bf16[256,128]{1,0:T(8,128)(2,1)}, bf16[272,128]{1,0:T(8,128)(2,1)}, bf16[256,128]{1,0:T(8,128)(2,1)}, bf16[256,128]{1,0:T(8,128)(2,1)}, bf16[24,128,128]{2,1,0:T(8,128)(2,1)}) custom-call(bf16[64,1024]{1,0:T(8,128)(2,1)} %occ.1, bf16[64,1024]{1,0:T(8,128)(2,1)} %virt.1, s32[1,4,4]{2,1,0:T(4,128)} %tiles.5, bf16[1,48,128,128]{3,2,1,0:T(8,128)(2,1)} %tensor.5), custom_call_target="tpu_custom_call" | custom-call | tf_op jit(solution)/shard_map/first/pallas_call | solution.py:363
  2.4 5.5 %collective-permute-start.1 = (bf16[256,128]{1,0:T(8,128)(2,1)}, bf16[256,128]{1,0:T(8,128)(2,1)S(1)}, u32[]{:S(2)}, u32[]{:S(2)}) collective-permute-start(bf16[256,128]{1,0:T(8,128)(2,1)} %get-tuple-element.29), channel_id=1, source_target_pairs={{0,15},{1,0},{2,1},{3,2},{4,3},{5,4},{6,5},{7,6},{8,7},{9,8},{10,9... | collective-permute-start | bytes 196616 | tf_op jit(solution)/shard_map/ppermute | solution.py:386
  7.9 0.0 collective-permute-start.2
  7.9 0.0 collective-permute-start
  7.9 0.0 collective-permute-start.6
  7.9 0.0 copy-done.3
  7.9 0.1 copy.6.win
  8.0 0.0 copy-done.2
  8.0 0.0 copy-done
  8.0 0.0 copy-start.1
  8.0 2.0 %far_tiles.1 = (bf16[768,128]{1,0:T(8,128)(2,1)S(1)}, bf16[768,128]{1,0:T(8,128)(2,1)S(1)}, bf16[48,16384]{1,0:T(8,128)(2,1)S(1)}) custom-call(s32[16,4]{1,0:T(8,128)S(1)} %copy.6.win, s32[1,4,4]{2,1,0:T(4,128)S(1)} %copy-done.2, bf16[1,48,128,128]{3,2,1,0:T(8,128)(2,1)S(1)} %copy-done), custom_call_target="tpu_custom_call" | custom-call | flops 68719476736 | tf_op jit(solution)/shard_map/far_tiles/pallas_call | solution.py:363
  10.0 0.1 collective-permute-done.1.g_after
  10.1 5.6 %collective-permute-done.2.g_far = bf16[256,128]{1,0:T(8,128)(2,1)S(1)} collective-permute-done((bf16[256,128]{1,0:T(8,128)(2,1)}, bf16[256,128]{1,0:T(8,128)(2,1)S(1)}, u32[]{:S(2)}, u32[]{:S(2)}) %collective-permute-start.2) | collective-permute-done | bytes 65568 | tf_op jit(solution)/shard_map/ppermute | solution.py:386
  15.7 0.0 collective-permute-done.g_before
  15.7 0.0 copy-done.1
  15.7 1.3 %choose.1.greens.g0 = bf16[512,128]{1,0:T(8,128)(2,1)S(1)} custom-call(s32[16,4]{1,0:T(8,128)S(1)} %copy.6.win, bf16[256,128]{1,0:T(8,128)(2,1)S(1)} %copy-done.1, bf16[272,128]{1,0:T(8,128)(2,1)S(1)} %collective-permute-done.g_before, bf16[256,128]{1,0:T(8,128)(2,1)S(1)} %collective-permute-done.1.g_after, bf16[256,128]{1,0:T(8,128)(2,1)S(1)} %collective-permute-done.2.g_far), custom_call_target="tpu_custom_call" | custom-call | tf_op jit(solution)/shard_map/choose/pallas_call | solution.py:363
  17.1 1.6 %collective-permute-start.3 = (bf16[512,128]{1,0:T(8,128)(2,1)S(1)}, bf16[512,128]{1,0:T(8,128)(2,1)S(1)}, u32[]{:S(2)}, u32[]{:S(2)}) collective-permute-start(bf16[512,128]{1,0:T(8,128)(2,1)S(1)} %choose.1.greens.g0), channel_id=1, source_target_pairs={{0,16},{1,17},{2,18},{3,19},{4,20},{5,21},{6,22},{7,23},{8,24},{9,... | collective-permute-start | bytes 393224 | tf_op jit(solution)/shard_map/ppermute | solution.py:386
  18.6 3.2 %dress_own.1 = (f32[48,48]{1,0:T(8,128)S(1)}, bf16[48,16384]{1,0:T(8,128)(2,1)S(1)}, bf16[48,8192]{1,0:T(8,128)(2,1)S(1)}) custom-call(s32[16,4]{1,0:T(8,128)S(1)} %copy.6.win, s32[1,4,4]{2,1,0:T(4,128)S(1)} %copy-done.2, bf16[1,48,128,128]{3,2,1,0:T(8,128)(2,1)S(1)} %copy-done, bf16[512,128]{1,0:T(8,128)(2,1)S(1)} %choose.1.greens.g0, ...), custom_call_target="tpu_custom_call" | custom-call | tf_op jit(solution)/shard_map/dress_own/pallas_call | solution.py:363
  21.8 0.0 collective-permute-start.4
  21.9 4.7 %collective-permute-start.5 = (bf16[768,128]{1,0:T(8,128)(2,1)S(1)}, bf16[768,128]{1,0:T(8,128)(2,1)S(1)}, u32[]{:S(2)}, u32[]{:S(2)}) collective-permute-start(bf16[768,128]{1,0:T(8,128)(2,1)S(1)} %get-tuple-element.45), channel_id=1, source_target_pairs={{0,14},{1,15},{2,0},{3,1},{4,2},{5,3},{6,4},{7,5},{8,6},{9,7},{10,... | collective-permute-start | bytes 589832 | tf_op jit(solution)/shard_map/ppermute | solution.py:386
  26.6 0.0 collective-permute-done.3.greens.g1
  26.6 2.3 %dress_partner.1 = (bf16[48,16384]{1,0:T(8,128)(2,1)S(1)}, bf16[48,8192]{1,0:T(8,128)(2,1)S(1)}) custom-call(s32[16,4]{1,0:T(8,128)S(1)} %copy.6.win, s32[1,4,4]{2,1,0:T(4,128)S(1)} %copy-done.2, bf16[1,48,128,128]{3,2,1,0:T(8,128)(2,1)S(1)} %copy-done, bf16[512,128]{1,0:T(8,128)(2,1)S(1)} %collective-permute-done.3.greens.g1), custom_call_target="tpu_custom_call" | custom-call | tf_op jit(solution)/shard_map/dress_partner/pallas_call | solution.py:363
  28.9 0.0 collective-permute-done.6.tensor
  28.9 2.4 %join_back.1 = f32[48,128]{1,0:T(8,128)S(1)} custom-call(bf16[24,128,128]{2,1,0:T(8,128)(2,1)S(1)} %collective-permute-done.6.tensor, bf16[272,128]{1,0:T(8,128)(2,1)S(1)} %collective-permute-done.g_before, bf16[512,128]{1,0:T(8,128)(2,1)S(1)} %choose.1.greens.g0, bf16[512,128]{1,0:T(8,128)(2,1)S(1)} %collective-permute-done.3.greens.g1, ...), custom_call_target="tpu_custom_call" | custom-call | tf_op jit(solution)/shard_map/join_back/pallas_call | solution.py:363
  31.3 0.0 collective-permute-start.7
  31.3 1.8 %join.1.down = f32[96,128]{1,0:T(8,128)S(1)} custom-call(s32[16,4]{1,0:T(8,128)S(1)} %copy.6.win, bf16[24,128,128]{2,1,0:T(8,128)(2,1)S(1)} %collective-permute-done.6.tensor, bf16[272,128]{1,0:T(8,128)(2,1)S(1)} %collective-permute-done.g_before, bf16[48,16384]{1,0:T(8,128)(2,1)S(1)} %get-tuple-element.47.dressed0, ...), custom_call_target="tpu_custom_call" | custom-call | flops 17179869184 | tf_op jit(solution)/shard_map/join/pallas_call | solution.py:363
  33.1 0.0 collective-permute-done.4.from_left
  33.1 0.0 collective-permute-done.5.from_right
  33.2 0.0 collective-permute-done.7.after
  33.2 0.7 %join_far.1 = (f32[48,128]{1,0:T(8,128)S(1)}, f32[48,128]{1,0:T(8,128)S(1)}) custom-call(bf16[48,8192]{1,0:T(8,128)(2,1)S(1)} %get-tuple-element.42.far0, bf16[48,8192]{1,0:T(8,128)(2,1)S(1)} %get-tuple-element.43.far1, bf16[768,128]{1,0:T(8,128)(2,1)S(1)} %collective-permute-done.4.from_left, bf16[768,128]{1,0:T(8,128)(2,1)S(1)} %collective-permute-done.5.from_right, ...), custom_call_target="tpu_custom_call" | custom-call | tf_op jit(solution)/shard_map/join_far/pallas_call | solution.py:363
  33.9 0.6 %collective-permute-start.8 = (f32[48,128]{1,0:T(8,128)S(1)}, f32[48,128]{1,0:T(8,128)S(1)}, u32[]{:S(2)}, u32[]{:S(2)}) collective-permute-start(f32[48,128]{1,0:T(8,128)S(1)} %get-tuple-element.50), channel_id=1, source_target_pairs={{0,16},{1,17},{2,18},{3,19},{4,20},{5,21},{6,22},{7,23},{8,24},{9,... | collective-permute-start | bytes 73736 | tf_op jit(solution)/shard_map/ppermute | solution.py:386
  34.5 3.3 %collective-permute-done.8.recv = f32[48,128]{1,0:T(8,128)S(1)} collective-permute-done((f32[48,128]{1,0:T(8,128)S(1)}, f32[48,128]{1,0:T(8,128)S(1)}, u32[]{:S(2)}, u32[]{:S(2)}) %collective-permute-start.8) | collective-permute-done | bytes 24608 | tf_op jit(solution)/shard_map/ppermute | solution.py:386
  37.8 0.7 %assemble.1 = f32[48,240]{1,0:T(8,128)} custom-call(f32[48,48]{1,0:T(8,128)S(1)} %get-tuple-element.41.polar0, f32[48,128]{1,0:T(8,128)S(1)} %get-tuple-element.49.own, f32[48,128]{1,0:T(8,128)S(1)} %collective-permute-done.8.recv), custom_call_target="tpu_custom_call" | custom-call | tf_op jit(solution)/shard_map/assemble/pallas_call | solution.py:363
Async XLA Ops:
  0.0 8.0 %copy-start.2 = (s32[1,4,4]{2,1,0:T(4,128)S(1)}, s32[1,4,4]{2,1,0:T(4,128)}, u32[]{:S(2)}) copy-start(s32[1,4,4]{2,1,0:T(4,128)} %tiles.5) | copy-start | bytes 196
  0.0 8.0 %copy-start = (bf16[1,48,128,128]{3,2,1,0:T(8,128)(2,1)S(1)}, bf16[1,48,128,128]{3,2,1,0:T(8,128)(2,1)}, u32[]{:S(2)}) copy-start(bf16[1,48,128,128]{3,2,1,0:T(8,128)(2,1)} %tensor.5) | copy-start | bytes 4718596
  0.0 7.9 %copy-start.3 = (s32[16,4]{0,1:T(4,128)S(1)}, s32[16,4]{0,1:T(4,128)}, u32[]{:S(2)}) copy-start(s32[16,4]{0,1:T(4,128)} %param.9) | copy-start | bytes 772
  2.4 7.7 %collective-permute-start.1 = (bf16[256,128]{1,0:T(8,128)(2,1)}, bf16[256,128]{1,0:T(8,128)(2,1)S(1)}, u32[]{:S(2)}, u32[]{:S(2)}) collective-permute-start(bf16[256,128]{1,0:T(8,128)(2,1)} %get-tuple-element.29), channel_id=1, source_target_pairs={{0,15},{1,0},{2,1},{3,2},{4,3},{5,4},{6,5},{7,6},{8,7},{9,8},{10,9... | collective-permute-start | bytes 196616 | tf_op jit(solution)/shard_map/ppermute | solution.py:386
  7.9 7.8 %collective-permute-start.2 = (bf16[256,128]{1,0:T(8,128)(2,1)}, bf16[256,128]{1,0:T(8,128)(2,1)S(1)}, u32[]{:S(2)}, u32[]{:S(2)}) collective-permute-start(bf16[256,128]{1,0:T(8,128)(2,1)} %get-tuple-element.30), channel_id=1, source_target_pairs={{0,2},{1,3},{2,4},{3,5},{4,6},{5,7},{6,8},{7,9},{8,10},{9,11},{10,... | collective-permute-start | bytes 196616 | tf_op jit(solution)/shard_map/ppermute | solution.py:386
  7.9 7.8 %collective-permute-start = (bf16[272,128]{1,0:T(8,128)(2,1)}, bf16[272,128]{1,0:T(8,128)(2,1)S(1)}, u32[]{:S(2)}, u32[]{:S(2)}) collective-permute-start(bf16[272,128]{1,0:T(8,128)(2,1)} %get-tuple-element.28), channel_id=1, source_target_pairs={{0,1},{1,2},{2,3},{3,4},{4,5},{5,6},{6,7},{7,8},{8,9},{9,10},{10,1... | collective-permute-start | bytes 208904 | tf_op jit(solution)/shard_map/ppermute | solution.py:386
  7.9 21.0 %collective-permute-start.6 = (bf16[24,128,128]{2,1,0:T(8,128)(2,1)}, bf16[24,128,128]{2,1,0:T(8,128)(2,1)S(1)}, u32[]{:S(2)}, u32[]{:S(2)}) collective-permute-start(bf16[24,128,128]{2,1,0:T(8,128)(2,1)} %get-tuple-element.46), channel_id=1, source_target_pairs={{0,1},{1,2},{2,3},{3,4},{4,5},{5,6},{6,7},{7,8},{8,9},{9,10},{10,1... | collective-permute-start | bytes 2359304 | tf_op jit(solution)/shard_map/ppermute | solution.py:386
  8.0 7.7 %copy-start.1 = (bf16[256,128]{1,0:T(8,128)(2,1)S(1)}, bf16[256,128]{1,0:T(8,128)(2,1)}, u32[]{:S(2)}) copy-start(bf16[256,128]{1,0:T(8,128)(2,1)} %get-tuple-element.35.g_self) | copy-start | bytes 196612
  17.1 9.5 %collective-permute-start.3 = (bf16[512,128]{1,0:T(8,128)(2,1)S(1)}, bf16[512,128]{1,0:T(8,128)(2,1)S(1)}, u32[]{:S(2)}, u32[]{:S(2)}) collective-permute-start(bf16[512,128]{1,0:T(8,128)(2,1)S(1)} %choose.1.greens.g0), channel_id=1, source_target_pairs={{0,16},{1,17},{2,18},{3,19},{4,20},{5,21},{6,22},{7,23},{8,24},{9,... | collective-permute-start | bytes 393224 | tf_op jit(solution)/shard_map/ppermute | solution.py:386
  21.8 11.3 %collective-permute-start.4 = (bf16[768,128]{1,0:T(8,128)(2,1)S(1)}, bf16[768,128]{1,0:T(8,128)(2,1)S(1)}, u32[]{:S(2)}, u32[]{:S(2)}) collective-permute-start(bf16[768,128]{1,0:T(8,128)(2,1)S(1)} %get-tuple-element.44), channel_id=1, source_target_pairs={{0,2},{1,3},{2,4},{3,5},{4,6},{5,7},{6,8},{7,9},{8,10},{9,11},{10,... | collective-permute-start | bytes 589832 | tf_op jit(solution)/shard_map/ppermute | solution.py:386
  21.9 11.3 %collective-permute-start.5 = (bf16[768,128]{1,0:T(8,128)(2,1)S(1)}, bf16[768,128]{1,0:T(8,128)(2,1)S(1)}, u32[]{:S(2)}, u32[]{:S(2)}) collective-permute-start(bf16[768,128]{1,0:T(8,128)(2,1)S(1)} %get-tuple-element.45), channel_id=1, source_target_pairs={{0,14},{1,15},{2,0},{3,1},{4,2},{5,3},{6,4},{7,5},{8,6},{9,7},{10,... | collective-permute-start | bytes 589832 | tf_op jit(solution)/shard_map/ppermute | solution.py:386
  31.3 1.9 %collective-permute-start.7 = (f32[48,128]{1,0:T(8,128)S(1)}, f32[48,128]{1,0:T(8,128)S(1)}, u32[]{:S(2)}, u32[]{:S(2)}) collective-permute-start(f32[48,128]{1,0:T(8,128)S(1)} %join_back.1), channel_id=1, source_target_pairs={{0,15},{1,0},{2,1},{3,2},{4,3},{5,4},{6,5},{7,6},{8,7},{9,8},{10,9... | collective-permute-start | bytes 73736 | tf_op jit(solution)/shard_map/ppermute | solution.py:386
  33.9 3.9 %collective-permute-start.8 = (f32[48,128]{1,0:T(8,128)S(1)}, f32[48,128]{1,0:T(8,128)S(1)}, u32[]{:S(2)}, u32[]{:S(2)}) collective-permute-start(f32[48,128]{1,0:T(8,128)S(1)} %get-tuple-element.50), channel_id=1, source_target_pairs={{0,16},{1,17},{2,18},{3,19},{4,20},{5,21},{6,22},{7,23},{8,24},{9,... | collective-permute-start | bytes 73736 | tf_op jit(solution)/shard_map/ppermute | solution.py:386

commit v7 on v6

--- a/solution.py
+++ b/solution.py
@@ -68,14 +68,14 @@
 
 
 def first(count, occ, virt, tiles_hbm, coulomb, *refs):
-    outs, (tiles, gs, part, sem, done) = refs[:5], refs[5:]
+    outs, (tiles, gs, part, sem, done) = refs[:4], refs[4:]
     d = lax.axis_index("row")
     funcs = part.shape[0]
     half = lax.rem(lax.axis_index("grp"), 2)
     list_copy = pltpu.make_async_copy(tiles_hbm, tiles, sem.at[16])
     list_copy.start()
     groups = []
-    for n, by in enumerate((0, 1, -1, 2)):
+    for n, by in enumerate((0, 1, -1)):
         start = column_chunk(near(d, by, count), count)
         copies = []
         for c in range(2):
@@ -90,7 +90,7 @@
     for n in range(3):
         piece = pl.ds(half * funcs + n * 8, 8)
         copy = pltpu.make_async_copy(coulomb.at[0, piece], part.at[n * 8 : n * 8 + 8], sem.at[17 + n])
-        out = pltpu.make_async_copy(part.at[n * 8 : n * 8 + 8], outs[4].at[n * 8 : n * 8 + 8], done.at[4 + n])
+        out = pltpu.make_async_copy(part.at[n * 8 : n * 8 + 8], outs[3].at[n * 8 : n * 8 + 8], done.at[4 + n])
         groups.append(([copy], out))
     for copies, _ in groups:
         for copy in copies:
@@ -137,12 +137,11 @@
         flat[:, m * 128 : (m + 1) * 128] = rows.astype(BF)
 
 
-def choose(count, win, g_self, g_before, g_after, g_far, out):
+def choose(count, win, g_self, g_before, g_after, out):
     d = lax.axis_index("row")
     atoms = 2 * count
     mine = window_at(win, d)
-    theirs = window_at(win, near(d, -1, count))
-    row0 = near(d, -2, count) * 2
+    row0 = near(d, -1, count) * 2
     col0 = column_chunk(d, count) * 4
 
     def position(atom, start):
@@ -152,33 +151,16 @@
         blocks = []
         for c in range(2):
             at = base + 64 * c
-            blocks.append(
-                jnp.concatenate(
-                    [
-                        g_far[at : at + 64, :],
-                        g_before[at : at + 64, :],
-                        g_self[at : at + 64, :],
-                        g_after[at : at + 64, :],
-                    ],
-                    axis=0,
-                )
-            )
+            parts = [g[at : at + 64, :] for g in (g_before, g_self, g_after, g_after)]
+            blocks.append(jnp.concatenate(parts, axis=0))
         return jnp.concatenate(blocks, axis=1)
 
-    occ, virt = whole(0), whole(128)
-    rows_mine = [position(a, row0) for a in mine]
-    rows_theirs = [position(a, row0) for a in theirs]
-    columns_mine = [position(a, col0) for a in mine]
-    columns_both = []
-    for i in range(4):
-        _, there = find(theirs, mine[i])
-        columns_both.append(jnp.where(there > 0, columns_mine[i], jnp.int32(MISSING)))
-    for base, rows, columns in ((0, rows_mine, columns_mine), (256, rows_theirs, columns_both)):
-        left = one_hot((128, 256), 0, columns)
-        x = dot_t(left, occ).astype(BF)
-        out[base : base + 128, :] = dot(x, one_hot((256, 128), 1, rows)).astype(BF)
-        y = dot(one_hot((128, 256), 0, rows), virt).astype(BF)
-        out[base + 128 : base + 256, :] = dot(y, one_hot((256, 128), 1, columns)).astype(BF)
+    rows = [position(a, row0) for a in mine]
+    columns = [position(a, col0) for a in mine]
+    x = dot_t(one_hot((128, 256), 0, columns), whole(0)).astype(BF)
+    out[0:128, :] = dot(x, one_hot((256, 128), 1, rows)).astype(BF)
+    y = dot(one_hot((128, 256), 0, rows), whole(128)).astype(BF)
+    out[128:256, :] = dot(y, one_hot((256, 128), 1, columns)).astype(BF)
 
 
 def frame_map(atoms_from, wanted):
@@ -266,13 +248,21 @@
     ).astype(BF)
 
 
-def join_back(tensor, g_before, g0, g1, flat, up, hs0, hs1, backs):
+def join_back(count, win, tensor, g_before, before, flat, up, hs0, hs1, backs):
+    d = lax.axis_index("row")
+    mine = window_at(win, d)
+    theirs = window_at(win, near(d, -1, count))
+    bases = []
+    for a in mine:
+        slot, there = find(theirs, a)
+        bases.append(jnp.where(there > 0, slot * 32, jnp.int32(MISSING)))
+    rows, columns = one_hot((128, 128), 0, bases), one_hot((128, 128), 1, bases)
     funcs = tensor.shape[0]
     full = 2 * funcs
     mask = neighbour_mask(g_before)
-    occ = jnp.concatenate([g0[256:384, :], g1[256:384, :]], axis=0)
+    occ = jnp.concatenate([dot(rows, before[at : at + 128, :]).astype(BF) for at in (0, 256)], axis=0)
     halves(occ, [functools.partial(lambda r: tensor[r] * mask, r) for r in range(funcs)], [hs0, hs1])
-    virts = [g0[384:512, :], g1[384:512, :]]
+    virts = [dot(before[at : at + 128, :], columns).astype(BF) for at in (128, 384)]
     for i in range(16):
         xs = []
         for hs, virt in zip((hs0, hs1), virts):
@@ -386,7 +376,7 @@
         return lax.ppermute(array, ("grp", "row"), pairs)
 
     far_rows = funcs * 32
-    g_self, g_right, g_left, g_far, tensor = call(
+    g_self, g_right, g_left, tensor = call(
         functools.partial(first, count),
         "first",
         hbm(4),
@@ -394,13 +384,12 @@
             shape((256, 128), BF),
             shape((272, 128), BF),
             shape((256, 128), BF),
-            shape((256, 128), BF),
             shape((funcs, 128, 128), BF),
         ],
         (green_occ, green_virt, tile_list, coulomb3c),
         [
             pltpu.SMEM((1, 4, 4), jnp.int32),
-            pltpu.VMEM((4, 272, 128), BF),
+            pltpu.VMEM((3, 272, 128), BF),
             pltpu.VMEM((funcs, 128, 128), BF),
             pltpu.SemaphoreType.DMA((20,)),
             pltpu.SemaphoreType.DMA((7,)),
@@ -410,7 +399,6 @@
     )
     g_before = send(g_right, 1)
     g_after = send(g_left, -1)
-    g_beyond = send(g_far, 2)
     wide = send(tensor, 1)
     flat_shape, far_shape = shape((full, 128 * 128), BF), shape((full, 64 * 128), BF)
     tall = pltpu.VMEM((full * PITCH, 128), F32)
@@ -425,15 +413,13 @@
         [pltpu.VMEM((128, 128), BF), tall],
         flops=1 << 36,
     )
-    g_before, g_after, g_beyond, far_right, far_left = lax.optimization_barrier(
-        (g_before, g_after, g_beyond, far_right, far_left)
-    )
+    g_before, g_after, far_right, far_left = lax.optimization_barrier((g_before, g_after, far_right, far_left))
     (mine,) = call(
         functools.partial(choose, count),
         "choose",
-        smem(1) + vmem(4),
-        [shape((512, 128), BF)],
-        (window, g_self, g_before, g_after, g_beyond),
+        smem(1) + vmem(3),
+        [shape((256, 128), BF)],
+        (window, g_self, g_before, g_after),
     )
     partner = send(mine, 0, True)
     polar0, dressed0, far0 = call(
@@ -444,7 +430,8 @@
         (window, tile_list, coulomb3c, mine, flat),
         [tall, pltpu.VMEM((full, 128 * 128), BF)],
     )
-    far_right, far_left, polar0 = lax.optimization_barrier((far_right, far_left, polar0))
+    far_right, far_left, polar0, partner = lax.optimization_barrier((far_right, far_left, polar0, partner))
+    before = send(jnp.concatenate([mine, partner], axis=0), 1)
     from_left = send(far_right, 2)
     from_right = send(far_left, -2)
     dressed1, far1 = call(
@@ -456,11 +443,11 @@
         [tall],
     )
     (up,) = call(
-        join_back,
+        functools.partial(join_back, count),
         "join_back",
-        vmem(5),
+        smem(1) + vmem(4),
         [message],
-        (wide, g_before, mine, partner, flat),
+        (window, wide, g_before, before, flat),
         [short, short, pltpu.VMEM((full, 128 * 128), BF)],
     )
     after = send(up, -1)

time: 38.6 us -> 39.4 us (1.021)
  starting transfers between devices: 12.4 us -> 14.1 us
  waiting for transfers between devices: 8.99 us -> 7.52 us
  Pallas kernels: 16.8 us -> 17.4 us
    ppermute x9, starting transfers between devices: 12.4 us -> 14.1 us  [send(): return lax.ppermute(array, ('grp', 'row'), pairs)]
    ppermute x9, waiting for transfers between devices: 8.99 us -> 7.52 us  [send(): return lax.ppermute(array, ('grp', 'row'), pairs)]
    pallas_call x9, Pallas kernels: 16.8 us -> 17.4 us  [call(): pl.pallas_call(kernel, name=name, in_specs=specs, out_specs=tuple((space...]
  transfers between devices with their start and end apart: 9 -> 9, of which waited for: 3 -> 5; matrix products, arithmetic and copies ran while one was open for 0% -> 0% of each run, Pallas kernels for 34% -> 35%
where the time goes in v7:
time: 39.4 us; the launch traced here: 39.3 us
  Pallas kernels  17.4 us (44%)
  starting transfers between devices  14.1 us (36%)
  waiting for transfers between devices  7.52 us (19%)
    pallas_call x9, Pallas kernels, call(): pl.pallas_call(kernel, name=name, in_specs=specs, out_specs=tuple((space...  17.4 us
    ppermute x9, starting transfers between devices, send(): return lax.ppermute(array, ('grp', 'row'), pairs)  14.1 us
    ppermute x9, waiting for transfers between devices, send(): return lax.ppermute(array, ('grp', 'row'), pairs)  7.52 us
  transfers between devices with their start and end apart: 9, of which 5 were waited for; matrix products, arithmetic and copies ran while one was open for 0% of the time, Pallas kernels for 35%

profile of v7, /device:TPU:0, one launch (start us, length us, event | category | flops | bytes accessed | tf_op | source)
XLA Modules:
  0.0 39.3 jit_solution(12618731797933057582)
XLA Ops:
  0.0 0.0 copy-start.2
  0.0 0.0 copy-start
  0.0 0.0 copy-start.3
  0.0 2.3 %first.1 = (bf16[256,128]{1,0:T(8,128)(2,1)}, bf16[272,128]{1,0:T(8,128)(2,1)}, bf16[256,128]{1,0:T(8,128)(2,1)}, bf16[24,128,128]{2,1,0:T(8,128)(2,1)}) custom-call(bf16[64,1024]{1,0:T(8,128)(2,1)} %occ.1, bf16[64,1024]{1,0:T(8,128)(2,1)} %virt.1, s32[1,4,4]{2,1,0:T(4,128)} %tiles.5, bf16[1,48,128,128]{3,2,1,0:T(8,128)(2,1)} %tensor.5), custom_call_target="tpu_custom_call" | custom-call | tf_op jit(solution)/shard_map/first/pallas_call | solution.py:353
  2.4 5.5 %collective-permute-start.1 = (bf16[256,128]{1,0:T(8,128)(2,1)}, bf16[256,128]{1,0:T(8,128)(2,1)S(1)}, u32[]{:S(2)}, u32[]{:S(2)}) collective-permute-start(bf16[256,128]{1,0:T(8,128)(2,1)} %get-tuple-element.28), channel_id=1, source_target_pairs={{0,15},{1,0},{2,1},{3,2},{4,3},{5,4},{6,5},{7,6},{8,7},{9,8},{10,9... | collective-permute-start | bytes 196616 | tf_op jit(solution)/shard_map/ppermute | solution.py:376
  7.9 0.0 collective-permute-start
  7.9 0.0 collective-permute-start.5
  7.9 0.0 copy-done.3
  7.9 0.1 copy.6.win
  8.0 0.0 copy-done.2
  8.0 0.0 copy-done
  8.0 0.0 copy-start.1
  8.0 2.0 %far_tiles.1 = (bf16[768,128]{1,0:T(8,128)(2,1)S(1)}, bf16[768,128]{1,0:T(8,128)(2,1)S(1)}, bf16[48,16384]{1,0:T(8,128)(2,1)S(1)}) custom-call(s32[16,4]{1,0:T(8,128)S(1)} %copy.6.win, s32[1,4,4]{2,1,0:T(4,128)S(1)} %copy-done.2, bf16[1,48,128,128]{3,2,1,0:T(8,128)(2,1)S(1)} %copy-done), custom_call_target="tpu_custom_call" | custom-call | flops 68719476736 | tf_op jit(solution)/shard_map/far_tiles/pallas_call | solution.py:353
  9.9 0.1 collective-permute-done.1.g_after
  10.1 4.4 %collective-permute-done.g_before = bf16[272,128]{1,0:T(8,128)(2,1)S(1)} collective-permute-done((bf16[272,128]{1,0:T(8,128)(2,1)}, bf16[272,128]{1,0:T(8,128)(2,1)S(1)}, u32[]{:S(2)}, u32[]{:S(2)}) %collective-permute-start) | collective-permute-done | bytes 69664 | tf_op jit(solution)/shard_map/ppermute | solution.py:376
  14.5 0.0 copy-done.1
  14.5 1.1 %choose.1.greens = bf16[256,128]{1,0:T(8,128)(2,1)S(1)} custom-call(s32[16,4]{1,0:T(8,128)S(1)} %copy.6.win, bf16[256,128]{1,0:T(8,128)(2,1)S(1)} %copy-done.1, bf16[272,128]{1,0:T(8,128)(2,1)S(1)} %collective-permute-done.g_before, bf16[256,128]{1,0:T(8,128)(2,1)S(1)} %collective-permute-done.1.g_after), custom_call_target="tpu_custom_call" | custom-call | tf_op jit(solution)/shard_map/choose/pallas_call | solution.py:353
  15.7 1.6 %collective-permute-start.2 = (bf16[256,128]{1,0:T(8,128)(2,1)S(1)}, bf16[256,128]{1,0:T(8,128)(2,1)S(1)}, u32[]{:S(2)}, u32[]{:S(2)}) collective-permute-start(bf16[256,128]{1,0:T(8,128)(2,1)S(1)} %choose.1.greens), channel_id=1, source_target_pairs={{0,16},{1,17},{2,18},{3,19},{4,20},{5,21},{6,22},{7,23},{8,24},{9,... | collective-permute-start | bytes 196616 | tf_op jit(solution)/shard_map/ppermute | solution.py:376
  17.2 3.2 %dress_own.1 = (f32[48,48]{1,0:T(8,128)S(1)}, bf16[48,16384]{1,0:T(8,128)(2,1)S(1)}, bf16[48,8192]{1,0:T(8,128)(2,1)S(1)}) custom-call(s32[16,4]{1,0:T(8,128)S(1)} %copy.6.win, s32[1,4,4]{2,1,0:T(4,128)S(1)} %copy-done.2, bf16[1,48,128,128]{3,2,1,0:T(8,128)(2,1)S(1)} %copy-done, bf16[256,128]{1,0:T(8,128)(2,1)S(1)} %choose.1.greens, ...), custom_call_target="tpu_custom_call" | custom-call | tf_op jit(solution)/shard_map/dress_own/pallas_call | solution.py:353
  20.4 0.0 collective-permute-done.2.greens
  20.5 0.1 collective-permute-start.6
  20.5 2.3 %dress_partner.1 = (bf16[48,16384]{1,0:T(8,128)(2,1)S(1)}, bf16[48,8192]{1,0:T(8,128)(2,1)S(1)}) custom-call(s32[16,4]{1,0:T(8,128)S(1)} %copy.6.win, s32[1,4,4]{2,1,0:T(4,128)S(1)} %copy-done.2, bf16[1,48,128,128]{3,2,1,0:T(8,128)(2,1)S(1)} %copy-done, bf16[256,128]{1,0:T(8,128)(2,1)S(1)} %collective-permute-done.2.greens), custom_call_target="tpu_custom_call" | custom-call | tf_op jit(solution)/shard_map/dress_partner/pallas_call | solution.py:353
  22.9 0.1 collective-permute-start.3
  22.9 4.7 %collective-permute-start.4 = (bf16[768,128]{1,0:T(8,128)(2,1)S(1)}, bf16[768,128]{1,0:T(8,128)(2,1)S(1)}, u32[]{:S(2)}, u32[]{:S(2)}) collective-permute-start(bf16[768,128]{1,0:T(8,128)(2,1)S(1)} %get-tuple-element.43), channel_id=1, source_target_pairs={{0,14},{1,15},{2,0},{3,1},{4,2},{5,3},{6,4},{7,5},{8,6},{9,7},{10,... | collective-permute-start | bytes 589832 | tf_op jit(solution)/shard_map/ppermute | solution.py:376
  27.6 0.1 collective-permute-done.6.before
  27.7 0.0 collective-permute-done.5.tensor
  27.7 3.1 %join_back.1 = f32[48,128]{1,0:T(8,128)S(1)} custom-call(s32[16,4]{1,0:T(8,128)S(1)} %copy.6.win, bf16[24,128,128]{2,1,0:T(8,128)(2,1)S(1)} %collective-permute-done.5.tensor, bf16[272,128]{1,0:T(8,128)(2,1)S(1)} %collective-permute-done.g_before, bf16[512,128]{1,0:T(8,128)(2,1)S(1)} %collective-permute-done.6.before, ...), custom_call_target="tpu_custom_call" | custom-call | tf_op jit(solution)/shard_map/join_back/pallas_call | solution.py:353
  30.9 1.1 %collective-permute-start.7 = (f32[48,128]{1,0:T(8,128)S(1)}, f32[48,128]{1,0:T(8,128)S(1)}, u32[]{:S(2)}, u32[]{:S(2)}) collective-permute-start(f32[48,128]{1,0:T(8,128)S(1)} %join_back.1), channel_id=1, source_target_pairs={{0,15},{1,0},{2,1},{3,2},{4,3},{5,4},{6,5},{7,6},{8,7},{9,8},{10,9... | collective-permute-start | bytes 73736 | tf_op jit(solution)/shard_map/ppermute | solution.py:376
  32.0 1.9 %join.1.down = f32[96,128]{1,0:T(8,128)S(1)} custom-call(s32[16,4]{1,0:T(8,128)S(1)} %copy.6.win, bf16[24,128,128]{2,1,0:T(8,128)(2,1)S(1)} %collective-permute-done.5.tensor, bf16[272,128]{1,0:T(8,128)(2,1)S(1)} %collective-permute-done.g_before, bf16[48,16384]{1,0:T(8,128)(2,1)S(1)} %get-tuple-element.45.dressed0, ...), custom_call_target="tpu_custom_call" | custom-call | flops 17179869184 | tf_op jit(solution)/shard_map/join/pallas_call | solution.py:353
  33.9 0.0 collective-permute-done.3.from_left
  33.9 0.1 collective-permute-done.4.from_right
  33.9 0.0 collective-permute-done.7.after
  33.9 0.7 %join_far.1 = (f32[48,128]{1,0:T(8,128)S(1)}, f32[48,128]{1,0:T(8,128)S(1)}) custom-call(bf16[48,8192]{1,0:T(8,128)(2,1)S(1)} %get-tuple-element.39.far0, bf16[48,8192]{1,0:T(8,128)(2,1)S(1)} %get-tuple-element.41.far1, bf16[768,128]{1,0:T(8,128)(2,1)S(1)} %collective-permute-done.3.from_left, bf16[768,128]{1,0:T(8,128)(2,1)S(1)} %collective-permute-done.4.from_right, ...), custom_call_target="tpu_custom_call" | custom-call | tf_op jit(solution)/shard_map/join_far/pallas_call | solution.py:353
  34.6 1.1 %collective-permute-start.8 = (f32[48,128]{1,0:T(8,128)S(1)}, f32[48,128]{1,0:T(8,128)S(1)}, u32[]{:S(2)}, u32[]{:S(2)}) collective-permute-start(f32[48,128]{1,0:T(8,128)S(1)} %get-tuple-element.48), channel_id=1, source_target_pairs={{0,16},{1,17},{2,18},{3,19},{4,20},{5,21},{6,22},{7,23},{8,24},{9,... | collective-permute-start | bytes 73736 | tf_op jit(solution)/shard_map/ppermute | solution.py:376
  35.7 2.8 %collective-permute-done.8.recv = f32[48,128]{1,0:T(8,128)S(1)} collective-permute-done((f32[48,128]{1,0:T(8,128)S(1)}, f32[48,128]{1,0:T(8,128)S(1)}, u32[]{:S(2)}, u32[]{:S(2)}) %collective-permute-start.8) | collective-permute-done | bytes 24608 | tf_op jit(solution)/shard_map/ppermute | solution.py:376
  38.5 0.7 %assemble.1 = f32[48,240]{1,0:T(8,128)} custom-call(f32[48,48]{1,0:T(8,128)S(1)} %get-tuple-element.38.polar0, f32[48,128]{1,0:T(8,128)S(1)} %get-tuple-element.47.own, f32[48,128]{1,0:T(8,128)S(1)} %collective-permute-done.8.recv), custom_call_target="tpu_custom_call" | custom-call | tf_op jit(solution)/shard_map/assemble/pallas_call | solution.py:353
  (1 shorter events, 0.0 us)
Async XLA Ops:
  0.0 8.0 %copy-start.2 = (s32[1,4,4]{2,1,0:T(4,128)S(1)}, s32[1,4,4]{2,1,0:T(4,128)}, u32[]{:S(2)}) copy-start(s32[1,4,4]{2,1,0:T(4,128)} %tiles.5) | copy-start | bytes 196
  0.0 8.0 %copy-start = (bf16[1,48,128,128]{3,2,1,0:T(8,128)(2,1)S(1)}, bf16[1,48,128,128]{3,2,1,0:T(8,128)(2,1)}, u32[]{:S(2)}) copy-start(bf16[1,48,128,128]{3,2,1,0:T(8,128)(2,1)} %tensor.5) | copy-start | bytes 4718596
  0.0 7.9 %copy-start.3 = (s32[16,4]{0,1:T(4,128)S(1)}, s32[16,4]{0,1:T(4,128)}, u32[]{:S(2)}) copy-start(s32[16,4]{0,1:T(4,128)} %param.9) | copy-start | bytes 772
  2.4 7.7 %collective-permute-start.1 = (bf16[256,128]{1,0:T(8,128)(2,1)}, bf16[256,128]{1,0:T(8,128)(2,1)S(1)}, u32[]{:S(2)}, u32[]{:S(2)}) collective-permute-start(bf16[256,128]{1,0:T(8,128)(2,1)} %get-tuple-element.28), channel_id=1, source_target_pairs={{0,15},{1,0},{2,1},{3,2},{4,3},{5,4},{6,5},{7,6},{8,7},{9,8},{10,9... | collective-permute-start | bytes 196616 | tf_op jit(solution)/shard_map/ppermute | solution.py:376
  7.9 6.6 %collective-permute-start = (bf16[272,128]{1,0:T(8,128)(2,1)}, bf16[272,128]{1,0:T(8,128)(2,1)S(1)}, u32[]{:S(2)}, u32[]{:S(2)}) collective-permute-start(bf16[272,128]{1,0:T(8,128)(2,1)} %get-tuple-element.27), channel_id=1, source_target_pairs={{0,1},{1,2},{2,3},{3,4},{4,5},{5,6},{6,7},{7,8},{8,9},{9,10},{10,1... | collective-permute-start | bytes 208904 | tf_op jit(solution)/shard_map/ppermute | solution.py:376
  7.9 19.8 %collective-permute-start.5 = (bf16[24,128,128]{2,1,0:T(8,128)(2,1)}, bf16[24,128,128]{2,1,0:T(8,128)(2,1)S(1)}, u32[]{:S(2)}, u32[]{:S(2)}) collective-permute-start(bf16[24,128,128]{2,1,0:T(8,128)(2,1)} %get-tuple-element.44), channel_id=1, source_target_pairs={{0,1},{1,2},{2,3},{3,4},{4,5},{5,6},{6,7},{7,8},{8,9},{9,10},{10,1... | collective-permute-start | bytes 2359304 | tf_op jit(solution)/shard_map/ppermute | solution.py:376
  8.0 6.5 %copy-start.1 = (bf16[256,128]{1,0:T(8,128)(2,1)S(1)}, bf16[256,128]{1,0:T(8,128)(2,1)}, u32[]{:S(2)}) copy-start(bf16[256,128]{1,0:T(8,128)(2,1)} %get-tuple-element.33.g_self) | copy-start | bytes 196612
  15.7 4.8 %collective-permute-start.2 = (bf16[256,128]{1,0:T(8,128)(2,1)S(1)}, bf16[256,128]{1,0:T(8,128)(2,1)S(1)}, u32[]{:S(2)}, u32[]{:S(2)}) collective-permute-start(bf16[256,128]{1,0:T(8,128)(2,1)S(1)} %choose.1.greens), channel_id=1, source_target_pairs={{0,16},{1,17},{2,18},{3,19},{4,20},{5,21},{6,22},{7,23},{8,24},{9,... | collective-permute-start | bytes 196616 | tf_op jit(solution)/shard_map/ppermute | solution.py:376
  20.5 7.2 %collective-permute-start.6 = (bf16[512,128]{1,0:T(8,128)(2,1)S(1)}, bf16[512,128]{1,0:T(8,128)(2,1)S(1)}, u32[]{:S(2)}, u32[]{:S(2)}) collective-permute-start(bf16[512,128]{1,0:T(8,128)(2,1)S(1)} %pad_maximum_fusion), channel_id=1, source_target_pairs={{0,1},{1,2},{2,3},{3,4},{4,5},{5,6},{6,7},{7,8},{8,9},{9,10},{10,1... | collective-permute-start | bytes 393224 | tf_op jit(solution)/shard_map/ppermute | solution.py:376
  22.9 11.0 %collective-permute-start.3 = (bf16[768,128]{1,0:T(8,128)(2,1)S(1)}, bf16[768,128]{1,0:T(8,128)(2,1)S(1)}, u32[]{:S(2)}, u32[]{:S(2)}) collective-permute-start(bf16[768,128]{1,0:T(8,128)(2,1)S(1)} %get-tuple-element.42), channel_id=1, source_target_pairs={{0,2},{1,3},{2,4},{3,5},{4,6},{5,7},{6,8},{7,9},{8,10},{9,11},{10,... | collective-permute-start | bytes 589832 | tf_op jit(solution)/shard_map/ppermute | solution.py:376
  22.9 11.0 %collective-permute-start.4 = (bf16[768,128]{1,0:T(8,128)(2,1)S(1)}, bf16[768,128]{1,0:T(8,128)(2,1)S(1)}, u32[]{:S(2)}, u32[]{:S(2)}) collective-permute-start(bf16[768,128]{1,0:T(8,128)(2,1)S(1)} %get-tuple-element.43), channel_id=1, source_target_pairs={{0,14},{1,15},{2,0},{3,1},{4,2},{5,3},{6,4},{7,5},{8,6},{9,7},{10,... | collective-permute-start | bytes 589832 | tf_op jit(solution)/shard_map/ppermute | solution.py:376
  30.9 3.1 %collective-permute-start.7 = (f32[48,128]{1,0:T(8,128)S(1)}, f32[48,128]{1,0:T(8,128)S(1)}, u32[]{:S(2)}, u32[]{:S(2)}) collective-permute-start(f32[48,128]{1,0:T(8,128)S(1)} %join_back.1), channel_id=1, source_target_pairs={{0,15},{1,0},{2,1},{3,2},{4,3},{5,4},{6,5},{7,6},{8,7},{9,8},{10,9... | collective-permute-start | bytes 73736 | tf_op jit(solution)/shard_map/ppermute | solution.py:376
  34.6 3.9 %collective-permute-start.8 = (f32[48,128]{1,0:T(8,128)S(1)}, f32[48,128]{1,0:T(8,128)S(1)}, u32[]{:S(2)}, u32[]{:S(2)}) collective-permute-start(f32[48,128]{1,0:T(8,128)S(1)} %get-tuple-element.48), channel_id=1, source_target_pairs={{0,16},{1,17},{2,18},{3,19},{4,20},{5,21},{6,22},{7,23},{8,24},{9,... | collective-permute-start | bytes 73736 | tf_op jit(solution)/shard_map/ppermute | solution.py:376

commit v8 on v6

--- a/solution.py
+++ b/solution.py
@@ -96,13 +96,19 @@
         for copy in copies:
             copy.start()
     list_copy.wait()
-    gs[1, 256:272, :] = tile_mask(tiles, 4).astype(BF)
+    short = tile_mask(tiles, 4).astype(BF)
+    gs[1, 256:272, :] = short
+    gs[3, 256:272, :] = short
     for copies, out in groups:
         for copy in copies:
             copy.wait()
         out.start()
     for _, out in groups:
         out.wait()
+
+
+def keep(array, out):
+    pass
 
 
 def far_tiles(count, win, tiles, tensor, far_right, far_left, flat, mask, ms):
@@ -359,7 +365,7 @@
     return [pl.BlockSpec(memory_space=pltpu.SMEM)] * count
 
 
-def call(kernel, name, specs, outs, args, scratch=(), flops=0, limit=40 << 20, space=None):
+def call(kernel, name, specs, outs, args, scratch=(), flops=0, limit=40 << 20, space=None, aliases={}):
     return pl.pallas_call(
         kernel,
         name=name,
@@ -367,6 +373,7 @@
         out_specs=tuple((space or vmem)(len(outs))),
         out_shape=tuple(outs),
         scratch_shapes=list(scratch),
+        input_output_aliases=aliases,
         compiler_params=pltpu.CompilerParams(vmem_limit_bytes=limit),
         cost_estimate=pl.CostEstimate(flops=flops, bytes_accessed=0, transcendentals=0),
     )(*args)
@@ -394,7 +401,7 @@
             shape((256, 128), BF),
             shape((272, 128), BF),
             shape((256, 128), BF),
-            shape((256, 128), BF),
+            shape((272, 128), BF),
             shape((funcs, 128, 128), BF),
         ],
         (green_occ, green_virt, tile_list, coulomb3c),
@@ -409,9 +416,19 @@
         space=hbm,
     )
     g_before = send(g_right, 1)
-    g_after = send(g_left, -1)
     g_beyond = send(g_far, 2)
     wide = send(tensor, 1)
+    (g_left,) = call(
+        keep,
+        "keep",
+        [pl.BlockSpec(memory_space=pl.ANY)],
+        [shape((256, 128), BF)],
+        (g_left,),
+        flops=1 << 36,
+        space=lambda n: [pl.BlockSpec(memory_space=pl.ANY)] * n,
+        aliases={0: 0},
+    )
+    g_after = send(g_left, -1)
     flat_shape, far_shape = shape((full, 128 * 128), BF), shape((full, 64 * 128), BF)
     tall = pltpu.VMEM((full * PITCH, 128), F32)
     short = pltpu.VMEM((funcs * PITCH, 128), F32)
@@ -423,7 +440,6 @@
         [shape((far_rows, 128), BF), shape((far_rows, 128), BF), flat_shape],
         (window, tile_list, coulomb3c),
         [pltpu.VMEM((128, 128), BF), tall],
-        flops=1 << 36,
     )
     g_before, g_after, g_beyond, far_right, far_left = lax.optimization_barrier(
         (g_before, g_after, g_beyond, far_right, far_left)
@@ -436,6 +452,9 @@
         (window, g_self, g_before, g_after, g_beyond),
     )
     partner = send(mine, 0, True)
+    far_right, far_left, mine = lax.optimization_barrier((far_right, far_left, mine))
+    from_left = send(far_right, 2)
+    from_right = send(far_left, -2)
     polar0, dressed0, far0 = call(
         functools.partial(dress, count, True),
         "dress_own",
@@ -444,9 +463,6 @@
         (window, tile_list, coulomb3c, mine, flat),
         [tall, pltpu.VMEM((full, 128 * 128), BF)],
     )
-    far_right, far_left, polar0 = lax.optimization_barrier((far_right, far_left, polar0))
-    from_left = send(far_right, 2)
-    from_right = send(far_left, -2)
     dressed1, far1 = call(
         functools.partial(dress, count, False),
         "dress_partner",

time: 38.6 us -> 42.9 us (1.11)
  starting transfers between devices: 12.4 us -> 22.1 us
  waiting for transfers between devices: 8.99 us -> 3.63 us
    ppermute x9, starting transfers between devices: 12.4 us -> 22.1 us  [send(): return lax.ppermute(array, ('grp', 'row'), pairs)]
    ppermute x9, waiting for transfers between devices: 8.99 us -> 3.63 us  [send(): return lax.ppermute(array, ('grp', 'row'), pairs)]
    pallas_call x9 -> x10, Pallas kernels: 16.8 us -> 16.8 us  [call(): pl.pallas_call(kernel, name=name, in_specs=specs, out_specs=tuple((space...]
  transfers between devices with their start and end apart: 9 -> 9, of which waited for: 3 -> 2; matrix products, arithmetic and copies ran while one was open for 0% -> 0% of each run, Pallas kernels for 34% -> 31%
where the time goes in v8:
time: 42.9 us; the launch traced here: 42.7 us
  starting transfers between devices  22.1 us (52%)
  Pallas kernels  16.8 us (39%)
  waiting for transfers between devices  3.63 us (8%)
    ppermute x9, starting transfers between devices, send(): return lax.ppermute(array, ('grp', 'row'), pairs)  22.1 us
    pallas_call x10, Pallas kernels, call(): pl.pallas_call(kernel, name=name, in_specs=specs, out_specs=tuple((space...  16.8 us
    ppermute x9, waiting for transfers between devices, send(): return lax.ppermute(array, ('grp', 'row'), pairs)  3.63 us
  transfers between devices with their start and end apart: 9, of which 2 were waited for; matrix products, arithmetic and copies ran while one was open for 0% of the time, Pallas kernels for 31%

profile of v8, /device:TPU:0, one launch (start us, length us, event | category | flops | bytes accessed | tf_op | source)
XLA Modules:
  0.0 42.7 jit_solution(2908369638803766964)
XLA Ops:
  0.0 2.3 %first.1 = (bf16[256,128]{1,0:T(8,128)(2,1)}, bf16[272,128]{1,0:T(8,128)(2,1)}, bf16[256,128]{1,0:T(8,128)(2,1)}, bf16[272,128]{1,0:T(8,128)(2,1)}, bf16[24,128,128]{2,1,0:T(8,128)(2,1)}) custom-call(bf16[64,1024]{1,0:T(8,128)(2,1)} %occ.1, bf16[64,1024]{1,0:T(8,128)(2,1)} %virt.1, s32[1,4,4]{2,1,0:T(4,128)} %tiles.5, bf16[1,48,128,128]{3,2,1,0:T(8,128)(2,1)} %tensor.5), custom_call_target="tpu_custom_call" | custom-call | tf_op jit(solution)/shard_map/first/pallas_call | solution.py:369
  2.3 0.5 %collective-permute-start = (bf16[272,128]{1,0:T(8,128)(2,1)}, bf16[272,128]{1,0:T(8,128)(2,1)S(1)}, u32[]{:S(2)}, u32[]{:S(2)}) collective-permute-start(bf16[272,128]{1,0:T(8,128)(2,1)} %get-tuple-element.28), channel_id=1, source_target_pairs={{0,1},{1,2},{2,3},{3,4},{4,5},{5,6},{6,7},{7,8},{8,9},{9,10},{10,1... | collective-permute-start | bytes 208904 | tf_op jit(solution)/shard_map/ppermute | solution.py:393
  2.8 2.6 %collective-permute-start.2 = (bf16[272,128]{1,0:T(8,128)(2,1)}, bf16[272,128]{1,0:T(8,128)(2,1)S(1)}, u32[]{:S(2)}, u32[]{:S(2)}) collective-permute-start(bf16[272,128]{1,0:T(8,128)(2,1)} %get-tuple-element.30), channel_id=1, source_target_pairs={{0,2},{1,3},{2,4},{3,5},{4,6},{5,7},{6,8},{7,9},{8,10},{9,11},{10,... | collective-permute-start | bytes 208904 | tf_op jit(solution)/shard_map/ppermute | solution.py:393
  5.4 1.3 %collective-permute-start.6 = (bf16[24,128,128]{2,1,0:T(8,128)(2,1)}, bf16[24,128,128]{2,1,0:T(8,128)(2,1)S(1)}, u32[]{:S(2)}, u32[]{:S(2)}) collective-permute-start(bf16[24,128,128]{2,1,0:T(8,128)(2,1)} %get-tuple-element.46), channel_id=1, source_target_pairs={{0,1},{1,2},{2,3},{3,4},{4,5},{5,6},{6,7},{7,8},{8,9},{9,10},{10,1... | collective-permute-start | bytes 2359304 | tf_op jit(solution)/shard_map/ppermute | solution.py:393
  6.6 0.0 copy-start.3
  6.7 0.0 copy-start
  6.7 0.0 copy-start.2
  6.7 0.0 copy-start.1
  6.7 3.2 %collective-permute-start.1 = (bf16[256,128]{1,0:T(8,128)(2,1)}, bf16[256,128]{1,0:T(8,128)(2,1)S(1)}, u32[]{:S(2)}, u32[]{:S(2)}) collective-permute-start(bf16[256,128]{1,0:T(8,128)(2,1)} %keep.1), channel_id=1, source_target_pairs={{0,15},{1,0},{2,1},{3,2},{4,3},{5,4},{6,5},{7,6},{8,7},{9,8},{10,9... | collective-permute-start | bytes 196616 | tf_op jit(solution)/shard_map/ppermute | solution.py:393
  9.9 0.0 copy-done.3
  9.9 0.1 copy.9.win
  10.0 0.0 copy-done
  10.0 0.0 copy-done.2
  10.0 2.0 %far_tiles.1 = (bf16[768,128]{1,0:T(8,128)(2,1)S(1)}, bf16[768,128]{1,0:T(8,128)(2,1)S(1)}, bf16[48,16384]{1,0:T(8,128)(2,1)S(1)}) custom-call(s32[16,4]{1,0:T(8,128)S(1)} %copy.9.win, s32[1,4,4]{2,1,0:T(4,128)S(1)} %copy-done.2, bf16[1,48,128,128]{3,2,1,0:T(8,128)(2,1)S(1)} %copy-done), custom_call_target="tpu_custom_call" | custom-call | tf_op jit(solution)/shard_map/far_tiles/pallas_call | solution.py:369
  12.0 0.1 collective-permute-done.1.g_after
  12.1 0.0 collective-permute-done.g_before
  12.1 0.0 collective-permute-done.2.g_far
  12.1 0.0 copy-done.1
  12.1 1.3 %choose.1.greens.g0 = bf16[512,128]{1,0:T(8,128)(2,1)S(1)} custom-call(s32[16,4]{1,0:T(8,128)S(1)} %copy.9.win, bf16[256,128]{1,0:T(8,128)(2,1)S(1)} %copy-done.1, bf16[272,128]{1,0:T(8,128)(2,1)S(1)} %collective-permute-done.g_before, bf16[256,128]{1,0:T(8,128)(2,1)S(1)} %collective-permute-done.1.g_after, bf16[272,128]{1,0:T(8,128)(2,1)S(1)} %collective-permute-done.2.g_far), custom_call_target="tpu_custom_call" | custom-call | tf_op jit(solution)/shard_map/choose/pallas_call | solution.py:369
  13.5 1.6 %collective-permute-start.3 = (bf16[512,128]{1,0:T(8,128)(2,1)S(1)}, bf16[512,128]{1,0:T(8,128)(2,1)S(1)}, u32[]{:S(2)}, u32[]{:S(2)}) collective-permute-start(bf16[512,128]{1,0:T(8,128)(2,1)S(1)} %choose.1.greens.g0), channel_id=1, source_target_pairs={{0,16},{1,17},{2,18},{3,19},{4,20},{5,21},{6,22},{7,23},{8,24},{9,... | collective-permute-start | bytes 393224 | tf_op jit(solution)/shard_map/ppermute | solution.py:393
  15.0 8.6 %collective-permute-start.4 = (bf16[768,128]{1,0:T(8,128)(2,1)S(1)}, bf16[768,128]{1,0:T(8,128)(2,1)S(1)}, u32[]{:S(2)}, u32[]{:S(2)}) collective-permute-start(bf16[768,128]{1,0:T(8,128)(2,1)S(1)} %get-tuple-element.44), channel_id=1, source_target_pairs={{0,2},{1,3},{2,4},{3,5},{4,6},{5,7},{6,8},{7,9},{8,10},{9,11},{10,... | collective-permute-start | bytes 589832 | tf_op jit(solution)/shard_map/ppermute | solution.py:393
  23.6 1.2 %collective-permute-start.5 = (bf16[768,128]{1,0:T(8,128)(2,1)S(1)}, bf16[768,128]{1,0:T(8,128)(2,1)S(1)}, u32[]{:S(2)}, u32[]{:S(2)}) collective-permute-start(bf16[768,128]{1,0:T(8,128)(2,1)S(1)} %get-tuple-element.45), channel_id=1, source_target_pairs={{0,14},{1,15},{2,0},{3,1},{4,2},{5,3},{6,4},{7,5},{8,6},{9,7},{10,... | collective-permute-start | bytes 589832 | tf_op jit(solution)/shard_map/ppermute | solution.py:393
  24.9 3.2 %dress_own.1 = (f32[48,48]{1,0:T(8,128)S(1)}, bf16[48,16384]{1,0:T(8,128)(2,1)S(1)}, bf16[48,8192]{1,0:T(8,128)(2,1)S(1)}) custom-call(s32[16,4]{1,0:T(8,128)S(1)} %copy.9.win, s32[1,4,4]{2,1,0:T(4,128)S(1)} %copy-done.2, bf16[1,48,128,128]{3,2,1,0:T(8,128)(2,1)S(1)} %copy-done, bf16[512,128]{1,0:T(8,128)(2,1)S(1)} %choose.1.greens.g0, ...), custom_call_target="tpu_custom_call" | custom-call | tf_op jit(solution)/shard_map/dress_own/pallas_call | solution.py:369
  28.1 0.0 collective-permute-done.3.greens.g1
  28.1 2.3 %dress_partner.1 = (bf16[48,16384]{1,0:T(8,128)(2,1)S(1)}, bf16[48,8192]{1,0:T(8,128)(2,1)S(1)}) custom-call(s32[16,4]{1,0:T(8,128)S(1)} %copy.9.win, s32[1,4,4]{2,1,0:T(4,128)S(1)} %copy-done.2, bf16[1,48,128,128]{3,2,1,0:T(8,128)(2,1)S(1)} %copy-done, bf16[512,128]{1,0:T(8,128)(2,1)S(1)} %collective-permute-done.3.greens.g1), custom_call_target="tpu_custom_call" | custom-call | tf_op jit(solution)/shard_map/dress_partner/pallas_call | solution.py:369
  30.5 0.0 collective-permute-done.6.tensor
  30.5 2.4 %join_back.1 = f32[48,128]{1,0:T(8,128)S(1)} custom-call(bf16[24,128,128]{2,1,0:T(8,128)(2,1)S(1)} %collective-permute-done.6.tensor, bf16[272,128]{1,0:T(8,128)(2,1)S(1)} %collective-permute-done.g_before, bf16[512,128]{1,0:T(8,128)(2,1)S(1)} %choose.1.greens.g0, bf16[512,128]{1,0:T(8,128)(2,1)S(1)} %collective-permute-done.3.greens.g1, ...), custom_call_target="tpu_custom_call" | custom-call | tf_op jit(solution)/shard_map/join_back/pallas_call | solution.py:369
  32.8 2.7 %collective-permute-start.7 = (f32[48,128]{1,0:T(8,128)S(1)}, f32[48,128]{1,0:T(8,128)S(1)}, u32[]{:S(2)}, u32[]{:S(2)}) collective-permute-start(f32[48,128]{1,0:T(8,128)S(1)} %join_back.1), channel_id=1, source_target_pairs={{0,15},{1,0},{2,1},{3,2},{4,3},{5,4},{6,5},{7,6},{8,7},{9,8},{10,9... | collective-permute-start | bytes 73736 | tf_op jit(solution)/shard_map/ppermute | solution.py:393
  35.5 1.8 %join.1.down = f32[96,128]{1,0:T(8,128)S(1)} custom-call(s32[16,4]{1,0:T(8,128)S(1)} %copy.9.win, bf16[24,128,128]{2,1,0:T(8,128)(2,1)S(1)} %collective-permute-done.6.tensor, bf16[272,128]{1,0:T(8,128)(2,1)S(1)} %collective-permute-done.g_before, bf16[48,16384]{1,0:T(8,128)(2,1)S(1)} %get-tuple-element.47.dressed0, ...), custom_call_target="tpu_custom_call" | custom-call | flops 17179869184 | tf_op jit(solution)/shard_map/join/pallas_call | solution.py:369
  37.4 0.0 collective-permute-done.4.from_left
  37.4 0.0 collective-permute-done.5.from_right
  37.4 0.0 collective-permute-done.7.after
  37.4 0.7 %join_far.1 = (f32[48,128]{1,0:T(8,128)S(1)}, f32[48,128]{1,0:T(8,128)S(1)}) custom-call(bf16[48,8192]{1,0:T(8,128)(2,1)S(1)} %get-tuple-element.42.far0, bf16[48,8192]{1,0:T(8,128)(2,1)S(1)} %get-tuple-element.43.far1, bf16[768,128]{1,0:T(8,128)(2,1)S(1)} %collective-permute-done.4.from_left, bf16[768,128]{1,0:T(8,128)(2,1)S(1)} %collective-permute-done.5.from_right, ...), custom_call_target="tpu_custom_call" | custom-call | tf_op jit(solution)/shard_map/join_far/pallas_call | solution.py:369
  38.1 0.4 collective-permute-start.8
  38.5 3.5 %collective-permute-done.8.recv = f32[48,128]{1,0:T(8,128)S(1)} collective-permute-done((f32[48,128]{1,0:T(8,128)S(1)}, f32[48,128]{1,0:T(8,128)S(1)}, u32[]{:S(2)}, u32[]{:S(2)}) %collective-permute-start.8) | collective-permute-done | bytes 24608 | tf_op jit(solution)/shard_map/ppermute | solution.py:393
  42.0 0.7 %assemble.1 = f32[48,240]{1,0:T(8,128)} custom-call(f32[48,48]{1,0:T(8,128)S(1)} %get-tuple-element.41.polar0, f32[48,128]{1,0:T(8,128)S(1)} %get-tuple-element.49.own, f32[48,128]{1,0:T(8,128)S(1)} %collective-permute-done.8.recv), custom_call_target="tpu_custom_call" | custom-call | tf_op jit(solution)/shard_map/assemble/pallas_call | solution.py:369
  (1 shorter events, 0.0 us)
Async XLA Ops:
  2.3 9.8 %collective-permute-start = (bf16[272,128]{1,0:T(8,128)(2,1)}, bf16[272,128]{1,0:T(8,128)(2,1)S(1)}, u32[]{:S(2)}, u32[]{:S(2)}) collective-permute-start(bf16[272,128]{1,0:T(8,128)(2,1)} %get-tuple-element.28), channel_id=1, source_target_pairs={{0,1},{1,2},{2,3},{3,4},{4,5},{5,6},{6,7},{7,8},{8,9},{9,10},{10,1... | collective-permute-start | bytes 208904 | tf_op jit(solution)/shard_map/ppermute | solution.py:393
  2.8 9.3 %collective-permute-start.2 = (bf16[272,128]{1,0:T(8,128)(2,1)}, bf16[272,128]{1,0:T(8,128)(2,1)S(1)}, u32[]{:S(2)}, u32[]{:S(2)}) collective-permute-start(bf16[272,128]{1,0:T(8,128)(2,1)} %get-tuple-element.30), channel_id=1, source_target_pairs={{0,2},{1,3},{2,4},{3,5},{4,6},{5,7},{6,8},{7,9},{8,10},{9,11},{10,... | collective-permute-start | bytes 208904 | tf_op jit(solution)/shard_map/ppermute | solution.py:393
  5.4 25.1 %collective-permute-start.6 = (bf16[24,128,128]{2,1,0:T(8,128)(2,1)}, bf16[24,128,128]{2,1,0:T(8,128)(2,1)S(1)}, u32[]{:S(2)}, u32[]{:S(2)}) collective-permute-start(bf16[24,128,128]{2,1,0:T(8,128)(2,1)} %get-tuple-element.46), channel_id=1, source_target_pairs={{0,1},{1,2},{2,3},{3,4},{4,5},{5,6},{6,7},{7,8},{8,9},{9,10},{10,1... | collective-permute-start | bytes 2359304 | tf_op jit(solution)/shard_map/ppermute | solution.py:393
  6.6 3.2 %copy-start.3 = (s32[16,4]{0,1:T(4,128)S(1)}, s32[16,4]{0,1:T(4,128)}, u32[]{:S(2)}) copy-start(s32[16,4]{0,1:T(4,128)} %param.9) | copy-start | bytes 772
  6.7 3.3 %copy-start = (bf16[1,48,128,128]{3,2,1,0:T(8,128)(2,1)S(1)}, bf16[1,48,128,128]{3,2,1,0:T(8,128)(2,1)}, u32[]{:S(2)}) copy-start(bf16[1,48,128,128]{3,2,1,0:T(8,128)(2,1)} %tensor.5) | copy-start | bytes 4718596
  6.7 3.3 %copy-start.2 = (s32[1,4,4]{2,1,0:T(4,128)S(1)}, s32[1,4,4]{2,1,0:T(4,128)}, u32[]{:S(2)}) copy-start(s32[1,4,4]{2,1,0:T(4,128)} %tiles.5) | copy-start | bytes 196
  6.7 5.4 %copy-start.1 = (bf16[256,128]{1,0:T(8,128)(2,1)S(1)}, bf16[256,128]{1,0:T(8,128)(2,1)}, u32[]{:S(2)}) copy-start(bf16[256,128]{1,0:T(8,128)(2,1)} %get-tuple-element.35.g_self) | copy-start | bytes 196612
  6.7 5.4 %collective-permute-start.1 = (bf16[256,128]{1,0:T(8,128)(2,1)}, bf16[256,128]{1,0:T(8,128)(2,1)S(1)}, u32[]{:S(2)}, u32[]{:S(2)}) collective-permute-start(bf16[256,128]{1,0:T(8,128)(2,1)} %keep.1), channel_id=1, source_target_pairs={{0,15},{1,0},{2,1},{3,2},{4,3},{5,4},{6,5},{7,6},{8,7},{9,8},{10,9... | collective-permute-start | bytes 196616 | tf_op jit(solution)/shard_map/ppermute | solution.py:393
  13.5 14.7 %collective-permute-start.3 = (bf16[512,128]{1,0:T(8,128)(2,1)S(1)}, bf16[512,128]{1,0:T(8,128)(2,1)S(1)}, u32[]{:S(2)}, u32[]{:S(2)}) collective-permute-start(bf16[512,128]{1,0:T(8,128)(2,1)S(1)} %choose.1.greens.g0), channel_id=1, source_target_pairs={{0,16},{1,17},{2,18},{3,19},{4,20},{5,21},{6,22},{7,23},{8,24},{9,... | collective-permute-start | bytes 393224 | tf_op jit(solution)/shard_map/ppermute | solution.py:393
  15.0 22.3 %collective-permute-start.4 = (bf16[768,128]{1,0:T(8,128)(2,1)S(1)}, bf16[768,128]{1,0:T(8,128)(2,1)S(1)}, u32[]{:S(2)}, u32[]{:S(2)}) collective-permute-start(bf16[768,128]{1,0:T(8,128)(2,1)S(1)} %get-tuple-element.44), channel_id=1, source_target_pairs={{0,2},{1,3},{2,4},{3,5},{4,6},{5,7},{6,8},{7,9},{8,10},{9,11},{10,... | collective-permute-start | bytes 589832 | tf_op jit(solution)/shard_map/ppermute | solution.py:393
  23.6 13.7 %collective-permute-start.5 = (bf16[768,128]{1,0:T(8,128)(2,1)S(1)}, bf16[768,128]{1,0:T(8,128)(2,1)S(1)}, u32[]{:S(2)}, u32[]{:S(2)}) collective-permute-start(bf16[768,128]{1,0:T(8,128)(2,1)S(1)} %get-tuple-element.45), channel_id=1, source_target_pairs={{0,14},{1,15},{2,0},{3,1},{4,2},{5,3},{6,4},{7,5},{8,6},{9,7},{10,... | collective-permute-start | bytes 589832 | tf_op jit(solution)/shard_map/ppermute | solution.py:393
  32.8 4.5 %collective-permute-start.7 = (f32[48,128]{1,0:T(8,128)S(1)}, f32[48,128]{1,0:T(8,128)S(1)}, u32[]{:S(2)}, u32[]{:S(2)}) collective-permute-start(f32[48,128]{1,0:T(8,128)S(1)} %join_back.1), channel_id=1, source_target_pairs={{0,15},{1,0},{2,1},{3,2},{4,3},{5,4},{6,5},{7,6},{8,7},{9,8},{10,9... | collective-permute-start | bytes 73736 | tf_op jit(solution)/shard_map/ppermute | solution.py:393
  38.1 3.9 %collective-permute-start.8 = (f32[48,128]{1,0:T(8,128)S(1)}, f32[48,128]{1,0:T(8,128)S(1)}, u32[]{:S(2)}, u32[]{:S(2)}) collective-permute-start(f32[48,128]{1,0:T(8,128)S(1)} %get-tuple-element.50), channel_id=1, source_target_pairs={{0,16},{1,17},{2,18},{3,19},{4,20},{5,21},{6,22},{7,23},{8,24},{9,... | collective-permute-start | bytes 73736 | tf_op jit(solution)/shard_map/ppermute | solution.py:393

commit v9 on v6

--- a/solution.py
+++ b/solution.py
@@ -96,7 +96,10 @@
         for copy in copies:
             copy.start()
     list_copy.wait()
-    gs[1, 256:272, :] = tile_mask(tiles, 4).astype(BF)
+    short = tile_mask(tiles, 4).astype(BF)
+    for n in range(1, 4):
+        for at in (256, 272, 288):
+            gs[n, at : at + 16, :] = short
     for copies, out in groups:
         for copy in copies:
             copy.wait()
@@ -359,7 +362,7 @@
     return [pl.BlockSpec(memory_space=pltpu.SMEM)] * count
 
 
-def call(kernel, name, specs, outs, args, scratch=(), flops=0, limit=40 << 20, space=None):
+def call(kernel, name, specs, outs, args, scratch=(), flops=0, limit=40 << 20, space=None, aliases={}):
     return pl.pallas_call(
         kernel,
         name=name,
@@ -367,6 +370,7 @@
         out_specs=tuple((space or vmem)(len(outs))),
         out_shape=tuple(outs),
         scratch_shapes=list(scratch),
+        input_output_aliases=aliases,
         compiler_params=pltpu.CompilerParams(vmem_limit_bytes=limit),
         cost_estimate=pl.CostEstimate(flops=flops, bytes_accessed=0, transcendentals=0),
     )(*args)
@@ -393,14 +397,14 @@
         [
             shape((256, 128), BF),
             shape((272, 128), BF),
-            shape((256, 128), BF),
-            shape((256, 128), BF),
+            shape((304, 128), BF),
+            shape((288, 128), BF),
             shape((funcs, 128, 128), BF),
         ],
         (green_occ, green_virt, tile_list, coulomb3c),
         [
             pltpu.SMEM((1, 4, 4), jnp.int32),
-            pltpu.VMEM((4, 272, 128), BF),
+            pltpu.VMEM((4, 304, 128), BF),
             pltpu.VMEM((funcs, 128, 128), BF),
             pltpu.SemaphoreType.DMA((20,)),
             pltpu.SemaphoreType.DMA((7,)),
@@ -409,8 +413,8 @@
         space=hbm,
     )
     g_before = send(g_right, 1)
+    g_beyond = send(g_far, 2)
     g_after = send(g_left, -1)
-    g_beyond = send(g_far, 2)
     wide = send(tensor, 1)
     flat_shape, far_shape = shape((full, 128 * 128), BF), shape((full, 64 * 128), BF)
     tall = pltpu.VMEM((full * PITCH, 128), F32)
@@ -436,6 +440,9 @@
         (window, g_self, g_before, g_after, g_beyond),
     )
     partner = send(mine, 0, True)
+    far_right, far_left, mine = lax.optimization_barrier((far_right, far_left, mine))
+    from_left = send(far_right, 2)
+    from_right = send(far_left, -2)
     polar0, dressed0, far0 = call(
         functools.partial(dress, count, True),
         "dress_own",
@@ -444,9 +451,6 @@
         (window, tile_list, coulomb3c, mine, flat),
         [tall, pltpu.VMEM((full, 128 * 128), BF)],
     )
-    far_right, far_left, polar0 = lax.optimization_barrier((far_right, far_left, polar0))
-    from_left = send(far_right, 2)
-    from_right = send(far_left, -2)
     dressed1, far1 = call(
         functools.partial(dress, count, False),
         "dress_partner",

time: 38.6 us -> 37.8 us (0.979)
  waiting for transfers between devices: 8.99 us -> 5.56 us
  starting transfers between devices: 12.4 us -> 15.1 us
    ppermute x9, waiting for transfers between devices: 8.99 us -> 5.56 us  [send(): return lax.ppermute(array, ('grp', 'row'), pairs)]
    ppermute x9, starting transfers between devices: 12.4 us -> 15.1 us  [send(): return lax.ppermute(array, ('grp', 'row'), pairs)]
  transfers between devices with their start and end apart: 9 -> 9, of which waited for: 3 -> 4; matrix products, arithmetic and copies ran while one was open for 0% -> 0% of each run, Pallas kernels for 34% -> 35%
where the time goes in v9:
time: 37.8 us; the launch traced here: 37.7 us
  Pallas kernels  16.8 us (44%)
  starting transfers between devices  15.1 us (40%)
  waiting for transfers between devices  5.56 us (15%)
    pallas_call x9, Pallas kernels, call(): pl.pallas_call(kernel, name=name, in_specs=specs, out_specs=tuple((space...  16.8 us
    ppermute x9, starting transfers between devices, send(): return lax.ppermute(array, ('grp', 'row'), pairs)  15.1 us
    ppermute x9, waiting for transfers between devices, send(): return lax.ppermute(array, ('grp', 'row'), pairs)  5.56 us
  transfers between devices with their start and end apart: 9, of which 4 were waited for; matrix products, arithmetic and copies ran while one was open for 0% of the time, Pallas kernels for 35%

profile of v9, /device:TPU:0, one launch (start us, length us, event | category | flops | bytes accessed | tf_op | source)
XLA Modules:
  0.0 37.7 jit_solution(8554790235810898244)
XLA Ops:
  0.0 0.0 copy-start.2
  0.0 0.0 copy-start
  0.0 0.0 copy-start.3
  0.0 2.4 %first.1 = (bf16[256,128]{1,0:T(8,128)(2,1)}, bf16[272,128]{1,0:T(8,128)(2,1)}, bf16[304,128]{1,0:T(8,128)(2,1)}, bf16[288,128]{1,0:T(8,128)(2,1)}, bf16[24,128,128]{2,1,0:T(8,128)(2,1)}) custom-call(bf16[64,1024]{1,0:T(8,128)(2,1)} %occ.1, bf16[64,1024]{1,0:T(8,128)(2,1)} %virt.1, s32[1,4,4]{2,1,0:T(4,128)} %tiles.5, bf16[1,48,128,128]{3,2,1,0:T(8,128)(2,1)} %tensor.5), custom_call_target="tpu_custom_call" | custom-call | tf_op jit(solution)/shard_map/first/pallas_call | solution.py:366
  2.4 0.5 %collective-permute-start = (bf16[272,128]{1,0:T(8,128)(2,1)}, bf16[272,128]{1,0:T(8,128)(2,1)S(1)}, u32[]{:S(2)}, u32[]{:S(2)}) collective-permute-start(bf16[272,128]{1,0:T(8,128)(2,1)} %get-tuple-element.28), channel_id=1, source_target_pairs={{0,1},{1,2},{2,3},{3,4},{4,5},{5,6},{6,7},{7,8},{8,9},{9,10},{10,1... | collective-permute-start | bytes 208904 | tf_op jit(solution)/shard_map/ppermute | solution.py:390
  2.9 2.6 %collective-permute-start.2 = (bf16[288,128]{1,0:T(8,128)(2,1)}, bf16[288,128]{1,0:T(8,128)(2,1)S(1)}, u32[]{:S(2)}, u32[]{:S(2)}) collective-permute-start(bf16[288,128]{1,0:T(8,128)(2,1)} %get-tuple-element.30), channel_id=1, source_target_pairs={{0,2},{1,3},{2,4},{3,5},{4,6},{5,7},{6,8},{7,9},{8,10},{9,11},{10,... | collective-permute-start | bytes 221192 | tf_op jit(solution)/shard_map/ppermute | solution.py:390
  5.5 4.1 %collective-permute-start.1 = (bf16[304,128]{1,0:T(8,128)(2,1)}, bf16[304,128]{1,0:T(8,128)(2,1)S(1)}, u32[]{:S(2)}, u32[]{:S(2)}) collective-permute-start(bf16[304,128]{1,0:T(8,128)(2,1)} %get-tuple-element.29), channel_id=1, source_target_pairs={{0,15},{1,0},{2,1},{3,2},{4,3},{5,4},{6,5},{7,6},{8,7},{9,8},{10,9... | collective-permute-start | bytes 233480 | tf_op jit(solution)/shard_map/ppermute | solution.py:390
  9.6 0.0 collective-permute-start.6
  9.6 0.0 copy-done.3
  9.6 0.1 copy.8.win
  9.7 0.0 copy-done.2
  9.7 0.0 copy-done
  9.7 0.0 copy-start.1
  9.7 2.0 %far_tiles.1 = (bf16[768,128]{1,0:T(8,128)(2,1)S(1)}, bf16[768,128]{1,0:T(8,128)(2,1)S(1)}, bf16[48,16384]{1,0:T(8,128)(2,1)S(1)}) custom-call(s32[16,4]{1,0:T(8,128)S(1)} %copy.8.win, s32[1,4,4]{2,1,0:T(4,128)S(1)} %copy-done.2, bf16[1,48,128,128]{3,2,1,0:T(8,128)(2,1)S(1)} %copy-done), custom_call_target="tpu_custom_call" | custom-call | flops 68719476736 | tf_op jit(solution)/shard_map/far_tiles/pallas_call | solution.py:366
  11.7 0.0 collective-permute-done.g_before
  11.7 0.0 collective-permute-done.2.g_far
  11.7 0.2 collective-permute-done.1.g_after
  11.9 0.0 copy-done.1
  11.9 1.3 %choose.1.greens.g0 = bf16[512,128]{1,0:T(8,128)(2,1)S(1)} custom-call(s32[16,4]{1,0:T(8,128)S(1)} %copy.8.win, bf16[256,128]{1,0:T(8,128)(2,1)S(1)} %copy-done.1, bf16[272,128]{1,0:T(8,128)(2,1)S(1)} %collective-permute-done.g_before, bf16[304,128]{1,0:T(8,128)(2,1)S(1)} %collective-permute-done.1.g_after, bf16[288,128]{1,0:T(8,128)(2,1)S(1)} %collective-permute-done.2.g_far), custom_call_target="tpu_custom_call" | custom-call | tf_op jit(solution)/shard_map/choose/pallas_call | solution.py:366
  13.3 1.6 %collective-permute-start.3 = (bf16[512,128]{1,0:T(8,128)(2,1)S(1)}, bf16[512,128]{1,0:T(8,128)(2,1)S(1)}, u32[]{:S(2)}, u32[]{:S(2)}) collective-permute-start(bf16[512,128]{1,0:T(8,128)(2,1)S(1)} %choose.1.greens.g0), channel_id=1, source_target_pairs={{0,16},{1,17},{2,18},{3,19},{4,20},{5,21},{6,22},{7,23},{8,24},{9,... | collective-permute-start | bytes 393224 | tf_op jit(solution)/shard_map/ppermute | solution.py:390
  14.8 0.7 %collective-permute-start.4 = (bf16[768,128]{1,0:T(8,128)(2,1)S(1)}, bf16[768,128]{1,0:T(8,128)(2,1)S(1)}, u32[]{:S(2)}, u32[]{:S(2)}) collective-permute-start(bf16[768,128]{1,0:T(8,128)(2,1)S(1)} %get-tuple-element.44), channel_id=1, source_target_pairs={{0,2},{1,3},{2,4},{3,5},{4,6},{5,7},{6,8},{7,9},{8,10},{9,11},{10,... | collective-permute-start | bytes 589832 | tf_op jit(solution)/shard_map/ppermute | solution.py:390
  15.5 4.0 %collective-permute-start.5 = (bf16[768,128]{1,0:T(8,128)(2,1)S(1)}, bf16[768,128]{1,0:T(8,128)(2,1)S(1)}, u32[]{:S(2)}, u32[]{:S(2)}) collective-permute-start(bf16[768,128]{1,0:T(8,128)(2,1)S(1)} %get-tuple-element.45), channel_id=1, source_target_pairs={{0,14},{1,15},{2,0},{3,1},{4,2},{5,3},{6,4},{7,5},{8,6},{9,7},{10,... | collective-permute-start | bytes 589832 | tf_op jit(solution)/shard_map/ppermute | solution.py:390
  19.6 3.2 %dress_own.1 = (f32[48,48]{1,0:T(8,128)S(1)}, bf16[48,16384]{1,0:T(8,128)(2,1)S(1)}, bf16[48,8192]{1,0:T(8,128)(2,1)S(1)}) custom-call(s32[16,4]{1,0:T(8,128)S(1)} %copy.8.win, s32[1,4,4]{2,1,0:T(4,128)S(1)} %copy-done.2, bf16[1,48,128,128]{3,2,1,0:T(8,128)(2,1)S(1)} %copy-done, bf16[512,128]{1,0:T(8,128)(2,1)S(1)} %choose.1.greens.g0, ...), custom_call_target="tpu_custom_call" | custom-call | tf_op jit(solution)/shard_map/dress_own/pallas_call | solution.py:366
  22.8 0.0 collective-permute-done.3.greens.g1
  22.8 2.3 %dress_partner.1 = (bf16[48,16384]{1,0:T(8,128)(2,1)S(1)}, bf16[48,8192]{1,0:T(8,128)(2,1)S(1)}) custom-call(s32[16,4]{1,0:T(8,128)S(1)} %copy.8.win, s32[1,4,4]{2,1,0:T(4,128)S(1)} %copy-done.2, bf16[1,48,128,128]{3,2,1,0:T(8,128)(2,1)S(1)} %copy-done, bf16[512,128]{1,0:T(8,128)(2,1)S(1)} %collective-permute-done.3.greens.g1), custom_call_target="tpu_custom_call" | custom-call | tf_op jit(solution)/shard_map/dress_partner/pallas_call | solution.py:366
  25.1 1.0 %collective-permute-done.6.tensor = bf16[24,128,128]{2,1,0:T(8,128)(2,1)S(1)} collective-permute-done((bf16[24,128,128]{2,1,0:T(8,128)(2,1)}, bf16[24,128,128]{2,1,0:T(8,128)(2,1)S(1)}, u32[]{:S(2)}, u32[]{:S(2)}) %collective-permute-start.6) | collective-permute-done | bytes 786464 | tf_op jit(solution)/shard_map/ppermute | solution.py:390
  26.1 2.4 %join_back.1 = f32[48,128]{1,0:T(8,128)S(1)} custom-call(bf16[24,128,128]{2,1,0:T(8,128)(2,1)S(1)} %collective-permute-done.6.tensor, bf16[272,128]{1,0:T(8,128)(2,1)S(1)} %collective-permute-done.g_before, bf16[512,128]{1,0:T(8,128)(2,1)S(1)} %choose.1.greens.g0, bf16[512,128]{1,0:T(8,128)(2,1)S(1)} %collective-permute-done.3.greens.g1, ...), custom_call_target="tpu_custom_call" | custom-call | tf_op jit(solution)/shard_map/join_back/pallas_call | solution.py:366
  28.5 0.0 collective-permute-start.7
  28.5 1.8 %join.1.down = f32[96,128]{1,0:T(8,128)S(1)} custom-call(s32[16,4]{1,0:T(8,128)S(1)} %copy.8.win, bf16[24,128,128]{2,1,0:T(8,128)(2,1)S(1)} %collective-permute-done.6.tensor, bf16[272,128]{1,0:T(8,128)(2,1)S(1)} %collective-permute-done.g_before, bf16[48,16384]{1,0:T(8,128)(2,1)S(1)} %get-tuple-element.47.dressed0, ...), custom_call_target="tpu_custom_call" | custom-call | flops 17179869184 | tf_op jit(solution)/shard_map/join/pallas_call | solution.py:366
  30.3 0.0 collective-permute-done.4.from_left
  30.3 2.0 %collective-permute-done.5.from_right = bf16[768,128]{1,0:T(8,128)(2,1)S(1)} collective-permute-done((bf16[768,128]{1,0:T(8,128)(2,1)S(1)}, bf16[768,128]{1,0:T(8,128)(2,1)S(1)}, u32[]{:S(2)}, u32[]{:S(2)}) %collective-permute-start.5) | collective-permute-done | bytes 196640 | tf_op jit(solution)/shard_map/ppermute | solution.py:390
  32.3 0.0 collective-permute-done.7.after
  32.3 0.7 %join_far.1 = (f32[48,128]{1,0:T(8,128)S(1)}, f32[48,128]{1,0:T(8,128)S(1)}) custom-call(bf16[48,8192]{1,0:T(8,128)(2,1)S(1)} %get-tuple-element.42.far0, bf16[48,8192]{1,0:T(8,128)(2,1)S(1)} %get-tuple-element.43.far1, bf16[768,128]{1,0:T(8,128)(2,1)S(1)} %collective-permute-done.4.from_left, bf16[768,128]{1,0:T(8,128)(2,1)S(1)} %collective-permute-done.5.from_right, ...), custom_call_target="tpu_custom_call" | custom-call | tf_op jit(solution)/shard_map/join_far/pallas_call | solution.py:366
  33.0 1.6 %collective-permute-start.8 = (f32[48,128]{1,0:T(8,128)S(1)}, f32[48,128]{1,0:T(8,128)S(1)}, u32[]{:S(2)}, u32[]{:S(2)}) collective-permute-start(f32[48,128]{1,0:T(8,128)S(1)} %get-tuple-element.50), channel_id=1, source_target_pairs={{0,16},{1,17},{2,18},{3,19},{4,20},{5,21},{6,22},{7,23},{8,24},{9,... | collective-permute-start | bytes 73736 | tf_op jit(solution)/shard_map/ppermute | solution.py:390
  34.6 2.3 %collective-permute-done.8.recv = f32[48,128]{1,0:T(8,128)S(1)} collective-permute-done((f32[48,128]{1,0:T(8,128)S(1)}, f32[48,128]{1,0:T(8,128)S(1)}, u32[]{:S(2)}, u32[]{:S(2)}) %collective-permute-start.8) | collective-permute-done | bytes 24608 | tf_op jit(solution)/shard_map/ppermute | solution.py:390
  36.9 0.7 %assemble.1 = f32[48,240]{1,0:T(8,128)} custom-call(f32[48,48]{1,0:T(8,128)S(1)} %get-tuple-element.41.polar0, f32[48,128]{1,0:T(8,128)S(1)} %get-tuple-element.49.own, f32[48,128]{1,0:T(8,128)S(1)} %collective-permute-done.8.recv), custom_call_target="tpu_custom_call" | custom-call | tf_op jit(solution)/shard_map/assemble/pallas_call | solution.py:366
Async XLA Ops:
  0.0 9.7 %copy-start.2 = (s32[1,4,4]{2,1,0:T(4,128)S(1)}, s32[1,4,4]{2,1,0:T(4,128)}, u32[]{:S(2)}) copy-start(s32[1,4,4]{2,1,0:T(4,128)} %tiles.5) | copy-start | bytes 196
  0.0 9.7 %copy-start = (bf16[1,48,128,128]{3,2,1,0:T(8,128)(2,1)S(1)}, bf16[1,48,128,128]{3,2,1,0:T(8,128)(2,1)}, u32[]{:S(2)}) copy-start(bf16[1,48,128,128]{3,2,1,0:T(8,128)(2,1)} %tensor.5) | copy-start | bytes 4718596
  0.0 9.6 %copy-start.3 = (s32[16,4]{0,1:T(4,128)S(1)}, s32[16,4]{0,1:T(4,128)}, u32[]{:S(2)}) copy-start(s32[16,4]{0,1:T(4,128)} %param.9) | copy-start | bytes 772
  2.4 9.3 %collective-permute-start = (bf16[272,128]{1,0:T(8,128)(2,1)}, bf16[272,128]{1,0:T(8,128)(2,1)S(1)}, u32[]{:S(2)}, u32[]{:S(2)}) collective-permute-start(bf16[272,128]{1,0:T(8,128)(2,1)} %get-tuple-element.28), channel_id=1, source_target_pairs={{0,1},{1,2},{2,3},{3,4},{4,5},{5,6},{6,7},{7,8},{8,9},{9,10},{10,1... | collective-permute-start | bytes 208904 | tf_op jit(solution)/shard_map/ppermute | solution.py:390
  2.9 8.8 %collective-permute-start.2 = (bf16[288,128]{1,0:T(8,128)(2,1)}, bf16[288,128]{1,0:T(8,128)(2,1)S(1)}, u32[]{:S(2)}, u32[]{:S(2)}) collective-permute-start(bf16[288,128]{1,0:T(8,128)(2,1)} %get-tuple-element.30), channel_id=1, source_target_pairs={{0,2},{1,3},{2,4},{3,5},{4,6},{5,7},{6,8},{7,9},{8,10},{9,11},{10,... | collective-permute-start | bytes 221192 | tf_op jit(solution)/shard_map/ppermute | solution.py:390
  5.5 6.4 %collective-permute-start.1 = (bf16[304,128]{1,0:T(8,128)(2,1)}, bf16[304,128]{1,0:T(8,128)(2,1)S(1)}, u32[]{:S(2)}, u32[]{:S(2)}) collective-permute-start(bf16[304,128]{1,0:T(8,128)(2,1)} %get-tuple-element.29), channel_id=1, source_target_pairs={{0,15},{1,0},{2,1},{3,2},{4,3},{5,4},{6,5},{7,6},{8,7},{9,8},{10,9... | collective-permute-start | bytes 233480 | tf_op jit(solution)/shard_map/ppermute | solution.py:390
  9.6 16.5 %collective-permute-start.6 = (bf16[24,128,128]{2,1,0:T(8,128)(2,1)}, bf16[24,128,128]{2,1,0:T(8,128)(2,1)S(1)}, u32[]{:S(2)}, u32[]{:S(2)}) collective-permute-start(bf16[24,128,128]{2,1,0:T(8,128)(2,1)} %get-tuple-element.46), channel_id=1, source_target_pairs={{0,1},{1,2},{2,3},{3,4},{4,5},{5,6},{6,7},{7,8},{8,9},{9,10},{10,1... | collective-permute-start | bytes 2359304 | tf_op jit(solution)/shard_map/ppermute | solution.py:390
  9.7 2.2 %copy-start.1 = (bf16[256,128]{1,0:T(8,128)(2,1)S(1)}, bf16[256,128]{1,0:T(8,128)(2,1)}, u32[]{:S(2)}) copy-start(bf16[256,128]{1,0:T(8,128)(2,1)} %get-tuple-element.35.g_self) | copy-start | bytes 196612
  13.3 9.5 %collective-permute-start.3 = (bf16[512,128]{1,0:T(8,128)(2,1)S(1)}, bf16[512,128]{1,0:T(8,128)(2,1)S(1)}, u32[]{:S(2)}, u32[]{:S(2)}) collective-permute-start(bf16[512,128]{1,0:T(8,128)(2,1)S(1)} %choose.1.greens.g0), channel_id=1, source_target_pairs={{0,16},{1,17},{2,18},{3,19},{4,20},{5,21},{6,22},{7,23},{8,24},{9,... | collective-permute-start | bytes 393224 | tf_op jit(solution)/shard_map/ppermute | solution.py:390
  14.8 15.5 %collective-permute-start.4 = (bf16[768,128]{1,0:T(8,128)(2,1)S(1)}, bf16[768,128]{1,0:T(8,128)(2,1)S(1)}, u32[]{:S(2)}, u32[]{:S(2)}) collective-permute-start(bf16[768,128]{1,0:T(8,128)(2,1)S(1)} %get-tuple-element.44), channel_id=1, source_target_pairs={{0,2},{1,3},{2,4},{3,5},{4,6},{5,7},{6,8},{7,9},{8,10},{9,11},{10,... | collective-permute-start | bytes 589832 | tf_op jit(solution)/shard_map/ppermute | solution.py:390
  15.5 16.8 %collective-permute-start.5 = (bf16[768,128]{1,0:T(8,128)(2,1)S(1)}, bf16[768,128]{1,0:T(8,128)(2,1)S(1)}, u32[]{:S(2)}, u32[]{:S(2)}) collective-permute-start(bf16[768,128]{1,0:T(8,128)(2,1)S(1)} %get-tuple-element.45), channel_id=1, source_target_pairs={{0,14},{1,15},{2,0},{3,1},{4,2},{5,3},{6,4},{7,5},{8,6},{9,7},{10,... | collective-permute-start | bytes 589832 | tf_op jit(solution)/shard_map/ppermute | solution.py:390
  28.5 3.9 %collective-permute-start.7 = (f32[48,128]{1,0:T(8,128)S(1)}, f32[48,128]{1,0:T(8,128)S(1)}, u32[]{:S(2)}, u32[]{:S(2)}) collective-permute-start(f32[48,128]{1,0:T(8,128)S(1)} %join_back.1), channel_id=1, source_target_pairs={{0,15},{1,0},{2,1},{3,2},{4,3},{5,4},{6,5},{7,6},{8,7},{9,8},{10,9... | collective-permute-start | bytes 73736 | tf_op jit(solution)/shard_map/ppermute | solution.py:390
  33.0 3.9 %collective-permute-start.8 = (f32[48,128]{1,0:T(8,128)S(1)}, f32[48,128]{1,0:T(8,128)S(1)}, u32[]{:S(2)}, u32[]{:S(2)}) collective-permute-start(f32[48,128]{1,0:T(8,128)S(1)} %get-tuple-element.50), channel_id=1, source_target_pairs={{0,16},{1,17},{2,18},{3,19},{4,20},{5,21},{6,22},{7,23},{8,24},{9,... | collective-permute-start | bytes 73736 | tf_op jit(solution)/shard_map/ppermute | solution.py:390

commit v10 on v9

--- a/solution.py
+++ b/solution.py
@@ -67,13 +67,10 @@
     return near(row, -1, count) >> 1
 
 
-def first(count, occ, virt, tiles_hbm, coulomb, *refs):
-    outs, (tiles, gs, part, sem, done) = refs[:5], refs[5:]
+def first(count, occ, virt, tiles_hbm, *refs):
+    outs, (tiles, gs, sem, done) = refs[:4], refs[4:]
     d = lax.axis_index("row")
-    funcs = part.shape[0]
-    half = lax.rem(lax.axis_index("grp"), 2)
     list_copy = pltpu.make_async_copy(tiles_hbm, tiles, sem.at[16])
-    list_copy.start()
     groups = []
     for n, by in enumerate((0, 1, -1, 2)):
         start = column_chunk(near(d, by, count), count)
@@ -87,11 +84,7 @@
                 copies.append(pltpu.make_async_copy(green.at[:, columns], place, sem.at[4 * n + len(copies)]))
         rows = outs[n].shape[0]
         groups.append((copies, pltpu.make_async_copy(gs.at[n, 0:rows], outs[n], done.at[n])))
-    for n in range(3):
-        piece = pl.ds(half * funcs + n * 8, 8)
-        copy = pltpu.make_async_copy(coulomb.at[0, piece], part.at[n * 8 : n * 8 + 8], sem.at[17 + n])
-        out = pltpu.make_async_copy(part.at[n * 8 : n * 8 + 8], outs[4].at[n * 8 : n * 8 + 8], done.at[4 + n])
-        groups.append(([copy], out))
+    list_copy.start()
     for copies, _ in groups:
         for copy in copies:
             copy.start()
@@ -105,6 +98,23 @@
             copy.wait()
         out.start()
     for _, out in groups:
+        out.wait()
+
+
+def take_half(coulomb, tensor, part, sem, done):
+    funcs = part.shape[0]
+    start = lax.rem(lax.axis_index("grp"), 2) * funcs
+    steps = []
+    for n in range(3):
+        rows = slice(n * 8, n * 8 + 8)
+        copy = pltpu.make_async_copy(coulomb.at[0, pl.ds(start + n * 8, 8)], part.at[rows], sem.at[n])
+        steps.append((copy, pltpu.make_async_copy(part.at[rows], tensor.at[rows], done.at[n])))
+    for copy, _ in steps:
+        copy.start()
+    for copy, out in steps:
+        copy.wait()
+        out.start()
+    for _, out in steps:
         out.wait()
 
 
@@ -390,24 +400,22 @@
         return lax.ppermute(array, ("grp", "row"), pairs)
 
     far_rows = funcs * 32
-    g_self, g_right, g_left, g_far, tensor = call(
+    g_self, g_right, g_left, g_far = call(
         functools.partial(first, count),
         "first",
-        hbm(4),
+        hbm(3),
         [
             shape((256, 128), BF),
             shape((272, 128), BF),
             shape((304, 128), BF),
             shape((288, 128), BF),
-            shape((funcs, 128, 128), BF),
         ],
-        (green_occ, green_virt, tile_list, coulomb3c),
+        (green_occ, green_virt, tile_list),
         [
             pltpu.SMEM((1, 4, 4), jnp.int32),
             pltpu.VMEM((4, 304, 128), BF),
-            pltpu.VMEM((funcs, 128, 128), BF),
-            pltpu.SemaphoreType.DMA((20,)),
-            pltpu.SemaphoreType.DMA((7,)),
+            pltpu.SemaphoreType.DMA((17,)),
+            pltpu.SemaphoreType.DMA((4,)),
         ],
         limit=60 << 20,
         space=hbm,
@@ -415,6 +423,21 @@
     g_before = send(g_right, 1)
     g_beyond = send(g_far, 2)
     g_after = send(g_left, -1)
+    tensor, _ = lax.optimization_barrier((coulomb3c, g_self))
+    (tensor,) = call(
+        take_half,
+        "take_half",
+        hbm(1),
+        [shape((funcs, 128, 128), BF)],
+        (tensor,),
+        [
+            pltpu.VMEM((funcs, 128, 128), BF),
+            pltpu.SemaphoreType.DMA((3,)),
+            pltpu.SemaphoreType.DMA((3,)),
+        ],
+        limit=60 << 20,
+        space=hbm,
+    )
     wide = send(tensor, 1)
     flat_shape, far_shape = shape((full, 128 * 128), BF), shape((full, 64 * 128), BF)
     tall = pltpu.VMEM((full * PITCH, 128), F32)
@@ -440,9 +463,6 @@
         (window, g_self, g_before, g_after, g_beyond),
     )
     partner = send(mine, 0, True)
-    far_right, far_left, mine = lax.optimization_barrier((far_right, far_left, mine))
-    from_left = send(far_right, 2)
-    from_right = send(far_left, -2)
     polar0, dressed0, far0 = call(
         functools.partial(dress, count, True),
         "dress_own",
@@ -451,6 +471,9 @@
         (window, tile_list, coulomb3c, mine, flat),
         [tall, pltpu.VMEM((full, 128 * 128), BF)],
     )
+    far_right, far_left, polar0 = lax.optimization_barrier((far_right, far_left, polar0))
+    from_left = send(far_right, 2)
+    from_right = send(far_left, -2)
     dressed1, far1 = call(
         functools.partial(dress, count, False),
         "dress_partner",

time: 37.8 us -> 39.2 us (1.037)
  Pallas kernels: 16.8 us -> 18.2 us
  waiting for transfers between devices: 5.56 us -> 4.64 us
  starting transfers between devices: 15.1 us -> 16 us
    pallas_call x9 -> x10, Pallas kernels: 16.8 us -> 18.2 us  [call(): pl.pallas_call(kernel, name=name, in_specs=specs, out_specs=tuple((space...]
    ppermute x9, starting transfers between devices: 15.1 us -> 16 us  [send(): return lax.ppermute(array, ('grp', 'row'), pairs)]
    ppermute x9, waiting for transfers between devices: 5.56 us -> 4.64 us  [send(): return lax.ppermute(array, ('grp', 'row'), pairs)]
  transfers between devices with their start and end apart: 9 -> 9, of which waited for: 4 -> 2; matrix products, arithmetic and copies ran while one was open for 0% -> 0% of each run, Pallas kernels for 35% -> 38%
where the time goes in v10:
time: 39.2 us; the launch traced here: 39.1 us
  Pallas kernels  18.2 us (46%)
  starting transfers between devices  16 us (41%)
  waiting for transfers between devices  4.64 us (12%)
    pallas_call x10, Pallas kernels, call(): pl.pallas_call(kernel, name=name, in_specs=specs, out_specs=tuple((space...  18.2 us
    ppermute x9, starting transfers between devices, send(): return lax.ppermute(array, ('grp', 'row'), pairs)  16 us
    ppermute x9, waiting for transfers between devices, send(): return lax.ppermute(array, ('grp', 'row'), pairs)  4.64 us
  transfers between devices with their start and end apart: 9, of which 2 were waited for; matrix products, arithmetic and copies ran while one was open for 0% of the time, Pallas kernels for 38%

profile of v10, /device:TPU:0, one launch (start us, length us, event | category | flops | bytes accessed | tf_op | source)
XLA Modules:
  0.0 39.1 jit_solution(14646258914828767913)
XLA Ops:
  0.0 0.0 copy-start.2
  0.0 0.0 copy-start
  0.0 0.0 copy-start.3
  0.0 1.8 %first.1 = (bf16[256,128]{1,0:T(8,128)(2,1)}, bf16[272,128]{1,0:T(8,128)(2,1)}, bf16[304,128]{1,0:T(8,128)(2,1)}, bf16[288,128]{1,0:T(8,128)(2,1)}) custom-call(bf16[64,1024]{1,0:T(8,128)(2,1)} %occ.1, bf16[64,1024]{1,0:T(8,128)(2,1)} %virt.1, s32[1,4,4]{2,1,0:T(4,128)} %tiles.5), custom_call_target="tpu_custom_call" | custom-call | tf_op jit(solution)/shard_map/first/pallas_call | solution.py:376
  1.8 0.5 %collective-permute-start = (bf16[272,128]{1,0:T(8,128)(2,1)}, bf16[272,128]{1,0:T(8,128)(2,1)S(1)}, u32[]{:S(2)}, u32[]{:S(2)}) collective-permute-start(bf16[272,128]{1,0:T(8,128)(2,1)} %get-tuple-element.28), channel_id=1, source_target_pairs={{0,1},{1,2},{2,3},{3,4},{4,5},{5,6},{6,7},{7,8},{8,9},{9,10},{10,1... | collective-permute-start | bytes 208904 | tf_op jit(solution)/shard_map/ppermute | solution.py:400
  2.4 2.6 %collective-permute-start.2 = (bf16[288,128]{1,0:T(8,128)(2,1)}, bf16[288,128]{1,0:T(8,128)(2,1)S(1)}, u32[]{:S(2)}, u32[]{:S(2)}) collective-permute-start(bf16[288,128]{1,0:T(8,128)(2,1)} %get-tuple-element.30), channel_id=1, source_target_pairs={{0,2},{1,3},{2,4},{3,5},{4,6},{5,7},{6,8},{7,9},{8,10},{9,11},{10,... | collective-permute-start | bytes 221192 | tf_op jit(solution)/shard_map/ppermute | solution.py:400
  5.0 4.1 %collective-permute-start.1 = (bf16[304,128]{1,0:T(8,128)(2,1)}, bf16[304,128]{1,0:T(8,128)(2,1)S(1)}, u32[]{:S(2)}, u32[]{:S(2)}) collective-permute-start(bf16[304,128]{1,0:T(8,128)(2,1)} %get-tuple-element.29), channel_id=1, source_target_pairs={{0,15},{1,0},{2,1},{3,2},{4,3},{5,4},{6,5},{7,6},{8,7},{9,8},{10,9... | collective-permute-start | bytes 233480 | tf_op jit(solution)/shard_map/ppermute | solution.py:400
  9.1 1.9 %take_half.1 = bf16[24,128,128]{2,1,0:T(8,128)(2,1)} custom-call(bf16[1,48,128,128]{3,2,1,0:T(8,128)(2,1)} %coulomb), custom_call_target="tpu_custom_call" | custom-call | tf_op jit(solution)/shard_map/take_half/pallas_call | solution.py:376
  11.0 0.1 collective-permute-start.6
  11.0 0.0 copy-done.3
  11.0 0.1 copy.6.win
  11.1 0.0 copy-done.2
  11.1 0.0 copy-done
  11.1 0.0 copy-start.1
  11.1 2.0 %far_tiles.1 = (bf16[768,128]{1,0:T(8,128)(2,1)S(1)}, bf16[768,128]{1,0:T(8,128)(2,1)S(1)}, bf16[48,16384]{1,0:T(8,128)(2,1)S(1)}) custom-call(s32[16,4]{1,0:T(8,128)S(1)} %copy.6.win, s32[1,4,4]{2,1,0:T(4,128)S(1)} %copy-done.2, bf16[1,48,128,128]{3,2,1,0:T(8,128)(2,1)S(1)} %copy-done), custom_call_target="tpu_custom_call" | custom-call | flops 68719476736 | tf_op jit(solution)/shard_map/far_tiles/pallas_call | solution.py:376
  13.1 0.0 collective-permute-done.g_before
  13.1 0.0 collective-permute-done.2.g_far
  13.1 0.0 collective-permute-done.1.g_after
  13.1 0.0 copy-done.1
  13.2 1.3 %choose.1.greens.g0 = bf16[512,128]{1,0:T(8,128)(2,1)S(1)} custom-call(s32[16,4]{1,0:T(8,128)S(1)} %copy.6.win, bf16[256,128]{1,0:T(8,128)(2,1)S(1)} %copy-done.1, bf16[272,128]{1,0:T(8,128)(2,1)S(1)} %collective-permute-done.g_before, bf16[304,128]{1,0:T(8,128)(2,1)S(1)} %collective-permute-done.1.g_after, bf16[288,128]{1,0:T(8,128)(2,1)S(1)} %collective-permute-done.2.g_far), custom_call_target="tpu_custom_call" | custom-call | tf_op jit(solution)/shard_map/choose/pallas_call | solution.py:376
  14.5 1.6 %collective-permute-start.3 = (bf16[512,128]{1,0:T(8,128)(2,1)S(1)}, bf16[512,128]{1,0:T(8,128)(2,1)S(1)}, u32[]{:S(2)}, u32[]{:S(2)}) collective-permute-start(bf16[512,128]{1,0:T(8,128)(2,1)S(1)} %choose.1.greens.g0), channel_id=1, source_target_pairs={{0,16},{1,17},{2,18},{3,19},{4,20},{5,21},{6,22},{7,23},{8,24},{9,... | collective-permute-start | bytes 393224 | tf_op jit(solution)/shard_map/ppermute | solution.py:400
  16.1 3.2 %dress_own.1 = (f32[48,48]{1,0:T(8,128)S(1)}, bf16[48,16384]{1,0:T(8,128)(2,1)S(1)}, bf16[48,8192]{1,0:T(8,128)(2,1)S(1)}) custom-call(s32[16,4]{1,0:T(8,128)S(1)} %copy.6.win, s32[1,4,4]{2,1,0:T(4,128)S(1)} %copy-done.2, bf16[1,48,128,128]{3,2,1,0:T(8,128)(2,1)S(1)} %copy-done, bf16[512,128]{1,0:T(8,128)(2,1)S(1)} %choose.1.greens.g0, ...), custom_call_target="tpu_custom_call" | custom-call | tf_op jit(solution)/shard_map/dress_own/pallas_call | solution.py:376
  19.3 0.0 collective-permute-start.4
  19.3 4.7 %collective-permute-start.5 = (bf16[768,128]{1,0:T(8,128)(2,1)S(1)}, bf16[768,128]{1,0:T(8,128)(2,1)S(1)}, u32[]{:S(2)}, u32[]{:S(2)}) collective-permute-start(bf16[768,128]{1,0:T(8,128)(2,1)S(1)} %get-tuple-element.45), channel_id=1, source_target_pairs={{0,14},{1,15},{2,0},{3,1},{4,2},{5,3},{6,4},{7,5},{8,6},{9,7},{10,... | collective-permute-start | bytes 589832 | tf_op jit(solution)/shard_map/ppermute | solution.py:400
  24.0 0.0 collective-permute-done.3.greens.g1
  24.0 2.3 %dress_partner.1 = (bf16[48,16384]{1,0:T(8,128)(2,1)S(1)}, bf16[48,8192]{1,0:T(8,128)(2,1)S(1)}) custom-call(s32[16,4]{1,0:T(8,128)S(1)} %copy.6.win, s32[1,4,4]{2,1,0:T(4,128)S(1)} %copy-done.2, bf16[1,48,128,128]{3,2,1,0:T(8,128)(2,1)S(1)} %copy-done, bf16[512,128]{1,0:T(8,128)(2,1)S(1)} %collective-permute-done.3.greens.g1), custom_call_target="tpu_custom_call" | custom-call | tf_op jit(solution)/shard_map/dress_partner/pallas_call | solution.py:376
  26.4 0.0 collective-permute-done.6.tensor
  26.4 2.4 %join_back.1 = f32[48,128]{1,0:T(8,128)S(1)} custom-call(bf16[24,128,128]{2,1,0:T(8,128)(2,1)S(1)} %collective-permute-done.6.tensor, bf16[272,128]{1,0:T(8,128)(2,1)S(1)} %collective-permute-done.g_before, bf16[512,128]{1,0:T(8,128)(2,1)S(1)} %choose.1.greens.g0, bf16[512,128]{1,0:T(8,128)(2,1)S(1)} %collective-permute-done.3.greens.g1, ...), custom_call_target="tpu_custom_call" | custom-call | tf_op jit(solution)/shard_map/join_back/pallas_call | solution.py:376
  28.7 0.9 %collective-permute-start.7 = (f32[48,128]{1,0:T(8,128)S(1)}, f32[48,128]{1,0:T(8,128)S(1)}, u32[]{:S(2)}, u32[]{:S(2)}) collective-permute-start(f32[48,128]{1,0:T(8,128)S(1)} %join_back.1), channel_id=1, source_target_pairs={{0,15},{1,0},{2,1},{3,2},{4,3},{5,4},{6,5},{7,6},{8,7},{9,8},{10,9... | collective-permute-start | bytes 73736 | tf_op jit(solution)/shard_map/ppermute | solution.py:400
  29.6 1.8 %join.1.down = f32[96,128]{1,0:T(8,128)S(1)} custom-call(s32[16,4]{1,0:T(8,128)S(1)} %copy.6.win, bf16[24,128,128]{2,1,0:T(8,128)(2,1)S(1)} %collective-permute-done.6.tensor, bf16[272,128]{1,0:T(8,128)(2,1)S(1)} %collective-permute-done.g_before, bf16[48,16384]{1,0:T(8,128)(2,1)S(1)} %get-tuple-element.47.dressed0, ...), custom_call_target="tpu_custom_call" | custom-call | flops 17179869184 | tf_op jit(solution)/shard_map/join/pallas_call | solution.py:376
  31.5 0.0 collective-permute-done.4.from_left
  31.5 2.3 %collective-permute-done.5.from_right = bf16[768,128]{1,0:T(8,128)(2,1)S(1)} collective-permute-done((bf16[768,128]{1,0:T(8,128)(2,1)S(1)}, bf16[768,128]{1,0:T(8,128)(2,1)S(1)}, u32[]{:S(2)}, u32[]{:S(2)}) %collective-permute-start.5) | collective-permute-done | bytes 196640 | tf_op jit(solution)/shard_map/ppermute | solution.py:400
  33.8 0.0 collective-permute-done.7.after
  33.8 0.7 %join_far.1 = (f32[48,128]{1,0:T(8,128)S(1)}, f32[48,128]{1,0:T(8,128)S(1)}) custom-call(bf16[48,8192]{1,0:T(8,128)(2,1)S(1)} %get-tuple-element.42.far0, bf16[48,8192]{1,0:T(8,128)(2,1)S(1)} %get-tuple-element.43.far1, bf16[768,128]{1,0:T(8,128)(2,1)S(1)} %collective-permute-done.4.from_left, bf16[768,128]{1,0:T(8,128)(2,1)S(1)} %collective-permute-done.5.from_right, ...), custom_call_target="tpu_custom_call" | custom-call | tf_op jit(solution)/shard_map/join_far/pallas_call | solution.py:376
  34.5 1.6 %collective-permute-start.8 = (f32[48,128]{1,0:T(8,128)S(1)}, f32[48,128]{1,0:T(8,128)S(1)}, u32[]{:S(2)}, u32[]{:S(2)}) collective-permute-start(f32[48,128]{1,0:T(8,128)S(1)} %get-tuple-element.50), channel_id=1, source_target_pairs={{0,16},{1,17},{2,18},{3,19},{4,20},{5,21},{6,22},{7,23},{8,24},{9,... | collective-permute-start | bytes 73736 | tf_op jit(solution)/shard_map/ppermute | solution.py:400
  36.0 2.3 %collective-permute-done.8.recv = f32[48,128]{1,0:T(8,128)S(1)} collective-permute-done((f32[48,128]{1,0:T(8,128)S(1)}, f32[48,128]{1,0:T(8,128)S(1)}, u32[]{:S(2)}, u32[]{:S(2)}) %collective-permute-start.8) | collective-permute-done | bytes 24608 | tf_op jit(solution)/shard_map/ppermute | solution.py:400
  38.4 0.7 %assemble.1 = f32[48,240]{1,0:T(8,128)} custom-call(f32[48,48]{1,0:T(8,128)S(1)} %get-tuple-element.41.polar0, f32[48,128]{1,0:T(8,128)S(1)} %get-tuple-element.49.own, f32[48,128]{1,0:T(8,128)S(1)} %collective-permute-done.8.recv), custom_call_target="tpu_custom_call" | custom-call | tf_op jit(solution)/shard_map/assemble/pallas_call | solution.py:376
Async XLA Ops:
  0.0 11.1 %copy-start.2 = (s32[1,4,4]{2,1,0:T(4,128)S(1)}, s32[1,4,4]{2,1,0:T(4,128)}, u32[]{:S(2)}) copy-start(s32[1,4,4]{2,1,0:T(4,128)} %tiles.5) | copy-start | bytes 196
  0.0 11.1 %copy-start = (bf16[1,48,128,128]{3,2,1,0:T(8,128)(2,1)S(1)}, bf16[1,48,128,128]{3,2,1,0:T(8,128)(2,1)}, u32[]{:S(2)}) copy-start(bf16[1,48,128,128]{3,2,1,0:T(8,128)(2,1)} %coulomb) | copy-start | bytes 4718596
  0.0 11.0 %copy-start.3 = (s32[16,4]{0,1:T(4,128)S(1)}, s32[16,4]{0,1:T(4,128)}, u32[]{:S(2)}) copy-start(s32[16,4]{0,1:T(4,128)} %param.9) | copy-start | bytes 772
  1.8 11.3 %collective-permute-start = (bf16[272,128]{1,0:T(8,128)(2,1)}, bf16[272,128]{1,0:T(8,128)(2,1)S(1)}, u32[]{:S(2)}, u32[]{:S(2)}) collective-permute-start(bf16[272,128]{1,0:T(8,128)(2,1)} %get-tuple-element.28), channel_id=1, source_target_pairs={{0,1},{1,2},{2,3},{3,4},{4,5},{5,6},{6,7},{7,8},{8,9},{9,10},{10,1... | collective-permute-start | bytes 208904 | tf_op jit(solution)/shard_map/ppermute | solution.py:400
  2.4 10.8 %collective-permute-start.2 = (bf16[288,128]{1,0:T(8,128)(2,1)}, bf16[288,128]{1,0:T(8,128)(2,1)S(1)}, u32[]{:S(2)}, u32[]{:S(2)}) collective-permute-start(bf16[288,128]{1,0:T(8,128)(2,1)} %get-tuple-element.30), channel_id=1, source_target_pairs={{0,2},{1,3},{2,4},{3,5},{4,6},{5,7},{6,8},{7,9},{8,10},{9,11},{10,... | collective-permute-start | bytes 221192 | tf_op jit(solution)/shard_map/ppermute | solution.py:400
  5.0 8.2 %collective-permute-start.1 = (bf16[304,128]{1,0:T(8,128)(2,1)}, bf16[304,128]{1,0:T(8,128)(2,1)S(1)}, u32[]{:S(2)}, u32[]{:S(2)}) collective-permute-start(bf16[304,128]{1,0:T(8,128)(2,1)} %get-tuple-element.29), channel_id=1, source_target_pairs={{0,15},{1,0},{2,1},{3,2},{4,3},{5,4},{6,5},{7,6},{8,7},{9,8},{10,9... | collective-permute-start | bytes 233480 | tf_op jit(solution)/shard_map/ppermute | solution.py:400
  11.0 15.4 %collective-permute-start.6 = (bf16[24,128,128]{2,1,0:T(8,128)(2,1)}, bf16[24,128,128]{2,1,0:T(8,128)(2,1)S(1)}, u32[]{:S(2)}, u32[]{:S(2)}) collective-permute-start(bf16[24,128,128]{2,1,0:T(8,128)(2,1)} %take_half.1), channel_id=1, source_target_pairs={{0,1},{1,2},{2,3},{3,4},{4,5},{5,6},{6,7},{7,8},{8,9},{9,10},{10,1... | collective-permute-start | bytes 2359304 | tf_op jit(solution)/shard_map/ppermute | solution.py:400
  11.1 2.0 %copy-start.1 = (bf16[256,128]{1,0:T(8,128)(2,1)S(1)}, bf16[256,128]{1,0:T(8,128)(2,1)}, u32[]{:S(2)}) copy-start(bf16[256,128]{1,0:T(8,128)(2,1)} %get-tuple-element.35.g_self) | copy-start | bytes 196612
  14.5 9.5 %collective-permute-start.3 = (bf16[512,128]{1,0:T(8,128)(2,1)S(1)}, bf16[512,128]{1,0:T(8,128)(2,1)S(1)}, u32[]{:S(2)}, u32[]{:S(2)}) collective-permute-start(bf16[512,128]{1,0:T(8,128)(2,1)S(1)} %choose.1.greens.g0), channel_id=1, source_target_pairs={{0,16},{1,17},{2,18},{3,19},{4,20},{5,21},{6,22},{7,23},{8,24},{9,... | collective-permute-start | bytes 393224 | tf_op jit(solution)/shard_map/ppermute | solution.py:400
  19.3 12.2 %collective-permute-start.4 = (bf16[768,128]{1,0:T(8,128)(2,1)S(1)}, bf16[768,128]{1,0:T(8,128)(2,1)S(1)}, u32[]{:S(2)}, u32[]{:S(2)}) collective-permute-start(bf16[768,128]{1,0:T(8,128)(2,1)S(1)} %get-tuple-element.44), channel_id=1, source_target_pairs={{0,2},{1,3},{2,4},{3,5},{4,6},{5,7},{6,8},{7,9},{8,10},{9,11},{10,... | collective-permute-start | bytes 589832 | tf_op jit(solution)/shard_map/ppermute | solution.py:400
  19.3 14.4 %collective-permute-start.5 = (bf16[768,128]{1,0:T(8,128)(2,1)S(1)}, bf16[768,128]{1,0:T(8,128)(2,1)S(1)}, u32[]{:S(2)}, u32[]{:S(2)}) collective-permute-start(bf16[768,128]{1,0:T(8,128)(2,1)S(1)} %get-tuple-element.45), channel_id=1, source_target_pairs={{0,14},{1,15},{2,0},{3,1},{4,2},{5,3},{6,4},{7,5},{8,6},{9,7},{10,... | collective-permute-start | bytes 589832 | tf_op jit(solution)/shard_map/ppermute | solution.py:400
  28.7 5.0 %collective-permute-start.7 = (f32[48,128]{1,0:T(8,128)S(1)}, f32[48,128]{1,0:T(8,128)S(1)}, u32[]{:S(2)}, u32[]{:S(2)}) collective-permute-start(f32[48,128]{1,0:T(8,128)S(1)} %join_back.1), channel_id=1, source_target_pairs={{0,15},{1,0},{2,1},{3,2},{4,3},{5,4},{6,5},{7,6},{8,7},{9,8},{10,9... | collective-permute-start | bytes 73736 | tf_op jit(solution)/shard_map/ppermute | solution.py:400
  34.5 3.9 %collective-permute-start.8 = (f32[48,128]{1,0:T(8,128)S(1)}, f32[48,128]{1,0:T(8,128)S(1)}, u32[]{:S(2)}, u32[]{:S(2)}) collective-permute-start(f32[48,128]{1,0:T(8,128)S(1)} %get-tuple-element.50), channel_id=1, source_target_pairs={{0,16},{1,17},{2,18},{3,19},{4,20},{5,21},{6,22},{7,23},{8,24},{9,... | collective-permute-start | bytes 73736 | tf_op jit(solution)/shard_map/ppermute | solution.py:400

commit v11 on v9

--- a/solution.py
+++ b/solution.py
@@ -67,13 +67,10 @@
     return near(row, -1, count) >> 1
 
 
-def first(count, occ, virt, tiles_hbm, coulomb, *refs):
-    outs, (tiles, gs, part, sem, done) = refs[:5], refs[5:]
+def first(count, occ, virt, tiles_hbm, *refs):
+    outs, (tiles, gs, sem, done) = refs[:4], refs[4:]
     d = lax.axis_index("row")
-    funcs = part.shape[0]
-    half = lax.rem(lax.axis_index("grp"), 2)
     list_copy = pltpu.make_async_copy(tiles_hbm, tiles, sem.at[16])
-    list_copy.start()
     groups = []
     for n, by in enumerate((0, 1, -1, 2)):
         start = column_chunk(near(d, by, count), count)
@@ -87,11 +84,7 @@
                 copies.append(pltpu.make_async_copy(green.at[:, columns], place, sem.at[4 * n + len(copies)]))
         rows = outs[n].shape[0]
         groups.append((copies, pltpu.make_async_copy(gs.at[n, 0:rows], outs[n], done.at[n])))
-    for n in range(3):
-        piece = pl.ds(half * funcs + n * 8, 8)
-        copy = pltpu.make_async_copy(coulomb.at[0, piece], part.at[n * 8 : n * 8 + 8], sem.at[17 + n])
-        out = pltpu.make_async_copy(part.at[n * 8 : n * 8 + 8], outs[4].at[n * 8 : n * 8 + 8], done.at[4 + n])
-        groups.append(([copy], out))
+    list_copy.start()
     for copies, _ in groups:
         for copy in copies:
             copy.start()
@@ -108,12 +101,14 @@
         out.wait()
 
 
-def far_tiles(count, win, tiles, tensor, far_right, far_left, flat, mask, ms):
+def far_tiles(count, win, tiles, tensor, far_right, far_left, part, mask):
     d = lax.axis_index("row")
     mine = window_at(win, d)
     funcs = tensor.shape[1] // 2
     start = lax.rem(lax.axis_index("grp"), 2) * funcs
     mask[...] = tile_mask(tiles, 32).astype(BF)
+    for r in range(funcs):
+        part[r] = tensor[0, start + r]
     for by, out in ((-1, far_left), (1, far_right)):
         base = near(d, by, count) * 2
         shape = (256, 128)
@@ -132,11 +127,15 @@
             ]
             x = dot(jnp.concatenate(sides, axis=1), select)
             out[r * 32 : r * 32 + 256, :] = x.astype(BF)
-    whole = mask[...]
-    for r in range(2 * funcs):
-        ms[r * PITCH : r * PITCH + 128, :] = (tensor[0, r] * whole).astype(F32)
+
+
+def flatten(tiles, tensor, flat, ms):
+    funcs = tensor.shape[1]
+    mask = tile_mask(tiles, 32).astype(BF)
+    for r in range(funcs):
+        ms[r * PITCH : r * PITCH + 128, :] = (tensor[0, r] * mask).astype(F32)
     for m in range(128):
-        rows = ms[pl.ds(m, 2 * funcs, stride=PITCH), :]
+        rows = ms[pl.ds(m, funcs, stride=PITCH), :]
         flat[:, m * 128 : (m + 1) * 128] = rows.astype(BF)
 
 
@@ -390,24 +389,22 @@
         return lax.ppermute(array, ("grp", "row"), pairs)
 
     far_rows = funcs * 32
-    g_self, g_right, g_left, g_far, tensor = call(
+    g_self, g_right, g_left, g_far = call(
         functools.partial(first, count),
         "first",
-        hbm(4),
+        hbm(3),
         [
             shape((256, 128), BF),
             shape((272, 128), BF),
             shape((304, 128), BF),
             shape((288, 128), BF),
-            shape((funcs, 128, 128), BF),
         ],
-        (green_occ, green_virt, tile_list, coulomb3c),
+        (green_occ, green_virt, tile_list),
         [
             pltpu.SMEM((1, 4, 4), jnp.int32),
             pltpu.VMEM((4, 304, 128), BF),
-            pltpu.VMEM((funcs, 128, 128), BF),
-            pltpu.SemaphoreType.DMA((20,)),
-            pltpu.SemaphoreType.DMA((7,)),
+            pltpu.SemaphoreType.DMA((17,)),
+            pltpu.SemaphoreType.DMA((4,)),
         ],
         limit=60 << 20,
         space=hbm,
@@ -415,34 +412,41 @@
     g_before = send(g_right, 1)
     g_beyond = send(g_far, 2)
     g_after = send(g_left, -1)
-    wide = send(tensor, 1)
     flat_shape, far_shape = shape((full, 128 * 128), BF), shape((full, 64 * 128), BF)
     tall = pltpu.VMEM((full * PITCH, 128), F32)
     short = pltpu.VMEM((funcs * PITCH, 128), F32)
     message = shape((full, 128), F32)
-    far_right, far_left, flat = call(
+    far_right, far_left, tensor = call(
         functools.partial(far_tiles, count),
         "far_tiles",
         smem(2) + vmem(1),
-        [shape((far_rows, 128), BF), shape((far_rows, 128), BF), flat_shape],
+        [shape((far_rows, 128), BF), shape((far_rows, 128), BF), shape((funcs, 128, 128), BF)],
         (window, tile_list, coulomb3c),
-        [pltpu.VMEM((128, 128), BF), tall],
+        [pltpu.VMEM((128, 128), BF)],
+    )
+    from_right = send(far_left, -2)
+    wide = send(tensor, 1)
+    here, _ = lax.optimization_barrier((tile_list, far_left))
+    (flat,) = call(
+        flatten,
+        "flatten",
+        smem(1) + vmem(1),
+        [flat_shape],
+        (here, coulomb3c),
+        [tall],
         flops=1 << 36,
     )
-    g_before, g_after, g_beyond, far_right, far_left = lax.optimization_barrier(
-        (g_before, g_after, g_beyond, far_right, far_left)
-    )
+    g_before, g_after, g_far, flat = lax.optimization_barrier((g_before, g_after, g_beyond, flat))
     (mine,) = call(
         functools.partial(choose, count),
         "choose",
         smem(1) + vmem(4),
         [shape((512, 128), BF)],
-        (window, g_self, g_before, g_after, g_beyond),
+        (window, g_self, g_before, g_after, g_far),
     )
     partner = send(mine, 0, True)
-    far_right, far_left, mine = lax.optimization_barrier((far_right, far_left, mine))
+    far_right, mine = lax.optimization_barrier((far_right, mine))
     from_left = send(far_right, 2)
-    from_right = send(far_left, -2)
     polar0, dressed0, far0 = call(
         functools.partial(dress, count, True),
         "dress_own",
@@ -451,6 +455,7 @@
         (window, tile_list, coulomb3c, mine, flat),
         [tall, pltpu.VMEM((full, 128 * 128), BF)],
     )
+    partner, from_right = lax.optimization_barrier((partner, from_right))
     dressed1, far1 = call(
         functools.partial(dress, count, False),
         "dress_partner",

time: 37.8 us -> 40.8 us (1.079)
  the two profiles are of different devices: /device:TPU:0 before, /device:TPU:15 now
where the time goes in v11:
time: 40.8 us; the launch traced here: 40.6 us
  Pallas kernels  16.9 us (41%)
  starting transfers between devices  14.3 us (35%)
  waiting for transfers between devices  6.41 us (16%)
  local copies, waits for them, and re-layouts  2.85 us (7%)
    pallas_call x10, Pallas kernels, call(): pl.pallas_call(kernel, name=name, in_specs=specs, out_specs=tuple((space...  16.9 us
    ppermute x9, starting transfers between devices, send(): return lax.ppermute(array, ('grp', 'row'), pairs)  14.3 us
    ppermute x9, waiting for transfers between devices, send(): return lax.ppermute(array, ('grp', 'row'), pairs)  6.41 us
    unnamed x9, local copies, waits for them, and re-layouts  2.85 us
  transfers between devices with their start and end apart: 9, of which 4 were waited for; matrix products, arithmetic and copies ran while one was open for 2% of the time, Pallas kernels for 34%

profile of v11, /device:TPU:15, one launch (start us, length us, event | category | flops | bytes accessed | tf_op | source)
XLA Modules:
  0.0 40.6 jit_solution(15374600833192843002)
XLA Ops:
  0.0 1.8 %first.1 = (bf16[256,128]{1,0:T(8,128)(2,1)}, bf16[272,128]{1,0:T(8,128)(2,1)}, bf16[304,128]{1,0:T(8,128)(2,1)}, bf16[288,128]{1,0:T(8,128)(2,1)}) custom-call(bf16[64,1024]{1,0:T(8,128)(2,1)} %occ.1, bf16[64,1024]{1,0:T(8,128)(2,1)} %virt.1, s32[1,4,4]{2,1,0:T(4,128)} %tiles.6), custom_call_target="tpu_custom_call" | custom-call | tf_op jit(solution)/shard_map/first/pallas_call | solution.py:365
  1.8 1.9 %collective-permute-start = (bf16[272,128]{1,0:T(8,128)(2,1)}, bf16[272,128]{1,0:T(8,128)(2,1)S(1)}, u32[]{:S(2)}, u32[]{:S(2)}) collective-permute-start(bf16[272,128]{1,0:T(8,128)(2,1)} %get-tuple-element.30), channel_id=1, source_target_pairs={{0,1},{1,2},{2,3},{3,4},{4,5},{5,6},{6,7},{7,8},{8,9},{9,10},{10,1... | collective-permute-start | bytes 208904 | tf_op jit(solution)/shard_map/ppermute | solution.py:389
  3.7 1.3 %collective-permute-start.2 = (bf16[288,128]{1,0:T(8,128)(2,1)}, bf16[288,128]{1,0:T(8,128)(2,1)S(1)}, u32[]{:S(2)}, u32[]{:S(2)}) collective-permute-start(bf16[288,128]{1,0:T(8,128)(2,1)} %get-tuple-element.32), channel_id=1, source_target_pairs={{0,2},{1,3},{2,4},{3,5},{4,6},{5,7},{6,8},{7,9},{8,10},{9,11},{10,... | collective-permute-start | bytes 221192 | tf_op jit(solution)/shard_map/ppermute | solution.py:389
  5.0 0.0 collective-permute-start.1
  5.0 0.8 %copy.8.win = s32[16,4]{1,0:T(8,128)S(1)} copy(s32[16,4]{0,1:T(4,128)} %param.9) | data formatting | bytes 512 | tf_op args[4]
  5.8 0.0 copy-start
  5.8 1.4 %copy-done = bf16[1,48,128,128]{3,2,1,0:T(8,128)(2,1)S(1)} copy-done((bf16[1,48,128,128]{3,2,1,0:T(8,128)(2,1)S(1)}, bf16[1,48,128,128]{3,2,1,0:T(8,128)(2,1)}, u32[]{:S(2)}) %copy-start) | copy-done | bytes 1572888
  7.2 0.0 copy-start.3
  7.2 0.7 %copy-done.3 = s32[1,4,4]{2,1,0:T(4,128)S(1)} copy-done((s32[1,4,4]{2,1,0:T(4,128)S(1)}, s32[1,4,4]{2,1,0:T(4,128)}, u32[]{:S(2)}) %copy-start.3) | copy-done | bytes 88
  7.8 0.0 copy-start.1
  7.9 1.2 %far_tiles.1 = (bf16[768,128]{1,0:T(8,128)(2,1)S(1)}, bf16[768,128]{1,0:T(8,128)(2,1)S(1)}, bf16[24,128,128]{2,1,0:T(8,128)(2,1)S(1)}) custom-call(s32[16,4]{1,0:T(8,128)S(1)} %copy.8.win, s32[1,4,4]{2,1,0:T(4,128)S(1)} %copy-done.3, bf16[1,48,128,128]{3,2,1,0:T(8,128)(2,1)S(1)} %copy-done), custom_call_target="tpu_custom_call" | custom-call | tf_op jit(solution)/shard_map/far_tiles/pallas_call | solution.py:365
  9.0 0.2 collective-permute-start.4
  9.3 0.0 copy-start.2
  9.3 2.9 %collective-permute-start.6 = (bf16[24,128,128]{2,1,0:T(8,128)(2,1)S(1)}, bf16[24,128,128]{2,1,0:T(8,128)(2,1)S(1)}, u32[]{:S(2)}, u32[]{:S(2)}) collective-permute-start(bf16[24,128,128]{2,1,0:T(8,128)(2,1)S(1)} %get-tuple-element.46), channel_id=1, source_target_pairs={{0,1},{1,2},{2,3},{3,4},{4,5},{5,6},{6,7},{7,8},{8,9},{9,10},{10,1... | collective-permute-start | bytes 2359304 | tf_op jit(solution)/shard_map/ppermute | solution.py:389
  12.2 0.0 copy-done.1
  12.2 1.4 %flatten.1.refs_0_.flat = bf16[48,16384]{1,0:T(8,128)(2,1)S(1)} custom-call(s32[1,4,4]{2,1,0:T(4,128)S(1)} %copy-done.3, bf16[1,48,128,128]{3,2,1,0:T(8,128)(2,1)S(1)} %copy-done.1), custom_call_target="tpu_custom_call" | custom-call | flops 68719476736 | tf_op jit(solution)/shard_map/flatten/pallas_call | solution.py:365
  13.6 0.0 collective-permute-done.g_before
  13.6 0.0 collective-permute-done.2.g_far
  13.6 0.0 collective-permute-done.1.g_after
  13.6 0.0 copy-done.2
  13.7 1.3 %choose.1.greens.g0 = bf16[512,128]{1,0:T(8,128)(2,1)S(1)} custom-call(s32[16,4]{1,0:T(8,128)S(1)} %copy.8.win, bf16[256,128]{1,0:T(8,128)(2,1)S(1)} %copy-done.2, bf16[272,128]{1,0:T(8,128)(2,1)S(1)} %collective-permute-done.g_before, bf16[304,128]{1,0:T(8,128)(2,1)S(1)} %collective-permute-done.1.g_after, bf16[288,128]{1,0:T(8,128)(2,1)S(1)} %collective-permute-done.2.g_far), custom_call_target="tpu_custom_call" | custom-call | tf_op jit(solution)/shard_map/choose/pallas_call | solution.py:365
  15.0 0.3 collective-permute-start.3
  15.3 1.3 %collective-permute-start.5 = (bf16[768,128]{1,0:T(8,128)(2,1)S(1)}, bf16[768,128]{1,0:T(8,128)(2,1)S(1)}, u32[]{:S(2)}, u32[]{:S(2)}) collective-permute-start(bf16[768,128]{1,0:T(8,128)(2,1)S(1)} %get-tuple-element.44), channel_id=1, source_target_pairs={{0,2},{1,3},{2,4},{3,5},{4,6},{5,7},{6,8},{7,9},{8,10},{9,11},{10,... | collective-permute-start | bytes 589832 | tf_op jit(solution)/shard_map/ppermute | solution.py:389
  16.6 3.2 %dress_own.1 = (f32[48,48]{1,0:T(8,128)S(1)}, bf16[48,16384]{1,0:T(8,128)(2,1)S(1)}, bf16[48,8192]{1,0:T(8,128)(2,1)S(1)}) custom-call(s32[16,4]{1,0:T(8,128)S(1)} %copy.8.win, s32[1,4,4]{2,1,0:T(4,128)S(1)} %copy-done.3, bf16[1,48,128,128]{3,2,1,0:T(8,128)(2,1)S(1)} %copy-done.1, bf16[512,128]{1,0:T(8,128)(2,1)S(1)} %choose.1.greens.g0, ...), custom_call_target="tpu_custom_call" | custom-call | tf_op jit(solution)/shard_map/dress_own/pallas_call | solution.py:365
  19.8 0.0 collective-permute-done.4.from_right
  19.8 0.1 collective-permute-done.3.greens.g1
  19.9 2.3 %dress_partner.1 = (bf16[48,16384]{1,0:T(8,128)(2,1)S(1)}, bf16[48,8192]{1,0:T(8,128)(2,1)S(1)}) custom-call(s32[16,4]{1,0:T(8,128)S(1)} %copy.8.win, s32[1,4,4]{2,1,0:T(4,128)S(1)} %copy-done.3, bf16[1,48,128,128]{3,2,1,0:T(8,128)(2,1)S(1)} %copy-done.1, bf16[512,128]{1,0:T(8,128)(2,1)S(1)} %collective-permute-done.3.greens.g1), custom_call_target="tpu_custom_call" | custom-call | tf_op jit(solution)/shard_map/dress_partner/pallas_call | solution.py:365
  22.2 1.1 %collective-permute-done.6.tensor = bf16[24,128,128]{2,1,0:T(8,128)(2,1)S(1)} collective-permute-done((bf16[24,128,128]{2,1,0:T(8,128)(2,1)S(1)}, bf16[24,128,128]{2,1,0:T(8,128)(2,1)S(1)}, u32[]{:S(2)}, u32[]{:S(2)}) %collective-permute-start.6) | collective-permute-done | bytes 786464 | tf_op jit(solution)/shard_map/ppermute | solution.py:389
  23.3 2.4 %join_back.1 = f32[48,128]{1,0:T(8,128)S(1)} custom-call(bf16[24,128,128]{2,1,0:T(8,128)(2,1)S(1)} %collective-permute-done.6.tensor, bf16[272,128]{1,0:T(8,128)(2,1)S(1)} %collective-permute-done.g_before, bf16[512,128]{1,0:T(8,128)(2,1)S(1)} %choose.1.greens.g0, bf16[512,128]{1,0:T(8,128)(2,1)S(1)} %collective-permute-done.3.greens.g1, ...), custom_call_target="tpu_custom_call" | custom-call | tf_op jit(solution)/shard_map/join_back/pallas_call | solution.py:365
  25.7 6.1 %collective-permute-start.7 = (f32[48,128]{1,0:T(8,128)S(1)}, f32[48,128]{1,0:T(8,128)S(1)}, u32[]{:S(2)}, u32[]{:S(2)}) collective-permute-start(f32[48,128]{1,0:T(8,128)S(1)} %join_back.1), channel_id=1, source_target_pairs={{0,15},{1,0},{2,1},{3,2},{4,3},{5,4},{6,5},{7,6},{8,7},{9,8},{10,9... | collective-permute-start | bytes 73736 | tf_op jit(solution)/shard_map/ppermute | solution.py:389
  31.7 1.8 %join.1.down = f32[96,128]{1,0:T(8,128)S(1)} custom-call(s32[16,4]{1,0:T(8,128)S(1)} %copy.8.win, bf16[24,128,128]{2,1,0:T(8,128)(2,1)S(1)} %collective-permute-done.6.tensor, bf16[272,128]{1,0:T(8,128)(2,1)S(1)} %collective-permute-done.g_before, bf16[48,16384]{1,0:T(8,128)(2,1)S(1)} %get-tuple-element.47.dressed0, ...), custom_call_target="tpu_custom_call" | custom-call | flops 17179869184 | tf_op jit(solution)/shard_map/join/pallas_call | solution.py:365
  33.6 0.0 collective-permute-done.5.from_left
  33.6 2.8 %collective-permute-done.7.after = f32[48,128]{1,0:T(8,128)S(1)} collective-permute-done((f32[48,128]{1,0:T(8,128)S(1)}, f32[48,128]{1,0:T(8,128)S(1)}, u32[]{:S(2)}, u32[]{:S(2)}) %collective-permute-start.7) | collective-permute-done | bytes 24608 | tf_op jit(solution)/shard_map/ppermute | solution.py:389
  36.4 0.7 %join_far.1 = (f32[48,128]{1,0:T(8,128)S(1)}, f32[48,128]{1,0:T(8,128)S(1)}) custom-call(bf16[48,8192]{1,0:T(8,128)(2,1)S(1)} %get-tuple-element.41.far0, bf16[48,8192]{1,0:T(8,128)(2,1)S(1)} %get-tuple-element.43.far1, bf16[768,128]{1,0:T(8,128)(2,1)S(1)} %collective-permute-done.5.from_left, bf16[768,128]{1,0:T(8,128)(2,1)S(1)} %collective-permute-done.4.from_right, ...), custom_call_target="tpu_custom_call" | custom-call | tf_op jit(solution)/shard_map/join_far/pallas_call | solution.py:365
  37.1 0.3 collective-permute-start.8
  37.4 2.4 %collective-permute-done.8.recv = f32[48,128]{1,0:T(8,128)S(1)} collective-permute-done((f32[48,128]{1,0:T(8,128)S(1)}, f32[48,128]{1,0:T(8,128)S(1)}, u32[]{:S(2)}, u32[]{:S(2)}) %collective-permute-start.8) | collective-permute-done | bytes 24608 | tf_op jit(solution)/shard_map/ppermute | solution.py:389
  39.8 0.7 %assemble.1 = f32[48,240]{1,0:T(8,128)} custom-call(f32[48,48]{1,0:T(8,128)S(1)} %get-tuple-element.40.polar0, f32[48,128]{1,0:T(8,128)S(1)} %get-tuple-element.49.own, f32[48,128]{1,0:T(8,128)S(1)} %collective-permute-done.8.recv), custom_call_target="tpu_custom_call" | custom-call | tf_op jit(solution)/shard_map/assemble/pallas_call | solution.py:365
Async XLA Ops:
  1.8 11.8 %collective-permute-start = (bf16[272,128]{1,0:T(8,128)(2,1)}, bf16[272,128]{1,0:T(8,128)(2,1)S(1)}, u32[]{:S(2)}, u32[]{:S(2)}) collective-permute-start(bf16[272,128]{1,0:T(8,128)(2,1)} %get-tuple-element.30), channel_id=1, source_target_pairs={{0,1},{1,2},{2,3},{3,4},{4,5},{5,6},{6,7},{7,8},{8,9},{9,10},{10,1... | collective-permute-start | bytes 208904 | tf_op jit(solution)/shard_map/ppermute | solution.py:389
  3.7 9.9 %collective-permute-start.2 = (bf16[288,128]{1,0:T(8,128)(2,1)}, bf16[288,128]{1,0:T(8,128)(2,1)S(1)}, u32[]{:S(2)}, u32[]{:S(2)}) collective-permute-start(bf16[288,128]{1,0:T(8,128)(2,1)} %get-tuple-element.32), channel_id=1, source_target_pairs={{0,2},{1,3},{2,4},{3,5},{4,6},{5,7},{6,8},{7,9},{8,10},{9,11},{10,... | collective-permute-start | bytes 221192 | tf_op jit(solution)/shard_map/ppermute | solution.py:389
  5.0 8.6 %collective-permute-start.1 = (bf16[304,128]{1,0:T(8,128)(2,1)}, bf16[304,128]{1,0:T(8,128)(2,1)S(1)}, u32[]{:S(2)}, u32[]{:S(2)}) collective-permute-start(bf16[304,128]{1,0:T(8,128)(2,1)} %get-tuple-element.31), channel_id=1, source_target_pairs={{0,15},{1,0},{2,1},{3,2},{4,3},{5,4},{6,5},{7,6},{8,7},{9,8},{10,9... | collective-permute-start | bytes 233480 | tf_op jit(solution)/shard_map/ppermute | solution.py:389
  5.8 1.4 %copy-start = (bf16[1,48,128,128]{3,2,1,0:T(8,128)(2,1)S(1)}, bf16[1,48,128,128]{3,2,1,0:T(8,128)(2,1)}, u32[]{:S(2)}) copy-start(bf16[1,48,128,128]{3,2,1,0:T(8,128)(2,1)} %tensor.7) | copy-start | bytes 4718596
  7.2 0.7 %copy-start.3 = (s32[1,4,4]{2,1,0:T(4,128)S(1)}, s32[1,4,4]{2,1,0:T(4,128)}, u32[]{:S(2)}) copy-start(s32[1,4,4]{2,1,0:T(4,128)} %tiles.6) | copy-start | bytes 196
  7.8 4.4 %copy-start.1 = (bf16[1,48,128,128]{3,2,1,0:T(8,128)(2,1)S(1)}, bf16[1,48,128,128]{3,2,1,0:T(8,128)(2,1)}, u32[]{:S(2)}) copy-start(bf16[1,48,128,128]{3,2,1,0:T(8,128)(2,1)} %tensor.7) | copy-start | bytes 4718596
  9.0 10.8 %collective-permute-start.4 = (bf16[768,128]{1,0:T(8,128)(2,1)S(1)}, bf16[768,128]{1,0:T(8,128)(2,1)S(1)}, u32[]{:S(2)}, u32[]{:S(2)}) collective-permute-start(bf16[768,128]{1,0:T(8,128)(2,1)S(1)} %get-tuple-element.33), channel_id=1, source_target_pairs={{0,14},{1,15},{2,0},{3,1},{4,2},{5,3},{6,4},{7,5},{8,6},{9,7},{10,... | collective-permute-start | bytes 589832 | tf_op jit(solution)/shard_map/ppermute | solution.py:389
  9.3 4.4 %copy-start.2 = (bf16[256,128]{1,0:T(8,128)(2,1)S(1)}, bf16[256,128]{1,0:T(8,128)(2,1)}, u32[]{:S(2)}) copy-start(bf16[256,128]{1,0:T(8,128)(2,1)} %get-tuple-element.29.g_self) | copy-start | bytes 196612
  9.3 14.0 %collective-permute-start.6 = (bf16[24,128,128]{2,1,0:T(8,128)(2,1)S(1)}, bf16[24,128,128]{2,1,0:T(8,128)(2,1)S(1)}, u32[]{:S(2)}, u32[]{:S(2)}) collective-permute-start(bf16[24,128,128]{2,1,0:T(8,128)(2,1)S(1)} %get-tuple-element.46), channel_id=1, source_target_pairs={{0,1},{1,2},{2,3},{3,4},{4,5},{5,6},{6,7},{7,8},{8,9},{9,10},{10,1... | collective-permute-start | bytes 2359304 | tf_op jit(solution)/shard_map/ppermute | solution.py:389
  15.0 4.9 %collective-permute-start.3 = (bf16[512,128]{1,0:T(8,128)(2,1)S(1)}, bf16[512,128]{1,0:T(8,128)(2,1)S(1)}, u32[]{:S(2)}, u32[]{:S(2)}) collective-permute-start(bf16[512,128]{1,0:T(8,128)(2,1)S(1)} %choose.1.greens.g0), channel_id=1, source_target_pairs={{0,16},{1,17},{2,18},{3,19},{4,20},{5,21},{6,22},{7,23},{8,24},{9,... | collective-permute-start | bytes 393224 | tf_op jit(solution)/shard_map/ppermute | solution.py:389
  15.3 18.3 %collective-permute-start.5 = (bf16[768,128]{1,0:T(8,128)(2,1)S(1)}, bf16[768,128]{1,0:T(8,128)(2,1)S(1)}, u32[]{:S(2)}, u32[]{:S(2)}) collective-permute-start(bf16[768,128]{1,0:T(8,128)(2,1)S(1)} %get-tuple-element.44), channel_id=1, source_target_pairs={{0,2},{1,3},{2,4},{3,5},{4,6},{5,7},{6,8},{7,9},{8,10},{9,11},{10,... | collective-permute-start | bytes 589832 | tf_op jit(solution)/shard_map/ppermute | solution.py:389
  25.7 10.7 %collective-permute-start.7 = (f32[48,128]{1,0:T(8,128)S(1)}, f32[48,128]{1,0:T(8,128)S(1)}, u32[]{:S(2)}, u32[]{:S(2)}) collective-permute-start(f32[48,128]{1,0:T(8,128)S(1)} %join_back.1), channel_id=1, source_target_pairs={{0,15},{1,0},{2,1},{3,2},{4,3},{5,4},{6,5},{7,6},{8,7},{9,8},{10,9... | collective-permute-start | bytes 73736 | tf_op jit(solution)/shard_map/ppermute | solution.py:389
  37.1 2.7 %collective-permute-start.8 = (f32[48,128]{1,0:T(8,128)S(1)}, f32[48,128]{1,0:T(8,128)S(1)}, u32[]{:S(2)}, u32[]{:S(2)}) collective-permute-start(f32[48,128]{1,0:T(8,128)S(1)} %get-tuple-element.50), channel_id=1, source_target_pairs={{0,16},{1,17},{2,18},{3,19},{4,20},{5,21},{6,22},{7,23},{8,24},{9,... | collective-permute-start | bytes 73736 | tf_op jit(solution)/shard_map/ppermute | solution.py:389

commit v12 on v9

--- a/solution.py
+++ b/solution.py
@@ -440,9 +440,8 @@
         (window, g_self, g_before, g_after, g_beyond),
     )
     partner = send(mine, 0, True)
-    far_right, far_left, mine = lax.optimization_barrier((far_right, far_left, mine))
+    far_right, mine = lax.optimization_barrier((far_right, mine))
     from_left = send(far_right, 2)
-    from_right = send(far_left, -2)
     polar0, dressed0, far0 = call(
         functools.partial(dress, count, True),
         "dress_own",
@@ -451,6 +450,8 @@
         (window, tile_list, coulomb3c, mine, flat),
         [tall, pltpu.VMEM((full, 128 * 128), BF)],
     )
+    far_left, polar0 = lax.optimization_barrier((far_left, polar0))
+    from_right = send(far_left, -2)
     dressed1, far1 = call(
         functools.partial(dress, count, False),
         "dress_partner",

time: 37.8 us -> 37.8 us (level)
  no operation moved by 1% of the time
where the time goes in v12:
time: 37.8 us; the launch traced here: 37.7 us
  Pallas kernels  16.9 us (45%)
  starting transfers between devices  15.1 us (40%)
  waiting for transfers between devices  5.52 us (15%)
    pallas_call x9, Pallas kernels, call(): pl.pallas_call(kernel, name=name, in_specs=specs, out_specs=tuple((space...  16.9 us
    ppermute x9, starting transfers between devices, send(): return lax.ppermute(array, ('grp', 'row'), pairs)  15.1 us
    ppermute x9, waiting for transfers between devices, send(): return lax.ppermute(array, ('grp', 'row'), pairs)  5.52 us
  transfers between devices with their start and end apart: 9, of which 4 were waited for; matrix products, arithmetic and copies ran while one was open for 0% of the time, Pallas kernels for 35%

profile of v12, /device:TPU:0, one launch (start us, length us, event | category | flops | bytes accessed | tf_op | source)
XLA Modules:
  0.0 37.7 jit_solution(4346854894193044216)
XLA Ops:
  0.0 0.0 copy-start.2
  0.0 0.0 copy-start
  0.0 0.0 copy-start.3
  0.0 2.4 %first.1 = (bf16[256,128]{1,0:T(8,128)(2,1)}, bf16[272,128]{1,0:T(8,128)(2,1)}, bf16[304,128]{1,0:T(8,128)(2,1)}, bf16[288,128]{1,0:T(8,128)(2,1)}, bf16[24,128,128]{2,1,0:T(8,128)(2,1)}) custom-call(bf16[64,1024]{1,0:T(8,128)(2,1)} %occ.1, bf16[64,1024]{1,0:T(8,128)(2,1)} %virt.1, s32[1,4,4]{2,1,0:T(4,128)} %tiles.5, bf16[1,48,128,128]{3,2,1,0:T(8,128)(2,1)} %tensor.5), custom_call_target="tpu_custom_call" | custom-call | tf_op jit(solution)/shard_map/first/pallas_call | solution.py:366
  2.4 0.5 %collective-permute-start = (bf16[272,128]{1,0:T(8,128)(2,1)}, bf16[272,128]{1,0:T(8,128)(2,1)S(1)}, u32[]{:S(2)}, u32[]{:S(2)}) collective-permute-start(bf16[272,128]{1,0:T(8,128)(2,1)} %get-tuple-element.29), channel_id=1, source_target_pairs={{0,1},{1,2},{2,3},{3,4},{4,5},{5,6},{6,7},{7,8},{8,9},{9,10},{10,1... | collective-permute-start | bytes 208904 | tf_op jit(solution)/shard_map/ppermute | solution.py:390
  2.9 2.6 %collective-permute-start.2 = (bf16[288,128]{1,0:T(8,128)(2,1)}, bf16[288,128]{1,0:T(8,128)(2,1)S(1)}, u32[]{:S(2)}, u32[]{:S(2)}) collective-permute-start(bf16[288,128]{1,0:T(8,128)(2,1)} %get-tuple-element.31), channel_id=1, source_target_pairs={{0,2},{1,3},{2,4},{3,5},{4,6},{5,7},{6,8},{7,9},{8,10},{9,11},{10,... | collective-permute-start | bytes 221192 | tf_op jit(solution)/shard_map/ppermute | solution.py:390
  5.5 4.1 %collective-permute-start.1 = (bf16[304,128]{1,0:T(8,128)(2,1)}, bf16[304,128]{1,0:T(8,128)(2,1)S(1)}, u32[]{:S(2)}, u32[]{:S(2)}) collective-permute-start(bf16[304,128]{1,0:T(8,128)(2,1)} %get-tuple-element.30), channel_id=1, source_target_pairs={{0,15},{1,0},{2,1},{3,2},{4,3},{5,4},{6,5},{7,6},{8,7},{9,8},{10,9... | collective-permute-start | bytes 233480 | tf_op jit(solution)/shard_map/ppermute | solution.py:390
  9.6 0.0 collective-permute-start.6
  9.6 0.0 copy-done.3
  9.6 0.1 copy.6.win
  9.7 0.0 copy-done.2
  9.7 0.0 copy-done
  9.7 0.0 copy-start.1
  9.7 2.0 %far_tiles.1 = (bf16[768,128]{1,0:T(8,128)(2,1)S(1)}, bf16[768,128]{1,0:T(8,128)(2,1)S(1)}, bf16[48,16384]{1,0:T(8,128)(2,1)S(1)}) custom-call(s32[16,4]{1,0:T(8,128)S(1)} %copy.6.win, s32[1,4,4]{2,1,0:T(4,128)S(1)} %copy-done.2, bf16[1,48,128,128]{3,2,1,0:T(8,128)(2,1)S(1)} %copy-done), custom_call_target="tpu_custom_call" | custom-call | flops 68719476736 | tf_op jit(solution)/shard_map/far_tiles/pallas_call | solution.py:366
  11.7 0.0 collective-permute-done.g_before
  11.7 0.0 collective-permute-done.2.g_far
  11.7 0.2 collective-permute-done.1.g_after
  11.9 0.0 copy-done.1
  11.9 1.3 %choose.1.greens.g0 = bf16[512,128]{1,0:T(8,128)(2,1)S(1)} custom-call(s32[16,4]{1,0:T(8,128)S(1)} %copy.6.win, bf16[256,128]{1,0:T(8,128)(2,1)S(1)} %copy-done.1, bf16[272,128]{1,0:T(8,128)(2,1)S(1)} %collective-permute-done.g_before, bf16[304,128]{1,0:T(8,128)(2,1)S(1)} %collective-permute-done.1.g_after, bf16[288,128]{1,0:T(8,128)(2,1)S(1)} %collective-permute-done.2.g_far), custom_call_target="tpu_custom_call" | custom-call | tf_op jit(solution)/shard_map/choose/pallas_call | solution.py:366
  13.3 1.6 %collective-permute-start.3 = (bf16[512,128]{1,0:T(8,128)(2,1)S(1)}, bf16[512,128]{1,0:T(8,128)(2,1)S(1)}, u32[]{:S(2)}, u32[]{:S(2)}) collective-permute-start(bf16[512,128]{1,0:T(8,128)(2,1)S(1)} %choose.1.greens.g0), channel_id=1, source_target_pairs={{0,16},{1,17},{2,18},{3,19},{4,20},{5,21},{6,22},{7,23},{8,24},{9,... | collective-permute-start | bytes 393224 | tf_op jit(solution)/shard_map/ppermute | solution.py:390
  14.8 0.7 %collective-permute-start.4 = (bf16[768,128]{1,0:T(8,128)(2,1)S(1)}, bf16[768,128]{1,0:T(8,128)(2,1)S(1)}, u32[]{:S(2)}, u32[]{:S(2)}) collective-permute-start(bf16[768,128]{1,0:T(8,128)(2,1)S(1)} %get-tuple-element.46), channel_id=1, source_target_pairs={{0,2},{1,3},{2,4},{3,5},{4,6},{5,7},{6,8},{7,9},{8,10},{9,11},{10,... | collective-permute-start | bytes 589832 | tf_op jit(solution)/shard_map/ppermute | solution.py:390
  15.5 3.2 %dress_own.1 = (f32[48,48]{1,0:T(8,128)S(1)}, bf16[48,16384]{1,0:T(8,128)(2,1)S(1)}, bf16[48,8192]{1,0:T(8,128)(2,1)S(1)}) custom-call(s32[16,4]{1,0:T(8,128)S(1)} %copy.6.win, s32[1,4,4]{2,1,0:T(4,128)S(1)} %copy-done.2, bf16[1,48,128,128]{3,2,1,0:T(8,128)(2,1)S(1)} %copy-done, bf16[512,128]{1,0:T(8,128)(2,1)S(1)} %choose.1.greens.g0, ...), custom_call_target="tpu_custom_call" | custom-call | tf_op jit(solution)/shard_map/dress_own/pallas_call | solution.py:366
  18.7 4.0 %collective-permute-start.5 = (bf16[768,128]{1,0:T(8,128)(2,1)S(1)}, bf16[768,128]{1,0:T(8,128)(2,1)S(1)}, u32[]{:S(2)}, u32[]{:S(2)}) collective-permute-start(bf16[768,128]{1,0:T(8,128)(2,1)S(1)} %get-tuple-element.47), channel_id=1, source_target_pairs={{0,14},{1,15},{2,0},{3,1},{4,2},{5,3},{6,4},{7,5},{8,6},{9,7},{10,... | collective-permute-start | bytes 589832 | tf_op jit(solution)/shard_map/ppermute | solution.py:390
  22.8 0.0 collective-permute-done.3.greens.g1
  22.8 2.3 %dress_partner.1 = (bf16[48,16384]{1,0:T(8,128)(2,1)S(1)}, bf16[48,8192]{1,0:T(8,128)(2,1)S(1)}) custom-call(s32[16,4]{1,0:T(8,128)S(1)} %copy.6.win, s32[1,4,4]{2,1,0:T(4,128)S(1)} %copy-done.2, bf16[1,48,128,128]{3,2,1,0:T(8,128)(2,1)S(1)} %copy-done, bf16[512,128]{1,0:T(8,128)(2,1)S(1)} %collective-permute-done.3.greens.g1), custom_call_target="tpu_custom_call" | custom-call | tf_op jit(solution)/shard_map/dress_partner/pallas_call | solution.py:366
  25.1 1.0 %collective-permute-done.6.tensor = bf16[24,128,128]{2,1,0:T(8,128)(2,1)S(1)} collective-permute-done((bf16[24,128,128]{2,1,0:T(8,128)(2,1)}, bf16[24,128,128]{2,1,0:T(8,128)(2,1)S(1)}, u32[]{:S(2)}, u32[]{:S(2)}) %collective-permute-start.6) | collective-permute-done | bytes 786464 | tf_op jit(solution)/shard_map/ppermute | solution.py:390
  26.1 2.4 %join_back.1 = f32[48,128]{1,0:T(8,128)S(1)} custom-call(bf16[24,128,128]{2,1,0:T(8,128)(2,1)S(1)} %collective-permute-done.6.tensor, bf16[272,128]{1,0:T(8,128)(2,1)S(1)} %collective-permute-done.g_before, bf16[512,128]{1,0:T(8,128)(2,1)S(1)} %choose.1.greens.g0, bf16[512,128]{1,0:T(8,128)(2,1)S(1)} %collective-permute-done.3.greens.g1, ...), custom_call_target="tpu_custom_call" | custom-call | tf_op jit(solution)/shard_map/join_back/pallas_call | solution.py:366
  28.5 0.0 collective-permute-start.7
  28.5 1.8 %join.1.down = f32[96,128]{1,0:T(8,128)S(1)} custom-call(s32[16,4]{1,0:T(8,128)S(1)} %copy.6.win, bf16[24,128,128]{2,1,0:T(8,128)(2,1)S(1)} %collective-permute-done.6.tensor, bf16[272,128]{1,0:T(8,128)(2,1)S(1)} %collective-permute-done.g_before, bf16[48,16384]{1,0:T(8,128)(2,1)S(1)} %get-tuple-element.49.dressed0, ...), custom_call_target="tpu_custom_call" | custom-call | flops 17179869184 | tf_op jit(solution)/shard_map/join/pallas_call | solution.py:366
  30.3 0.0 collective-permute-done.4.from_left
  30.4 2.0 %collective-permute-done.5.from_right = bf16[768,128]{1,0:T(8,128)(2,1)S(1)} collective-permute-done((bf16[768,128]{1,0:T(8,128)(2,1)S(1)}, bf16[768,128]{1,0:T(8,128)(2,1)S(1)}, u32[]{:S(2)}, u32[]{:S(2)}) %collective-permute-start.5) | collective-permute-done | bytes 196640 | tf_op jit(solution)/shard_map/ppermute | solution.py:390
  32.3 0.0 collective-permute-done.7.after
  32.3 0.7 %join_far.1 = (f32[48,128]{1,0:T(8,128)S(1)}, f32[48,128]{1,0:T(8,128)S(1)}) custom-call(bf16[48,8192]{1,0:T(8,128)(2,1)S(1)} %get-tuple-element.44.far0, bf16[48,8192]{1,0:T(8,128)(2,1)S(1)} %get-tuple-element.45.far1, bf16[768,128]{1,0:T(8,128)(2,1)S(1)} %collective-permute-done.4.from_left, bf16[768,128]{1,0:T(8,128)(2,1)S(1)} %collective-permute-done.5.from_right, ...), custom_call_target="tpu_custom_call" | custom-call | tf_op jit(solution)/shard_map/join_far/pallas_call | solution.py:366
  33.0 1.6 %collective-permute-start.8 = (f32[48,128]{1,0:T(8,128)S(1)}, f32[48,128]{1,0:T(8,128)S(1)}, u32[]{:S(2)}, u32[]{:S(2)}) collective-permute-start(f32[48,128]{1,0:T(8,128)S(1)} %get-tuple-element.52), channel_id=1, source_target_pairs={{0,16},{1,17},{2,18},{3,19},{4,20},{5,21},{6,22},{7,23},{8,24},{9,... | collective-permute-start | bytes 73736 | tf_op jit(solution)/shard_map/ppermute | solution.py:390
  34.6 2.3 %collective-permute-done.8.recv = f32[48,128]{1,0:T(8,128)S(1)} collective-permute-done((f32[48,128]{1,0:T(8,128)S(1)}, f32[48,128]{1,0:T(8,128)S(1)}, u32[]{:S(2)}, u32[]{:S(2)}) %collective-permute-start.8) | collective-permute-done | bytes 24608 | tf_op jit(solution)/shard_map/ppermute | solution.py:390
  36.9 0.7 %assemble.1 = f32[48,240]{1,0:T(8,128)} custom-call(f32[48,48]{1,0:T(8,128)S(1)} %get-tuple-element.43.polar0, f32[48,128]{1,0:T(8,128)S(1)} %get-tuple-element.51.own, f32[48,128]{1,0:T(8,128)S(1)} %collective-permute-done.8.recv), custom_call_target="tpu_custom_call" | custom-call | tf_op jit(solution)/shard_map/assemble/pallas_call | solution.py:366
Async XLA Ops:
  0.0 9.7 %copy-start.2 = (s32[1,4,4]{2,1,0:T(4,128)S(1)}, s32[1,4,4]{2,1,0:T(4,128)}, u32[]{:S(2)}) copy-start(s32[1,4,4]{2,1,0:T(4,128)} %tiles.5) | copy-start | bytes 196
  0.0 9.7 %copy-start = (bf16[1,48,128,128]{3,2,1,0:T(8,128)(2,1)S(1)}, bf16[1,48,128,128]{3,2,1,0:T(8,128)(2,1)}, u32[]{:S(2)}) copy-start(bf16[1,48,128,128]{3,2,1,0:T(8,128)(2,1)} %tensor.5) | copy-start | bytes 4718596
  0.0 9.6 %copy-start.3 = (s32[16,4]{0,1:T(4,128)S(1)}, s32[16,4]{0,1:T(4,128)}, u32[]{:S(2)}) copy-start(s32[16,4]{0,1:T(4,128)} %param.9) | copy-start | bytes 772
  2.4 9.3 %collective-permute-start = (bf16[272,128]{1,0:T(8,128)(2,1)}, bf16[272,128]{1,0:T(8,128)(2,1)S(1)}, u32[]{:S(2)}, u32[]{:S(2)}) collective-permute-start(bf16[272,128]{1,0:T(8,128)(2,1)} %get-tuple-element.29), channel_id=1, source_target_pairs={{0,1},{1,2},{2,3},{3,4},{4,5},{5,6},{6,7},{7,8},{8,9},{9,10},{10,1... | collective-permute-start | bytes 208904 | tf_op jit(solution)/shard_map/ppermute | solution.py:390
  2.9 8.8 %collective-permute-start.2 = (bf16[288,128]{1,0:T(8,128)(2,1)}, bf16[288,128]{1,0:T(8,128)(2,1)S(1)}, u32[]{:S(2)}, u32[]{:S(2)}) collective-permute-start(bf16[288,128]{1,0:T(8,128)(2,1)} %get-tuple-element.31), channel_id=1, source_target_pairs={{0,2},{1,3},{2,4},{3,5},{4,6},{5,7},{6,8},{7,9},{8,10},{9,11},{10,... | collective-permute-start | bytes 221192 | tf_op jit(solution)/shard_map/ppermute | solution.py:390
  5.5 6.4 %collective-permute-start.1 = (bf16[304,128]{1,0:T(8,128)(2,1)}, bf16[304,128]{1,0:T(8,128)(2,1)S(1)}, u32[]{:S(2)}, u32[]{:S(2)}) collective-permute-start(bf16[304,128]{1,0:T(8,128)(2,1)} %get-tuple-element.30), channel_id=1, source_target_pairs={{0,15},{1,0},{2,1},{3,2},{4,3},{5,4},{6,5},{7,6},{8,7},{9,8},{10,9... | collective-permute-start | bytes 233480 | tf_op jit(solution)/shard_map/ppermute | solution.py:390
  9.6 16.5 %collective-permute-start.6 = (bf16[24,128,128]{2,1,0:T(8,128)(2,1)}, bf16[24,128,128]{2,1,0:T(8,128)(2,1)S(1)}, u32[]{:S(2)}, u32[]{:S(2)}) collective-permute-start(bf16[24,128,128]{2,1,0:T(8,128)(2,1)} %get-tuple-element.48), channel_id=1, source_target_pairs={{0,1},{1,2},{2,3},{3,4},{4,5},{5,6},{6,7},{7,8},{8,9},{9,10},{10,1... | collective-permute-start | bytes 2359304 | tf_op jit(solution)/shard_map/ppermute | solution.py:390
  9.7 2.2 %copy-start.1 = (bf16[256,128]{1,0:T(8,128)(2,1)S(1)}, bf16[256,128]{1,0:T(8,128)(2,1)}, u32[]{:S(2)}) copy-start(bf16[256,128]{1,0:T(8,128)(2,1)} %get-tuple-element.36.g_self) | copy-start | bytes 196612
  13.3 9.5 %collective-permute-start.3 = (bf16[512,128]{1,0:T(8,128)(2,1)S(1)}, bf16[512,128]{1,0:T(8,128)(2,1)S(1)}, u32[]{:S(2)}, u32[]{:S(2)}) collective-permute-start(bf16[512,128]{1,0:T(8,128)(2,1)S(1)} %choose.1.greens.g0), channel_id=1, source_target_pairs={{0,16},{1,17},{2,18},{3,19},{4,20},{5,21},{6,22},{7,23},{8,24},{9,... | collective-permute-start | bytes 393224 | tf_op jit(solution)/shard_map/ppermute | solution.py:390
  14.8 15.5 %collective-permute-start.4 = (bf16[768,128]{1,0:T(8,128)(2,1)S(1)}, bf16[768,128]{1,0:T(8,128)(2,1)S(1)}, u32[]{:S(2)}, u32[]{:S(2)}) collective-permute-start(bf16[768,128]{1,0:T(8,128)(2,1)S(1)} %get-tuple-element.46), channel_id=1, source_target_pairs={{0,2},{1,3},{2,4},{3,5},{4,6},{5,7},{6,8},{7,9},{8,10},{9,11},{10,... | collective-permute-start | bytes 589832 | tf_op jit(solution)/shard_map/ppermute | solution.py:390
  18.7 13.6 %collective-permute-start.5 = (bf16[768,128]{1,0:T(8,128)(2,1)S(1)}, bf16[768,128]{1,0:T(8,128)(2,1)S(1)}, u32[]{:S(2)}, u32[]{:S(2)}) collective-permute-start(bf16[768,128]{1,0:T(8,128)(2,1)S(1)} %get-tuple-element.47), channel_id=1, source_target_pairs={{0,14},{1,15},{2,0},{3,1},{4,2},{5,3},{6,4},{7,5},{8,6},{9,7},{10,... | collective-permute-start | bytes 589832 | tf_op jit(solution)/shard_map/ppermute | solution.py:390
  28.5 3.9 %collective-permute-start.7 = (f32[48,128]{1,0:T(8,128)S(1)}, f32[48,128]{1,0:T(8,128)S(1)}, u32[]{:S(2)}, u32[]{:S(2)}) collective-permute-start(f32[48,128]{1,0:T(8,128)S(1)} %join_back.1), channel_id=1, source_target_pairs={{0,15},{1,0},{2,1},{3,2},{4,3},{5,4},{6,5},{7,6},{8,7},{9,8},{10,9... | collective-permute-start | bytes 73736 | tf_op jit(solution)/shard_map/ppermute | solution.py:390
  33.0 3.9 %collective-permute-start.8 = (f32[48,128]{1,0:T(8,128)S(1)}, f32[48,128]{1,0:T(8,128)S(1)}, u32[]{:S(2)}, u32[]{:S(2)}) collective-permute-start(f32[48,128]{1,0:T(8,128)S(1)} %get-tuple-element.52), channel_id=1, source_target_pairs={{0,16},{1,17},{2,18},{3,19},{4,20},{5,21},{6,22},{7,23},{8,24},{9,... | collective-permute-start | bytes 73736 | tf_op jit(solution)/shard_map/ppermute | solution.py:390

commit v13 on v12

--- a/solution.py
+++ b/solution.py
@@ -108,7 +108,7 @@
         out.wait()
 
 
-def far_tiles(count, win, tiles, tensor, far_right, far_left, flat, mask, ms):
+def far_tiles(count, win, tiles, tensor, token, far_right, far_left, mask):
     d = lax.axis_index("row")
     mine = window_at(win, d)
     funcs = tensor.shape[1] // 2
@@ -132,11 +132,15 @@
             ]
             x = dot(jnp.concatenate(sides, axis=1), select)
             out[r * 32 : r * 32 + 256, :] = x.astype(BF)
-    whole = mask[...]
-    for r in range(2 * funcs):
-        ms[r * PITCH : r * PITCH + 128, :] = (tensor[0, r] * whole).astype(F32)
+
+
+def flatten(tiles, tensor, flat, ms):
+    funcs = tensor.shape[1]
+    mask = tile_mask(tiles, 32).astype(BF)
+    for r in range(funcs):
+        ms[r * PITCH : r * PITCH + 128, :] = (tensor[0, r] * mask).astype(F32)
     for m in range(128):
-        rows = ms[pl.ds(m, 2 * funcs, stride=PITCH), :]
+        rows = ms[pl.ds(m, funcs, stride=PITCH), :]
         flat[:, m * 128 : (m + 1) * 128] = rows.astype(BF)
 
 
@@ -420,18 +424,26 @@
     tall = pltpu.VMEM((full * PITCH, 128), F32)
     short = pltpu.VMEM((funcs * PITCH, 128), F32)
     message = shape((full, 128), F32)
-    far_right, far_left, flat = call(
+    far_right, far_left = call(
         functools.partial(far_tiles, count),
         "far_tiles",
-        smem(2) + vmem(1),
-        [shape((far_rows, 128), BF), shape((far_rows, 128), BF), flat_shape],
-        (window, tile_list, coulomb3c),
-        [pltpu.VMEM((128, 128), BF), tall],
+        smem(2) + vmem(1) + [pl.BlockSpec(memory_space=pl.ANY)],
+        [shape((far_rows, 128), BF), shape((far_rows, 128), BF)],
+        (window, tile_list, coulomb3c, g_self),
+        [pltpu.VMEM((128, 128), BF)],
+    )
+    from_right = send(far_left, -2)
+    here, _ = lax.optimization_barrier((tile_list, far_left))
+    (flat,) = call(
+        flatten,
+        "flatten",
+        smem(1) + vmem(1),
+        [flat_shape],
+        (here, coulomb3c),
+        [tall],
         flops=1 << 36,
     )
-    g_before, g_after, g_beyond, far_right, far_left = lax.optimization_barrier(
-        (g_before, g_after, g_beyond, far_right, far_left)
-    )
+    g_before, g_after, g_beyond, flat = lax.optimization_barrier((g_before, g_after, g_beyond, flat))
     (mine,) = call(
         functools.partial(choose, count),
         "choose",
@@ -450,8 +462,6 @@
         (window, tile_list, coulomb3c, mine, flat),
         [tall, pltpu.VMEM((full, 128 * 128), BF)],
     )
-    far_left, polar0 = lax.optimization_barrier((far_left, polar0))
-    from_right = send(far_left, -2)
     dressed1, far1 = call(
         functools.partial(dress, count, False),
         "dress_partner",
@@ -460,6 +470,7 @@
         (window, tile_list, coulomb3c, partner),
         [tall],
     )
+    wide, from_right = lax.optimization_barrier((wide, from_right))
     (up,) = call(
         join_back,
         "join_back",

time: 37.8 us -> 38.3 us (1.013)
  starting transfers between devices: 15.1 us -> 12.4 us
  waiting for transfers between devices: 5.52 us -> 7.22 us
  local copies, waits for them, and re-layouts: 0.1 us -> 0.94 us
  Pallas kernels: 16.9 us -> 17.4 us
    ppermute x9, starting transfers between devices: 15.1 us -> 12.4 us  [send(): return lax.ppermute(array, ('grp', 'row'), pairs)]
    ppermute x9, waiting for transfers between devices: 5.52 us -> 7.22 us  [send(): return lax.ppermute(array, ('grp', 'row'), pairs)]
    unnamed x9 -> x13, local copies, waits for them, and re-layouts: 0.1 us -> 0.94 us
    pallas_call x9 -> x10, Pallas kernels: 16.9 us -> 17.4 us  [call(): pl.pallas_call(kernel, name=name, in_specs=specs, out_specs=tuple((space...]
  transfers between devices with their start and end apart: 9 -> 9, of which waited for: 4 -> 2; matrix products, arithmetic and copies ran while one was open for 0% -> 0% of each run, Pallas kernels for 35% -> 36%
where the time goes in v13:
time: 38.3 us; the launch traced here: 38.1 us
  Pallas kernels  17.4 us (45%)
  starting transfers between devices  12.4 us (32%)
  waiting for transfers between devices  7.22 us (19%)
  local copies, waits for them, and re-layouts  0.94 us (2%)
    pallas_call x10, Pallas kernels, call(): pl.pallas_call(kernel, name=name, in_specs=specs, out_specs=tuple((space...  17.4 us
    ppermute x9, starting transfers between devices, send(): return lax.ppermute(array, ('grp', 'row'), pairs)  12.4 us
    ppermute x9, waiting for transfers between devices, send(): return lax.ppermute(array, ('grp', 'row'), pairs)  7.22 us
    unnamed x13, local copies, waits for them, and re-layouts  0.94 us
  transfers between devices with their start and end apart: 9, of which 2 were waited for; matrix products, arithmetic and copies ran while one was open for 0% of the time, Pallas kernels for 36%

profile of v13, /device:TPU:0, one launch (start us, length us, event | category | flops | bytes accessed | tf_op | source)
XLA Modules:
  0.0 38.1 jit_solution(11882643040210331086)
XLA Ops:
  0.0 0.0 copy-start.3
  0.0 0.0 copy-start
  0.0 0.0 copy-start.4
  0.0 2.4 %first.1 = (bf16[256,128]{1,0:T(8,128)(2,1)}, bf16[272,128]{1,0:T(8,128)(2,1)}, bf16[304,128]{1,0:T(8,128)(2,1)}, bf16[288,128]{1,0:T(8,128)(2,1)}, bf16[24,128,128]{2,1,0:T(8,128)(2,1)}) custom-call(bf16[64,1024]{1,0:T(8,128)(2,1)} %occ.1, bf16[64,1024]{1,0:T(8,128)(2,1)} %virt.1, s32[1,4,4]{2,1,0:T(4,128)} %tiles.6, bf16[1,48,128,128]{3,2,1,0:T(8,128)(2,1)} %tensor.7), custom_call_target="tpu_custom_call" | custom-call | tf_op jit(solution)/shard_map/first/pallas_call | solution.py:370
  2.4 0.5 %collective-permute-start = (bf16[272,128]{1,0:T(8,128)(2,1)}, bf16[272,128]{1,0:T(8,128)(2,1)S(1)}, u32[]{:S(2)}, u32[]{:S(2)}) collective-permute-start(bf16[272,128]{1,0:T(8,128)(2,1)} %get-tuple-element.30), channel_id=1, source_target_pairs={{0,1},{1,2},{2,3},{3,4},{4,5},{5,6},{6,7},{7,8},{8,9},{9,10},{10,1... | collective-permute-start | bytes 208904 | tf_op jit(solution)/shard_map/ppermute | solution.py:394
  2.9 2.6 %collective-permute-start.2 = (bf16[288,128]{1,0:T(8,128)(2,1)}, bf16[288,128]{1,0:T(8,128)(2,1)S(1)}, u32[]{:S(2)}, u32[]{:S(2)}) collective-permute-start(bf16[288,128]{1,0:T(8,128)(2,1)} %get-tuple-element.32), channel_id=1, source_target_pairs={{0,2},{1,3},{2,4},{3,5},{4,6},{5,7},{6,8},{7,9},{8,10},{9,11},{10,... | collective-permute-start | bytes 221192 | tf_op jit(solution)/shard_map/ppermute | solution.py:394
  5.5 4.1 %collective-permute-start.1 = (bf16[304,128]{1,0:T(8,128)(2,1)}, bf16[304,128]{1,0:T(8,128)(2,1)S(1)}, u32[]{:S(2)}, u32[]{:S(2)}) collective-permute-start(bf16[304,128]{1,0:T(8,128)(2,1)} %get-tuple-element.31), channel_id=1, source_target_pairs={{0,15},{1,0},{2,1},{3,2},{4,3},{5,4},{6,5},{7,6},{8,7},{9,8},{10,9... | collective-permute-start | bytes 233480 | tf_op jit(solution)/shard_map/ppermute | solution.py:394
  9.6 0.0 copy-done.4
  9.6 0.1 copy.8.win
  9.7 0.0 copy-done.3
  9.7 0.0 copy-done
  9.7 0.0 copy-start.1
  9.7 0.8 %copy-done.1 = bf16[256,128]{1,0:T(8,128)(2,1)S(1)} copy-done((bf16[256,128]{1,0:T(8,128)(2,1)S(1)}, bf16[256,128]{1,0:T(8,128)(2,1)}, u32[]{:S(2)}) %copy-start.1) | copy-done | bytes 65560
  10.5 0.0 copy-start.5
  10.5 1.1 %far_tiles.1 = (bf16[768,128]{1,0:T(8,128)(2,1)S(1)}, bf16[768,128]{1,0:T(8,128)(2,1)S(1)}) custom-call(s32[16,4]{1,0:T(8,128)S(1)} %copy.8.win, s32[1,4,4]{2,1,0:T(4,128)S(1)} %copy-done.3, bf16[1,48,128,128]{3,2,1,0:T(8,128)(2,1)S(1)} %copy-done, bf16[256,128]{1,0:T(8,128)(2,1)S(1)} %copy-done.1), custom_call_target="tpu_custom_call" | custom-call | tf_op jit(solution)/shard_map/far_tiles/pallas_call | solution.py:370
  11.6 0.7 %collective-permute-start.6 = (bf16[768,128]{1,0:T(8,128)(2,1)S(1)}, bf16[768,128]{1,0:T(8,128)(2,1)S(1)}, u32[]{:S(2)}, u32[]{:S(2)}) collective-permute-start(bf16[768,128]{1,0:T(8,128)(2,1)S(1)} %get-tuple-element.33), channel_id=1, source_target_pairs={{0,14},{1,15},{2,0},{3,1},{4,2},{5,3},{6,4},{7,5},{8,6},{9,7},{10,... | collective-permute-start | bytes 589832 | tf_op jit(solution)/shard_map/ppermute | solution.py:394
  12.3 0.0 copy-done.5
  12.3 0.0 copy-start.2
  12.3 0.0 collective-permute-start.5
  12.3 1.4 %flatten.1.refs_0_.flat = bf16[48,16384]{1,0:T(8,128)(2,1)S(1)} custom-call(s32[1,4,4]{2,1,0:T(4,128)S(1)} %copy-done.3, bf16[1,48,128,128]{3,2,1,0:T(8,128)(2,1)S(1)} %copy-done), custom_call_target="tpu_custom_call" | custom-call | flops 68719476736 | tf_op jit(solution)/shard_map/flatten/pallas_call | solution.py:370
  13.7 0.0 collective-permute-done.g_before
  13.7 0.0 collective-permute-done.2.g_far
  13.8 0.0 collective-permute-done.1.g_after
  13.8 0.0 copy-done.2
  13.8 1.4 %choose.1.greens.g0 = bf16[512,128]{1,0:T(8,128)(2,1)S(1)} custom-call(s32[16,4]{1,0:T(8,128)S(1)} %copy.8.win, bf16[256,128]{1,0:T(8,128)(2,1)S(1)} %copy-done.2, bf16[272,128]{1,0:T(8,128)(2,1)S(1)} %collective-permute-done.g_before, bf16[304,128]{1,0:T(8,128)(2,1)S(1)} %collective-permute-done.1.g_after, bf16[288,128]{1,0:T(8,128)(2,1)S(1)} %collective-permute-done.2.g_far), custom_call_target="tpu_custom_call" | custom-call | tf_op jit(solution)/shard_map/choose/pallas_call | solution.py:370
  15.1 1.6 %collective-permute-start.3 = (bf16[512,128]{1,0:T(8,128)(2,1)S(1)}, bf16[512,128]{1,0:T(8,128)(2,1)S(1)}, u32[]{:S(2)}, u32[]{:S(2)}) collective-permute-start(bf16[512,128]{1,0:T(8,128)(2,1)S(1)} %choose.1.greens.g0), channel_id=1, source_target_pairs={{0,16},{1,17},{2,18},{3,19},{4,20},{5,21},{6,22},{7,23},{8,24},{9,... | collective-permute-start | bytes 393224 | tf_op jit(solution)/shard_map/ppermute | solution.py:394
  16.7 1.4 %collective-permute-start.4 = (bf16[768,128]{1,0:T(8,128)(2,1)S(1)}, bf16[768,128]{1,0:T(8,128)(2,1)S(1)}, u32[]{:S(2)}, u32[]{:S(2)}) collective-permute-start(bf16[768,128]{1,0:T(8,128)(2,1)S(1)} %get-tuple-element.43), channel_id=1, source_target_pairs={{0,2},{1,3},{2,4},{3,5},{4,6},{5,7},{6,8},{7,9},{8,10},{9,11},{10,... | collective-permute-start | bytes 589832 | tf_op jit(solution)/shard_map/ppermute | solution.py:394
  18.1 3.2 %dress_own.1 = (f32[48,48]{1,0:T(8,128)S(1)}, bf16[48,16384]{1,0:T(8,128)(2,1)S(1)}, bf16[48,8192]{1,0:T(8,128)(2,1)S(1)}) custom-call(s32[16,4]{1,0:T(8,128)S(1)} %copy.8.win, s32[1,4,4]{2,1,0:T(4,128)S(1)} %copy-done.3, bf16[1,48,128,128]{3,2,1,0:T(8,128)(2,1)S(1)} %copy-done, bf16[512,128]{1,0:T(8,128)(2,1)S(1)} %choose.1.greens.g0, ...), custom_call_target="tpu_custom_call" | custom-call | tf_op jit(solution)/shard_map/dress_own/pallas_call | solution.py:370
  21.3 0.0 collective-permute-done.3.greens.g1
  21.3 2.3 %dress_partner.1 = (bf16[48,16384]{1,0:T(8,128)(2,1)S(1)}, bf16[48,8192]{1,0:T(8,128)(2,1)S(1)}) custom-call(s32[16,4]{1,0:T(8,128)S(1)} %copy.8.win, s32[1,4,4]{2,1,0:T(4,128)S(1)} %copy-done.3, bf16[1,48,128,128]{3,2,1,0:T(8,128)(2,1)S(1)} %copy-done, bf16[512,128]{1,0:T(8,128)(2,1)S(1)} %collective-permute-done.3.greens.g1), custom_call_target="tpu_custom_call" | custom-call | tf_op jit(solution)/shard_map/dress_partner/pallas_call | solution.py:370
  23.7 0.0 collective-permute-done.6.from_right
  23.7 4.9 %collective-permute-done.5.tensor = bf16[24,128,128]{2,1,0:T(8,128)(2,1)S(1)} collective-permute-done((bf16[24,128,128]{2,1,0:T(8,128)(2,1)S(1)}, bf16[24,128,128]{2,1,0:T(8,128)(2,1)S(1)}, u32[]{:S(2)}, u32[]{:S(2)}) %collective-permute-start.5) | collective-permute-done | bytes 786464 | tf_op jit(solution)/shard_map/ppermute | solution.py:394
  28.5 2.4 %join_back.1 = f32[48,128]{1,0:T(8,128)S(1)} custom-call(bf16[24,128,128]{2,1,0:T(8,128)(2,1)S(1)} %collective-permute-done.5.tensor, bf16[272,128]{1,0:T(8,128)(2,1)S(1)} %collective-permute-done.g_before, bf16[512,128]{1,0:T(8,128)(2,1)S(1)} %choose.1.greens.g0, bf16[512,128]{1,0:T(8,128)(2,1)S(1)} %collective-permute-done.3.greens.g1, ...), custom_call_target="tpu_custom_call" | custom-call | tf_op jit(solution)/shard_map/join_back/pallas_call | solution.py:370
  30.9 0.0 collective-permute-start.7
  30.9 1.8 %join.1.down = f32[96,128]{1,0:T(8,128)S(1)} custom-call(s32[16,4]{1,0:T(8,128)S(1)} %copy.8.win, bf16[24,128,128]{2,1,0:T(8,128)(2,1)S(1)} %collective-permute-done.5.tensor, bf16[272,128]{1,0:T(8,128)(2,1)S(1)} %collective-permute-done.g_before, bf16[48,16384]{1,0:T(8,128)(2,1)S(1)} %get-tuple-element.47.dressed0, ...), custom_call_target="tpu_custom_call" | custom-call | flops 17179869184 | tf_op jit(solution)/shard_map/join/pallas_call | solution.py:370
  32.8 0.0 collective-permute-done.4.from_left
  32.8 0.0 collective-permute-done.7.after
  32.8 0.7 %join_far.1 = (f32[48,128]{1,0:T(8,128)S(1)}, f32[48,128]{1,0:T(8,128)S(1)}) custom-call(bf16[48,8192]{1,0:T(8,128)(2,1)S(1)} %get-tuple-element.41.far0, bf16[48,8192]{1,0:T(8,128)(2,1)S(1)} %get-tuple-element.42.far1, bf16[768,128]{1,0:T(8,128)(2,1)S(1)} %collective-permute-done.4.from_left, bf16[768,128]{1,0:T(8,128)(2,1)S(1)} %collective-permute-done.6.from_right, ...), custom_call_target="tpu_custom_call" | custom-call | tf_op jit(solution)/shard_map/join_far/pallas_call | solution.py:370
  33.5 1.6 %collective-permute-start.8 = (f32[48,128]{1,0:T(8,128)S(1)}, f32[48,128]{1,0:T(8,128)S(1)}, u32[]{:S(2)}, u32[]{:S(2)}) collective-permute-start(f32[48,128]{1,0:T(8,128)S(1)} %get-tuple-element.50), channel_id=1, source_target_pairs={{0,16},{1,17},{2,18},{3,19},{4,20},{5,21},{6,22},{7,23},{8,24},{9,... | collective-permute-start | bytes 73736 | tf_op jit(solution)/shard_map/ppermute | solution.py:394
  35.0 2.3 %collective-permute-done.8.recv = f32[48,128]{1,0:T(8,128)S(1)} collective-permute-done((f32[48,128]{1,0:T(8,128)S(1)}, f32[48,128]{1,0:T(8,128)S(1)}, u32[]{:S(2)}, u32[]{:S(2)}) %collective-permute-start.8) | collective-permute-done | bytes 24608 | tf_op jit(solution)/shard_map/ppermute | solution.py:394
  37.4 0.7 %assemble.1 = f32[48,240]{1,0:T(8,128)} custom-call(f32[48,48]{1,0:T(8,128)S(1)} %get-tuple-element.40.polar0, f32[48,128]{1,0:T(8,128)S(1)} %get-tuple-element.49.own, f32[48,128]{1,0:T(8,128)S(1)} %collective-permute-done.8.recv), custom_call_target="tpu_custom_call" | custom-call | tf_op jit(solution)/shard_map/assemble/pallas_call | solution.py:370
Async XLA Ops:
  0.0 9.7 %copy-start.3 = (s32[1,4,4]{2,1,0:T(4,128)S(1)}, s32[1,4,4]{2,1,0:T(4,128)}, u32[]{:S(2)}) copy-start(s32[1,4,4]{2,1,0:T(4,128)} %tiles.6) | copy-start | bytes 196
  0.0 9.7 %copy-start = (bf16[1,48,128,128]{3,2,1,0:T(8,128)(2,1)S(1)}, bf16[1,48,128,128]{3,2,1,0:T(8,128)(2,1)}, u32[]{:S(2)}) copy-start(bf16[1,48,128,128]{3,2,1,0:T(8,128)(2,1)} %tensor.7) | copy-start | bytes 4718596
  0.0 9.6 %copy-start.4 = (s32[16,4]{0,1:T(4,128)S(1)}, s32[16,4]{0,1:T(4,128)}, u32[]{:S(2)}) copy-start(s32[16,4]{0,1:T(4,128)} %param.9) | copy-start | bytes 772
  2.4 11.4 %collective-permute-start = (bf16[272,128]{1,0:T(8,128)(2,1)}, bf16[272,128]{1,0:T(8,128)(2,1)S(1)}, u32[]{:S(2)}, u32[]{:S(2)}) collective-permute-start(bf16[272,128]{1,0:T(8,128)(2,1)} %get-tuple-element.30), channel_id=1, source_target_pairs={{0,1},{1,2},{2,3},{3,4},{4,5},{5,6},{6,7},{7,8},{8,9},{9,10},{10,1... | collective-permute-start | bytes 208904 | tf_op jit(solution)/shard_map/ppermute | solution.py:394
  2.9 10.9 %collective-permute-start.2 = (bf16[288,128]{1,0:T(8,128)(2,1)}, bf16[288,128]{1,0:T(8,128)(2,1)S(1)}, u32[]{:S(2)}, u32[]{:S(2)}) collective-permute-start(bf16[288,128]{1,0:T(8,128)(2,1)} %get-tuple-element.32), channel_id=1, source_target_pairs={{0,2},{1,3},{2,4},{3,5},{4,6},{5,7},{6,8},{7,9},{8,10},{9,11},{10,... | collective-permute-start | bytes 221192 | tf_op jit(solution)/shard_map/ppermute | solution.py:394
  5.5 8.3 %collective-permute-start.1 = (bf16[304,128]{1,0:T(8,128)(2,1)}, bf16[304,128]{1,0:T(8,128)(2,1)S(1)}, u32[]{:S(2)}, u32[]{:S(2)}) collective-permute-start(bf16[304,128]{1,0:T(8,128)(2,1)} %get-tuple-element.31), channel_id=1, source_target_pairs={{0,15},{1,0},{2,1},{3,2},{4,3},{5,4},{6,5},{7,6},{8,7},{9,8},{10,9... | collective-permute-start | bytes 233480 | tf_op jit(solution)/shard_map/ppermute | solution.py:394
  9.7 0.8 %copy-start.1 = (bf16[256,128]{1,0:T(8,128)(2,1)S(1)}, bf16[256,128]{1,0:T(8,128)(2,1)}, u32[]{:S(2)}) copy-start(bf16[256,128]{1,0:T(8,128)(2,1)} %get-tuple-element.28.token.g_self) | copy-start | bytes 196612
  10.5 1.8 %copy-start.5 = (bf16[24,128,128]{2,1,0:T(8,128)(2,1)S(1)}, bf16[24,128,128]{2,1,0:T(8,128)(2,1)}, u32[]{:S(2)}) copy-start(bf16[24,128,128]{2,1,0:T(8,128)(2,1)} %get-tuple-element.44) | copy-start | bytes 2359300
  11.6 12.0 %collective-permute-start.6 = (bf16[768,128]{1,0:T(8,128)(2,1)S(1)}, bf16[768,128]{1,0:T(8,128)(2,1)S(1)}, u32[]{:S(2)}, u32[]{:S(2)}) collective-permute-start(bf16[768,128]{1,0:T(8,128)(2,1)S(1)} %get-tuple-element.33), channel_id=1, source_target_pairs={{0,14},{1,15},{2,0},{3,1},{4,2},{5,3},{6,4},{7,5},{8,6},{9,7},{10,... | collective-permute-start | bytes 589832 | tf_op jit(solution)/shard_map/ppermute | solution.py:394
  12.3 1.4 %copy-start.2 = (bf16[256,128]{1,0:T(8,128)(2,1)S(1)}, bf16[256,128]{1,0:T(8,128)(2,1)}, u32[]{:S(2)}) copy-start(bf16[256,128]{1,0:T(8,128)(2,1)} %get-tuple-element.28.token.g_self) | copy-start | bytes 196612
  12.3 16.2 %collective-permute-start.5 = (bf16[24,128,128]{2,1,0:T(8,128)(2,1)S(1)}, bf16[24,128,128]{2,1,0:T(8,128)(2,1)S(1)}, u32[]{:S(2)}, u32[]{:S(2)}) collective-permute-start(bf16[24,128,128]{2,1,0:T(8,128)(2,1)S(1)} %copy-done.5), channel_id=1, source_target_pairs={{0,1},{1,2},{2,3},{3,4},{4,5},{5,6},{6,7},{7,8},{8,9},{9,10},{10,1... | collective-permute-start | bytes 2359304 | tf_op jit(solution)/shard_map/ppermute | solution.py:394
  15.1 6.2 %collective-permute-start.3 = (bf16[512,128]{1,0:T(8,128)(2,1)S(1)}, bf16[512,128]{1,0:T(8,128)(2,1)S(1)}, u32[]{:S(2)}, u32[]{:S(2)}) collective-permute-start(bf16[512,128]{1,0:T(8,128)(2,1)S(1)} %choose.1.greens.g0), channel_id=1, source_target_pairs={{0,16},{1,17},{2,18},{3,19},{4,20},{5,21},{6,22},{7,23},{8,24},{9,... | collective-permute-start | bytes 393224 | tf_op jit(solution)/shard_map/ppermute | solution.py:394
  16.7 16.1 %collective-permute-start.4 = (bf16[768,128]{1,0:T(8,128)(2,1)S(1)}, bf16[768,128]{1,0:T(8,128)(2,1)S(1)}, u32[]{:S(2)}, u32[]{:S(2)}) collective-permute-start(bf16[768,128]{1,0:T(8,128)(2,1)S(1)} %get-tuple-element.43), channel_id=1, source_target_pairs={{0,2},{1,3},{2,4},{3,5},{4,6},{5,7},{6,8},{7,9},{8,10},{9,11},{10,... | collective-permute-start | bytes 589832 | tf_op jit(solution)/shard_map/ppermute | solution.py:394
  30.9 1.9 %collective-permute-start.7 = (f32[48,128]{1,0:T(8,128)S(1)}, f32[48,128]{1,0:T(8,128)S(1)}, u32[]{:S(2)}, u32[]{:S(2)}) collective-permute-start(f32[48,128]{1,0:T(8,128)S(1)} %join_back.1), channel_id=1, source_target_pairs={{0,15},{1,0},{2,1},{3,2},{4,3},{5,4},{6,5},{7,6},{8,7},{9,8},{10,9... | collective-permute-start | bytes 73736 | tf_op jit(solution)/shard_map/ppermute | solution.py:394
  33.5 3.9 %collective-permute-start.8 = (f32[48,128]{1,0:T(8,128)S(1)}, f32[48,128]{1,0:T(8,128)S(1)}, u32[]{:S(2)}, u32[]{:S(2)}) collective-permute-start(f32[48,128]{1,0:T(8,128)S(1)} %get-tuple-element.50), channel_id=1, source_target_pairs={{0,16},{1,17},{2,18},{3,19},{4,20},{5,21},{6,22},{7,23},{8,24},{9,... | collective-permute-start | bytes 73736 | tf_op jit(solution)/shard_map/ppermute | solution.py:394

commit v14 on v9

--- a/solution.py
+++ b/solution.py
@@ -108,7 +108,7 @@
         out.wait()
 
 
-def far_tiles(count, win, tiles, tensor, far_right, far_left, flat, mask, ms):
+def far_tiles(count, win, tiles, tensor, far_right, far_left, mask):
     d = lax.axis_index("row")
     mine = window_at(win, d)
     funcs = tensor.shape[1] // 2
@@ -132,12 +132,6 @@
             ]
             x = dot(jnp.concatenate(sides, axis=1), select)
             out[r * 32 : r * 32 + 256, :] = x.astype(BF)
-    whole = mask[...]
-    for r in range(2 * funcs):
-        ms[r * PITCH : r * PITCH + 128, :] = (tensor[0, r] * whole).astype(F32)
-    for m in range(128):
-        rows = ms[pl.ds(m, 2 * funcs, stride=PITCH), :]
-        flat[:, m * 128 : (m + 1) * 128] = rows.astype(BF)
 
 
 def choose(count, win, g_self, g_before, g_after, g_far, out):
@@ -195,10 +189,13 @@
 PITCH = 136
 
 
-def halves(occ, blocks, outs):
+def halves(occ, blocks, outs, ms):
     rows = occ.shape[0] // len(outs)
     for i in range(0, len(blocks), 2):
         m0, m1 = blocks[i](), blocks[i + 1]()
+        if ms is not None:
+            ms[i * PITCH : i * PITCH + 128, :] = m0.astype(F32)
+            ms[(i + 1) * PITCH : (i + 1) * PITCH + 128, :] = m1.astype(F32)
         h = dot(occ, jnp.concatenate([m0, m1], axis=1))
         for n, out in enumerate(outs):
             part = h[n * rows : (n + 1) * rows]
@@ -212,9 +209,9 @@
 
 def dress(count, own, win, tiles, tensor, greens, *refs):
     if own:
-        flat, polar0, dressed, far, hs, same = refs
+        polar0, flat, dressed, far, hs, ms, same = refs
     else:
-        dressed, far, hs = refs
+        (dressed, far, hs), ms = refs, None
     d = lax.axis_index("row")
     funcs = tensor.shape[1]
     mine = window_at(win, d)
@@ -222,7 +219,7 @@
     left, right = near(d, -1, count) * 2, near(d, 1, count) * 2
     mask = tile_mask(tiles, 32).astype(BF)
     occ, virt = greens[0:128, :], greens[128:256, :]
-    halves(occ, [functools.partial(lambda r: tensor[0, r] * mask, r) for r in range(funcs)], [hs])
+    halves(occ, [functools.partial(lambda r: tensor[0, r] * mask, r) for r in range(funcs)], [hs], ms)
     wide, outs = dot(virt, frame_map(mine, theirs)).astype(BF), [dressed]
     if own:
         wide, outs = jnp.concatenate([virt, wide], axis=1), [same, dressed]
@@ -243,6 +240,10 @@
                 block = x[t * funcs : (t + 1) * funcs].astype(BF)
                 for n, out in enumerate(outs):
                     out[:, at : at + 128] = block[:, n * 128 : (n + 1) * 128]
+            if own:
+                for t, rows in enumerate(gather(ms, funcs, i * 32 + c * 8)):
+                    at = (i * 32 + c * 8 + t) * 128
+                    flat[:, at : at + 128] = rows.astype(BF)
         x = dot(jnp.concatenate(parts, axis=1), packs)
         for t in range(8):
             at = (c * 8 + t) * 128
@@ -274,7 +275,7 @@
     full = 2 * funcs
     mask = neighbour_mask(g_before)
     occ = jnp.concatenate([g0[256:384, :], g1[256:384, :]], axis=0)
-    halves(occ, [functools.partial(lambda r: tensor[r] * mask, r) for r in range(funcs)], [hs0, hs1])
+    halves(occ, [functools.partial(lambda r: tensor[r] * mask, r) for r in range(funcs)], [hs0, hs1], None)
     virts = [g0[384:512, :], g1[384:512, :]]
     for i in range(16):
         xs = []
@@ -362,7 +363,7 @@
     return [pl.BlockSpec(memory_space=pltpu.SMEM)] * count
 
 
-def call(kernel, name, specs, outs, args, scratch=(), flops=0, limit=40 << 20, space=None, aliases={}):
+def call(kernel, name, specs, outs, args, scratch=(), flops=0, limit=40 << 20, space=None):
     return pl.pallas_call(
         kernel,
         name=name,
@@ -370,7 +371,6 @@
         out_specs=tuple((space or vmem)(len(outs))),
         out_shape=tuple(outs),
         scratch_shapes=list(scratch),
-        input_output_aliases=aliases,
         compiler_params=pltpu.CompilerParams(vmem_limit_bytes=limit),
         cost_estimate=pl.CostEstimate(flops=flops, bytes_accessed=0, transcendentals=0),
     )(*args)
@@ -413,22 +413,20 @@
         space=hbm,
     )
     g_before = send(g_right, 1)
+    g_after = send(g_left, -1)
     g_beyond = send(g_far, 2)
-    g_after = send(g_left, -1)
     wide = send(tensor, 1)
-    flat_shape, far_shape = shape((full, 128 * 128), BF), shape((full, 64 * 128), BF)
-    tall = pltpu.VMEM((full * PITCH, 128), F32)
-    short = pltpu.VMEM((funcs * PITCH, 128), F32)
-    message = shape((full, 128), F32)
-    far_right, far_left, flat = call(
+    far_right, far_left = call(
         functools.partial(far_tiles, count),
         "far_tiles",
         smem(2) + vmem(1),
-        [shape((far_rows, 128), BF), shape((far_rows, 128), BF), flat_shape],
+        [shape((far_rows, 128), BF), shape((far_rows, 128), BF)],
         (window, tile_list, coulomb3c),
-        [pltpu.VMEM((128, 128), BF), tall],
+        [pltpu.VMEM((128, 128), BF)],
         flops=1 << 36,
     )
+    from_left = send(far_right, 2)
+    from_right = send(far_left, -2)
     g_before, g_after, g_beyond, far_right, far_left = lax.optimization_barrier(
         (g_before, g_after, g_beyond, far_right, far_left)
     )
@@ -440,16 +438,17 @@
         (window, g_self, g_before, g_after, g_beyond),
     )
     partner = send(mine, 0, True)
-    far_right, far_left, mine = lax.optimization_barrier((far_right, far_left, mine))
-    from_left = send(far_right, 2)
-    from_right = send(far_left, -2)
-    polar0, dressed0, far0 = call(
+    flat_shape, far_shape = shape((full, 128 * 128), BF), shape((full, 64 * 128), BF)
+    tall = pltpu.VMEM((full * PITCH, 128), F32)
+    short = pltpu.VMEM((funcs * PITCH, 128), F32)
+    message = shape((full, 128), F32)
+    polar0, flat, dressed0, far0 = call(
         functools.partial(dress, count, True),
         "dress_own",
-        smem(2) + vmem(3),
-        [shape((full, full), F32), flat_shape, far_shape],
-        (window, tile_list, coulomb3c, mine, flat),
-        [tall, pltpu.VMEM((full, 128 * 128), BF)],
+        smem(2) + vmem(2),
+        [shape((full, full), F32), flat_shape, flat_shape, far_shape],
+        (window, tile_list, coulomb3c, mine),
+        [tall, tall, pltpu.VMEM((full, 128 * 128), BF)],
     )
     dressed1, far1 = call(
         functools.partial(dress, count, False),
@@ -459,6 +458,7 @@
         (window, tile_list, coulomb3c, partner),
         [tall],
     )
+    g_before, dressed1 = lax.optimization_barrier((g_before, dressed1))
     (up,) = call(
         join_back,
         "join_back",
@@ -475,7 +475,6 @@
         [shape((2 * full, 128), F32)],
         (window, wide, g_before, dressed0, dressed1),
         [short, pltpu.VMEM((funcs, 128 * 128), BF)],
-        flops=1 << 34,
     )
     own, other = call(
         join_far,

time: 37.8 us -> 36.8 us (0.974)
  Pallas kernels: 16.8 us -> 16.3 us
  waiting for transfers between devices: 5.56 us -> 5.06 us
    pallas_call x9, Pallas kernels: 16.8 us -> 16.3 us  [call(): pl.pallas_call(kernel, name=name, in_specs=specs, out_specs=tuple((space...]
    ppermute x9, waiting for transfers between devices: 5.56 us -> 5.06 us  [send(): return lax.ppermute(array, ('grp', 'row'), pairs)]
  transfers between devices with their start and end apart: 9 -> 9, of which waited for: 4 -> 4; matrix products, arithmetic and copies ran while one was open for 0% -> 0% of each run, Pallas kernels for 35% -> 34%
where the time goes in v14:
time: 36.8 us; the launch traced here: 36.7 us
  Pallas kernels  16.3 us (44%)
  starting transfers between devices  15.1 us (41%)
  waiting for transfers between devices  5.06 us (14%)
    pallas_call x9, Pallas kernels, call(): pl.pallas_call(kernel, name=name, in_specs=specs, out_specs=tuple((space...  16.3 us
    ppermute x9, starting transfers between devices, send(): return lax.ppermute(array, ('grp', 'row'), pairs)  15.1 us
    ppermute x9, waiting for transfers between devices, send(): return lax.ppermute(array, ('grp', 'row'), pairs)  5.06 us
  transfers between devices with their start and end apart: 9, of which 4 were waited for; matrix products, arithmetic and copies ran while one was open for 0% of the time, Pallas kernels for 34%

profile of v14, /device:TPU:0, one launch (start us, length us, event | category | flops | bytes accessed | tf_op | source)
XLA Modules:
  0.0 36.7 jit_solution(8346821882119763846)
XLA Ops:
  0.0 0.0 copy-start.2
  0.0 0.0 copy-start
  0.0 0.0 copy-start.3
  0.0 2.4 %first.1 = (bf16[256,128]{1,0:T(8,128)(2,1)}, bf16[272,128]{1,0:T(8,128)(2,1)}, bf16[304,128]{1,0:T(8,128)(2,1)}, bf16[288,128]{1,0:T(8,128)(2,1)}, bf16[24,128,128]{2,1,0:T(8,128)(2,1)}) custom-call(bf16[64,1024]{1,0:T(8,128)(2,1)} %occ.1, bf16[64,1024]{1,0:T(8,128)(2,1)} %virt.1, s32[1,4,4]{2,1,0:T(4,128)} %tiles.5, bf16[1,48,128,128]{3,2,1,0:T(8,128)(2,1)} %tensor.5), custom_call_target="tpu_custom_call" | custom-call | tf_op jit(solution)/shard_map/first/pallas_call | solution.py:367
  2.4 0.5 %collective-permute-start = (bf16[272,128]{1,0:T(8,128)(2,1)}, bf16[272,128]{1,0:T(8,128)(2,1)S(1)}, u32[]{:S(2)}, u32[]{:S(2)}) collective-permute-start(bf16[272,128]{1,0:T(8,128)(2,1)} %get-tuple-element.26), channel_id=1, source_target_pairs={{0,1},{1,2},{2,3},{3,4},{4,5},{5,6},{6,7},{7,8},{8,9},{9,10},{10,1... | collective-permute-start | bytes 208904 | tf_op jit(solution)/shard_map/ppermute | solution.py:390
  2.9 2.6 %collective-permute-start.2 = (bf16[288,128]{1,0:T(8,128)(2,1)}, bf16[288,128]{1,0:T(8,128)(2,1)S(1)}, u32[]{:S(2)}, u32[]{:S(2)}) collective-permute-start(bf16[288,128]{1,0:T(8,128)(2,1)} %get-tuple-element.28), channel_id=1, source_target_pairs={{0,2},{1,3},{2,4},{3,5},{4,6},{5,7},{6,8},{7,9},{8,10},{9,11},{10,... | collective-permute-start | bytes 221192 | tf_op jit(solution)/shard_map/ppermute | solution.py:390
  5.5 4.1 %collective-permute-start.1 = (bf16[304,128]{1,0:T(8,128)(2,1)}, bf16[304,128]{1,0:T(8,128)(2,1)S(1)}, u32[]{:S(2)}, u32[]{:S(2)}) collective-permute-start(bf16[304,128]{1,0:T(8,128)(2,1)} %get-tuple-element.27), channel_id=1, source_target_pairs={{0,15},{1,0},{2,1},{3,2},{4,3},{5,4},{6,5},{7,6},{8,7},{9,8},{10,9... | collective-permute-start | bytes 233480 | tf_op jit(solution)/shard_map/ppermute | solution.py:390
  9.6 0.0 collective-permute-start.6
  9.6 0.0 copy-done.3
  9.6 0.1 copy.8.win
  9.7 0.0 copy-done.2
  9.7 0.0 copy-done
  9.7 0.0 copy-start.1
  9.7 1.1 %far_tiles.1 = (bf16[768,128]{1,0:T(8,128)(2,1)S(1)}, bf16[768,128]{1,0:T(8,128)(2,1)S(1)}) custom-call(s32[16,4]{1,0:T(8,128)S(1)} %copy.8.win, s32[1,4,4]{2,1,0:T(4,128)S(1)} %copy-done.2, bf16[1,48,128,128]{3,2,1,0:T(8,128)(2,1)S(1)} %copy-done), custom_call_target="tpu_custom_call" | custom-call | flops 68719476736 | tf_op jit(solution)/shard_map/far_tiles/pallas_call | solution.py:367
  10.8 0.1 collective-permute-start.4
  10.9 0.0 collective-permute-done.g_before
  10.9 4.7 %collective-permute-start.5 = (bf16[768,128]{1,0:T(8,128)(2,1)S(1)}, bf16[768,128]{1,0:T(8,128)(2,1)S(1)}, u32[]{:S(2)}, u32[]{:S(2)}) collective-permute-start(bf16[768,128]{1,0:T(8,128)(2,1)S(1)} %get-tuple-element.30), channel_id=1, source_target_pairs={{0,14},{1,15},{2,0},{3,1},{4,2},{5,3},{6,4},{7,5},{8,6},{9,7},{10,... | collective-permute-start | bytes 589832 | tf_op jit(solution)/shard_map/ppermute | solution.py:390
  15.6 0.0 collective-permute-done.2.g_far
  15.6 0.0 collective-permute-done.1.g_after
  15.6 0.0 copy-done.1
  15.6 1.4 %choose.1.greens.g0 = bf16[512,128]{1,0:T(8,128)(2,1)S(1)} custom-call(s32[16,4]{1,0:T(8,128)S(1)} %copy.8.win, bf16[256,128]{1,0:T(8,128)(2,1)S(1)} %copy-done.1, bf16[272,128]{1,0:T(8,128)(2,1)S(1)} %collective-permute-done.g_before, bf16[304,128]{1,0:T(8,128)(2,1)S(1)} %collective-permute-done.1.g_after, bf16[288,128]{1,0:T(8,128)(2,1)S(1)} %collective-permute-done.2.g_far), custom_call_target="tpu_custom_call" | custom-call | tf_op jit(solution)/shard_map/choose/pallas_call | solution.py:367
  17.0 1.6 %collective-permute-start.3 = (bf16[512,128]{1,0:T(8,128)(2,1)S(1)}, bf16[512,128]{1,0:T(8,128)(2,1)S(1)}, u32[]{:S(2)}, u32[]{:S(2)}) collective-permute-start(bf16[512,128]{1,0:T(8,128)(2,1)S(1)} %choose.1.greens.g0), channel_id=1, source_target_pairs={{0,16},{1,17},{2,18},{3,19},{4,20},{5,21},{6,22},{7,23},{8,24},{9,... | collective-permute-start | bytes 393224 | tf_op jit(solution)/shard_map/ppermute | solution.py:390
  18.5 3.5 %dress_own.1 = (f32[48,48]{1,0:T(8,128)S(1)}, bf16[48,16384]{1,0:T(8,128)(2,1)S(1)}, bf16[48,16384]{1,0:T(8,128)(2,1)S(1)}, bf16[48,8192]{1,0:T(8,128)(2,1)S(1)}) custom-call(s32[16,4]{1,0:T(8,128)S(1)} %copy.8.win, s32[1,4,4]{2,1,0:T(4,128)S(1)} %copy-done.2, bf16[1,48,128,128]{3,2,1,0:T(8,128)(2,1)S(1)} %copy-done, bf16[512,128]{1,0:T(8,128)(2,1)S(1)} %choose.1.greens.g0), custom_call_target="tpu_custom_call" | custom-call | tf_op jit(solution)/shard_map/dress_own/pallas_call | solution.py:367
  22.1 0.3 collective-permute-done.3.greens.g1
  22.3 2.3 %dress_partner.1 = (bf16[48,16384]{1,0:T(8,128)(2,1)S(1)}, bf16[48,8192]{1,0:T(8,128)(2,1)S(1)}) custom-call(s32[16,4]{1,0:T(8,128)S(1)} %copy.8.win, s32[1,4,4]{2,1,0:T(4,128)S(1)} %copy-done.2, bf16[1,48,128,128]{3,2,1,0:T(8,128)(2,1)S(1)} %copy-done, bf16[512,128]{1,0:T(8,128)(2,1)S(1)} %collective-permute-done.3.greens.g1), custom_call_target="tpu_custom_call" | custom-call | tf_op jit(solution)/shard_map/dress_partner/pallas_call | solution.py:367
  24.7 1.4 %collective-permute-done.6.tensor = bf16[24,128,128]{2,1,0:T(8,128)(2,1)S(1)} collective-permute-done((bf16[24,128,128]{2,1,0:T(8,128)(2,1)}, bf16[24,128,128]{2,1,0:T(8,128)(2,1)S(1)}, u32[]{:S(2)}, u32[]{:S(2)}) %collective-permute-start.6) | collective-permute-done | bytes 786464 | tf_op jit(solution)/shard_map/ppermute | solution.py:390
  26.1 2.4 %join_back.1 = f32[48,128]{1,0:T(8,128)S(1)} custom-call(bf16[24,128,128]{2,1,0:T(8,128)(2,1)S(1)} %collective-permute-done.6.tensor, bf16[272,128]{1,0:T(8,128)(2,1)S(1)} %collective-permute-done.g_before, bf16[512,128]{1,0:T(8,128)(2,1)S(1)} %choose.1.greens.g0, bf16[512,128]{1,0:T(8,128)(2,1)S(1)} %collective-permute-done.3.greens.g1, ...), custom_call_target="tpu_custom_call" | custom-call | tf_op jit(solution)/shard_map/join_back/pallas_call | solution.py:367
  28.5 0.0 collective-permute-start.7
  28.5 1.8 %join.1.down = f32[96,128]{1,0:T(8,128)S(1)} custom-call(s32[16,4]{1,0:T(8,128)S(1)} %copy.8.win, bf16[24,128,128]{2,1,0:T(8,128)(2,1)S(1)} %collective-permute-done.6.tensor, bf16[272,128]{1,0:T(8,128)(2,1)S(1)} %collective-permute-done.g_before, bf16[48,16384]{1,0:T(8,128)(2,1)S(1)} %get-tuple-element.40.dressed0, ...), custom_call_target="tpu_custom_call" | custom-call | tf_op jit(solution)/shard_map/join/pallas_call | solution.py:367
  30.3 0.0 collective-permute-done.4.from_left
  30.3 1.0 %collective-permute-done.5.from_right = bf16[768,128]{1,0:T(8,128)(2,1)S(1)} collective-permute-done((bf16[768,128]{1,0:T(8,128)(2,1)S(1)}, bf16[768,128]{1,0:T(8,128)(2,1)S(1)}, u32[]{:S(2)}, u32[]{:S(2)}) %collective-permute-start.5) | collective-permute-done | bytes 196640 | tf_op jit(solution)/shard_map/ppermute | solution.py:390
  31.3 0.0 collective-permute-done.7.after
  31.3 0.7 %join_far.1 = (f32[48,128]{1,0:T(8,128)S(1)}, f32[48,128]{1,0:T(8,128)S(1)}) custom-call(bf16[48,8192]{1,0:T(8,128)(2,1)S(1)} %get-tuple-element.35.far0, bf16[48,8192]{1,0:T(8,128)(2,1)S(1)} %get-tuple-element.36.far1, bf16[768,128]{1,0:T(8,128)(2,1)S(1)} %collective-permute-done.4.from_left, bf16[768,128]{1,0:T(8,128)(2,1)S(1)} %collective-permute-done.5.from_right, ...), custom_call_target="tpu_custom_call" | custom-call | tf_op jit(solution)/shard_map/join_far/pallas_call | solution.py:367
  32.0 1.6 %collective-permute-start.8 = (f32[48,128]{1,0:T(8,128)S(1)}, f32[48,128]{1,0:T(8,128)S(1)}, u32[]{:S(2)}, u32[]{:S(2)}) collective-permute-start(f32[48,128]{1,0:T(8,128)S(1)} %get-tuple-element.44), channel_id=1, source_target_pairs={{0,16},{1,17},{2,18},{3,19},{4,20},{5,21},{6,22},{7,23},{8,24},{9,... | collective-permute-start | bytes 73736 | tf_op jit(solution)/shard_map/ppermute | solution.py:390
  33.6 2.3 %collective-permute-done.8.recv = f32[48,128]{1,0:T(8,128)S(1)} collective-permute-done((f32[48,128]{1,0:T(8,128)S(1)}, f32[48,128]{1,0:T(8,128)S(1)}, u32[]{:S(2)}, u32[]{:S(2)}) %collective-permute-start.8) | collective-permute-done | bytes 24608 | tf_op jit(solution)/shard_map/ppermute | solution.py:390
  35.9 0.7 %assemble.1 = f32[48,240]{1,0:T(8,128)} custom-call(f32[48,48]{1,0:T(8,128)S(1)} %get-tuple-element.34.polar0, f32[48,128]{1,0:T(8,128)S(1)} %get-tuple-element.43.own, f32[48,128]{1,0:T(8,128)S(1)} %collective-permute-done.8.recv), custom_call_target="tpu_custom_call" | custom-call | tf_op jit(solution)/shard_map/assemble/pallas_call | solution.py:367
Async XLA Ops:
  0.0 9.7 %copy-start.2 = (s32[1,4,4]{2,1,0:T(4,128)S(1)}, s32[1,4,4]{2,1,0:T(4,128)}, u32[]{:S(2)}) copy-start(s32[1,4,4]{2,1,0:T(4,128)} %tiles.5) | copy-start | bytes 196
  0.0 9.7 %copy-start = (bf16[1,48,128,128]{3,2,1,0:T(8,128)(2,1)S(1)}, bf16[1,48,128,128]{3,2,1,0:T(8,128)(2,1)}, u32[]{:S(2)}) copy-start(bf16[1,48,128,128]{3,2,1,0:T(8,128)(2,1)} %tensor.5) | copy-start | bytes 4718596
  0.0 9.6 %copy-start.3 = (s32[16,4]{0,1:T(4,128)S(1)}, s32[16,4]{0,1:T(4,128)}, u32[]{:S(2)}) copy-start(s32[16,4]{0,1:T(4,128)} %param.9) | copy-start | bytes 772
  2.4 8.5 %collective-permute-start = (bf16[272,128]{1,0:T(8,128)(2,1)}, bf16[272,128]{1,0:T(8,128)(2,1)S(1)}, u32[]{:S(2)}, u32[]{:S(2)}) collective-permute-start(bf16[272,128]{1,0:T(8,128)(2,1)} %get-tuple-element.26), channel_id=1, source_target_pairs={{0,1},{1,2},{2,3},{3,4},{4,5},{5,6},{6,7},{7,8},{8,9},{9,10},{10,1... | collective-permute-start | bytes 208904 | tf_op jit(solution)/shard_map/ppermute | solution.py:390
  2.9 12.7 %collective-permute-start.2 = (bf16[288,128]{1,0:T(8,128)(2,1)}, bf16[288,128]{1,0:T(8,128)(2,1)S(1)}, u32[]{:S(2)}, u32[]{:S(2)}) collective-permute-start(bf16[288,128]{1,0:T(8,128)(2,1)} %get-tuple-element.28), channel_id=1, source_target_pairs={{0,2},{1,3},{2,4},{3,5},{4,6},{5,7},{6,8},{7,9},{8,10},{9,11},{10,... | collective-permute-start | bytes 221192 | tf_op jit(solution)/shard_map/ppermute | solution.py:390
  5.5 10.1 %collective-permute-start.1 = (bf16[304,128]{1,0:T(8,128)(2,1)}, bf16[304,128]{1,0:T(8,128)(2,1)S(1)}, u32[]{:S(2)}, u32[]{:S(2)}) collective-permute-start(bf16[304,128]{1,0:T(8,128)(2,1)} %get-tuple-element.27), channel_id=1, source_target_pairs={{0,15},{1,0},{2,1},{3,2},{4,3},{5,4},{6,5},{7,6},{8,7},{9,8},{10,9... | collective-permute-start | bytes 233480 | tf_op jit(solution)/shard_map/ppermute | solution.py:390
  9.6 16.5 %collective-permute-start.6 = (bf16[24,128,128]{2,1,0:T(8,128)(2,1)}, bf16[24,128,128]{2,1,0:T(8,128)(2,1)S(1)}, u32[]{:S(2)}, u32[]{:S(2)}) collective-permute-start(bf16[24,128,128]{2,1,0:T(8,128)(2,1)} %get-tuple-element.37), channel_id=1, source_target_pairs={{0,1},{1,2},{2,3},{3,4},{4,5},{5,6},{6,7},{7,8},{8,9},{9,10},{10,1... | collective-permute-start | bytes 2359304 | tf_op jit(solution)/shard_map/ppermute | solution.py:390
  9.7 5.9 %copy-start.1 = (bf16[256,128]{1,0:T(8,128)(2,1)S(1)}, bf16[256,128]{1,0:T(8,128)(2,1)}, u32[]{:S(2)}) copy-start(bf16[256,128]{1,0:T(8,128)(2,1)} %get-tuple-element.25.g_self) | copy-start | bytes 196612
  10.8 19.5 %collective-permute-start.4 = (bf16[768,128]{1,0:T(8,128)(2,1)S(1)}, bf16[768,128]{1,0:T(8,128)(2,1)S(1)}, u32[]{:S(2)}, u32[]{:S(2)}) collective-permute-start(bf16[768,128]{1,0:T(8,128)(2,1)S(1)} %get-tuple-element.29), channel_id=1, source_target_pairs={{0,2},{1,3},{2,4},{3,5},{4,6},{5,7},{6,8},{7,9},{8,10},{9,11},{10,... | collective-permute-start | bytes 589832 | tf_op jit(solution)/shard_map/ppermute | solution.py:390
  10.9 20.4 %collective-permute-start.5 = (bf16[768,128]{1,0:T(8,128)(2,1)S(1)}, bf16[768,128]{1,0:T(8,128)(2,1)S(1)}, u32[]{:S(2)}, u32[]{:S(2)}) collective-permute-start(bf16[768,128]{1,0:T(8,128)(2,1)S(1)} %get-tuple-element.30), channel_id=1, source_target_pairs={{0,14},{1,15},{2,0},{3,1},{4,2},{5,3},{6,4},{7,5},{8,6},{9,7},{10,... | collective-permute-start | bytes 589832 | tf_op jit(solution)/shard_map/ppermute | solution.py:390
  17.0 5.4 %collective-permute-start.3 = (bf16[512,128]{1,0:T(8,128)(2,1)S(1)}, bf16[512,128]{1,0:T(8,128)(2,1)S(1)}, u32[]{:S(2)}, u32[]{:S(2)}) collective-permute-start(bf16[512,128]{1,0:T(8,128)(2,1)S(1)} %choose.1.greens.g0), channel_id=1, source_target_pairs={{0,16},{1,17},{2,18},{3,19},{4,20},{5,21},{6,22},{7,23},{8,24},{9,... | collective-permute-start | bytes 393224 | tf_op jit(solution)/shard_map/ppermute | solution.py:390
  28.5 2.9 %collective-permute-start.7 = (f32[48,128]{1,0:T(8,128)S(1)}, f32[48,128]{1,0:T(8,128)S(1)}, u32[]{:S(2)}, u32[]{:S(2)}) collective-permute-start(f32[48,128]{1,0:T(8,128)S(1)} %join_back.1), channel_id=1, source_target_pairs={{0,15},{1,0},{2,1},{3,2},{4,3},{5,4},{6,5},{7,6},{8,7},{9,8},{10,9... | collective-permute-start | bytes 73736 | tf_op jit(solution)/shard_map/ppermute | solution.py:390
  32.0 3.9 %collective-permute-start.8 = (f32[48,128]{1,0:T(8,128)S(1)}, f32[48,128]{1,0:T(8,128)S(1)}, u32[]{:S(2)}, u32[]{:S(2)}) collective-permute-start(f32[48,128]{1,0:T(8,128)S(1)} %get-tuple-element.44), channel_id=1, source_target_pairs={{0,16},{1,17},{2,18},{3,19},{4,20},{5,21},{6,22},{7,23},{8,24},{9,... | collective-permute-start | bytes 73736 | tf_op jit(solution)/shard_map/ppermute | solution.py:390

commit v15 on v14

--- a/solution.py
+++ b/solution.py
@@ -68,7 +68,7 @@
 
 
 def first(count, occ, virt, tiles_hbm, coulomb, *refs):
-    outs, (tiles, gs, part, sem, done) = refs[:5], refs[5:]
+    outs, (tiles, gs, fs, part, sem, done) = refs[:5], refs[5:]
     d = lax.axis_index("row")
     funcs = part.shape[0]
     half = lax.rem(lax.axis_index("grp"), 2)
@@ -86,7 +86,8 @@
                 place = gs.at[n, at : at + 64]
                 copies.append(pltpu.make_async_copy(green.at[:, columns], place, sem.at[4 * n + len(copies)]))
         rows = outs[n].shape[0]
-        groups.append((copies, pltpu.make_async_copy(gs.at[n, 0:rows], outs[n], done.at[n])))
+        source = fs if n == 3 else gs.at[n, 0:rows]
+        groups.append((copies, pltpu.make_async_copy(source, outs[n], done.at[n])))
     for n in range(3):
         piece = pl.ds(half * funcs + n * 8, 8)
         copy = pltpu.make_async_copy(coulomb.at[0, piece], part.at[n * 8 : n * 8 + 8], sem.at[17 + n])
@@ -97,12 +98,19 @@
             copy.start()
     list_copy.wait()
     short = tile_mask(tiles, 4).astype(BF)
-    for n in range(1, 4):
-        for at in (256, 272, 288):
+    for n in range(1, 3):
+        for at in (256, 272):
             gs[n, at : at + 16, :] = short
-    for copies, out in groups:
+    for n, (copies, out) in enumerate(groups):
         for copy in copies:
             copy.wait()
+        if n == 3:
+            lane = iota((64, 128), 1)
+            for base, at in ((0, 0), (128, 64)):
+                low = gs[3, base : base + 64, :].astype(F32)
+                high = gs[3, base + 64 : base + 128, :].astype(F32)
+                turned = jnp.where(lane < 64, pltpu.roll(low, 64, 1), pltpu.roll(high, 64, 1))
+                fs[at : at + 64, :] = jnp.where(lax.rem(d, 2) == 1, low, turned).astype(BF)
         out.start()
     for _, out in groups:
         out.wait()
@@ -145,21 +153,21 @@
     def position(atom, start):
         return lax.rem(atom - start + atoms, atoms) * 32
 
+    odd = lax.rem(d, 2) == 1
+    lane = iota((64, 128), 1)
+
     def whole(base):
+        far = g_far[base // 2 : base // 2 + 64, :].astype(F32)
+        turned = pltpu.roll(far, 64, 1)
+        fars = (
+            jnp.where(odd, far, jnp.where(lane < 64, 0.0, turned)).astype(BF),
+            jnp.where(odd, 0.0, jnp.where(lane < 64, turned, 0.0)).astype(BF),
+        )
         blocks = []
         for c in range(2):
             at = base + 64 * c
-            blocks.append(
-                jnp.concatenate(
-                    [
-                        g_far[at : at + 64, :],
-                        g_before[at : at + 64, :],
-                        g_self[at : at + 64, :],
-                        g_after[at : at + 64, :],
-                    ],
-                    axis=0,
-                )
-            )
+            parts = [fars[c]] + [g[at : at + 64, :] for g in (g_before, g_self, g_after)]
+            blocks.append(jnp.concatenate(parts, axis=0))
         return jnp.concatenate(blocks, axis=1)
 
     occ, virt = whole(0), whole(128)
@@ -397,14 +405,15 @@
         [
             shape((256, 128), BF),
             shape((272, 128), BF),
-            shape((304, 128), BF),
             shape((288, 128), BF),
+            shape((128, 128), BF),
             shape((funcs, 128, 128), BF),
         ],
         (green_occ, green_virt, tile_list, coulomb3c),
         [
             pltpu.SMEM((1, 4, 4), jnp.int32),
-            pltpu.VMEM((4, 304, 128), BF),
+            pltpu.VMEM((4, 288, 128), BF),
+            pltpu.VMEM((128, 128), BF),
             pltpu.VMEM((funcs, 128, 128), BF),
             pltpu.SemaphoreType.DMA((20,)),
             pltpu.SemaphoreType.DMA((7,)),

time: 36.8 us -> 37.1 us (level)
  no operation moved by 1% of the time
where the time goes in v15:
time: 37.1 us; the launch traced here: 36.9 us
  Pallas kernels  16.4 us (44%)
  starting transfers between devices  15.4 us (42%)
  waiting for transfers between devices  4.99 us (13%)
    pallas_call x9, Pallas kernels, call(): pl.pallas_call(kernel, name=name, in_specs=specs, out_specs=tuple((space...  16.4 us
    ppermute x9, starting transfers between devices, send(): return lax.ppermute(array, ('grp', 'row'), pairs)  15.4 us
    ppermute x9, waiting for transfers between devices, send(): return lax.ppermute(array, ('grp', 'row'), pairs)  4.99 us
  transfers between devices with their start and end apart: 9, of which 4 were waited for; matrix products, arithmetic and copies ran while one was open for 0% of the time, Pallas kernels for 34%

profile of v15, /device:TPU:0, one launch (start us, length us, event | category | flops | bytes accessed | tf_op | source)
XLA Modules:
  0.0 36.9 jit_solution(5794965285205557629)
XLA Ops:
  0.0 0.0 copy-start.2
  0.0 0.0 copy-start
  0.0 0.0 copy-start.3
  0.0 2.3 %first.1 = (bf16[256,128]{1,0:T(8,128)(2,1)}, bf16[272,128]{1,0:T(8,128)(2,1)}, bf16[288,128]{1,0:T(8,128)(2,1)}, bf16[128,128]{1,0:T(8,128)(2,1)}, bf16[24,128,128]{2,1,0:T(8,128)(2,1)}) custom-call(bf16[64,1024]{1,0:T(8,128)(2,1)} %occ.1, bf16[64,1024]{1,0:T(8,128)(2,1)} %virt.1, s32[1,4,4]{2,1,0:T(4,128)} %tiles.5, bf16[1,48,128,128]{3,2,1,0:T(8,128)(2,1)} %tensor.5), custom_call_target="tpu_custom_call" | custom-call | tf_op jit(solution)/shard_map/first/pallas_call | solution.py:375
  2.4 3.0 %collective-permute-start.2 = (bf16[128,128]{1,0:T(8,128)(2,1)}, bf16[128,128]{1,0:T(8,128)(2,1)S(1)}, u32[]{:S(2)}, u32[]{:S(2)}) collective-permute-start(bf16[128,128]{1,0:T(8,128)(2,1)} %get-tuple-element.28), channel_id=1, source_target_pairs={{0,2},{1,3},{2,4},{3,5},{4,6},{5,7},{6,8},{7,9},{8,10},{9,11},{10,... | collective-permute-start | bytes 98312 | tf_op jit(solution)/shard_map/ppermute | solution.py:398
  5.4 0.0 collective-permute-start
  5.4 4.4 %collective-permute-start.1 = (bf16[288,128]{1,0:T(8,128)(2,1)}, bf16[288,128]{1,0:T(8,128)(2,1)S(1)}, u32[]{:S(2)}, u32[]{:S(2)}) collective-permute-start(bf16[288,128]{1,0:T(8,128)(2,1)} %get-tuple-element.27), channel_id=1, source_target_pairs={{0,15},{1,0},{2,1},{3,2},{4,3},{5,4},{6,5},{7,6},{8,7},{9,8},{10,9... | collective-permute-start | bytes 221192 | tf_op jit(solution)/shard_map/ppermute | solution.py:398
  9.8 0.0 collective-permute-start.6
  9.8 0.0 copy-done.3
  9.8 0.1 copy.8.win
  9.9 0.0 copy-done.2
  9.9 0.0 copy-done
  9.9 0.0 copy-start.1
  9.9 1.1 %far_tiles.1 = (bf16[768,128]{1,0:T(8,128)(2,1)S(1)}, bf16[768,128]{1,0:T(8,128)(2,1)S(1)}) custom-call(s32[16,4]{1,0:T(8,128)S(1)} %copy.8.win, s32[1,4,4]{2,1,0:T(4,128)S(1)} %copy-done.2, bf16[1,48,128,128]{3,2,1,0:T(8,128)(2,1)S(1)} %copy-done), custom_call_target="tpu_custom_call" | custom-call | flops 68719476736 | tf_op jit(solution)/shard_map/far_tiles/pallas_call | solution.py:375
  11.1 0.1 collective-permute-start.4
  11.1 0.0 collective-permute-done.2.g_far
  11.1 4.7 %collective-permute-start.5 = (bf16[768,128]{1,0:T(8,128)(2,1)S(1)}, bf16[768,128]{1,0:T(8,128)(2,1)S(1)}, u32[]{:S(2)}, u32[]{:S(2)}) collective-permute-start(bf16[768,128]{1,0:T(8,128)(2,1)S(1)} %get-tuple-element.30), channel_id=1, source_target_pairs={{0,14},{1,15},{2,0},{3,1},{4,2},{5,3},{6,4},{7,5},{8,6},{9,7},{10,... | collective-permute-start | bytes 589832 | tf_op jit(solution)/shard_map/ppermute | solution.py:398
  15.9 0.0 collective-permute-done.g_before
  15.9 0.0 collective-permute-done.1.g_after
  15.9 0.0 copy-done.1
  15.9 1.4 %choose.1.greens.g0 = bf16[512,128]{1,0:T(8,128)(2,1)S(1)} custom-call(s32[16,4]{1,0:T(8,128)S(1)} %copy.8.win, bf16[256,128]{1,0:T(8,128)(2,1)S(1)} %copy-done.1, bf16[272,128]{1,0:T(8,128)(2,1)S(1)} %collective-permute-done.g_before, bf16[288,128]{1,0:T(8,128)(2,1)S(1)} %collective-permute-done.1.g_after, bf16[128,128]{1,0:T(8,128)(2,1)S(1)} %collective-permute-done.2.g_far), custom_call_target="tpu_custom_call" | custom-call | tf_op jit(solution)/shard_map/choose/pallas_call | solution.py:375
  17.3 1.6 %collective-permute-start.3 = (bf16[512,128]{1,0:T(8,128)(2,1)S(1)}, bf16[512,128]{1,0:T(8,128)(2,1)S(1)}, u32[]{:S(2)}, u32[]{:S(2)}) collective-permute-start(bf16[512,128]{1,0:T(8,128)(2,1)S(1)} %choose.1.greens.g0), channel_id=1, source_target_pairs={{0,16},{1,17},{2,18},{3,19},{4,20},{5,21},{6,22},{7,23},{8,24},{9,... | collective-permute-start | bytes 393224 | tf_op jit(solution)/shard_map/ppermute | solution.py:398
  18.9 3.5 %dress_own.1 = (f32[48,48]{1,0:T(8,128)S(1)}, bf16[48,16384]{1,0:T(8,128)(2,1)S(1)}, bf16[48,16384]{1,0:T(8,128)(2,1)S(1)}, bf16[48,8192]{1,0:T(8,128)(2,1)S(1)}) custom-call(s32[16,4]{1,0:T(8,128)S(1)} %copy.8.win, s32[1,4,4]{2,1,0:T(4,128)S(1)} %copy-done.2, bf16[1,48,128,128]{3,2,1,0:T(8,128)(2,1)S(1)} %copy-done, bf16[512,128]{1,0:T(8,128)(2,1)S(1)} %choose.1.greens.g0), custom_call_target="tpu_custom_call" | custom-call | tf_op jit(solution)/shard_map/dress_own/pallas_call | solution.py:375
  22.4 0.3 collective-permute-done.3.greens.g1
  22.7 2.3 %dress_partner.1 = (bf16[48,16384]{1,0:T(8,128)(2,1)S(1)}, bf16[48,8192]{1,0:T(8,128)(2,1)S(1)}) custom-call(s32[16,4]{1,0:T(8,128)S(1)} %copy.8.win, s32[1,4,4]{2,1,0:T(4,128)S(1)} %copy-done.2, bf16[1,48,128,128]{3,2,1,0:T(8,128)(2,1)S(1)} %copy-done, bf16[512,128]{1,0:T(8,128)(2,1)S(1)} %collective-permute-done.3.greens.g1), custom_call_target="tpu_custom_call" | custom-call | tf_op jit(solution)/shard_map/dress_partner/pallas_call | solution.py:375
  25.0 1.4 %collective-permute-done.6.tensor = bf16[24,128,128]{2,1,0:T(8,128)(2,1)S(1)} collective-permute-done((bf16[24,128,128]{2,1,0:T(8,128)(2,1)}, bf16[24,128,128]{2,1,0:T(8,128)(2,1)S(1)}, u32[]{:S(2)}, u32[]{:S(2)}) %collective-permute-start.6) | collective-permute-done | bytes 786464 | tf_op jit(solution)/shard_map/ppermute | solution.py:398
  26.4 2.4 %join_back.1 = f32[48,128]{1,0:T(8,128)S(1)} custom-call(bf16[24,128,128]{2,1,0:T(8,128)(2,1)S(1)} %collective-permute-done.6.tensor, bf16[272,128]{1,0:T(8,128)(2,1)S(1)} %collective-permute-done.g_before, bf16[512,128]{1,0:T(8,128)(2,1)S(1)} %choose.1.greens.g0, bf16[512,128]{1,0:T(8,128)(2,1)S(1)} %collective-permute-done.3.greens.g1, ...), custom_call_target="tpu_custom_call" | custom-call | tf_op jit(solution)/shard_map/join_back/pallas_call | solution.py:375
  28.7 0.0 collective-permute-start.7
  28.8 1.8 %join.1.down = f32[96,128]{1,0:T(8,128)S(1)} custom-call(s32[16,4]{1,0:T(8,128)S(1)} %copy.8.win, bf16[24,128,128]{2,1,0:T(8,128)(2,1)S(1)} %collective-permute-done.6.tensor, bf16[272,128]{1,0:T(8,128)(2,1)S(1)} %collective-permute-done.g_before, bf16[48,16384]{1,0:T(8,128)(2,1)S(1)} %get-tuple-element.40.dressed0, ...), custom_call_target="tpu_custom_call" | custom-call | tf_op jit(solution)/shard_map/join/pallas_call | solution.py:375
  30.6 0.0 collective-permute-done.4.from_left
  30.6 1.0 %collective-permute-done.5.from_right = bf16[768,128]{1,0:T(8,128)(2,1)S(1)} collective-permute-done((bf16[768,128]{1,0:T(8,128)(2,1)S(1)}, bf16[768,128]{1,0:T(8,128)(2,1)S(1)}, u32[]{:S(2)}, u32[]{:S(2)}) %collective-permute-start.5) | collective-permute-done | bytes 196640 | tf_op jit(solution)/shard_map/ppermute | solution.py:398
  31.6 0.0 collective-permute-done.7.after
  31.6 0.7 %join_far.1 = (f32[48,128]{1,0:T(8,128)S(1)}, f32[48,128]{1,0:T(8,128)S(1)}) custom-call(bf16[48,8192]{1,0:T(8,128)(2,1)S(1)} %get-tuple-element.35.far0, bf16[48,8192]{1,0:T(8,128)(2,1)S(1)} %get-tuple-element.36.far1, bf16[768,128]{1,0:T(8,128)(2,1)S(1)} %collective-permute-done.4.from_left, bf16[768,128]{1,0:T(8,128)(2,1)S(1)} %collective-permute-done.5.from_right, ...), custom_call_target="tpu_custom_call" | custom-call | tf_op jit(solution)/shard_map/join_far/pallas_call | solution.py:375
  32.3 1.6 %collective-permute-start.8 = (f32[48,128]{1,0:T(8,128)S(1)}, f32[48,128]{1,0:T(8,128)S(1)}, u32[]{:S(2)}, u32[]{:S(2)}) collective-permute-start(f32[48,128]{1,0:T(8,128)S(1)} %get-tuple-element.44), channel_id=1, source_target_pairs={{0,16},{1,17},{2,18},{3,19},{4,20},{5,21},{6,22},{7,23},{8,24},{9,... | collective-permute-start | bytes 73736 | tf_op jit(solution)/shard_map/ppermute | solution.py:398
  33.8 2.3 %collective-permute-done.8.recv = f32[48,128]{1,0:T(8,128)S(1)} collective-permute-done((f32[48,128]{1,0:T(8,128)S(1)}, f32[48,128]{1,0:T(8,128)S(1)}, u32[]{:S(2)}, u32[]{:S(2)}) %collective-permute-start.8) | collective-permute-done | bytes 24608 | tf_op jit(solution)/shard_map/ppermute | solution.py:398
  36.2 0.7 %assemble.1 = f32[48,240]{1,0:T(8,128)} custom-call(f32[48,48]{1,0:T(8,128)S(1)} %get-tuple-element.34.polar0, f32[48,128]{1,0:T(8,128)S(1)} %get-tuple-element.43.own, f32[48,128]{1,0:T(8,128)S(1)} %collective-permute-done.8.recv), custom_call_target="tpu_custom_call" | custom-call | tf_op jit(solution)/shard_map/assemble/pallas_call | solution.py:375
Async XLA Ops:
  0.0 9.9 %copy-start.2 = (s32[1,4,4]{2,1,0:T(4,128)S(1)}, s32[1,4,4]{2,1,0:T(4,128)}, u32[]{:S(2)}) copy-start(s32[1,4,4]{2,1,0:T(4,128)} %tiles.5) | copy-start | bytes 196
  0.0 9.9 %copy-start = (bf16[1,48,128,128]{3,2,1,0:T(8,128)(2,1)S(1)}, bf16[1,48,128,128]{3,2,1,0:T(8,128)(2,1)}, u32[]{:S(2)}) copy-start(bf16[1,48,128,128]{3,2,1,0:T(8,128)(2,1)} %tensor.5) | copy-start | bytes 4718596
  0.0 9.8 %copy-start.3 = (s32[16,4]{0,1:T(4,128)S(1)}, s32[16,4]{0,1:T(4,128)}, u32[]{:S(2)}) copy-start(s32[16,4]{0,1:T(4,128)} %param.9) | copy-start | bytes 772
  2.4 8.8 %collective-permute-start.2 = (bf16[128,128]{1,0:T(8,128)(2,1)}, bf16[128,128]{1,0:T(8,128)(2,1)S(1)}, u32[]{:S(2)}, u32[]{:S(2)}) collective-permute-start(bf16[128,128]{1,0:T(8,128)(2,1)} %get-tuple-element.28), channel_id=1, source_target_pairs={{0,2},{1,3},{2,4},{3,5},{4,6},{5,7},{6,8},{7,9},{8,10},{9,11},{10,... | collective-permute-start | bytes 98312 | tf_op jit(solution)/shard_map/ppermute | solution.py:398
  5.4 10.5 %collective-permute-start = (bf16[272,128]{1,0:T(8,128)(2,1)}, bf16[272,128]{1,0:T(8,128)(2,1)S(1)}, u32[]{:S(2)}, u32[]{:S(2)}) collective-permute-start(bf16[272,128]{1,0:T(8,128)(2,1)} %get-tuple-element.26), channel_id=1, source_target_pairs={{0,1},{1,2},{2,3},{3,4},{4,5},{5,6},{6,7},{7,8},{8,9},{9,10},{10,1... | collective-permute-start | bytes 208904 | tf_op jit(solution)/shard_map/ppermute | solution.py:398
  5.4 10.5 %collective-permute-start.1 = (bf16[288,128]{1,0:T(8,128)(2,1)}, bf16[288,128]{1,0:T(8,128)(2,1)S(1)}, u32[]{:S(2)}, u32[]{:S(2)}) collective-permute-start(bf16[288,128]{1,0:T(8,128)(2,1)} %get-tuple-element.27), channel_id=1, source_target_pairs={{0,15},{1,0},{2,1},{3,2},{4,3},{5,4},{6,5},{7,6},{8,7},{9,8},{10,9... | collective-permute-start | bytes 221192 | tf_op jit(solution)/shard_map/ppermute | solution.py:398
  9.8 16.5 %collective-permute-start.6 = (bf16[24,128,128]{2,1,0:T(8,128)(2,1)}, bf16[24,128,128]{2,1,0:T(8,128)(2,1)S(1)}, u32[]{:S(2)}, u32[]{:S(2)}) collective-permute-start(bf16[24,128,128]{2,1,0:T(8,128)(2,1)} %get-tuple-element.37), channel_id=1, source_target_pairs={{0,1},{1,2},{2,3},{3,4},{4,5},{5,6},{6,7},{7,8},{8,9},{9,10},{10,1... | collective-permute-start | bytes 2359304 | tf_op jit(solution)/shard_map/ppermute | solution.py:398
  9.9 5.9 %copy-start.1 = (bf16[256,128]{1,0:T(8,128)(2,1)S(1)}, bf16[256,128]{1,0:T(8,128)(2,1)}, u32[]{:S(2)}) copy-start(bf16[256,128]{1,0:T(8,128)(2,1)} %get-tuple-element.25.g_self) | copy-start | bytes 196612
  11.1 19.5 %collective-permute-start.4 = (bf16[768,128]{1,0:T(8,128)(2,1)S(1)}, bf16[768,128]{1,0:T(8,128)(2,1)S(1)}, u32[]{:S(2)}, u32[]{:S(2)}) collective-permute-start(bf16[768,128]{1,0:T(8,128)(2,1)S(1)} %get-tuple-element.29), channel_id=1, source_target_pairs={{0,2},{1,3},{2,4},{3,5},{4,6},{5,7},{6,8},{7,9},{8,10},{9,11},{10,... | collective-permute-start | bytes 589832 | tf_op jit(solution)/shard_map/ppermute | solution.py:398
  11.1 20.4 %collective-permute-start.5 = (bf16[768,128]{1,0:T(8,128)(2,1)S(1)}, bf16[768,128]{1,0:T(8,128)(2,1)S(1)}, u32[]{:S(2)}, u32[]{:S(2)}) collective-permute-start(bf16[768,128]{1,0:T(8,128)(2,1)S(1)} %get-tuple-element.30), channel_id=1, source_target_pairs={{0,14},{1,15},{2,0},{3,1},{4,2},{5,3},{6,4},{7,5},{8,6},{9,7},{10,... | collective-permute-start | bytes 589832 | tf_op jit(solution)/shard_map/ppermute | solution.py:398
  17.3 5.4 %collective-permute-start.3 = (bf16[512,128]{1,0:T(8,128)(2,1)S(1)}, bf16[512,128]{1,0:T(8,128)(2,1)S(1)}, u32[]{:S(2)}, u32[]{:S(2)}) collective-permute-start(bf16[512,128]{1,0:T(8,128)(2,1)S(1)} %choose.1.greens.g0), channel_id=1, source_target_pairs={{0,16},{1,17},{2,18},{3,19},{4,20},{5,21},{6,22},{7,23},{8,24},{9,... | collective-permute-start | bytes 393224 | tf_op jit(solution)/shard_map/ppermute | solution.py:398
  28.7 2.9 %collective-permute-start.7 = (f32[48,128]{1,0:T(8,128)S(1)}, f32[48,128]{1,0:T(8,128)S(1)}, u32[]{:S(2)}, u32[]{:S(2)}) collective-permute-start(f32[48,128]{1,0:T(8,128)S(1)} %join_back.1), channel_id=1, source_target_pairs={{0,15},{1,0},{2,1},{3,2},{4,3},{5,4},{6,5},{7,6},{8,7},{9,8},{10,9... | collective-permute-start | bytes 73736 | tf_op jit(solution)/shard_map/ppermute | solution.py:398
  32.3 3.9 %collective-permute-start.8 = (f32[48,128]{1,0:T(8,128)S(1)}, f32[48,128]{1,0:T(8,128)S(1)}, u32[]{:S(2)}, u32[]{:S(2)}) collective-permute-start(f32[48,128]{1,0:T(8,128)S(1)} %get-tuple-element.44), channel_id=1, source_target_pairs={{0,16},{1,17},{2,18},{3,19},{4,20},{5,21},{6,22},{7,23},{8,24},{9,... | collective-permute-start | bytes 73736 | tf_op jit(solution)/shard_map/ppermute | solution.py:398

commit v16 on v14

--- a/solution.py
+++ b/solution.py
@@ -92,6 +92,7 @@
         copy = pltpu.make_async_copy(coulomb.at[0, piece], part.at[n * 8 : n * 8 + 8], sem.at[17 + n])
         out = pltpu.make_async_copy(part.at[n * 8 : n * 8 + 8], outs[4].at[n * 8 : n * 8 + 8], done.at[4 + n])
         groups.append(([copy], out))
+    groups = groups[4:] + groups[:4]
     for copies, _ in groups:
         for copy in copies:
             copy.start()

time: 36.8 us -> 36.8 us (level)
  no operation moved by 1% of the time
where the time goes in v16:
time: 36.8 us; the launch traced here: 36.6 us
  Pallas kernels  16.3 us (44%)
  starting transfers between devices  15.1 us (41%)
  waiting for transfers between devices  5.06 us (14%)
    pallas_call x9, Pallas kernels, call(): pl.pallas_call(kernel, name=name, in_specs=specs, out_specs=tuple((space...  16.3 us
    ppermute x9, starting transfers between devices, send(): return lax.ppermute(array, ('grp', 'row'), pairs)  15.1 us
    ppermute x9, waiting for transfers between devices, send(): return lax.ppermute(array, ('grp', 'row'), pairs)  5.06 us
  transfers between devices with their start and end apart: 9, of which 4 were waited for; matrix products, arithmetic and copies ran while one was open for 0% of the time, Pallas kernels for 34%

profile of v16, /device:TPU:0, one launch (start us, length us, event | category | flops | bytes accessed | tf_op | source)
XLA Modules:
  0.0 36.6 jit_solution(9396938198461995455)
XLA Ops:
  0.0 0.0 copy-start.2
  0.0 0.0 copy-start
  0.0 0.0 copy-start.3
  0.0 2.3 %first.1 = (bf16[256,128]{1,0:T(8,128)(2,1)}, bf16[272,128]{1,0:T(8,128)(2,1)}, bf16[304,128]{1,0:T(8,128)(2,1)}, bf16[288,128]{1,0:T(8,128)(2,1)}, bf16[24,128,128]{2,1,0:T(8,128)(2,1)}) custom-call(bf16[64,1024]{1,0:T(8,128)(2,1)} %occ.1, bf16[64,1024]{1,0:T(8,128)(2,1)} %virt.1, s32[1,4,4]{2,1,0:T(4,128)} %tiles.5, bf16[1,48,128,128]{3,2,1,0:T(8,128)(2,1)} %tensor.5), custom_call_target="tpu_custom_call" | custom-call | tf_op jit(solution)/shard_map/first/pallas_call | solution.py:368
  2.3 0.5 %collective-permute-start = (bf16[272,128]{1,0:T(8,128)(2,1)}, bf16[272,128]{1,0:T(8,128)(2,1)S(1)}, u32[]{:S(2)}, u32[]{:S(2)}) collective-permute-start(bf16[272,128]{1,0:T(8,128)(2,1)} %get-tuple-element.26), channel_id=1, source_target_pairs={{0,1},{1,2},{2,3},{3,4},{4,5},{5,6},{6,7},{7,8},{8,9},{9,10},{10,1... | collective-permute-start | bytes 208904 | tf_op jit(solution)/shard_map/ppermute | solution.py:391
  2.9 2.6 %collective-permute-start.2 = (bf16[288,128]{1,0:T(8,128)(2,1)}, bf16[288,128]{1,0:T(8,128)(2,1)S(1)}, u32[]{:S(2)}, u32[]{:S(2)}) collective-permute-start(bf16[288,128]{1,0:T(8,128)(2,1)} %get-tuple-element.28), channel_id=1, source_target_pairs={{0,2},{1,3},{2,4},{3,5},{4,6},{5,7},{6,8},{7,9},{8,10},{9,11},{10,... | collective-permute-start | bytes 221192 | tf_op jit(solution)/shard_map/ppermute | solution.py:391
  5.4 4.1 %collective-permute-start.1 = (bf16[304,128]{1,0:T(8,128)(2,1)}, bf16[304,128]{1,0:T(8,128)(2,1)S(1)}, u32[]{:S(2)}, u32[]{:S(2)}) collective-permute-start(bf16[304,128]{1,0:T(8,128)(2,1)} %get-tuple-element.27), channel_id=1, source_target_pairs={{0,15},{1,0},{2,1},{3,2},{4,3},{5,4},{6,5},{7,6},{8,7},{9,8},{10,9... | collective-permute-start | bytes 233480 | tf_op jit(solution)/shard_map/ppermute | solution.py:391
  9.5 0.0 collective-permute-start.6
  9.5 0.0 copy-done.3
  9.5 0.1 copy.8.win
  9.6 0.0 copy-done.2
  9.6 0.0 copy-done
  9.6 0.0 copy-start.1
  9.6 1.1 %far_tiles.1 = (bf16[768,128]{1,0:T(8,128)(2,1)S(1)}, bf16[768,128]{1,0:T(8,128)(2,1)S(1)}) custom-call(s32[16,4]{1,0:T(8,128)S(1)} %copy.8.win, s32[1,4,4]{2,1,0:T(4,128)S(1)} %copy-done.2, bf16[1,48,128,128]{3,2,1,0:T(8,128)(2,1)S(1)} %copy-done), custom_call_target="tpu_custom_call" | custom-call | flops 68719476736 | tf_op jit(solution)/shard_map/far_tiles/pallas_call | solution.py:368
  10.8 0.1 collective-permute-start.4
  10.8 0.0 collective-permute-done.g_before
  10.8 4.7 %collective-permute-start.5 = (bf16[768,128]{1,0:T(8,128)(2,1)S(1)}, bf16[768,128]{1,0:T(8,128)(2,1)S(1)}, u32[]{:S(2)}, u32[]{:S(2)}) collective-permute-start(bf16[768,128]{1,0:T(8,128)(2,1)S(1)} %get-tuple-element.30), channel_id=1, source_target_pairs={{0,14},{1,15},{2,0},{3,1},{4,2},{5,3},{6,4},{7,5},{8,6},{9,7},{10,... | collective-permute-start | bytes 589832 | tf_op jit(solution)/shard_map/ppermute | solution.py:391
  15.5 0.0 collective-permute-done.2.g_far
  15.5 0.0 collective-permute-done.1.g_after
  15.6 0.0 copy-done.1
  15.6 1.4 %choose.1.greens.g0 = bf16[512,128]{1,0:T(8,128)(2,1)S(1)} custom-call(s32[16,4]{1,0:T(8,128)S(1)} %copy.8.win, bf16[256,128]{1,0:T(8,128)(2,1)S(1)} %copy-done.1, bf16[272,128]{1,0:T(8,128)(2,1)S(1)} %collective-permute-done.g_before, bf16[304,128]{1,0:T(8,128)(2,1)S(1)} %collective-permute-done.1.g_after, bf16[288,128]{1,0:T(8,128)(2,1)S(1)} %collective-permute-done.2.g_far), custom_call_target="tpu_custom_call" | custom-call | tf_op jit(solution)/shard_map/choose/pallas_call | solution.py:368
  16.9 1.6 %collective-permute-start.3 = (bf16[512,128]{1,0:T(8,128)(2,1)S(1)}, bf16[512,128]{1,0:T(8,128)(2,1)S(1)}, u32[]{:S(2)}, u32[]{:S(2)}) collective-permute-start(bf16[512,128]{1,0:T(8,128)(2,1)S(1)} %choose.1.greens.g0), channel_id=1, source_target_pairs={{0,16},{1,17},{2,18},{3,19},{4,20},{5,21},{6,22},{7,23},{8,24},{9,... | collective-permute-start | bytes 393224 | tf_op jit(solution)/shard_map/ppermute | solution.py:391
  18.5 3.5 %dress_own.1 = (f32[48,48]{1,0:T(8,128)S(1)}, bf16[48,16384]{1,0:T(8,128)(2,1)S(1)}, bf16[48,16384]{1,0:T(8,128)(2,1)S(1)}, bf16[48,8192]{1,0:T(8,128)(2,1)S(1)}) custom-call(s32[16,4]{1,0:T(8,128)S(1)} %copy.8.win, s32[1,4,4]{2,1,0:T(4,128)S(1)} %copy-done.2, bf16[1,48,128,128]{3,2,1,0:T(8,128)(2,1)S(1)} %copy-done, bf16[512,128]{1,0:T(8,128)(2,1)S(1)} %choose.1.greens.g0), custom_call_target="tpu_custom_call" | custom-call | tf_op jit(solution)/shard_map/dress_own/pallas_call | solution.py:368
  22.0 0.3 collective-permute-done.3.greens.g1
  22.3 2.3 %dress_partner.1 = (bf16[48,16384]{1,0:T(8,128)(2,1)S(1)}, bf16[48,8192]{1,0:T(8,128)(2,1)S(1)}) custom-call(s32[16,4]{1,0:T(8,128)S(1)} %copy.8.win, s32[1,4,4]{2,1,0:T(4,128)S(1)} %copy-done.2, bf16[1,48,128,128]{3,2,1,0:T(8,128)(2,1)S(1)} %copy-done, bf16[512,128]{1,0:T(8,128)(2,1)S(1)} %collective-permute-done.3.greens.g1), custom_call_target="tpu_custom_call" | custom-call | tf_op jit(solution)/shard_map/dress_partner/pallas_call | solution.py:368
  24.6 1.4 %collective-permute-done.6.tensor = bf16[24,128,128]{2,1,0:T(8,128)(2,1)S(1)} collective-permute-done((bf16[24,128,128]{2,1,0:T(8,128)(2,1)}, bf16[24,128,128]{2,1,0:T(8,128)(2,1)S(1)}, u32[]{:S(2)}, u32[]{:S(2)}) %collective-permute-start.6) | collective-permute-done | bytes 786464 | tf_op jit(solution)/shard_map/ppermute | solution.py:391
  26.1 2.4 %join_back.1 = f32[48,128]{1,0:T(8,128)S(1)} custom-call(bf16[24,128,128]{2,1,0:T(8,128)(2,1)S(1)} %collective-permute-done.6.tensor, bf16[272,128]{1,0:T(8,128)(2,1)S(1)} %collective-permute-done.g_before, bf16[512,128]{1,0:T(8,128)(2,1)S(1)} %choose.1.greens.g0, bf16[512,128]{1,0:T(8,128)(2,1)S(1)} %collective-permute-done.3.greens.g1, ...), custom_call_target="tpu_custom_call" | custom-call | tf_op jit(solution)/shard_map/join_back/pallas_call | solution.py:368
  28.4 0.0 collective-permute-start.7
  28.4 1.8 %join.1.down = f32[96,128]{1,0:T(8,128)S(1)} custom-call(s32[16,4]{1,0:T(8,128)S(1)} %copy.8.win, bf16[24,128,128]{2,1,0:T(8,128)(2,1)S(1)} %collective-permute-done.6.tensor, bf16[272,128]{1,0:T(8,128)(2,1)S(1)} %collective-permute-done.g_before, bf16[48,16384]{1,0:T(8,128)(2,1)S(1)} %get-tuple-element.40.dressed0, ...), custom_call_target="tpu_custom_call" | custom-call | tf_op jit(solution)/shard_map/join/pallas_call | solution.py:368
  30.3 0.0 collective-permute-done.4.from_left
  30.3 1.0 %collective-permute-done.5.from_right = bf16[768,128]{1,0:T(8,128)(2,1)S(1)} collective-permute-done((bf16[768,128]{1,0:T(8,128)(2,1)S(1)}, bf16[768,128]{1,0:T(8,128)(2,1)S(1)}, u32[]{:S(2)}, u32[]{:S(2)}) %collective-permute-start.5) | collective-permute-done | bytes 196640 | tf_op jit(solution)/shard_map/ppermute | solution.py:391
  31.3 0.0 collective-permute-done.7.after
  31.3 0.7 %join_far.1 = (f32[48,128]{1,0:T(8,128)S(1)}, f32[48,128]{1,0:T(8,128)S(1)}) custom-call(bf16[48,8192]{1,0:T(8,128)(2,1)S(1)} %get-tuple-element.35.far0, bf16[48,8192]{1,0:T(8,128)(2,1)S(1)} %get-tuple-element.36.far1, bf16[768,128]{1,0:T(8,128)(2,1)S(1)} %collective-permute-done.4.from_left, bf16[768,128]{1,0:T(8,128)(2,1)S(1)} %collective-permute-done.5.from_right, ...), custom_call_target="tpu_custom_call" | custom-call | tf_op jit(solution)/shard_map/join_far/pallas_call | solution.py:368
  32.0 1.6 %collective-permute-start.8 = (f32[48,128]{1,0:T(8,128)S(1)}, f32[48,128]{1,0:T(8,128)S(1)}, u32[]{:S(2)}, u32[]{:S(2)}) collective-permute-start(f32[48,128]{1,0:T(8,128)S(1)} %get-tuple-element.44), channel_id=1, source_target_pairs={{0,16},{1,17},{2,18},{3,19},{4,20},{5,21},{6,22},{7,23},{8,24},{9,... | collective-permute-start | bytes 73736 | tf_op jit(solution)/shard_map/ppermute | solution.py:391
  33.5 2.3 %collective-permute-done.8.recv = f32[48,128]{1,0:T(8,128)S(1)} collective-permute-done((f32[48,128]{1,0:T(8,128)S(1)}, f32[48,128]{1,0:T(8,128)S(1)}, u32[]{:S(2)}, u32[]{:S(2)}) %collective-permute-start.8) | collective-permute-done | bytes 24608 | tf_op jit(solution)/shard_map/ppermute | solution.py:391
  35.9 0.7 %assemble.1 = f32[48,240]{1,0:T(8,128)} custom-call(f32[48,48]{1,0:T(8,128)S(1)} %get-tuple-element.34.polar0, f32[48,128]{1,0:T(8,128)S(1)} %get-tuple-element.43.own, f32[48,128]{1,0:T(8,128)S(1)} %collective-permute-done.8.recv), custom_call_target="tpu_custom_call" | custom-call | tf_op jit(solution)/shard_map/assemble/pallas_call | solution.py:368
Async XLA Ops:
  0.0 9.6 %copy-start.2 = (s32[1,4,4]{2,1,0:T(4,128)S(1)}, s32[1,4,4]{2,1,0:T(4,128)}, u32[]{:S(2)}) copy-start(s32[1,4,4]{2,1,0:T(4,128)} %tiles.5) | copy-start | bytes 196
  0.0 9.6 %copy-start = (bf16[1,48,128,128]{3,2,1,0:T(8,128)(2,1)S(1)}, bf16[1,48,128,128]{3,2,1,0:T(8,128)(2,1)}, u32[]{:S(2)}) copy-start(bf16[1,48,128,128]{3,2,1,0:T(8,128)(2,1)} %tensor.5) | copy-start | bytes 4718596
  0.0 9.5 %copy-start.3 = (s32[16,4]{0,1:T(4,128)S(1)}, s32[16,4]{0,1:T(4,128)}, u32[]{:S(2)}) copy-start(s32[16,4]{0,1:T(4,128)} %param.9) | copy-start | bytes 772
  2.3 8.5 %collective-permute-start = (bf16[272,128]{1,0:T(8,128)(2,1)}, bf16[272,128]{1,0:T(8,128)(2,1)S(1)}, u32[]{:S(2)}, u32[]{:S(2)}) collective-permute-start(bf16[272,128]{1,0:T(8,128)(2,1)} %get-tuple-element.26), channel_id=1, source_target_pairs={{0,1},{1,2},{2,3},{3,4},{4,5},{5,6},{6,7},{7,8},{8,9},{9,10},{10,1... | collective-permute-start | bytes 208904 | tf_op jit(solution)/shard_map/ppermute | solution.py:391
  2.9 12.7 %collective-permute-start.2 = (bf16[288,128]{1,0:T(8,128)(2,1)}, bf16[288,128]{1,0:T(8,128)(2,1)S(1)}, u32[]{:S(2)}, u32[]{:S(2)}) collective-permute-start(bf16[288,128]{1,0:T(8,128)(2,1)} %get-tuple-element.28), channel_id=1, source_target_pairs={{0,2},{1,3},{2,4},{3,5},{4,6},{5,7},{6,8},{7,9},{8,10},{9,11},{10,... | collective-permute-start | bytes 221192 | tf_op jit(solution)/shard_map/ppermute | solution.py:391
  5.4 10.1 %collective-permute-start.1 = (bf16[304,128]{1,0:T(8,128)(2,1)}, bf16[304,128]{1,0:T(8,128)(2,1)S(1)}, u32[]{:S(2)}, u32[]{:S(2)}) collective-permute-start(bf16[304,128]{1,0:T(8,128)(2,1)} %get-tuple-element.27), channel_id=1, source_target_pairs={{0,15},{1,0},{2,1},{3,2},{4,3},{5,4},{6,5},{7,6},{8,7},{9,8},{10,9... | collective-permute-start | bytes 233480 | tf_op jit(solution)/shard_map/ppermute | solution.py:391
  9.5 16.5 %collective-permute-start.6 = (bf16[24,128,128]{2,1,0:T(8,128)(2,1)}, bf16[24,128,128]{2,1,0:T(8,128)(2,1)S(1)}, u32[]{:S(2)}, u32[]{:S(2)}) collective-permute-start(bf16[24,128,128]{2,1,0:T(8,128)(2,1)} %get-tuple-element.37), channel_id=1, source_target_pairs={{0,1},{1,2},{2,3},{3,4},{4,5},{5,6},{6,7},{7,8},{8,9},{9,10},{10,1... | collective-permute-start | bytes 2359304 | tf_op jit(solution)/shard_map/ppermute | solution.py:391
  9.6 5.9 %copy-start.1 = (bf16[256,128]{1,0:T(8,128)(2,1)S(1)}, bf16[256,128]{1,0:T(8,128)(2,1)}, u32[]{:S(2)}) copy-start(bf16[256,128]{1,0:T(8,128)(2,1)} %get-tuple-element.25.g_self) | copy-start | bytes 196612
  10.8 19.5 %collective-permute-start.4 = (bf16[768,128]{1,0:T(8,128)(2,1)S(1)}, bf16[768,128]{1,0:T(8,128)(2,1)S(1)}, u32[]{:S(2)}, u32[]{:S(2)}) collective-permute-start(bf16[768,128]{1,0:T(8,128)(2,1)S(1)} %get-tuple-element.29), channel_id=1, source_target_pairs={{0,2},{1,3},{2,4},{3,5},{4,6},{5,7},{6,8},{7,9},{8,10},{9,11},{10,... | collective-permute-start | bytes 589832 | tf_op jit(solution)/shard_map/ppermute | solution.py:391
  10.8 20.4 %collective-permute-start.5 = (bf16[768,128]{1,0:T(8,128)(2,1)S(1)}, bf16[768,128]{1,0:T(8,128)(2,1)S(1)}, u32[]{:S(2)}, u32[]{:S(2)}) collective-permute-start(bf16[768,128]{1,0:T(8,128)(2,1)S(1)} %get-tuple-element.30), channel_id=1, source_target_pairs={{0,14},{1,15},{2,0},{3,1},{4,2},{5,3},{6,4},{7,5},{8,6},{9,7},{10,... | collective-permute-start | bytes 589832 | tf_op jit(solution)/shard_map/ppermute | solution.py:391
  16.9 5.4 %collective-permute-start.3 = (bf16[512,128]{1,0:T(8,128)(2,1)S(1)}, bf16[512,128]{1,0:T(8,128)(2,1)S(1)}, u32[]{:S(2)}, u32[]{:S(2)}) collective-permute-start(bf16[512,128]{1,0:T(8,128)(2,1)S(1)} %choose.1.greens.g0), channel_id=1, source_target_pairs={{0,16},{1,17},{2,18},{3,19},{4,20},{5,21},{6,22},{7,23},{8,24},{9,... | collective-permute-start | bytes 393224 | tf_op jit(solution)/shard_map/ppermute | solution.py:391
  28.4 2.9 %collective-permute-start.7 = (f32[48,128]{1,0:T(8,128)S(1)}, f32[48,128]{1,0:T(8,128)S(1)}, u32[]{:S(2)}, u32[]{:S(2)}) collective-permute-start(f32[48,128]{1,0:T(8,128)S(1)} %join_back.1), channel_id=1, source_target_pairs={{0,15},{1,0},{2,1},{3,2},{4,3},{5,4},{6,5},{7,6},{8,7},{9,8},{10,9... | collective-permute-start | bytes 73736 | tf_op jit(solution)/shard_map/ppermute | solution.py:391
  32.0 3.9 %collective-permute-start.8 = (f32[48,128]{1,0:T(8,128)S(1)}, f32[48,128]{1,0:T(8,128)S(1)}, u32[]{:S(2)}, u32[]{:S(2)}) collective-permute-start(f32[48,128]{1,0:T(8,128)S(1)} %get-tuple-element.44), channel_id=1, source_target_pairs={{0,16},{1,17},{2,18},{3,19},{4,20},{5,21},{6,22},{7,23},{8,24},{9,... | collective-permute-start | bytes 73736 | tf_op jit(solution)/shard_map/ppermute | solution.py:391

commit v17 on v14

--- a/solution.py
+++ b/solution.py
@@ -132,6 +132,7 @@
             ]
             x = dot(jnp.concatenate(sides, axis=1), select)
             out[r * 32 : r * 32 + 256, :] = x.astype(BF)
+    far_right[funcs * 32 : funcs * 32 + 16, :] = jnp.zeros((16, 128), BF)
 
 
 def choose(count, win, g_self, g_before, g_after, g_far, out):
@@ -420,7 +421,7 @@
         functools.partial(far_tiles, count),
         "far_tiles",
         smem(2) + vmem(1),
-        [shape((far_rows, 128), BF), shape((far_rows, 128), BF)],
+        [shape((far_rows + 16, 128), BF), shape((far_rows, 128), BF)],
         (window, tile_list, coulomb3c),
         [pltpu.VMEM((128, 128), BF)],
         flops=1 << 36,

time: 36.8 us -> 36.9 us (level)
  no operation moved by 1% of the time
where the time goes in v17:
time: 36.9 us; the launch traced here: 36.7 us
  Pallas kernels  16.3 us (44%)
  starting transfers between devices  15.1 us (41%)
  waiting for transfers between devices  5.17 us (14%)
    pallas_call x9, Pallas kernels, call(): pl.pallas_call(kernel, name=name, in_specs=specs, out_specs=tuple((space...  16.3 us
    ppermute x9, starting transfers between devices, send(): return lax.ppermute(array, ('grp', 'row'), pairs)  15.1 us
    ppermute x9, waiting for transfers between devices, send(): return lax.ppermute(array, ('grp', 'row'), pairs)  5.17 us
  transfers between devices with their start and end apart: 9, of which 4 were waited for; matrix products, arithmetic and copies ran while one was open for 0% of the time, Pallas kernels for 34%

profile of v17, /device:TPU:0, one launch (start us, length us, event | category | flops | bytes accessed | tf_op | source)
XLA Modules:
  0.0 36.7 jit_solution(11472221675748369895)
XLA Ops:
  0.0 0.0 copy-start.2
  0.0 0.0 copy-start
  0.0 0.0 copy-start.3
  0.0 2.4 %first.1 = (bf16[256,128]{1,0:T(8,128)(2,1)}, bf16[272,128]{1,0:T(8,128)(2,1)}, bf16[304,128]{1,0:T(8,128)(2,1)}, bf16[288,128]{1,0:T(8,128)(2,1)}, bf16[24,128,128]{2,1,0:T(8,128)(2,1)}) custom-call(bf16[64,1024]{1,0:T(8,128)(2,1)} %occ.1, bf16[64,1024]{1,0:T(8,128)(2,1)} %virt.1, s32[1,4,4]{2,1,0:T(4,128)} %tiles.5, bf16[1,48,128,128]{3,2,1,0:T(8,128)(2,1)} %tensor.5), custom_call_target="tpu_custom_call" | custom-call | tf_op jit(solution)/shard_map/first/pallas_call | solution.py:368
  2.4 0.5 %collective-permute-start = (bf16[272,128]{1,0:T(8,128)(2,1)}, bf16[272,128]{1,0:T(8,128)(2,1)S(1)}, u32[]{:S(2)}, u32[]{:S(2)}) collective-permute-start(bf16[272,128]{1,0:T(8,128)(2,1)} %get-tuple-element.26), channel_id=1, source_target_pairs={{0,1},{1,2},{2,3},{3,4},{4,5},{5,6},{6,7},{7,8},{8,9},{9,10},{10,1... | collective-permute-start | bytes 208904 | tf_op jit(solution)/shard_map/ppermute | solution.py:391
  2.9 2.6 %collective-permute-start.2 = (bf16[288,128]{1,0:T(8,128)(2,1)}, bf16[288,128]{1,0:T(8,128)(2,1)S(1)}, u32[]{:S(2)}, u32[]{:S(2)}) collective-permute-start(bf16[288,128]{1,0:T(8,128)(2,1)} %get-tuple-element.28), channel_id=1, source_target_pairs={{0,2},{1,3},{2,4},{3,5},{4,6},{5,7},{6,8},{7,9},{8,10},{9,11},{10,... | collective-permute-start | bytes 221192 | tf_op jit(solution)/shard_map/ppermute | solution.py:391
  5.5 4.1 %collective-permute-start.1 = (bf16[304,128]{1,0:T(8,128)(2,1)}, bf16[304,128]{1,0:T(8,128)(2,1)S(1)}, u32[]{:S(2)}, u32[]{:S(2)}) collective-permute-start(bf16[304,128]{1,0:T(8,128)(2,1)} %get-tuple-element.27), channel_id=1, source_target_pairs={{0,15},{1,0},{2,1},{3,2},{4,3},{5,4},{6,5},{7,6},{8,7},{9,8},{10,9... | collective-permute-start | bytes 233480 | tf_op jit(solution)/shard_map/ppermute | solution.py:391
  9.6 0.0 collective-permute-start.6
  9.6 0.0 copy-done.3
  9.6 0.1 copy.8.win
  9.7 0.0 copy-done.2
  9.7 0.0 copy-done
  9.7 0.0 copy-start.1
  9.7 1.1 %far_tiles.1 = (bf16[784,128]{1,0:T(8,128)(2,1)S(1)}, bf16[768,128]{1,0:T(8,128)(2,1)S(1)}) custom-call(s32[16,4]{1,0:T(8,128)S(1)} %copy.8.win, s32[1,4,4]{2,1,0:T(4,128)S(1)} %copy-done.2, bf16[1,48,128,128]{3,2,1,0:T(8,128)(2,1)S(1)} %copy-done), custom_call_target="tpu_custom_call" | custom-call | flops 68719476736 | tf_op jit(solution)/shard_map/far_tiles/pallas_call | solution.py:368
  10.8 0.1 collective-permute-start.4
  10.9 0.0 collective-permute-done.g_before
  10.9 4.7 %collective-permute-start.5 = (bf16[768,128]{1,0:T(8,128)(2,1)S(1)}, bf16[768,128]{1,0:T(8,128)(2,1)S(1)}, u32[]{:S(2)}, u32[]{:S(2)}) collective-permute-start(bf16[768,128]{1,0:T(8,128)(2,1)S(1)} %get-tuple-element.30), channel_id=1, source_target_pairs={{0,14},{1,15},{2,0},{3,1},{4,2},{5,3},{6,4},{7,5},{8,6},{9,7},{10,... | collective-permute-start | bytes 589832 | tf_op jit(solution)/shard_map/ppermute | solution.py:391
  15.6 0.0 collective-permute-done.2.g_far
  15.6 0.0 collective-permute-done.1.g_after
  15.6 0.0 copy-done.1
  15.6 1.3 %choose.1.greens.g0 = bf16[512,128]{1,0:T(8,128)(2,1)S(1)} custom-call(s32[16,4]{1,0:T(8,128)S(1)} %copy.8.win, bf16[256,128]{1,0:T(8,128)(2,1)S(1)} %copy-done.1, bf16[272,128]{1,0:T(8,128)(2,1)S(1)} %collective-permute-done.g_before, bf16[304,128]{1,0:T(8,128)(2,1)S(1)} %collective-permute-done.1.g_after, bf16[288,128]{1,0:T(8,128)(2,1)S(1)} %collective-permute-done.2.g_far), custom_call_target="tpu_custom_call" | custom-call | tf_op jit(solution)/shard_map/choose/pallas_call | solution.py:368
  17.0 1.6 %collective-permute-start.3 = (bf16[512,128]{1,0:T(8,128)(2,1)S(1)}, bf16[512,128]{1,0:T(8,128)(2,1)S(1)}, u32[]{:S(2)}, u32[]{:S(2)}) collective-permute-start(bf16[512,128]{1,0:T(8,128)(2,1)S(1)} %choose.1.greens.g0), channel_id=1, source_target_pairs={{0,16},{1,17},{2,18},{3,19},{4,20},{5,21},{6,22},{7,23},{8,24},{9,... | collective-permute-start | bytes 393224 | tf_op jit(solution)/shard_map/ppermute | solution.py:391
  18.5 3.5 %dress_own.1 = (f32[48,48]{1,0:T(8,128)S(1)}, bf16[48,16384]{1,0:T(8,128)(2,1)S(1)}, bf16[48,16384]{1,0:T(8,128)(2,1)S(1)}, bf16[48,8192]{1,0:T(8,128)(2,1)S(1)}) custom-call(s32[16,4]{1,0:T(8,128)S(1)} %copy.8.win, s32[1,4,4]{2,1,0:T(4,128)S(1)} %copy-done.2, bf16[1,48,128,128]{3,2,1,0:T(8,128)(2,1)S(1)} %copy-done, bf16[512,128]{1,0:T(8,128)(2,1)S(1)} %choose.1.greens.g0), custom_call_target="tpu_custom_call" | custom-call | tf_op jit(solution)/shard_map/dress_own/pallas_call | solution.py:368
  22.1 0.3 collective-permute-done.3.greens.g1
  22.3 2.3 %dress_partner.1 = (bf16[48,16384]{1,0:T(8,128)(2,1)S(1)}, bf16[48,8192]{1,0:T(8,128)(2,1)S(1)}) custom-call(s32[16,4]{1,0:T(8,128)S(1)} %copy.8.win, s32[1,4,4]{2,1,0:T(4,128)S(1)} %copy-done.2, bf16[1,48,128,128]{3,2,1,0:T(8,128)(2,1)S(1)} %copy-done, bf16[512,128]{1,0:T(8,128)(2,1)S(1)} %collective-permute-done.3.greens.g1), custom_call_target="tpu_custom_call" | custom-call | tf_op jit(solution)/shard_map/dress_partner/pallas_call | solution.py:368
  24.7 1.5 %collective-permute-done.6.tensor = bf16[24,128,128]{2,1,0:T(8,128)(2,1)S(1)} collective-permute-done((bf16[24,128,128]{2,1,0:T(8,128)(2,1)}, bf16[24,128,128]{2,1,0:T(8,128)(2,1)S(1)}, u32[]{:S(2)}, u32[]{:S(2)}) %collective-permute-start.6) | collective-permute-done | bytes 786464 | tf_op jit(solution)/shard_map/ppermute | solution.py:391
  26.2 2.4 %join_back.1 = f32[48,128]{1,0:T(8,128)S(1)} custom-call(bf16[24,128,128]{2,1,0:T(8,128)(2,1)S(1)} %collective-permute-done.6.tensor, bf16[272,128]{1,0:T(8,128)(2,1)S(1)} %collective-permute-done.g_before, bf16[512,128]{1,0:T(8,128)(2,1)S(1)} %choose.1.greens.g0, bf16[512,128]{1,0:T(8,128)(2,1)S(1)} %collective-permute-done.3.greens.g1, ...), custom_call_target="tpu_custom_call" | custom-call | tf_op jit(solution)/shard_map/join_back/pallas_call | solution.py:368
  28.5 0.0 collective-permute-start.7
  28.5 1.8 %join.1.down = f32[96,128]{1,0:T(8,128)S(1)} custom-call(s32[16,4]{1,0:T(8,128)S(1)} %copy.8.win, bf16[24,128,128]{2,1,0:T(8,128)(2,1)S(1)} %collective-permute-done.6.tensor, bf16[272,128]{1,0:T(8,128)(2,1)S(1)} %collective-permute-done.g_before, bf16[48,16384]{1,0:T(8,128)(2,1)S(1)} %get-tuple-element.40.dressed0, ...), custom_call_target="tpu_custom_call" | custom-call | tf_op jit(solution)/shard_map/join/pallas_call | solution.py:368
  30.4 1.1 %collective-permute-done.5.from_right = bf16[768,128]{1,0:T(8,128)(2,1)S(1)} collective-permute-done((bf16[768,128]{1,0:T(8,128)(2,1)S(1)}, bf16[768,128]{1,0:T(8,128)(2,1)S(1)}, u32[]{:S(2)}, u32[]{:S(2)}) %collective-permute-start.5) | collective-permute-done | bytes 196640 | tf_op jit(solution)/shard_map/ppermute | solution.py:391
  31.4 0.0 collective-permute-done.4.from_left
  31.4 0.0 collective-permute-done.7.after
  31.4 0.7 %join_far.1 = (f32[48,128]{1,0:T(8,128)S(1)}, f32[48,128]{1,0:T(8,128)S(1)}) custom-call(bf16[48,8192]{1,0:T(8,128)(2,1)S(1)} %get-tuple-element.35.far0, bf16[48,8192]{1,0:T(8,128)(2,1)S(1)} %get-tuple-element.36.far1, bf16[784,128]{1,0:T(8,128)(2,1)S(1)} %collective-permute-done.4.from_left, bf16[768,128]{1,0:T(8,128)(2,1)S(1)} %collective-permute-done.5.from_right, ...), custom_call_target="tpu_custom_call" | custom-call | tf_op jit(solution)/shard_map/join_far/pallas_call | solution.py:368
  32.1 1.6 %collective-permute-start.8 = (f32[48,128]{1,0:T(8,128)S(1)}, f32[48,128]{1,0:T(8,128)S(1)}, u32[]{:S(2)}, u32[]{:S(2)}) collective-permute-start(f32[48,128]{1,0:T(8,128)S(1)} %get-tuple-element.44), channel_id=1, source_target_pairs={{0,16},{1,17},{2,18},{3,19},{4,20},{5,21},{6,22},{7,23},{8,24},{9,... | collective-permute-start | bytes 73736 | tf_op jit(solution)/shard_map/ppermute | solution.py:391
  33.7 2.3 %collective-permute-done.8.recv = f32[48,128]{1,0:T(8,128)S(1)} collective-permute-done((f32[48,128]{1,0:T(8,128)S(1)}, f32[48,128]{1,0:T(8,128)S(1)}, u32[]{:S(2)}, u32[]{:S(2)}) %collective-permute-start.8) | collective-permute-done | bytes 24608 | tf_op jit(solution)/shard_map/ppermute | solution.py:391
  36.0 0.7 %assemble.1 = f32[48,240]{1,0:T(8,128)} custom-call(f32[48,48]{1,0:T(8,128)S(1)} %get-tuple-element.34.polar0, f32[48,128]{1,0:T(8,128)S(1)} %get-tuple-element.43.own, f32[48,128]{1,0:T(8,128)S(1)} %collective-permute-done.8.recv), custom_call_target="tpu_custom_call" | custom-call | tf_op jit(solution)/shard_map/assemble/pallas_call | solution.py:368
Async XLA Ops:
  0.0 9.7 %copy-start.2 = (s32[1,4,4]{2,1,0:T(4,128)S(1)}, s32[1,4,4]{2,1,0:T(4,128)}, u32[]{:S(2)}) copy-start(s32[1,4,4]{2,1,0:T(4,128)} %tiles.5) | copy-start | bytes 196
  0.0 9.7 %copy-start = (bf16[1,48,128,128]{3,2,1,0:T(8,128)(2,1)S(1)}, bf16[1,48,128,128]{3,2,1,0:T(8,128)(2,1)}, u32[]{:S(2)}) copy-start(bf16[1,48,128,128]{3,2,1,0:T(8,128)(2,1)} %tensor.5) | copy-start | bytes 4718596
  0.0 9.6 %copy-start.3 = (s32[16,4]{0,1:T(4,128)S(1)}, s32[16,4]{0,1:T(4,128)}, u32[]{:S(2)}) copy-start(s32[16,4]{0,1:T(4,128)} %param.9) | copy-start | bytes 772
  2.4 8.5 %collective-permute-start = (bf16[272,128]{1,0:T(8,128)(2,1)}, bf16[272,128]{1,0:T(8,128)(2,1)S(1)}, u32[]{:S(2)}, u32[]{:S(2)}) collective-permute-start(bf16[272,128]{1,0:T(8,128)(2,1)} %get-tuple-element.26), channel_id=1, source_target_pairs={{0,1},{1,2},{2,3},{3,4},{4,5},{5,6},{6,7},{7,8},{8,9},{9,10},{10,1... | collective-permute-start | bytes 208904 | tf_op jit(solution)/shard_map/ppermute | solution.py:391
  2.9 12.7 %collective-permute-start.2 = (bf16[288,128]{1,0:T(8,128)(2,1)}, bf16[288,128]{1,0:T(8,128)(2,1)S(1)}, u32[]{:S(2)}, u32[]{:S(2)}) collective-permute-start(bf16[288,128]{1,0:T(8,128)(2,1)} %get-tuple-element.28), channel_id=1, source_target_pairs={{0,2},{1,3},{2,4},{3,5},{4,6},{5,7},{6,8},{7,9},{8,10},{9,11},{10,... | collective-permute-start | bytes 221192 | tf_op jit(solution)/shard_map/ppermute | solution.py:391
  5.5 10.1 %collective-permute-start.1 = (bf16[304,128]{1,0:T(8,128)(2,1)}, bf16[304,128]{1,0:T(8,128)(2,1)S(1)}, u32[]{:S(2)}, u32[]{:S(2)}) collective-permute-start(bf16[304,128]{1,0:T(8,128)(2,1)} %get-tuple-element.27), channel_id=1, source_target_pairs={{0,15},{1,0},{2,1},{3,2},{4,3},{5,4},{6,5},{7,6},{8,7},{9,8},{10,9... | collective-permute-start | bytes 233480 | tf_op jit(solution)/shard_map/ppermute | solution.py:391
  9.6 16.6 %collective-permute-start.6 = (bf16[24,128,128]{2,1,0:T(8,128)(2,1)}, bf16[24,128,128]{2,1,0:T(8,128)(2,1)S(1)}, u32[]{:S(2)}, u32[]{:S(2)}) collective-permute-start(bf16[24,128,128]{2,1,0:T(8,128)(2,1)} %get-tuple-element.37), channel_id=1, source_target_pairs={{0,1},{1,2},{2,3},{3,4},{4,5},{5,6},{6,7},{7,8},{8,9},{9,10},{10,1... | collective-permute-start | bytes 2359304 | tf_op jit(solution)/shard_map/ppermute | solution.py:391
  9.7 5.9 %copy-start.1 = (bf16[256,128]{1,0:T(8,128)(2,1)S(1)}, bf16[256,128]{1,0:T(8,128)(2,1)}, u32[]{:S(2)}) copy-start(bf16[256,128]{1,0:T(8,128)(2,1)} %get-tuple-element.25.g_self) | copy-start | bytes 196612
  10.8 20.6 %collective-permute-start.4 = (bf16[784,128]{1,0:T(8,128)(2,1)S(1)}, bf16[784,128]{1,0:T(8,128)(2,1)S(1)}, u32[]{:S(2)}, u32[]{:S(2)}) collective-permute-start(bf16[784,128]{1,0:T(8,128)(2,1)S(1)} %get-tuple-element.29), channel_id=1, source_target_pairs={{0,2},{1,3},{2,4},{3,5},{4,6},{5,7},{6,8},{7,9},{8,10},{9,11},{10,... | collective-permute-start | bytes 602120 | tf_op jit(solution)/shard_map/ppermute | solution.py:391
  10.9 20.5 %collective-permute-start.5 = (bf16[768,128]{1,0:T(8,128)(2,1)S(1)}, bf16[768,128]{1,0:T(8,128)(2,1)S(1)}, u32[]{:S(2)}, u32[]{:S(2)}) collective-permute-start(bf16[768,128]{1,0:T(8,128)(2,1)S(1)} %get-tuple-element.30), channel_id=1, source_target_pairs={{0,14},{1,15},{2,0},{3,1},{4,2},{5,3},{6,4},{7,5},{8,6},{9,7},{10,... | collective-permute-start | bytes 589832 | tf_op jit(solution)/shard_map/ppermute | solution.py:391
  17.0 5.4 %collective-permute-start.3 = (bf16[512,128]{1,0:T(8,128)(2,1)S(1)}, bf16[512,128]{1,0:T(8,128)(2,1)S(1)}, u32[]{:S(2)}, u32[]{:S(2)}) collective-permute-start(bf16[512,128]{1,0:T(8,128)(2,1)S(1)} %choose.1.greens.g0), channel_id=1, source_target_pairs={{0,16},{1,17},{2,18},{3,19},{4,20},{5,21},{6,22},{7,23},{8,24},{9,... | collective-permute-start | bytes 393224 | tf_op jit(solution)/shard_map/ppermute | solution.py:391
  28.5 2.9 %collective-permute-start.7 = (f32[48,128]{1,0:T(8,128)S(1)}, f32[48,128]{1,0:T(8,128)S(1)}, u32[]{:S(2)}, u32[]{:S(2)}) collective-permute-start(f32[48,128]{1,0:T(8,128)S(1)} %join_back.1), channel_id=1, source_target_pairs={{0,15},{1,0},{2,1},{3,2},{4,3},{5,4},{6,5},{7,6},{8,7},{9,8},{10,9... | collective-permute-start | bytes 73736 | tf_op jit(solution)/shard_map/ppermute | solution.py:391
  32.1 3.9 %collective-permute-start.8 = (f32[48,128]{1,0:T(8,128)S(1)}, f32[48,128]{1,0:T(8,128)S(1)}, u32[]{:S(2)}, u32[]{:S(2)}) collective-permute-start(f32[48,128]{1,0:T(8,128)S(1)} %get-tuple-element.44), channel_id=1, source_target_pairs={{0,16},{1,17},{2,18},{3,19},{4,20},{5,21},{6,22},{7,23},{8,24},{9,... | collective-permute-start | bytes 73736 | tf_op jit(solution)/shard_map/ppermute | solution.py:391
